TPU v7x, 32 devices: a whole 2x2x4 slice. The times are simulated.
32 devices in a mesh: seq: 8 (over z, y), fsdp: 4 (over x, core).
Axes of the slice: x: 2, y: 2, z: 4, core: 2. Of those that a mesh axis runs over, the one named last changes fastest.
Arguments:
- block_input: bfloat16 [8, 512, 2048], P('fsdp', 'seq'), may hold values from -6 to 6
- seq_lengths: int32 [8, 2], replicated, may hold values from 0 to 512, as said below
- mixer_gain: bfloat16 [2048], P(('seq', 'fsdp')), may hold values from 0.5 to 1.5
- branch_weight: bfloat16 [2560, 2048], P(('seq', 'fsdp')), may hold values from -0.125 to 0.125
- recur_weight: bfloat16 [2560, 2048], P(('seq', 'fsdp')), may hold values from -0.125 to 0.125
- conv_kernel: bfloat16 [2560, 4], P(('seq', 'fsdp')), may hold values from -3 to 3
- conv_bias: bfloat16 [2560], P(('seq', 'fsdp')), may hold values from -3 to 3
- recur_gate_weight: bfloat16 [2560, 160], P(('seq', 'fsdp')), may hold values from -0.5 to 0.5
- recur_gate_bias: bfloat16 [2560], P(('seq', 'fsdp')), may hold values from -3 to 3
- input_gate_weight: bfloat16 [2560, 160], P(('seq', 'fsdp')), may hold values from -0.5 to 0.5
- input_gate_bias: bfloat16 [2560], P(('seq', 'fsdp')), may hold values from -3 to 3
- decay_param: bfloat16 [2560], P(('seq', 'fsdp')), may hold values from 3 to 16
- mixer_weight: bfloat16 [2048, 2560], P(('seq', 'fsdp')), may hold values from -0.25 to 0.25
- mlp_gain: bfloat16 [2048], P(('seq', 'fsdp')), may hold values from 0.5 to 1.5
- gate_weight: bfloat16 [6144, 2048], P(('seq', 'fsdp')), may hold values from -0.125 to 0.125
- up_weight: bfloat16 [6144, 2048], P(('seq', 'fsdp')), may hold values from -0.125 to 0.125
- down_weight: bfloat16 [2048, 6144], P(('seq', 'fsdp')), may hold values from -0.109375 to 0.109375
- cotangent: bfloat16 [8, 512, 2048], P('fsdp', 'seq'), may hold values from -6 to 6
Outputs:
- block_output: bfloat16 [8, 512, 2048], P('fsdp', 'seq')
- input_grad: bfloat16 [8, 512, 2048], P('fsdp', 'seq')
- mixer_gain_grad: float32 [2048], P(('seq', 'fsdp'))
- branch_weight_grad: float32 [2560, 2048], P(('seq', 'fsdp'))
- recur_weight_grad: float32 [2560, 2048], P(('seq', 'fsdp'))
- conv_kernel_grad: float32 [2560, 4], P(('seq', 'fsdp'))
- conv_bias_grad: float32 [2560], P(('seq', 'fsdp'))
- recur_gate_weight_grad: float32 [2560, 160], P(('seq', 'fsdp'))
- recur_gate_bias_grad: float32 [2560], P(('seq', 'fsdp'))
- input_gate_weight_grad: float32 [2560, 160], P(('seq', 'fsdp'))
- input_gate_bias_grad: float32 [2560], P(('seq', 'fsdp'))
- decay_param_grad: float32 [2560], P(('seq', 'fsdp'))
- mixer_weight_grad: float32 [2048, 2560], P(('seq', 'fsdp'))
- mlp_gain_grad: float32 [2048], P(('seq', 'fsdp'))
- gate_weight_grad: float32 [6144, 2048], P(('seq', 'fsdp'))
- up_weight_grad: float32 [6144, 2048], P(('seq', 'fsdp'))
- down_weight_grad: float32 [2048, 6144], P(('seq', 'fsdp'))
Inputs may be any that keep to these rules, and one draw needn't show every extreme that they name: `seq_lengths`: each row lists the lengths of the sequences packed one after another into its 512 positions, in order, followed by zeros; the positive ones sum to 512 and are 128 or more. In each aligned block of 2 rows one row holds a single sequence of 512 positions.
All inputs are finite; a program needn't handle non-finite values.
Results may differ from a plain program's by a relative error of at most 0.025.
Values may be sent and summed in bfloat16 or wider, within the bound.
No kernel may reach another device: no remote copies, remote signals or barrier semaphores. Data moves between devices by JAX's collectives and lax.ppermute only.
A program may use at most 256 MiB of HBM per device.

v0:
```python
import jax
import jax.numpy as jnp
from jax import lax
from jax.sharding import PartitionSpec as P

CONV = 4


epsilon = 1e-06
decay_scale = 8.0


def passed_along(value, axis, steps):
    count = lax.axis_size(axis)
    initial, last = (max(0, -steps), min(count, count - steps))
    return lax.ppermute(value, axis, [(source, source + steps) for source in range(initial, last)])


def carried_in(value, axis, combine, identity, reverse):
    length, place = (lax.axis_size(axis), lax.axis_index(axis))
    everything = jax.tree.map(
        lambda part, kind: lax.all_gather(part.astype(kind), axis),
        value,
        (jnp.bfloat16, jnp.bfloat16),
    )
    start = jax.tree.map(
        lambda part, zero: jnp.broadcast_to(jnp.asarray(zero, part.dtype), part.shape),
        value,
        identity,
    )

    def lap(k, before):
        at = length - 1 - k if reverse else k
        reached = at > place if reverse else at < place
        new = combine(
            before, jax.tree.map(lambda part, own: part[at].astype(own.dtype), everything, value)
        )
        return jax.tree.map(lambda a, b: jnp.where(reached, a, b), new, before)

    return lax.fori_loop(0, length, lap, start)


def rms_scale(values, gain_vec):
    return (
        values * lax.rsqrt(jnp.mean(values * values, axis=-1, keepdims=True) + epsilon) * gain_vec
    )


def combine(earlier, later_pair):
    return (earlier[0] * later_pair[0], later_pair[0] * earlier[1] + later_pair[1])


def recur_terms(rate_pre, gate_pre, conv_vals, decay_param, first_mask):
    rate_open = jax.nn.sigmoid(rate_pre)
    log_decay = -decay_scale * rate_open * jax.nn.softplus(-decay_param)
    decay_gate = jnp.exp(log_decay) * (1.0 - first_mask)[..., None]
    inject = jnp.sqrt(-jnp.expm1(2.0 * log_decay)) * jax.nn.sigmoid(gate_pre) * conv_vals
    return (decay_gate, inject)


def mlp_act(gate_val, up_val):
    return jax.nn.gelu(gate_val) * up_val


def project(left_rows, weight):
    return lax.dot_general(
        left_rows, weight, (((1,), (1,)), ((), ())), preferred_element_type=jnp.float32
    )


def back_project(grad_rows, weight):
    return jnp.dot(grad_rows, weight, preferred_element_type=jnp.float32)


def outer_full(grad_rows, left_rows):
    return lax.dot_general(
        grad_rows, left_rows, (((0,), (0,)), ((), ())), preferred_element_type=jnp.float32
    )


def segment_masks(lengths, span_len):
    margin = CONV - 1
    offsets = jnp.cumsum(lengths, axis=1, dtype=jnp.int32) - lengths
    is_live = lengths > 0
    places = lax.axis_index("seq") * span_len + jnp.arange(
        -margin, span_len + margin, dtype=jnp.int32
    )
    covered = is_live[:, :, None] & (offsets[:, :, None] <= places[None, None, :])
    segment = jnp.sum(covered.astype(jnp.int32), axis=1, dtype=jnp.int32) - 1
    starting = is_live[:, :, None] & (offsets[:, :, None] == places[None, None, :])
    first_mask = jnp.any(starting, axis=1)[:, margin : margin + span_len].astype(jnp.float32)
    centre = segment[:, margin : margin + span_len]
    same_back = [
        (segment[:, margin - lag_index : margin - lag_index + span_len] == centre).astype(
            jnp.float32
        )[..., None]
        for lag_index in range(CONV)
    ]
    same_ahead = [
        (segment[:, margin + lag_index : margin + lag_index + span_len] == centre).astype(
            jnp.float32
        )[..., None]
        for lag_index in range(CONV)
    ]
    return (first_mask, same_back, same_ahead)


def mixer_forward(normed, weights, seg_masks, row_count, span_len):
    branch_w, recur_w, kernel, offset, rate_w, rate_b, input_w, input_b, decay_vec = weights
    first_mask, same_back, same_ahead = seg_masks
    margin = CONV - 1
    tokens = normed.shape[0]
    channels = branch_w.shape[0]
    block_size = rate_w.shape[1]
    block_count = channels // block_size
    branch = project(normed, branch_w)
    branch_act, pull_gelu = jax.vjp(jax.nn.gelu, branch)
    recur_in = project(normed, recur_w).astype(jnp.bfloat16).reshape(row_count, span_len, channels)
    kernel_wide = kernel.astype(jnp.float32)
    rim_in = passed_along(recur_in[:, span_len - margin :], "seq", 1)
    padded_in = jnp.concatenate([rim_in, recur_in], axis=1).astype(jnp.float32)
    conv_acc = jnp.broadcast_to(offset.astype(jnp.float32), (row_count, span_len, channels))
    for lag_index in range(CONV):
        conv_acc = (
            conv_acc
            + kernel_wide[:, lag_index]
            * padded_in[:, margin - lag_index : margin - lag_index + span_len]
            * same_back[lag_index]
        )
    conv_out = conv_acc.astype(jnp.bfloat16)
    conv_wide = conv_out.astype(jnp.float32)
    blocks = conv_out.reshape(tokens, block_count, block_size)
    rate_blocks = rate_w.reshape(block_count, block_size, block_size)
    input_blocks = input_w.reshape(block_count, block_size, block_size)
    rate_pre = jnp.einsum(
        "nbi,bji->nbj", blocks, rate_blocks, preferred_element_type=jnp.float32
    ).reshape(row_count, span_len, channels) + rate_b.astype(jnp.float32)
    gate_pre = jnp.einsum(
        "nbi,bji->nbj", blocks, input_blocks, preferred_element_type=jnp.float32
    ).reshape(row_count, span_len, channels) + input_b.astype(jnp.float32)

    def local_terms(rate_arg, gate_arg, conv_arg, decay_arg):
        return recur_terms(rate_arg, gate_arg, conv_arg, decay_arg, first_mask)

    (decay_gate, inject), pull_terms = jax.vjp(
        local_terms, rate_pre, gate_pre, conv_wide, decay_vec.astype(jnp.float32)
    )
    decay_prod, partial_value = lax.associative_scan(combine, (decay_gate, inject), axis=1)
    unit_carry = jnp.ones((row_count, channels), jnp.float32)
    zero_carry = jnp.zeros((row_count, channels), jnp.float32)
    carry_in = carried_in(
        (decay_prod[:, -1], partial_value[:, -1]), "seq", combine, (unit_carry, zero_carry), False
    )[1]
    hidden_state = partial_value + decay_prod * carry_in[:, None, :]
    state_flat = hidden_state.reshape(tokens, channels)
    mixed_out = (state_flat * branch_act).astype(jnp.bfloat16)
    kept_state = (
        branch_act,
        pull_gelu,
        state_flat,
        decay_gate,
        carry_in,
        hidden_state,
        pull_terms,
        padded_in,
        conv_wide,
        rate_blocks,
        input_blocks,
        kernel_wide,
    )
    return (mixed_out, kept_state)


def mixer_backward(grad_mixed, kept_state, seg_masks, row_count, span_len):
    (
        branch_act,
        pull_gelu,
        state_flat,
        decay_gate,
        carry_in,
        hidden_state,
        pull_terms,
        padded_in,
        conv_wide,
        rate_blocks,
        input_blocks,
        kernel_wide,
    ) = kept_state
    first_mask, same_back, same_ahead = seg_masks
    margin = CONV - 1
    tokens, channels = state_flat.shape
    block_count, block_size = (rate_blocks.shape[0], rate_blocks.shape[1])
    grad_branch = pull_gelu(grad_mixed * state_flat)[0].astype(jnp.bfloat16)
    grad_state = (grad_mixed * branch_act).reshape(row_count, span_len, channels)
    next_decay = jnp.concatenate([decay_gate[:, 1:], jnp.ones_like(decay_gate[:, :1])], axis=1)
    suffix_prod, suffix_sum = lax.associative_scan(
        combine, (next_decay, grad_state), axis=1, reverse=True
    )
    lead_decay = decay_gate[:, 0]
    unit_carry = jnp.ones((row_count, channels), jnp.float32)
    zero_carry = jnp.zeros((row_count, channels), jnp.float32)
    carry_back = carried_in(
        (lead_decay * suffix_prod[:, 0], lead_decay * suffix_sum[:, 0]),
        "seq",
        combine,
        (unit_carry, zero_carry),
        True,
    )[1]
    grad_total = suffix_sum + suffix_prod * carry_back[:, None, :]
    prev_state = jnp.concatenate([carry_in[:, None, :], hidden_state[:, :-1]], axis=1)
    grad_rate_pre, grad_gate_pre, grad_conv_direct, grad_decay = pull_terms(
        (grad_total * prev_state, grad_total)
    )
    grad_rate_blocks = grad_rate_pre.reshape(tokens, block_count, block_size)
    grad_input_blocks = grad_gate_pre.reshape(tokens, block_count, block_size)
    conv_blocks = conv_wide.reshape(tokens, block_count, block_size)
    through_gates = jnp.einsum(
        "nbj,bji->nbi",
        grad_rate_blocks,
        rate_blocks.astype(jnp.float32),
        precision=lax.Precision.HIGHEST,
    ) + jnp.einsum(
        "nbj,bji->nbi",
        grad_input_blocks,
        input_blocks.astype(jnp.float32),
        precision=lax.Precision.HIGHEST,
    )
    grad_conv = grad_conv_direct + through_gates.reshape(row_count, span_len, channels)
    grad_rate_weight = jnp.einsum(
        "nbj,nbi->bji", grad_rate_blocks, conv_blocks, precision=lax.Precision.HIGHEST
    ).reshape(channels, block_size)
    grad_input_weight = jnp.einsum(
        "nbj,nbi->bji", grad_input_blocks, conv_blocks, precision=lax.Precision.HIGHEST
    ).reshape(channels, block_size)
    grad_rate_bias = jnp.sum(grad_rate_pre, axis=(0, 1))
    grad_input_bias = jnp.sum(grad_gate_pre, axis=(0, 1))
    rim_back = passed_along(grad_conv[:, :margin].astype(jnp.bfloat16), "seq", -1).astype(
        jnp.float32
    )
    grad_ahead = jnp.concatenate([grad_conv, rim_back], axis=1)
    grad_recur_wide = jnp.zeros_like(grad_conv)
    kernel_terms = []
    for lag_index in range(CONV):
        grad_recur_wide = (
            grad_recur_wide
            + kernel_wide[:, lag_index]
            * grad_ahead[:, lag_index : lag_index + span_len]
            * same_ahead[lag_index]
        )
        kernel_terms.append(
            jnp.sum(
                grad_conv
                * padded_in[:, margin - lag_index : margin - lag_index + span_len]
                * same_back[lag_index],
                axis=(0, 1),
            )
        )
    grad_kernel = jnp.stack(kernel_terms, axis=1)
    grad_conv_offset = jnp.sum(grad_conv, axis=(0, 1))
    grad_recur = grad_recur_wide.reshape(tokens, channels).astype(jnp.bfloat16)
    small_grads = (
        grad_kernel,
        grad_conv_offset,
        grad_rate_weight,
        grad_rate_bias,
        grad_input_weight,
        grad_input_bias,
        grad_decay,
    )
    return (grad_branch, grad_recur, small_grads)


def shards(
    block_input,
    seq_lengths,
    mixer_gain,
    branch_weight,
    recur_weight,
    conv_kernel,
    conv_bias,
    recur_gate_weight,
    recur_gate_bias,
    input_gate_weight,
    input_gate_bias,
    decay_param,
    mixer_weight,
    mlp_gain,
    gate_weight,
    up_weight,
    down_weight,
    cotangent,
):
    rows_dev, span_len, model_width = block_input.shape
    tokens = rows_dev * span_len
    seq_count = lax.axis_size("seq")
    fsdp_count = lax.axis_size("fsdp")
    fsdp_index = lax.axis_index("fsdp")
    low_count = seq_count // fsdp_count

    def column_view(weight):
        piece_rows, width = weight.shape
        return jnp.transpose(
            weight.reshape(piece_rows, fsdp_count, width // fsdp_count), (1, 0, 2)
        )[:, None]

    def gain_view(gain_vec):
        return jnp.broadcast_to(gain_vec[None, None, :], (fsdp_count, 1, gain_vec.shape[0]))

    fetched = (
        lax.all_gather(branch_weight[None, None], "seq", axis=1, tiled=True),
        lax.all_gather(recur_weight[None, None], "seq", axis=1, tiled=True),
        lax.all_gather(gate_weight[None, None], "seq", axis=1, tiled=True),
        lax.all_gather(up_weight[None, None], "seq", axis=1, tiled=True),
        lax.all_gather(conv_kernel[None, None], "seq", axis=1, tiled=True),
        lax.all_gather(conv_bias[None, None], "seq", axis=1, tiled=True),
        lax.all_gather(recur_gate_weight[None, None], "seq", axis=1, tiled=True),
        lax.all_gather(recur_gate_bias[None, None], "seq", axis=1, tiled=True),
        lax.all_gather(input_gate_weight[None, None], "seq", axis=1, tiled=True),
        lax.all_gather(input_gate_bias[None, None], "seq", axis=1, tiled=True),
        lax.all_gather(decay_param[None, None], "seq", axis=1, tiled=True),
        lax.all_gather(column_view(mixer_weight), "seq", axis=1, tiled=True),
        lax.all_gather(column_view(down_weight), "seq", axis=1, tiled=True),
        lax.all_gather(gain_view(mixer_gain), "seq", axis=1, tiled=True),
        lax.all_gather(gain_view(mlp_gain), "seq", axis=1, tiled=True),
    )
    row_parts = [
        member.reshape((fsdp_count, low_count, 1) + member.shape[2:]) for member in fetched[:11]
    ]
    col_parts = [
        member.reshape((fsdp_count, seq_count, 1) + member.shape[2:]) for member in fetched[11:]
    ]
    swapped = (
        lax.all_to_all(row_parts[0], "fsdp", split_axis=0, concat_axis=2, tiled=True),
        lax.all_to_all(row_parts[1], "fsdp", split_axis=0, concat_axis=2, tiled=True),
        lax.all_to_all(row_parts[2], "fsdp", split_axis=0, concat_axis=2, tiled=True),
        lax.all_to_all(row_parts[3], "fsdp", split_axis=0, concat_axis=2, tiled=True),
        lax.all_to_all(row_parts[4], "fsdp", split_axis=0, concat_axis=2, tiled=True),
        lax.all_to_all(row_parts[5], "fsdp", split_axis=0, concat_axis=2, tiled=True),
        lax.all_to_all(row_parts[6], "fsdp", split_axis=0, concat_axis=2, tiled=True),
        lax.all_to_all(row_parts[7], "fsdp", split_axis=0, concat_axis=2, tiled=True),
        lax.all_to_all(row_parts[8], "fsdp", split_axis=0, concat_axis=2, tiled=True),
        lax.all_to_all(row_parts[9], "fsdp", split_axis=0, concat_axis=2, tiled=True),
        lax.all_to_all(row_parts[10], "fsdp", split_axis=0, concat_axis=2, tiled=True),
        lax.all_to_all(col_parts[0], "fsdp", split_axis=0, concat_axis=2, tiled=True),
        lax.all_to_all(col_parts[1], "fsdp", split_axis=0, concat_axis=2, tiled=True),
        lax.all_to_all(col_parts[2], "fsdp", split_axis=0, concat_axis=2, tiled=True),
        lax.all_to_all(col_parts[3], "fsdp", split_axis=0, concat_axis=2, tiled=True),
    )
    own_parts = [member.reshape((-1,) + member.shape[4:]) for member in swapped[:11]]
    (
        branch_q,
        recur_q,
        gate_q,
        up_q,
        kernel_q,
        offset_q,
        rate_q,
        rate_bias_q,
        input_q,
        input_bias_q,
        decay_q,
    ) = own_parts
    mixer_cols = swapped[11].reshape(model_width, -1)
    down_cols = swapped[12].reshape(model_width, -1)
    gain_one_wide = swapped[13].reshape(-1).astype(jnp.float32)
    gain_two_wide = swapped[14].reshape(-1).astype(jnp.float32)
    input_all, cot_all = (
        lax.all_gather(block_input, "fsdp", axis=0, tiled=True),
        lax.all_gather(cotangent, "fsdp", axis=0, tiled=True),
    )
    group_rows = input_all.shape[0]
    total_tokens = group_rows * span_len
    own_start = fsdp_index * tokens
    seg_masks = segment_masks(seq_lengths, span_len)
    flat_all = input_all.reshape(total_tokens, model_width).astype(jnp.float32)
    normed = rms_scale(flat_all, gain_one_wide).astype(jnp.bfloat16)
    mixed_out, kept_state = mixer_forward(
        normed,
        (
            branch_q,
            recur_q,
            kernel_q,
            offset_q,
            rate_q,
            rate_bias_q,
            input_q,
            input_bias_q,
            decay_q,
        ),
        seg_masks,
        group_rows,
        span_len,
    )
    residual = flat_all + lax.psum(
        project(mixed_out, mixer_cols).astype(jnp.bfloat16), "fsdp"
    ).astype(jnp.float32)
    normed_two_wide, pull_norm_two = jax.vjp(rms_scale, residual, gain_two_wide)
    normed_two = normed_two_wide.astype(jnp.bfloat16)
    gate_val = project(normed_two, gate_q)
    up_val = project(normed_two, up_q)
    hidden_wide, pull_mlp = jax.vjp(mlp_act, gate_val, up_val)
    hidden = hidden_wide.astype(jnp.bfloat16)
    down_own = lax.psum_scatter(
        project(hidden, down_cols).astype(jnp.bfloat16), "fsdp", scatter_dimension=0, tiled=True
    ).astype(jnp.float32)
    residual_own = lax.dynamic_slice_in_dim(residual, own_start, tokens, 0)
    block_output = (
        (residual_own + down_own).astype(jnp.bfloat16).reshape(rows_dev, span_len, model_width)
    )
    grad_out = cot_all.reshape(total_tokens, model_width)
    grad_hidden = back_project(grad_out, down_cols)
    grad_gate_wide, grad_up_wide = pull_mlp(grad_hidden)
    grad_gate = grad_gate_wide.astype(jnp.bfloat16)
    grad_up = grad_up_wide.astype(jnp.bfloat16)
    grad_normed_two = lax.psum(
        (back_project(grad_gate, gate_q) + back_project(grad_up, up_q)).astype(jnp.bfloat16), "fsdp"
    ).astype(jnp.float32)
    grad_resid_norm = pull_norm_two(grad_normed_two)[0]
    grad_two_own = lax.dynamic_slice_in_dim(grad_normed_two, own_start, tokens, 0)
    unit_two = residual_own * lax.rsqrt(
        jnp.mean(residual_own * residual_own, axis=-1, keepdims=True) + epsilon
    )
    gain_two_term = jnp.sum(grad_two_own * unit_two, axis=0)
    grad_residual = grad_out.astype(jnp.float32) + grad_resid_norm
    grad_mix = grad_residual.astype(jnp.bfloat16)
    grad_mixed = back_project(grad_mix, mixer_cols)
    grad_branch, grad_recur, small_grads = mixer_backward(
        grad_mixed, kept_state, seg_masks, group_rows, span_len
    )
    (
        grad_kernel,
        grad_conv_offset,
        grad_rate_weight,
        grad_rate_bias,
        grad_input_weight,
        grad_input_bias,
        grad_decay,
    ) = small_grads
    grad_normed_own = lax.psum_scatter(
        (back_project(grad_branch, branch_q) + back_project(grad_recur, recur_q)).astype(
            jnp.bfloat16
        ),
        "fsdp",
        scatter_dimension=0,
        tiled=True,
    ).astype(jnp.float32)
    input_own = lax.dynamic_slice_in_dim(flat_all, own_start, tokens, 0)
    pull_norm_one = jax.vjp(rms_scale, input_own, gain_one_wide)[1]
    grad_in_norm, gain_one_term = pull_norm_one(grad_normed_own)
    grad_residual_own = lax.dynamic_slice_in_dim(grad_residual, own_start, tokens, 0)
    input_grad = (
        (grad_residual_own + grad_in_norm)
        .astype(jnp.bfloat16)
        .reshape(rows_dev, span_len, model_width)
    )
    row_terms = [
        outer_full(grad_branch, normed),
        outer_full(grad_recur, normed),
        outer_full(grad_gate, normed_two),
        outer_full(grad_up, normed_two),
        grad_kernel,
        grad_conv_offset,
        grad_rate_weight,
        grad_rate_bias,
        grad_input_weight,
        grad_input_bias,
        grad_decay,
    ]
    row_sent = [
        member.reshape((1, low_count, fsdp_count, member.shape[0] // seq_count) + member.shape[1:])
        for member in row_terms
    ]
    col_terms = [outer_full(grad_mix, mixed_out), outer_full(grad_out, hidden)]
    col_sent = [
        member.reshape(
            1, seq_count, fsdp_count, member.shape[0] // (seq_count * fsdp_count), member.shape[1]
        )
        for member in col_terms
    ]
    gain_sent = [
        member.reshape(1, seq_count, fsdp_count, -1) for member in (gain_one_term, gain_two_term)
    ]
    received = (
        lax.all_to_all(
            row_sent[0].astype(jnp.bfloat16), "fsdp", split_axis=2, concat_axis=0, tiled=True
        ).astype(jnp.float32),
        lax.all_to_all(
            row_sent[1].astype(jnp.bfloat16), "fsdp", split_axis=2, concat_axis=0, tiled=True
        ).astype(jnp.float32),
        lax.all_to_all(
            row_sent[2].astype(jnp.bfloat16), "fsdp", split_axis=2, concat_axis=0, tiled=True
        ).astype(jnp.float32),
        lax.all_to_all(
            row_sent[3].astype(jnp.bfloat16), "fsdp", split_axis=2, concat_axis=0, tiled=True
        ).astype(jnp.float32),
        lax.all_to_all(
            row_sent[4].astype(jnp.bfloat16), "fsdp", split_axis=2, concat_axis=0, tiled=True
        ).astype(jnp.float32),
        lax.all_to_all(
            row_sent[5].astype(jnp.bfloat16), "fsdp", split_axis=2, concat_axis=0, tiled=True
        ).astype(jnp.float32),
        lax.all_to_all(
            row_sent[6].astype(jnp.bfloat16), "fsdp", split_axis=2, concat_axis=0, tiled=True
        ).astype(jnp.float32),
        lax.all_to_all(
            row_sent[7].astype(jnp.bfloat16), "fsdp", split_axis=2, concat_axis=0, tiled=True
        ).astype(jnp.float32),
        lax.all_to_all(
            row_sent[8].astype(jnp.bfloat16), "fsdp", split_axis=2, concat_axis=0, tiled=True
        ).astype(jnp.float32),
        lax.all_to_all(
            row_sent[9].astype(jnp.bfloat16), "fsdp", split_axis=2, concat_axis=0, tiled=True
        ).astype(jnp.float32),
        lax.all_to_all(
            row_sent[10].astype(jnp.bfloat16), "fsdp", split_axis=2, concat_axis=0, tiled=True
        ).astype(jnp.float32),
        lax.all_to_all(
            col_sent[0].astype(jnp.bfloat16), "fsdp", split_axis=2, concat_axis=0, tiled=True
        ).astype(jnp.float32),
        lax.all_to_all(
            col_sent[1].astype(jnp.bfloat16), "fsdp", split_axis=2, concat_axis=0, tiled=True
        ).astype(jnp.float32),
        lax.all_to_all(
            gain_sent[0].astype(jnp.bfloat16), "fsdp", split_axis=2, concat_axis=0, tiled=True
        ).astype(jnp.float32),
        lax.all_to_all(
            gain_sent[1].astype(jnp.bfloat16), "fsdp", split_axis=2, concat_axis=0, tiled=True
        ).astype(jnp.float32),
    )
    row_back = [member.reshape((1, seq_count) + member.shape[3:]) for member in received[:11]]
    gain_back = [jnp.sum(member, axis=0, keepdims=True) for member in received[13:]]
    totals = (
        lax.psum_scatter(
            row_back[0].astype(jnp.bfloat16), "seq", scatter_dimension=1, tiled=True
        ).astype(jnp.float32),
        lax.psum_scatter(
            row_back[1].astype(jnp.bfloat16), "seq", scatter_dimension=1, tiled=True
        ).astype(jnp.float32),
        lax.psum_scatter(
            row_back[2].astype(jnp.bfloat16), "seq", scatter_dimension=1, tiled=True
        ).astype(jnp.float32),
        lax.psum_scatter(
            row_back[3].astype(jnp.bfloat16), "seq", scatter_dimension=1, tiled=True
        ).astype(jnp.float32),
        lax.psum_scatter(
            row_back[4].astype(jnp.bfloat16), "seq", scatter_dimension=1, tiled=True
        ).astype(jnp.float32),
        lax.psum_scatter(
            row_back[5].astype(jnp.bfloat16), "seq", scatter_dimension=1, tiled=True
        ).astype(jnp.float32),
        lax.psum_scatter(
            row_back[6].astype(jnp.bfloat16), "seq", scatter_dimension=1, tiled=True
        ).astype(jnp.float32),
        lax.psum_scatter(
            row_back[7].astype(jnp.bfloat16), "seq", scatter_dimension=1, tiled=True
        ).astype(jnp.float32),
        lax.psum_scatter(
            row_back[8].astype(jnp.bfloat16), "seq", scatter_dimension=1, tiled=True
        ).astype(jnp.float32),
        lax.psum_scatter(
            row_back[9].astype(jnp.bfloat16), "seq", scatter_dimension=1, tiled=True
        ).astype(jnp.float32),
        lax.psum_scatter(
            row_back[10].astype(jnp.bfloat16), "seq", scatter_dimension=1, tiled=True
        ).astype(jnp.float32),
        lax.psum_scatter(
            received[11].astype(jnp.bfloat16), "seq", scatter_dimension=1, tiled=True
        ).astype(jnp.float32),
        lax.psum_scatter(
            received[12].astype(jnp.bfloat16), "seq", scatter_dimension=1, tiled=True
        ).astype(jnp.float32),
        lax.psum_scatter(
            gain_back[0].astype(jnp.bfloat16), "seq", scatter_dimension=1, tiled=True
        ).astype(jnp.float32),
        lax.psum_scatter(
            gain_back[1].astype(jnp.bfloat16), "seq", scatter_dimension=1, tiled=True
        ).astype(jnp.float32),
    )
    row_done = [member.reshape(member.shape[2:]) for member in totals[:11]]
    col_done = [
        jnp.transpose(
            member.reshape(fsdp_count, member.shape[3], member.shape[4]), (1, 0, 2)
        ).reshape(member.shape[3], -1)
        for member in totals[11:13]
    ]
    gain_one_grad = totals[13].reshape(-1)
    gain_two_grad = totals[14].reshape(-1)
    return (
        block_output,
        input_grad,
        gain_one_grad,
        row_done[0],
        row_done[1],
        row_done[4],
        row_done[5],
        row_done[6],
        row_done[7],
        row_done[8],
        row_done[9],
        row_done[10],
        col_done[0],
        gain_two_grad,
        row_done[2],
        row_done[3],
        col_done[1],
    )


def solution(mesh):
    in_specs = (
        P("fsdp", "seq", None),
        P(),
        P(("seq", "fsdp")),
        P(("seq", "fsdp"), None),
        P(("seq", "fsdp"), None),
        P(("seq", "fsdp"), None),
        P(("seq", "fsdp")),
        P(("seq", "fsdp"), None),
        P(("seq", "fsdp")),
        P(("seq", "fsdp"), None),
        P(("seq", "fsdp")),
        P(("seq", "fsdp")),
        P(("seq", "fsdp"), None),
        P(("seq", "fsdp")),
        P(("seq", "fsdp"), None),
        P(("seq", "fsdp"), None),
        P(("seq", "fsdp"), None),
        P("fsdp", "seq", None),
    )
    out_specs = (
        P("fsdp", "seq", None),
        P("fsdp", "seq", None),
        P(("seq", "fsdp")),
        P(("seq", "fsdp"), None),
        P(("seq", "fsdp"), None),
        P(("seq", "fsdp"), None),
        P(("seq", "fsdp")),
        P(("seq", "fsdp"), None),
        P(("seq", "fsdp")),
        P(("seq", "fsdp"), None),
        P(("seq", "fsdp")),
        P(("seq", "fsdp")),
        P(("seq", "fsdp"), None),
        P(("seq", "fsdp")),
        P(("seq", "fsdp"), None),
        P(("seq", "fsdp"), None),
        P(("seq", "fsdp"), None),
    )
    return jax.shard_map(shards, mesh=mesh, in_specs=in_specs, out_specs=out_specs, check_vma=False)
```

profile of v0, /device:TPU:20, one launch (start us, length us, event | category | flops | bytes accessed | tf_op | source)
XLA Modules:
  0.0 2118.9 jit_solution(15798713473446613752)
XLA Ops:
  15.8 31.2 %all-reduce.66 = (bf16[512]{0:T(512)(128)(2,1)S(1)}, bf16[640]{0:T(1024)(128)(2,1)S(1)}, bf16[512]{0:T(512)(128)(2,1)S(1)}, bf16[640]{0:T(1024)(128)(2,1)S(1)}, ...) all-reduce(bf16[512]{0:T(512)(128)(2,1)S(1)} %dynamic-update-slice., ...), channel_id=17, replica_groups=mesh['seq'=8,'fsdp'=4] {'seq'}, use_global_device_ids=true, to_apply=%add.55 | all-reduce | flops 3584 | bytes 14336
  85.4 18.9 all-gather.19
  108.2 33.7 %all-gather.7 = bf16[640,160]{1,0:T(8,128)(2,1)} all-gather(bf16[80,160]{1,0:T(8,128)(2,1)S(1)} %copy-done.103), channel_id=11, replica_groups=mesh['seq'=8,'fsdp'=4] {'seq'}, dimensions={0}, use_global_device_ids=true | all-gather | bytes 230400 | tf_op jit(solution)/shard_map/all_gather | solution.py:318
  145.3 31.8 %all-gather.4 = bf16[640,160]{1,0:T(8,128)(2,1)S(1)} all-gather(bf16[80,160]{1,0:T(8,128)(2,1)S(1)} %copy-done.104), channel_id=8, replica_groups=mesh['seq'=8,'fsdp'=4] {'seq'}, dimensions={0}, use_global_device_ids=true | all-gather | bytes 230400 | tf_op jit(solution)/shard_map/all_gather | solution.py:316
  177.1 9.8 all_to_all.435
  190.6 31.3 %all-to-all-done.3 = bf16[4,2,1,80,2048]{4,3,1,2,0:T(8,128)(2,1)S(1)} async-done(((bf16[4,2,1,80,2048]{4,3,1,2,0:T(8,128)(2,1)}), bf16[4,2,1,80,2048]{4,3,1,2,0:T(8,128)(2,1)S(1)}, u32[]{:S(2)}, u32[]{:S(2)}) %all-to-all-start.3) | async-done | bytes 2621472 | tf_op jit(solution)/shard_map/all_to_all | solution.py:334
  231.4 26.9 %all-to-all-done.9 = bf16[4,2,1,80,2048]{4,3,1,2,0:T(8,128)(2,1)S(1)} async-done(((bf16[4,2,1,80,2048]{4,3,1,2,0:T(8,128)(2,1)}), bf16[4,2,1,80,2048]{4,3,1,2,0:T(8,128)(2,1)S(1)}, u32[]{:S(2)}, u32[]{:S(2)}) %all-to-all-start.9) | async-done | bytes 2621472 | tf_op jit(solution)/shard_map/all_to_all | solution.py:333
  267.6 30.6 %all-to-all-done.10 = bf16[4,8,1,64,640]{4,3,1,2,0:T(8,128)(2,1)} async-done(((bf16[4,8,1,64,640]{4,3,1,2,0:T(8,128)(2,1)}), bf16[4,8,1,64,640]{4,3,1,2,0:T(8,128)(2,1)}, u32[]{:S(2)}, u32[]{:S(2)}) %all-to-all-start.10) | async-done | bytes 2621472 | tf_op jit(solution)/shard_map/all_to_all | solution.py:344
  298.2 5.3 all-to-all-start.12
  316.5 6.8 collective-permute-start
  355.7 55.6 %all-gather.41.cloned.1.call-done = bf16[1536,2048]{1,0:T(8,128)(2,1)} async-done(((bf16[192,2048]{1,0:T(8,128)(2,1)}), bf16[1536,2048]{1,0:T(8,128)(2,1)}) %all-gather.41.cloned.1.call-update) | async-done | bytes 6291472 | tf_op jit(solution)/shard_map/all_gather | solution.py:313
  411.3 5.3 all-to-all-start.13
  475.0 8.8 pad.159
  500.0 8.8 pad.158
  508.8 8.8 pad.171
  519.3 8.8 pad.170
  535.2 15.9 pad.172
  551.0 15.9 pad.173
  568.9 15.9 pad.160
  584.7 15.9 pad.161
  601.4 29.7 %all-gather.9 = bf16[64,1,640]{2,0,1:T(8,128)(2,1)} all-gather(bf16[8,1,640]{2,0,1:T(8,128)(2,1)S(1)} %add_convert_fusion.5), channel_id=13, replica_groups=mesh['seq'=8,'fsdp'=4] {'seq'}, dimensions={0}, use_global_device_ids=true | all-gather | bytes 92160 | tf_op jit(solution)/shard_map/all_gather | solution.py:22
  631.9 32.4 %all-gather.10 = bf16[64,1,640]{2,0,1:T(8,128)(2,1)} all-gather(bf16[8,1,640]{2,0,1:T(8,128)(2,1)S(1)} %add_convert_fusion.4), channel_id=14, replica_groups=mesh['seq'=8,'fsdp'=4] {'seq'}, dimensions={0}, use_global_device_ids=true | all-gather | bytes 92160 | tf_op jit(solution)/shard_map/all_gather | solution.py:22
  664.3 6.8 copy.647
  671.1 5.2 all-to-all-start.14
  676.4 5.8 while.30
  700.2 80.8 %all-reduce.72.cloned.1.call-done = bf16[512,2048]{1,0:T(8,128)(2,1)} async-done(((bf16[512,2048]{1,0:T(8,128)(2,1)}), bf16[512,2048]{1,0:T(8,128)(2,1)}) %all-reduce.72.cloned.1.call-update) | async-done | bytes 2097168 | tf_op jit(solution)/shard_map/psum | solution.py:394
  787.1 6.5 copy.643
  793.6 6.5 copy.645
  800.2 6.8 copy.648
  812.1 5.1 fusion.112
  817.3 11.9 multiply_convert_fusion.2
  829.2 6.8 fusion.113
  836.0 7.8 add_convert_fusion.1
  848.5 48.8 %all-reduce.74.cloned.1.call-done = bf16[512,2048]{1,0:T(8,128)(2,1)} async-done(((bf16[512,2048]{1,0:T(8,128)(2,1)}), bf16[512,2048]{1,0:T(8,128)(2,1)}) %all-reduce.74.cloned.1.call-update) | async-done | bytes 2097168 | tf_op jit(solution)/shard_map/psum | solution.py:415
  998.1 8.8 pad.182
  1006.9 8.8 pad.183
  1018.0 15.9 pad.185
  1036.2 8.8 pad.195
  1046.7 8.8 pad.194
  1062.1 15.9 pad.184
  1078.0 15.9 pad.197
  1095.8 15.8 pad.196
  1116.8 30.7 %all-gather.17 = bf16[64,1,640]{2,0,1:T(8,128)(2,1)} all-gather(bf16[8,1,640]{2,0,1:T(8,128)(2,1)S(1)} %get-tuple-element.349), channel_id=21, replica_groups=mesh['seq'=8,'fsdp'=4] {'seq'}, dimensions={0}, use_global_device_ids=true | all-gather | bytes 92160 | tf_op jit(solution)/shard_map/all_gather | solution.py:22
  1147.5 32.9 %all-gather.18 = bf16[64,1,640]{2,0,1:T(8,128)(2,1)} all-gather(bf16[8,1,640]{2,0,1:T(8,128)(2,1)S(1)} %get-tuple-element.348), channel_id=22, replica_groups=mesh['seq'=8,'fsdp'=4] {'seq'}, dimensions={0}, use_global_device_ids=true | all-gather | bytes 92160 | tf_op jit(solution)/shard_map/all_gather | solution.py:22
  1180.4 10.8 while.31
  1191.3 5.5 multiply_reduce_fusion.3
  1209.1 9.8 all_to_all.436
  1219.0 8.1 convolution_convert_fusion.6
  1269.3 6.2 add_convert_fusion
  1281.3 45.8 %all_to_all.437 = bf16[1,2,4,80,2048]{4,3,1,0,2:T(8,128)(2,1)} all-to-all(bf16[1,2,4,80,2048]{4,3,1,0,2:T(8,128)(2,1)S(1)} %copy.667), channel_id=1, replica_groups=mesh['seq'=8,'fsdp'=4] {'fsdp'}, dimensions={2} | all-to-all | bytes 5242880 | tf_op jit(solution)/shard_map/all_to_all | solution.py:484
  1342.9 25.5 %all-to-all-done.17 = bf16[1,2,4,80,2048]{4,3,1,0,2:T(8,128)(2,1)} async-done(((bf16[1,2,4,80,2048]{4,3,1,0,2:T(8,128)(2,1)}), bf16[1,2,4,80,2048]{4,3,1,0,2:T(8,128)(2,1)}, u32[]{:S(2)}, u32[]{:S(2)}) %all-to-all-start.17) | async-done | bytes 2621472 | tf_op jit(solution)/shard_map/all_to_all | solution.py:487
  1373.6 8.2 fusion.2
  1381.8 8.7 copy.688
  1390.5 6.1 copy.689
  1396.6 7.8 all-to-all-done.25
  1404.3 86.6 %all_to_all.438 = bf16[1,8,4,64,1536]{4,3,1,0,2:T(8,128)(2,1)} all-to-all(bf16[1,8,4,64,1536]{4,3,1,0,2:T(8,128)(2,1)} %copy.689), channel_id=1, replica_groups=mesh['seq'=8,'fsdp'=4] {'fsdp'}, dimensions={2} | all-to-all | bytes 12582912 | tf_op jit(solution)/shard_map/all_to_all | solution.py:520
  1491.2 5.8 convolution_convert_fusion.2
  1498.1 74.2 %all_to_all.439 = bf16[1,2,4,192,2048]{4,3,1,0,2:T(8,128)(2,1)} all-to-all(bf16[1,2,4,192,2048]{4,3,1,0,2:T(8,128)(2,1)S(1)} %copy.686), channel_id=1, replica_groups=mesh['seq'=8,'fsdp'=4] {'fsdp'}, dimensions={2} | all-to-all | bytes 12582912 | tf_op jit(solution)/shard_map/all_to_all | solution.py:490
  1572.4 5.6 convolution_convert_fusion.1
  1579.1 74.3 %all_to_all.440 = bf16[1,2,4,192,2048]{4,3,1,0,2:T(8,128)(2,1)} all-to-all(bf16[1,2,4,192,2048]{4,3,1,0,2:T(8,128)(2,1)S(1)} %copy.687), channel_id=1, replica_groups=mesh['seq'=8,'fsdp'=4] {'fsdp'}, dimensions={2} | all-to-all | bytes 12582912 | tf_op jit(solution)/shard_map/all_to_all | solution.py:493
  1713.7 31.6 %all-reduce.65 = (bf16[1,8,1,64]{3,1,2,0:T(8,128)(2,1)S(1)}, bf16[1,8,80,4]{2,3,0,1:T(4,128)(2,1)S(1)}, bf16[1,8,80]{2,1,0:T(8,128)(2,1)S(1)}, bf16[1,8,80]{2,1,...) all-reduce(bf16[1,8,1,64]{3,1,2,0:T(8,128)(2,1)S(1)} %bitcast.517, ...), channel_id=25, replica_groups=mesh['seq'=8,'fsdp'=4] {'seq'}, use_global_device_ids=true, to_apply=%region_18.19.clone | all-reduce | flops 6144 | bytes 24576
  1757.6 110.0 %all-reduce.76.cloned.1.call-done = (bf16[4,8,1,64,640]{4,3,1,0,2:T(8,128)(2,1)}, bf16[4,8,1,64,1536]{4,3,1,0,2:T(8,128)(2,1)}) async-done(((bf16[4,8,1,64,640]{4,3,1,0,2:T(8,128)(2,1)}, bf16[4,8,1,64,1536]{4,3,1,0,2:T(8,128)(2,1)}), (bf16[4,8,1,64,640]{4,3,1,0,2:T(8,128)(2,1)}, bf16[4,8,1,64,1536]{4,3,1,0,2:T(8,128)(2,1)})) %all-reduce.76.cloned.1.call-update) | async-done | bytes 8912912
  1873.4 115.1 %reduce-scatter.33.cloned.1.call-done = bf16[1,1,192,2048]{3,2,1,0:T(8,128)(2,1)} async-done(((bf16[1,8,192,2048]{3,2,1,0:T(8,128)(2,1)}), bf16[1,1,192,2048]{3,2,1,0:T(8,128)(2,1)}) %reduce-scatter.33.cloned.1.call-update) | async-done | bytes 786448 | tf_op jit(solution)/shard_map/reduce_scatter | solution.py:539
  1991.0 118.7 %reduce-scatter.35.cloned.1.call-done = bf16[1,1,192,2048]{3,2,1,0:T(8,128)(2,1)} async-done(((bf16[1,8,192,2048]{3,2,1,0:T(8,128)(2,1)}), bf16[1,1,192,2048]{3,2,1,0:T(8,128)(2,1)}) %reduce-scatter.35.cloned.1.call-update) | async-done | bytes 786448 | tf_op jit(solution)/shard_map/reduce_scatter | solution.py:542
  (688 shorter events, 544.3 us)
Async XLA Ops:
  7.2 179.8 %all-gather.33.cloned.1.call-start = ((), (), s32[]{:S(2)}) async-start(), calls=%async_computation.50 | async-start | bytes 2949120 | tf_op jit(solution)/shard_map/all_gather | solution.py:311
  7.9 182.7 %all-gather.35.cloned.1.call-start = ((), (), s32[]{:S(2)}) async-start(), calls=%async_computation.51 | async-start | bytes 2949120 | tf_op jit(solution)/shard_map/all_gather | solution.py:310
  8.7 218.4 %all-gather.37.cloned.1.call-start = ((), (), s32[]{:S(2)}) async-start(), calls=%async_computation.52 | async-start | bytes 2949120 | tf_op jit(solution)/shard_map/all_gather | solution.py:321
  10.5 74.9 %copy-start.124 = (bf16[80,4]{0,1:T(4,128)(2,1)S(1)}, bf16[80,4]{0,1:T(4,128)(2,1)}, u32[]{:S(2)}) copy-start(bf16[80,4]{0,1:T(4,128)(2,1)} %param.27) | copy-start | bytes 1924
  10.6 97.6 %copy-start.103 = (bf16[80,160]{1,0:T(8,128)(2,1)S(1)}, bf16[80,160]{1,0:T(8,128)(2,1)}, u32[]{:S(2)}) copy-start(bf16[80,160]{1,0:T(8,128)(2,1)} %param.31) | copy-start | bytes 76804
  10.6 287.6 %all-gather.39.cloned.1.call-start = ((), (), s32[]{:S(2)}) async-start(), calls=%async_computation.53 | async-start | bytes 7077888 | tf_op jit(solution)/shard_map/all_gather | solution.py:312
  11.2 134.1 %copy-start.104 = (bf16[80,160]{1,0:T(8,128)(2,1)S(1)}, bf16[80,160]{1,0:T(8,128)(2,1)}, u32[]{:S(2)}) copy-start(bf16[80,160]{1,0:T(8,128)(2,1)} %param.29) | copy-start | bytes 76804
  11.2 297.7 %all-gather.29.cloned.1.call-start = ((), (), s32[]{:S(2)}) async-start(), calls=%async_computation.38 | async-start | bytes 2621440 | tf_op jit(solution)/shard_map/all_gather | solution.py:368
  11.8 399.5 %all-gather.41.cloned.1.call-start = ((), (), s32[]{:S(2)}) async-start(), calls=%async_computation.54 | async-start | bytes 7077888 | tf_op jit(solution)/shard_map/all_gather | solution.py:313
  47.7 6.9 all-to-all-start.6
  54.5 251.3 %copy-start.108 = (bf16[4,2,1,80]{3,1,2,0:T(2,128)(2,1)}, bf16[4,2,1,80]{3,1,2,0:T(2,128)(2,1)S(1)}, u32[]{:S(2)}) copy-start(bf16[4,2,1,80]{3,1,2,0:T(2,128)(2,1)S(1)} %all-to-all-done.6) | copy-start | bytes 3844
  54.5 6.9 all-to-all-start
  61.4 6.9 all-to-all-start.8
  68.3 6.9 all-to-all-start.5
  75.2 7.0 all-to-all-start.11
  82.2 104.8 %copy-start.111 = (bf16[4,2,256]{2,1,0:T(2,128)(2,1)}, bf16[4,2,256]{2,1,0:T(2,128)(2,1)S(1)}, u32[]{:S(2)}) copy-start(bf16[4,2,256]{2,1,0:T(2,128)(2,1)S(1)} %all-to-all-done.11) | copy-start | bytes 12292
  82.2 22.7 %all-to-all-start.2 = ((bf16[4,2,256]{2,1,0:T(2,128)(2,1)}), bf16[4,2,256]{2,1,0:T(2,128)(2,1)S(1)}, u32[]{:S(2)}, u32[]{:S(2)}) async-start(bf16[4,2,256]{2,1,0:T(2,128)(2,1)} %reshape.1213), calls=%async_computation.2 | async-start | bytes 8192 | tf_op jit(solution)/shard_map/all_to_all | solution.py:346
  104.9 36.9 %all-to-all-start.1 = ((bf16[4,2,1,80,4]{3,1,4,2,0:T(2,128)(2,1)}), bf16[4,2,1,80,4]{3,1,4,2,0:T(2,128)(2,1)S(1)}, u32[]{:S(2)}, u32[]{:S(2)}) async-start(bf16[4,2,1,80,4]{3,1,4,2,0:T(2,128)(2,1)} %copy.609), calls=%async_computation.1 | async-start | bytes 16384 | tf_op jit(solution)/shard_map/all_to_all | solution.py:337
  141.8 35.3 %all-to-all-start.7 = ((bf16[4,2,1,80,160]{4,3,1,2,0:T(8,128)(2,1)}), bf16[4,2,1,80,160]{4,3,1,2,0:T(8,128)(2,1)S(1)}, u32[]{:S(2)}, u32[]{:S(2)}) async-start(bf16[4,2,1,80,160]{4,3,1,2,0:T(8,128)(2,1)} %bitcast.30), calls=%async_computation.7 | async-start | bytes 655360 | tf_op jit(solution)/shard_map/all_to_all | solution.py:341
  186.9 34.9 %all-to-all-start.3 = ((bf16[4,2,1,80,2048]{4,3,1,2,0:T(8,128)(2,1)}), bf16[4,2,1,80,2048]{4,3,1,2,0:T(8,128)(2,1)S(1)}, u32[]{:S(2)}, u32[]{:S(2)}) async-start(bf16[4,2,1,80,2048]{4,3,1,2,0:T(8,128)(2,1)} %bitcast.480), calls=%async_computation.3 | async-start | bytes 5242880 | tf_op jit(solution)/shard_map/all_to_all | solution.py:334
  223.4 34.9 %all-to-all-start.9 = ((bf16[4,2,1,80,2048]{4,3,1,2,0:T(8,128)(2,1)}), bf16[4,2,1,80,2048]{4,3,1,2,0:T(8,128)(2,1)S(1)}, u32[]{:S(2)}, u32[]{:S(2)}) async-start(bf16[4,2,1,80,2048]{4,3,1,2,0:T(8,128)(2,1)} %bitcast.479), calls=%async_computation.9 | async-start | bytes 5242880 | tf_op jit(solution)/shard_map/all_to_all | solution.py:333
  259.8 38.4 %all-to-all-start.10 = ((bf16[4,8,1,64,640]{4,3,1,2,0:T(8,128)(2,1)}), bf16[4,8,1,64,640]{4,3,1,2,0:T(8,128)(2,1)}, u32[]{:S(2)}, u32[]{:S(2)}) async-start(bf16[4,8,1,64,640]{4,3,1,2,0:T(8,128)(2,1)} %copy.639), calls=%async_computation.10 | async-start | bytes 5242880 | tf_op jit(solution)/shard_map/all_to_all | solution.py:344
  264.3 400.0 %all-gather.43.cloned.1.call-start = ((), (), s32[]{:S(2)}) async-start(), calls=%async_computation.55 | async-start | bytes 7077888 | tf_op jit(solution)/shard_map/all_gather | solution.py:322
  298.2 113.1 %all-to-all-start.12 = ((bf16[4,2,1,192,2048]{4,3,1,2,0:T(8,128)(2,1)}), bf16[4,2,1,192,2048]{4,3,1,2,0:T(8,128)(2,1)}, u32[]{:S(2)}, u32[]{:S(2)}) async-start(bf16[4,2,1,192,2048]{4,3,1,2,0:T(8,128)(2,1)} %bitcast.452), calls=%async_computation.12 | async-start | bytes 12582912 | tf_op jit(solution)/shard_map/all_to_all | solution.py:335
  316.1 8.8 copy-start.16
  316.5 13.7 collective-permute-start
  323.4 7.0 copy-start.73
  323.4 7.0 copy-start.76
  323.4 7.0 copy-start.79
  323.4 7.0 copy-start.82
  411.3 259.9 %all-to-all-start.13 = ((bf16[4,2,1,192,2048]{4,3,1,2,0:T(8,128)(2,1)}), bf16[4,2,1,192,2048]{4,3,1,2,0:T(8,128)(2,1)}, u32[]{:S(2)}, u32[]{:S(2)}) async-start(bf16[4,2,1,192,2048]{4,3,1,2,0:T(8,128)(2,1)} %bitcast.451), calls=%async_computation.13 | async-start | bytes 12582912 | tf_op jit(solution)/shard_map/all_to_all | solution.py:336
  671.1 129.0 %all-to-all-start.14 = ((bf16[4,8,1,64,1536]{4,3,1,2,0:T(8,128)(2,1)}), bf16[4,8,1,64,1536]{4,3,1,2,0:T(8,128)(2,1)}, u32[]{:S(2)}, u32[]{:S(2)}) async-start(bf16[4,8,1,64,1536]{4,3,1,2,0:T(8,128)(2,1)} %copy.647), calls=%async_computation.14 | async-start | bytes 12582912 | tf_op jit(solution)/shard_map/all_to_all | solution.py:345
  676.4 104.7 %all-reduce.72.cloned.1.call-start = ((), (), s32[]{:S(2)}) async-start(), calls=%async_computation.39 | async-start | bytes 4194304 | tf_op jit(solution)/shard_map/psum | solution.py:394
  695.0 122.3 %all-gather.31.cloned.1.call-start = ((), (), s32[]{:S(2)}) async-start(), calls=%async_computation.41 | async-start | bytes 2621440 | tf_op jit(solution)/shard_map/all_gather | solution.py:369
  695.7 201.6 %all-reduce.74.cloned.1.call-start = ((), (), s32[]{:S(2)}) async-start(), calls=%async_computation.42 | async-start | bytes 4194304 | tf_op jit(solution)/shard_map/psum | solution.py:415
  800.1 6.8 copy-start.21
  800.2 6.9 copy-start.48
  800.2 12.0 slice-start
  829.2 6.8 copy-start.135
  829.2 6.8 copy-start.134
  843.7 823.4 %reduce-scatter.29.cloned.1.call-start = ((), (), s32[]{:S(2)}) async-start(), calls=%async_computation.46 | async-start | bytes 368640 | tf_op jit(solution)/shard_map/reduce_scatter | solution.py:551
  1219.0 449.6 %reduce-scatter.21.cloned.1.call-start = ((), (), s32[]{:S(2)}) async-start(), calls=%async_computation.40 | async-start | bytes 2621440 | tf_op jit(solution)/shard_map/reduce_scatter | solution.py:403
  1250.9 11.5 collective-permute-start.1
  1258.3 10.9 all-to-all-start.22
  1262.4 413.0 %reduce-scatter.31.cloned.1.call-start = ((), (), s32[]{:S(2)}) async-start(), calls=%async_computation.47 | async-start | bytes 368640 | tf_op jit(solution)/shard_map/reduce_scatter | solution.py:557
  1269.2 420.1 %reduce-scatter.23.cloned.1.call-start = ((), (), s32[]{:S(2)}) async-start(), calls=%async_computation.43 | async-start | bytes 2621440 | tf_op jit(solution)/shard_map/reduce_scatter | solution.py:439
  1275.5 478.3 %reduce-scatter.25.cloned.1.call-start = ((), (), s32[]{:S(2)}) async-start(), calls=%async_computation.44 | async-start | bytes 2949120 | tf_op jit(solution)/shard_map/reduce_scatter | solution.py:533
  1332.3 36.1 %all-to-all-start.17 = ((bf16[1,2,4,80,2048]{4,3,1,0,2:T(8,128)(2,1)}), bf16[1,2,4,80,2048]{4,3,1,0,2:T(8,128)(2,1)}, u32[]{:S(2)}, u32[]{:S(2)}) async-start(bf16[1,2,4,80,2048]{4,3,1,0,2:T(8,128)(2,1)} %copy.669), calls=%async_computation.20 | async-start | bytes 5242880 | tf_op jit(solution)/shard_map/all_to_all | solution.py:487
  1368.4 35.9 %all-to-all-start.25 = ((bf16[1,8,4,64,640]{4,3,1,0,2:T(8,128)(2,1)}), bf16[1,8,4,64,640]{4,3,1,0,2:T(8,128)(2,1)}, u32[]{:S(2)}, u32[]{:S(2)}) async-start(bf16[1,8,4,64,640]{4,3,1,0,2:T(8,128)(2,1)} %copy.683), calls=%async_computation.31 | async-start | bytes 5242880 | tf_op jit(solution)/shard_map/all_to_all | solution.py:517
  1373.0 382.7 %reduce-scatter.27.cloned.1.call-start = ((), (), s32[]{:S(2)}) async-start(), calls=%async_computation.45 | async-start | bytes 2949120 | tf_op jit(solution)/shard_map/reduce_scatter | solution.py:536
  1373.5 494.0 %all-reduce.76.cloned.1.call-start = ((), (), s32[]{:S(2)}) async-start(), calls=%async_computation.56 | async-start | bytes 17825792
  1491.0 497.6 %reduce-scatter.33.cloned.1.call-start = ((), (), s32[]{:S(2)}) async-start(), calls=%async_computation.48 | async-start | bytes 7077888 | tf_op jit(solution)/shard_map/reduce_scatter | solution.py:539
  1572.3 537.4 %reduce-scatter.35.cloned.1.call-start = ((), (), s32[]{:S(2)}) async-start(), calls=%async_computation.49 | async-start | bytes 7077888 | tf_op jit(solution)/shard_map/reduce_scatter | solution.py:542
  1653.5 7.0 copy-start.115
  1656.0 8.6 copy-start.6
  1657.2 10.0 all-to-all-start.18
  1668.6 20.7 copy-start.86
  1672.1 7.1 all-to-all-start.26
  1679.2 6.9 all-to-all-start.19
  1686.1 6.9 all-to-all-start.21
  1689.4 13.8 copy-start.50
  1693.0 7.0 all-to-all-start.15
  1700.0 6.9 all-to-all-start.23
  1706.8 6.9 all-to-all-start.24
  (119 other events, 396.8 us)
Sparse Core Ops, SparseCore 0:
  10.2 54.6 all-gather.32
  67.1 54.0 all-gather.34
  124.0 58.9 all-gather.36
  185.0 97.0 all-gather.38
  283.6 24.8 all-gather.28
  310.5 100.7 all-gather.40
  413.4 97.1 all-gather.42
  695.1 85.8 all-reduce.71
  782.7 24.4 all-gather.30
  843.9 53.3 all-reduce.73
  1219.1 62.1 reduce-scatter.28
  1283.7 42.7 reduce-scatter.20
  1330.1 60.3 reduce-scatter.30
  1393.0 40.7 reduce-scatter.22
  1437.2 68.8 reduce-scatter.24
  1509.4 69.3 reduce-scatter.26
  1582.7 284.7 all-reduce.75
  1871.4 117.0 reduce-scatter.32
  1992.6 117.0 reduce-scatter.34
where the time goes:
time: 2160 us; the launch traced here: 2120 us
  waiting for transfers between devices  690 us (32%)
  blocking collectives  573 us (27%)
  local copies, waits for them, and re-layouts  459 us (21%)
  other arithmetic  170 us (8%)
  matrix products  109 us (5%)
  starting transfers between devices  100 us (5%)
    pad x20, local copies, waits for them, and re-layouts, mixer_forward(): lax.associative_scan(combine, (decay_gate, inject), axis=1)  140 us
    pad x20, local copies, waits for them, and re-layouts, mixer_backward(): lax.associative_scan(combine, (next_decay, grad_state), axis=1, reverse=T...  140 us
    all_gather x4, blocking collectives, carried_in(): lax.all_gather(part.astype(kind), axis)  126 us
    reduce_scatter x1, waiting for transfers between devices, shards(): lax.psum_scatter(row_back[3].astype(jnp.bfloat16), 'seq', scatter_dimensi...  119 us
    reduce_scatter x1, waiting for transfers between devices, shards(): lax.psum_scatter(row_back[2].astype(jnp.bfloat16), 'seq', scatter_dimensi...  115 us
    unnamed x20, waiting for transfers between devices  114 us
    all_to_all x1, blocking collectives, shards(): lax.all_to_all(col_sent[1].astype(jnp.bfloat16), 'fsdp', split_axis=2, co...  86.6 us
    psum x1, waiting for transfers between devices, shards(): lax.psum(project(mixed_out, mixer_cols).astype(jnp.bfloat16), 'fsdp')  80.8 us
  transfers between devices with their start and end apart: 45, of which 23 were waited for; matrix products, arithmetic and copies ran while one was open for 21% of the time, Pallas kernels for 0%

commit v1 on v0

v1 whole, which is shorter than its diff:
```python
import functools

import jax
import jax.numpy as jnp
from jax import lax
from jax.experimental import pallas as pl
from jax.experimental.pallas import tpu as pltpu
from jax.sharding import PartitionSpec as P

AXES = ("seq", "fsdp")
TAPS = 4
EPSILON = 1e-06
DECAY_SCALE = 8.0
VMEM_BYTES = 56 * 1024 * 1024
BF16 = jnp.bfloat16
F32 = jnp.float32


def device_bits(seq_count, fsdp_count, rows, block):
    low = fsdp_count
    while low * rows < block:
        low *= 2
    total = seq_count * fsdp_count
    every = [1 << k for k in range(total.bit_length() - 1)]
    dp = tuple(b for b in every if b not in (low, 2 * low))
    return low, dp


def linear_index():
    return lax.axis_index("seq") * lax.axis_size("fsdp") + lax.axis_index("fsdp")


def bit_of(index, bit):
    return lax.rem(lax.div(index, jnp.int32(bit)), jnp.int32(2))


def number_of(index, bits):
    value = jnp.int32(0)
    for b in bits:
        value = value * 2 + bit_of(index, b)
    return value


def trade(value, mask):
    count = lax.axis_size("seq") * lax.axis_size("fsdp")
    return lax.ppermute(value, AXES, [(i, i ^ mask) for i in range(count)])


def pick(value, index, axis):
    return lax.dynamic_index_in_dim(value, index, axis, keepdims=False)


def put(buffer, part, index, axis):
    return lax.dynamic_update_index_in_dim(buffer, part, index, axis)


def gather_units(own, dp):
    units = [(0, own)]
    for b in reversed(dp):
        units += [(mask | b, trade(unit, b)) for mask, unit in units]
    return units


def gather_rows(own, dp, me):
    units = gather_units(own, dp)
    whole = jnp.zeros((len(units),) + own.shape, own.dtype)
    for mask, unit in units:
        whole = put(whole, unit, number_of(jnp.bitwise_xor(me, mask), dp), 0)
    return whole


def scatter_bit(value, axis, bit, me):
    mine = bit_of(me, bit)
    sent = trade(pick(value, 1 - mine, axis).astype(BF16), bit)
    return pick(value, mine, axis).astype(F32) + sent.astype(F32)


def scatter_rows(value, dp, me):
    value = value.reshape((2,) * len(dp) + value.shape[1:])
    for b in dp:
        value = scatter_bit(value, 0, b, me)
        if b != dp[-1]:
            value = value.astype(BF16)
    return value


def share_tokens(own, low):
    half = own.shape[0] // 2
    one, two = trade(own, low), trade(own, 2 * low)
    three = [trade(two[:half], low), trade(one[half:], 2 * low)]
    return jnp.concatenate([own, one, two] + three, axis=0)


def sum_tokens(partial, low):
    rows = partial.shape[0] // 4
    total = partial[:rows].astype(F32)
    for j in (1, 2, 3):
        total = total + trade(partial[j * rows : (j + 1) * rows], j * low).astype(F32)
    return total


def project(left, weight):
    return lax.dot_general(left, weight, (((1,), (1,)), ((), ())), preferred_element_type=F32)


def back_project(left, weight):
    return lax.dot_general(left, weight, (((1,), (0,)), ((), ())), preferred_element_type=F32)


def outer(grads, values):
    return lax.dot_general(grads, values, (((0,), (0,)), ((), ())), preferred_element_type=F32)


def inverse_rms(values):
    return lax.rsqrt(jnp.mean(values * values, axis=-1, keepdims=True) + EPSILON)


def gelu_parts(v):
    c = 0.7978845608028654
    t = jnp.tanh(c * (v + 0.044715 * v * v * v))
    act = 0.5 * v * (1.0 + t)
    slope = 0.5 * (1.0 + t) + 0.5 * v * (1.0 - t * t) * c * (1.0 + 3 * 0.044715 * v * v)
    return act, slope


def call(body, outs, scalars, arrays, scratch=()):
    return pl.pallas_call(
        body,
        out_shape=[jax.ShapeDtypeStruct(shape, kind) for shape, kind in outs],
        in_specs=[pl.BlockSpec(memory_space=pltpu.SMEM)]
        + [pl.BlockSpec(memory_space=pltpu.VMEM)] * len(arrays),
        out_specs=[pl.BlockSpec(memory_space=pltpu.VMEM)] * len(outs),
        scratch_shapes=list(scratch),
        compiler_params=pltpu.CompilerParams(vmem_limit_bytes=VMEM_BYTES),
    )(scalars, *arrays)


def block_number(scalars, n, rows, step):
    return jnp.bitwise_xor(scalars[0], (n // rows) * step)


def injection(s, speed):
    y = speed * s
    e = jnp.exp(-y)
    z = 2.0 * y
    series = 1.0 - z * (1 / 7)
    for k in (6, 5, 4, 3, 2):
        series = 1.0 - z * (1 / k) * series
    return e, jnp.sqrt(jnp.where(z < 0.35, z * series, 1.0 - e * e))


def span_scan(a, b, reverse):
    span, channels = a.shape
    within = lax.broadcasted_iota(jnp.int32, (span, channels), 0) % 8
    for k in (1, 2, 4):
        turn = span - k if reverse else k
        reached = within < 8 - k if reverse else within >= k
        a_far = jnp.where(reached, pltpu.roll(a, turn, 0), 1.0)
        b_far = jnp.where(reached, pltpu.roll(b, turn, 0), 0.0)
        b = b + a * b_far
        a = a * a_far
    count = span // 8
    order = range(count - 1, -1, -1) if reverse else range(count)
    edge = 0 if reverse else 7
    a_all, b_all = [None] * count, [None] * count
    p = jnp.ones((1, channels), F32)
    h = jnp.zeros((1, channels), F32)
    for i in order:
        a_i, b_i = a[8 * i : 8 * i + 8], b[8 * i : 8 * i + 8]
        b_all[i] = b_i + a_i * h
        a_all[i] = a_i * p
        p = a_all[i][edge : edge + 1]
        h = b_all[i][edge : edge + 1]
    return jnp.concatenate(a_all, axis=0), jnp.concatenate(b_all, axis=0), p, h


def forward_kernel(
    rows, step, scalars, recur, halo, marks, coef, rate_w, gate_w,
    conv, s_out, q_out, prod, part, ends, pad,
):
    count, span, channels = recur.shape

    def convolve(n, carry):
        block = block_number(scalars, n, rows, step)
        before = jnp.bitwise_xor(jnp.maximum(block - 1, 0), scalars[0])
        pad[4:8, :] = halo[before * rows + n % rows]
        pad[8:, :] = recur[n].astype(F32)
        total = coef[4:5, :] + coef[0:1, :] * pad[8:, :]
        for k in range(1, TAPS):
            total = total + coef[k : k + 1, :] * pad[8 - k : 8 - k + span, :] * marks[n][:, k : k + 1]
        conv[n] = total.astype(BF16)
        return carry

    lax.fori_loop(0, count, convolve, 0)
    flat = conv[...].reshape(count * span, channels)
    s_out[...] = project(flat, rate_w[...]).reshape(count, span, channels)
    q_out[...] = project(flat, gate_w[...]).reshape(count, span, channels)

    def scan(n, carry):
        s = jax.nn.sigmoid(s_out[n] + coef[5:6, :])
        q = jax.nn.sigmoid(q_out[n] + coef[6:7, :])
        s_out[n] = s
        q_out[n] = q
        e, m = injection(s, coef[7:8, :])
        decay = e * (1.0 - marks[n][:, 0:1])
        p_all, h_all, p, h = span_scan(decay, m * q * conv[n].astype(F32), False)
        prod[n] = p_all
        part[n] = h_all
        ends[n, 0:1, :] = p
        ends[n, 1:2, :] = h
        return carry

    lax.fori_loop(0, count, scan, 0)


def join(ends, into, scalars, rows, blocks, reverse):
    def lap(k, carry):
        block = blocks - 1 - k if reverse else k
        place = jnp.bitwise_xor(block, scalars[0]) * rows
        new = []
        for r in range(rows):
            into[block * rows + r] = carry[r]
            pair = ends[place + r]
            new.append(pair[0:1] * carry[r] + pair[1:2])
        return tuple(new)

    channels = into.shape[-1]
    lax.fori_loop(0, blocks, lap, (jnp.zeros((1, channels), F32),) * rows)


def state_kernel(rows, step, scalars, prod, part, ends, branch, state, mixed, came, into):
    count = prod.shape[0]
    join(ends, into, scalars, rows, into.shape[0] // rows, False)

    def finish(n, carry):
        incoming = into[block_number(scalars, n, rows, step) * rows + n % rows]
        h = part[n] + prod[n] * incoming
        came[n] = incoming
        state[n] = h
        mixed[n] = (h * gelu_parts(branch[n])[0]).astype(BF16)
        return carry

    lax.fori_loop(0, count, finish, 0)


def adjoint_kernel(
    scalars, grad_mixed, state, branch, s_in, marks, coef, grad_branch, prod, part, ends, pad
):
    count, span, channels = state.shape
    pad[span:, :] = jnp.ones((8, channels), F32)

    def scan(n, carry):
        act, slope = gelu_parts(branch[n])
        grad = grad_mixed[n]
        grad_branch[n] = (grad * state[n] * slope).astype(BF16)
        decay = jnp.exp(-coef[7:8, :] * s_in[n]) * (1.0 - marks[n][:, 0:1])
        pad[:span, :] = decay
        p_all, h_all, p, h = span_scan(pad[1 : span + 1, :], grad * act, True)
        prod[n] = p_all
        part[n] = h_all
        ends[n, 0:1, :] = decay[0:1] * p
        ends[n, 1:2, :] = decay[0:1] * h
        return carry

    lax.fori_loop(0, count, scan, 0)


def gates_kernel(
    rows, step, scalars, prod, part, ends, s_in, q_in, conv, state, came, recur, halo, marks, coef,
    rate_w, gate_w, grad_conv, rate_grad, gate_grad, sums, grad_rate, grad_gate, into, pad, pad_two,
):
    count, span, channels = prod.shape
    join(ends, into, scalars, rows, into.shape[0] // rows, True)
    sums[...] = jnp.zeros((8, channels), F32)

    def terms(n, carry):
        block = block_number(scalars, n, rows, step)
        total = part[n] + prod[n] * into[block * rows + n % rows]
        pad[7:8, :] = came[n]
        pad[8:, :] = state[n]
        s, q = s_in[n], q_in[n]
        e, m = injection(s, coef[7:8, :])
        c = conv[n].astype(F32)
        first = marks[n][:, 0:1]
        grad_log = total * (pad[7 : 7 + span, :] * e * (1.0 - first) - e * e * q * c / m)
        rate = -coef[7:8, :] * s * (1.0 - s) * grad_log
        gate = total * m * c * q * (1.0 - q)
        grad_conv[n] = total * m * q
        grad_rate[pl.ds(pl.multiple_of(n * span, span), span), :] = rate.astype(BF16)
        grad_gate[pl.ds(pl.multiple_of(n * span, span), span), :] = gate.astype(BF16)
        sums[0:1, :] += jnp.sum(rate, axis=0, keepdims=True)
        sums[1:2, :] += jnp.sum(gate, axis=0, keepdims=True)
        sums[2:3, :] += jnp.sum(s * grad_log, axis=0, keepdims=True)
        return carry

    lax.fori_loop(0, count, terms, 0)
    through = back_project(grad_rate[...], rate_w[...]) + back_project(grad_gate[...], gate_w[...])
    grad_conv[...] += through.reshape(count, span, channels)
    flat = conv[...].reshape(count * span, channels)
    rate_grad[...] = outer(grad_rate[...], flat)
    gate_grad[...] = outer(grad_gate[...], flat)

    def kernel_terms(n, carry):
        block = block_number(scalars, n, rows, step)
        before = jnp.bitwise_xor(jnp.maximum(block - 1, 0), scalars[0])
        pad_two[4:8, :] = halo[before * rows + n % rows]
        pad_two[8:, :] = recur[n].astype(F32)
        grad = grad_conv[n]
        sums[3:4, :] += jnp.sum(grad, axis=0, keepdims=True)
        sums[4:5, :] += jnp.sum(grad * pad_two[8:, :], axis=0, keepdims=True)
        for k in range(1, TAPS):
            term = grad * pad_two[8 - k : 8 - k + span, :] * marks[n][:, k : k + 1]
            sums[4 + k : 5 + k, :] += jnp.sum(term, axis=0, keepdims=True)
        return carry

    lax.fori_loop(0, count, kernel_terms, 0)


def unconvolve_kernel(rows, step, blocks, scalars, grad_conv, halo, marks, coef, grad_recur, pad):
    count, span, channels = grad_conv.shape

    def body(n, carry):
        block = block_number(scalars, n, rows, step)
        behind = jnp.bitwise_xor(jnp.minimum(block + 1, blocks - 1), scalars[0])
        pad[:span, :] = grad_conv[n]
        pad[span : span + 4, :] = halo[behind * rows + n % rows]
        total = coef[0:1, :] * pad[:span, :]
        for k in range(1, TAPS):
            seen = marks[n][:, 3 + k : 4 + k]
            total = total + coef[k : k + 1, :] * pad[k : k + span, :] * seen
        grad_recur[n] = total.astype(BF16)
        return carry

    lax.fori_loop(0, count, body, 0)


def sequence_marks(lengths, block_ids, span, total_len):
    reach = TAPS - 1
    offsets = jnp.cumsum(lengths, axis=1, dtype=jnp.int32) - lengths
    live = (lengths > 0)[None, :, :, None]
    places = block_ids[:, None] * span + jnp.arange(-reach, span + reach, dtype=jnp.int32)
    starts = offsets[None, :, :, None]
    at = places[:, None, None, :]
    segment = jnp.sum((live & (starts <= at)).astype(jnp.int32), axis=2) - 1
    segment = jnp.where(places[:, None, :] < total_len, segment, -2)
    first = jnp.any(live & (starts == at), axis=2)[:, :, reach : reach + span]
    here = segment[:, :, reach : reach + span]
    columns = [first]
    for k in range(1, TAPS):
        columns.append(segment[:, :, reach - k : reach - k + span] == here)
    for k in range(1, TAPS):
        columns.append(segment[:, :, reach + k : reach + k + span] == here)
    columns.append(jnp.zeros_like(first))
    return jnp.stack(columns, axis=-1).astype(F32)


def shards(
    block_input,
    seq_lengths,
    mixer_gain,
    branch_weight,
    recur_weight,
    conv_kernel,
    conv_bias,
    recur_gate_weight,
    recur_gate_bias,
    input_gate_weight,
    input_gate_bias,
    decay_param,
    mixer_weight,
    mlp_gain,
    gate_weight,
    up_weight,
    down_weight,
    cotangent,
):
    rows, span, width = block_input.shape
    tokens = rows * span
    seq_count, fsdp_count = lax.axis_size("seq"), lax.axis_size("fsdp")
    device_count = seq_count * fsdp_count
    channel_rows = branch_weight.shape[0]
    block_size = recur_gate_weight.shape[1]
    low, dp = device_bits(seq_count, fsdp_count, channel_rows, block_size)
    step = low // fsdp_count
    me = linear_index()
    seq_index = lax.axis_index("seq")
    tp_index = number_of(me, (2 * low, low))
    share = 1 << len(dp)
    channels = share * channel_rows
    blocks = 4 * rows
    scalars = seq_index.astype(jnp.int32).reshape(1)
    place_bits = len(dp) + 2
    high_bits = tuple(b for b in reversed(dp) if b > low)
    low_bits = tuple(b for b in reversed(dp) if b < low)
    high, deep = 1 << len(high_bits), 1 << len(low_bits)
    seq_dp = tuple(b for b in dp if b >= fsdp_count)

    def across_blocks(own):
        found = {}
        for mask, unit in gather_units(own, seq_dp):
            for j in range(4):
                found[mask // fsdp_count | j * step] = unit[j]
        return jnp.stack([found[x] for x in range(seq_count)])

    def by_owner(weight, unit):
        names = list(range(place_bits - 1, -1, -1))
        where = {1 << k: 1 + i for i, k in enumerate(names)}
        split = weight.reshape((weight.shape[0],) + (2,) * place_bits + (unit,))
        axes = (where[2 * low], where[low], 0) + tuple(where[b] for b in dp) + (place_bits + 1,)
        return jnp.transpose(split, axes).reshape(4, weight.shape[0], share * unit)

    def from_owner(parts, unit):
        count = parts.shape[1]
        split = parts.reshape((2, 2, count) + (2,) * len(dp) + (unit,))
        where = {2 * low: 0, low: 1}
        where.update({b: 3 + i for i, b in enumerate(dp)})
        names = [1 << k for k in range(place_bits - 1, -1, -1)]
        axes = (2,) + tuple(where[b] for b in names) + (3 + len(dp),)
        return jnp.transpose(split, axes).reshape(count, device_count * unit)

    def swap_owners(parts):
        got = jnp.zeros_like(parts)
        for j in range(4):
            peer = jnp.bitwise_xor(tp_index, j)
            part = pick(parts, peer, 0)
            got = put(got, trade(part, j * low) if j else part, peer, 0)
        return got

    def gather_columns(weight, unit):
        piece = swap_owners(by_owner(weight, unit))
        whole = jnp.zeros((high, 4, deep) + piece.shape[1:], weight.dtype)
        for mask, got in gather_units(piece, dp):
            owner = jnp.bitwise_xor(me, mask)
            whole = lax.dynamic_update_slice(
                whole,
                got[None, :, None],
                (number_of(owner, high_bits), 0, number_of(owner, low_bits), 0, 0),
            )
        return whole.reshape(-1, piece.shape[-1])

    def scatter_columns(grads, unit):
        rows_each = grads.shape[0] // device_count
        value = grads.reshape(
            (2,) * len(high_bits) + (4,) + (2,) * len(low_bits) + (rows_each, grads.shape[1])
        )
        for b in dp:
            axis = len(high_bits) - 1 if b > low else len(high_bits) + 1 + len(low_bits) - 1
            left = [c for c in dp if c >= b]
            axis = sum(c > low for c in left) - 1 if b > low else (
                sum(c > low for c in left) + sum(c < low for c in left)
            )
            value = scatter_bit(value, axis, b, me).astype(BF16)
        return from_owner(swap_owners(value).astype(F32), unit)

    gains = jnp.stack([mixer_gain, mlp_gain])[None]
    for b in dp:
        got = trade(gains, b)
        mine = bit_of(me, b) == 0
        gains = jnp.concatenate([jnp.where(mine, gains, got), jnp.where(mine, got, gains)])
    gains = jnp.stack([gains] + [trade(gains, j * low) for j in (1, 2, 3)])
    gains = jnp.take(gains, jnp.bitwise_xor(tp_index, jnp.arange(4)), axis=0)
    gains = gains.reshape(4, high, deep, 2, -1).transpose(3, 1, 0, 2, 4).reshape(2, width)
    gain_one, gain_two = gains[0].astype(F32), gains[1].astype(F32)

    small = jnp.concatenate(
        [
            conv_kernel,
            conv_bias[:, None],
            recur_gate_bias[:, None],
            input_gate_bias[:, None],
            decay_param[:, None],
            recur_gate_weight,
            input_gate_weight,
        ],
        axis=1,
    )
    small = gather_rows(small, dp, me).reshape(channels, -1)
    coef = small[:, :8].astype(F32).T
    decay_vec = coef[7]
    speed = DECAY_SCALE * jax.nn.softplus(-decay_vec)
    coef = jnp.concatenate([coef[:7], speed[None]])
    in_block = block_size // channel_rows
    place = jnp.arange(share, dtype=jnp.int32)
    spots = [(place >> (len(dp) - 1 - i)) & 1 for i in range(len(dp))]
    inner_bits = [b for b in dp if b < in_block]
    offset = sum((spots[dp.index(b)] * b for b in inner_bits), jnp.zeros_like(place))
    group = sum(
        (spots[dp.index(b)] * b for b in dp if b >= in_block), jnp.zeros_like(place)
    )
    same_block = group[:, None] == group[None, :]

    def widen(gate_rows):
        parts = gate_rows.reshape(share, channel_rows, in_block, channel_rows)
        spread = jnp.take(parts, offset, axis=2)
        spread = jnp.where(same_block[:, None, :, None], spread, jnp.zeros_like(spread))
        return spread.reshape(channels, channels)

    def narrow(wide):
        parts = wide.reshape(share, channel_rows, share, channel_rows)
        out = []
        for i in range(in_block):
            chosen = same_block & (offset == i)[None, :]
            out.append(jnp.sum(jnp.where(chosen[:, None, :, None], parts, 0.0), axis=2))
        return jnp.stack(out, axis=2).reshape(channels, block_size)

    rate_wide = widen(small[:, 8 : 8 + block_size])
    gate_wide = widen(small[:, 8 + block_size :])

    lengths = lax.dynamic_slice_in_dim(seq_lengths, lax.axis_index("fsdp") * rows, rows, 0)
    block_ids = jnp.bitwise_xor(seq_index, jnp.arange(4, dtype=jnp.int32) * step)
    marks = sequence_marks(lengths, block_ids, span, seq_count * span).reshape(blocks, span, 8)

    branch_q = gather_rows(branch_weight, dp, me).reshape(channels, width)
    recur_q = gather_rows(recur_weight, dp, me).reshape(channels, width)
    mixer_q = gather_columns(mixer_weight, channel_rows)
    hidden_rows = gate_weight.shape[0]
    gate_q = gather_rows(gate_weight, dp, me).reshape(-1, width)
    up_q = gather_rows(up_weight, dp, me).reshape(-1, width)
    down_q = gather_columns(down_weight, hidden_rows)

    input_own = block_input.reshape(tokens, width)
    cot_own = cotangent.reshape(tokens, width)
    input_all = share_tokens(input_own, low).astype(F32)
    scale_one = inverse_rms(input_all)
    normed = (input_all * scale_one * gain_one).astype(BF16)
    recur_in = project(normed, recur_q).astype(BF16).reshape(blocks, span, channels)
    edge = recur_in[:, span - 4 :].reshape(4, rows, 4, channels)
    halo = across_blocks(edge).astype(F32).reshape(seq_count * rows, 4, channels)
    branch = project(normed, branch_q).reshape(blocks, span, channels)
    shape = (blocks, span, channels)
    one = (blocks, 1, channels)
    everything = (seq_count * rows, 1, channels)
    conv, s_val, q_val, prod, part, ends = call(
        functools.partial(forward_kernel, rows, step),
        [(shape, BF16)] + [(shape, F32)] * 4 + [((blocks, 2, channels), F32)],
        scalars,
        [recur_in, halo, marks, coef, rate_wide, gate_wide],
        [pltpu.VMEM((span + 8, channels), F32)],
    )
    ends = across_blocks(ends.reshape(4, rows, 2, channels)).reshape(-1, 2, channels)
    state, mixed, came = call(
        functools.partial(state_kernel, rows, step),
        [(shape, F32), (shape, BF16), (one, F32)],
        scalars,
        [prod, part, ends, branch],
        [pltpu.VMEM(everything, F32)],
    )
    mixed_flat = mixed.reshape(4 * tokens, channels)
    residual = input_own.astype(F32) + sum_tokens(project(mixed_flat, mixer_q).astype(BF16), low)

    scale_two = inverse_rms(residual)
    unit_two = residual * scale_two
    normed_two = share_tokens((unit_two * gain_two).astype(BF16), low)
    cot_all = share_tokens(cot_own, low)
    gate_val = project(normed_two, gate_q)
    up_val = project(normed_two, up_q)
    act, slope = gelu_parts(gate_val)
    hidden = (act * up_val).astype(BF16)
    down_part = project(hidden, down_q).astype(BF16)
    grad_hidden = back_project(cot_all, down_q)
    grad_gate = (grad_hidden * up_val * slope).astype(BF16)
    grad_up = (grad_hidden * act).astype(BF16)
    grad_two_part = (back_project(grad_gate, gate_q) + back_project(grad_up, up_q)).astype(BF16)
    grad_two = sum_tokens(grad_two_part, low)
    block_output = (residual + sum_tokens(down_part, low)).astype(BF16)
    scaled = grad_two * gain_two
    grad_residual = cot_own.astype(F32) + scale_two * (
        scaled - unit_two * jnp.mean(scaled * unit_two, axis=-1, keepdims=True)
    )
    gain_two_part = jnp.sum(grad_two * unit_two, axis=0)

    grad_mix = share_tokens(grad_residual.astype(BF16), low)
    grad_mixed = back_project(grad_mix, mixer_q).reshape(shape)
    grad_branch, prod_back, part_back, ends_back = call(
        adjoint_kernel,
        [(shape, BF16), (shape, F32), (shape, F32), ((blocks, 2, channels), F32)],
        scalars,
        [grad_mixed, state, branch, s_val, marks, coef],
        [pltpu.VMEM((span + 8, channels), F32)],
    )
    ends_back = across_blocks(ends_back.reshape(4, rows, 2, channels)).reshape(-1, 2, channels)
    square = (channels, channels)
    grad_conv, rate_square, gate_square, sums = call(
        functools.partial(gates_kernel, rows, step),
        [(shape, F32), (square, F32), (square, F32), ((8, channels), F32)],
        scalars,
        [
            prod_back, part_back, ends_back, s_val, q_val, conv, state, came, recur_in, halo,
            marks, coef, rate_wide, gate_wide,
        ],
        [
            pltpu.VMEM((4 * tokens, channels), BF16),
            pltpu.VMEM((4 * tokens, channels), BF16),
            pltpu.VMEM(everything, F32),
            pltpu.VMEM((span + 8, channels), F32),
            pltpu.VMEM((span + 8, channels), F32),
        ],
    )
    edge_back = grad_conv[:, :4].astype(BF16).reshape(4, rows, 4, channels)
    halo_back = across_blocks(edge_back).astype(F32).reshape(seq_count * rows, 4, channels)
    (grad_recur,) = call(
        functools.partial(unconvolve_kernel, rows, step, seq_count),
        [(shape, BF16)],
        scalars,
        [grad_conv, halo_back, marks, coef],
        [pltpu.VMEM((span + 8, channels), F32)],
    )
    grad_branch = grad_branch.reshape(4 * tokens, channels)
    grad_recur = grad_recur.reshape(4 * tokens, channels)
    grad_normed_part = back_project(grad_branch, branch_q) + back_project(grad_recur, recur_q)
    gain_one_part = jnp.sum(grad_normed_part * input_all * scale_one, axis=0)
    grad_normed = sum_tokens(grad_normed_part.astype(BF16), low)
    own_scale = scale_one[:tokens]
    unit_one = input_own.astype(F32) * own_scale
    scaled_one = grad_normed * gain_one
    input_grad = (
        grad_residual
        + own_scale
        * (scaled_one - unit_one * jnp.mean(scaled_one * unit_one, axis=-1, keepdims=True))
    ).astype(BF16)

    def row_grad(grads, values):
        whole = outer(grads, values).astype(BF16)
        return scatter_rows(whole.reshape(share, -1, width), dp, me)

    gate_weight_grad = row_grad(grad_gate, normed_two)
    up_weight_grad = row_grad(grad_up, normed_two)
    down_weight_grad = scatter_columns(outer(cot_all, hidden).astype(BF16), hidden_rows)
    mixer_weight_grad = scatter_columns(outer(grad_mix, mixed_flat).astype(BF16), channel_rows)
    branch_weight_grad = row_grad(grad_branch, normed)
    recur_weight_grad = row_grad(grad_recur, normed)

    gain_parts = jnp.stack([gain_one_part, gain_two_part]).reshape(2, high, 4, deep, -1)
    gain_parts = gain_parts.transpose(2, 1, 3, 0, 4).reshape(4, share, -1).astype(BF16)
    gain_sum = pick(gain_parts, tp_index, 0).astype(F32)
    for j in (1, 2, 3):
        sent = pick(gain_parts, jnp.bitwise_xor(tp_index, j), 0)
        gain_sum = gain_sum + trade(sent, j * low).astype(F32)
    gain_sum = gain_sum.reshape((2,) * len(dp) + (-1,))
    gain_sum = jnp.transpose(gain_sum, tuple(reversed(range(len(dp)))) + (len(dp),))
    gain_sum = gain_sum.reshape(share, -1)
    decay_sum = DECAY_SCALE * jax.nn.sigmoid(-decay_vec) * sums[2]
    small_grads = jnp.concatenate(
        [
            sums[4:8].T,
            sums[3][:, None],
            sums[0][:, None],
            sums[1][:, None],
            decay_sum[:, None],
            narrow(rate_square),
            narrow(gate_square),
        ],
        axis=1,
    )
    per_row = small_grads.shape[1]
    packed = jnp.concatenate([small_grads.reshape(share, -1), gain_sum], axis=1).astype(BF16)
    packed = scatter_rows(packed, dp, me)
    gain_grads = packed[channel_rows * per_row :].reshape(2, -1)
    mine = packed[: channel_rows * per_row].reshape(channel_rows, per_row)
    return (
        block_output.reshape(rows, span, width),
        input_grad.reshape(rows, span, width),
        gain_grads[0],
        branch_weight_grad,
        recur_weight_grad,
        mine[:, :TAPS],
        mine[:, 4],
        mine[:, 8 : 8 + block_size],
        mine[:, 5],
        mine[:, 8 + block_size :],
        mine[:, 6],
        mine[:, 7],
        mixer_weight_grad,
        gain_grads[1],
        gate_weight_grad,
        up_weight_grad,
        down_weight_grad,
    )


def solution(mesh):
    tokens, spread, table = P("fsdp", "seq", None), P(AXES), P(AXES, None)
    in_specs = (
        tokens, P(), spread, table, table, table, spread, table, spread, table, spread, spread,
        table, spread, table, table, table, tokens,
    )
    out_specs = (
        tokens, tokens, spread, table, table, table, spread, table, spread, table, spread, spread,
        table, spread, table, table, table,
    )
    return jax.shard_map(shards, mesh=mesh, in_specs=in_specs, out_specs=out_specs, check_vma=False)
```

time: 2160 us -> 998 us (0.46); the launches traced: 2120 us -> 986 us
  blocking collectives: 573 us -> 0 us
  local copies, waits for them, and re-layouts: 459 us -> 203 us
  waiting for transfers between devices: 690 us -> 457 us
  other arithmetic: 170 us -> 59.3 us
  Pallas kernels: 0 us -> 42.1 us
  starting transfers between devices: 100 us -> 134 us
  matrix products: 109 us -> 87.3 us
    ppermute x2 -> x123, waiting for transfers between devices: 0.01 us -> 457 us  [trade(): return lax.ppermute(value, AXES, [(i, i ^ mask) for i in range(count)])]
    all_to_all x6 -> x0, blocking collectives: 301 us -> none  [the longest x1 86.6 us: shards(): lax.all_to_all(col_sent[1].astype(jnp.bfloat16), 'fsdp', split_axis=2, co...]
    pad x40 -> x0, local copies, waits for them, and re-layouts: 279 us -> none  [the longest x20 140 us: mixer_forward(): lax.associative_scan(combine, (decay_gate, inject), axis=1)]
    reduce_scatter x8 -> x0, waiting for transfers between devices: 234 us -> none  [the longest x1 119 us: shards(): lax.psum_scatter(row_back[3].astype(jnp.bfloat16), 'seq', scatter_dimensi...]
    all_gather x7 -> x0, blocking collectives: 210 us -> none  [the longest x4 126 us: carried_in(): lax.all_gather(part.astype(kind), axis)]
    all_to_all x24 -> x0, waiting for transfers between devices: 157 us -> none  [the longest x1 31.3 us: shards(): lax.all_to_all(row_parts[1], 'fsdp', split_axis=0, concat_axis=2, tiled=T...]
    psum x2 -> x0, waiting for transfers between devices: 130 us -> none  [the longest x1 80.8 us: shards(): lax.psum(project(mixed_out, mixer_cols).astype(jnp.bfloat16), 'fsdp')]
    ppermute x2 -> x123, starting transfers between devices: 8.75 us -> 134 us  [trade(): return lax.ppermute(value, AXES, [(i, i ^ mask) for i in range(count)])]
  transfers between devices with their start and end apart: 45 -> 123, of which waited for: 23 -> 62; matrix products, arithmetic and copies ran while one was open for 21% -> 30% of each run, Pallas kernels for 0% -> 4%
where the time goes in v1:
time: 998 us; the launch traced here: 986 us
  waiting for transfers between devices  457 us (46%)
  local copies, waits for them, and re-layouts  203 us (20%)
  starting transfers between devices  134 us (13%)
  matrix products  87.3 us (9%)
  other arithmetic  59.3 us (6%)
  Pallas kernels  42.1 us (4%)
    ppermute x123, waiting for transfers between devices, trade(): return lax.ppermute(value, AXES, [(i, i ^ mask) for i in range(count)])  457 us
    ppermute x123, starting transfers between devices, trade(): return lax.ppermute(value, AXES, [(i, i ^ mask) for i in range(count)])  134 us
    pallas_call x5, Pallas kernels, call(): pl.pallas_call(body, out_shape=[jax.ShapeDtypeStruct(shape, kind) for sha...  42.1 us
    dynamic_update_slice x52, local copies, waits for them, and re-layouts, put(): return lax.dynamic_update_index_in_dim(buffer, part, index, axis)  38.2 us
    dot_general x6, matrix products, project(): lax.dot_general(left, weight, (((1,), (1,)), ((), ())), preferred_element...  34.6 us
    dot_general x6, matrix products, back_project(): lax.dot_general(left, weight, (((1,), (0,)), ((), ())), preferred_element...  31.9 us
    unnamed x183, local copies, waits for them, and re-layouts  24 us
    dot_general x6, matrix products, outer(): lax.dot_general(grads, values, (((0,), (0,)), ((), ())), preferred_elemen...  20.7 us
  transfers between devices with their start and end apart: 123, of which 62 were waited for; matrix products, arithmetic and copies ran while one was open for 30% of the time, Pallas kernels for 4%

profile of v1, /device:TPU:20, one launch (start us, length us, event | category | flops | bytes accessed | tf_op | source)
XLA Modules:
  0.0 985.6 jit_solution(10440473840207705180)
XLA Ops:
  20.9 4.6 reshape.665
  42.5 4.0 broadcast.463.clone.1
  54.7 4.1 collective-permute-done.6
  68.8 8.9 collective-permute-done.18
  86.4 3.7 collective-permute-start.34
  130.3 3.5 collective-permute-done.65
  137.0 3.8 collective-permute-done.66
  141.5 3.3 broadcast_in_dim.402
  153.4 10.7 %collective-permute-done.26 = bf16[80,2048]{1,0:T(8,128)(2,1)S(1)} collective-permute-done((bf16[80,2048]{1,0:T(8,128)(2,1)S(1)}, bf16[80,2048]{1,0:T(8,128)(2,1)S(1)}, u32[]{:S(2)}, u32[]{:S(2)}) %collective-permute-start.26) | collective-permute-done | bytes 327712 | tf_op jit(solution)/shard_map/ppermute | solution.py:46
  164.1 3.4 collective-permute-start.36
  169.4 11.4 %collective-permute-done.36 = bf16[4,64,640]{2,1,0:T(8,128)(2,1)S(1)} collective-permute-done((bf16[4,64,640]{2,1,0:T(8,128)(2,1)}, bf16[4,64,640]{2,1,0:T(8,128)(2,1)S(1)}, u32[]{:S(2)}, u32[]{:S(2)}) %collective-permute-start.36) | collective-permute-done | bytes 327712 | tf_op jit(solution)/shard_map/ppermute | solution.py:46
  189.3 6.6 collective-permute-done.77
  199.3 8.1 collective-permute-done.78
  215.8 17.4 %collective-permute-done.28 = bf16[80,2048]{1,0:T(8,128)(2,1)S(1)} collective-permute-done((bf16[80,2048]{1,0:T(8,128)(2,1)S(1)}, bf16[80,2048]{1,0:T(8,128)(2,1)S(1)}, u32[]{:S(2)}, u32[]{:S(2)}) %collective-permute-start.28) | collective-permute-done | bytes 327712 | tf_op jit(solution)/shard_map/ppermute | solution.py:46
  238.8 8.6 collective-permute-done.38
  254.6 4.5 collective-permute-done.2
  275.1 44.1 %collective-permute-done.50 = bf16[192,2048]{1,0:T(8,128)(2,1)S(1)} collective-permute-done((bf16[192,2048]{1,0:T(8,128)(2,1)}, bf16[192,2048]{1,0:T(8,128)(2,1)S(1)}, u32[]{:S(2)}, u32[]{:S(2)}) %collective-permute-start.50) | collective-permute-done | bytes 786464 | tf_op jit(solution)/shard_map/ppermute | solution.py:46
  323.4 3.6 convolution_convert_fusion.8
  328.2 4.7 fusion.60.branch
  343.6 11.2 %shard_map.305 = (bf16[8,64,640]{2,1,0:T(8,128)(2,1)}, f32[8,64,640]{2,1,0:T(8,128)}, f32[8,64,640]{2,1,0:T(8,128)}, f32[8,64,640]{2,1,0:T(8,128)}, f32[8,64,640]{2,1,0:T(8,128)}, /*index=5*/f32[8,2,640]{2,1,0:T(2,128)}) custom-call(s32[1]{0:T(128)} %bitcast.1.scalars, bf16[8,64,640]{2,1,0:T(8,128)(2,1)} %bitcast.531, ...), custom_call_target="tpu_custom_call" | custom-call | tf_op jit(solution)/shard_map/pallas_call | solution.py:127
  363.6 4.3 shard_map.306
  378.4 15.0 %collective-permute-done.52 = bf16[192,2048]{1,0:T(8,128)(2,1)S(1)} collective-permute-done((bf16[192,2048]{1,0:T(8,128)(2,1)S(1)}, bf16[192,2048]{1,0:T(8,128)(2,1)S(1)}, u32[]{:S(2)}, u32[]{:S(2)}) %collective-permute-start.52) | collective-permute-done | bytes 786464 | tf_op jit(solution)/shard_map/ppermute | solution.py:46
  404.3 4.9 collective-permute-done.45
  409.2 9.8 collective-permute-done.44
  428.5 10.3 %collective-permute-done.47 = bf16[128,2048]{1,0:T(8,128)(2,1)S(1)} collective-permute-done((bf16[128,2048]{1,0:T(8,128)(2,1)S(1)}, bf16[128,2048]{1,0:T(8,128)(2,1)S(1)}, u32[]{:S(2)}, u32[]{:S(2)}) %collective-permute-start.47) | collective-permute-done | bytes 524320 | tf_op jit(solution)/shard_map/ppermute | solution.py:46
  442.7 3.8 collective-permute-done.48
  447.0 5.1 fusion.61
  453.1 8.0 fusion.62
  461.1 10.6 %fusion.14 = (bf16[512,1536]{1,0:T(8,128)(2,1)S(1)}, bf16[512,1536]{1,0:T(8,128)(2,1)S(1)}, bf16[512,1536]{1,0:T(8,128)(2,1)}) fusion(f32[512,1536]{1,0:T(8,128)} %fusion.62, f32[512,1536]{1,0:T(8,128)S(1)} %copy-done.67, bf16[512,2048]{1,0:T(8,128)(2,1)S(1)} %copy-done.46, bf16[1536,2048]{1,0:T(8,128)(2,1)} %bitcast.90), kind=kOutput, calls=%fused_computation.32 | convolution fusion | flops 3240886272 | bytes 19398656 | tf_op jit(solution)/shard_map/dot_general | solution.py:103
  471.7 3.4 fusion.63
  475.1 3.7 convolution_convert_fusion.1
  478.8 3.7 convolution_convert_fusion.2
  482.5 8.8 add_convert_fusion
  493.9 7.5 convolution_convert_fusion.6
  501.4 5.6 convolution_convert_fusion
  514.5 7.5 collective-permute-done.82
  522.0 11.7 %collective-permute-done.81 = bf16[128,2048]{1,0:T(8,128)(2,1)S(1)} collective-permute-done((bf16[128,2048]{1,0:T(8,128)(2,1)S(1)}, bf16[128,2048]{1,0:T(8,128)(2,1)S(1)}, u32[]{:S(2)}, u32[]{:S(2)}) %collective-permute-start.81) | collective-permute-done | bytes 524320 | tf_op jit(solution)/shard_map/ppermute | solution.py:46
  534.2 7.1 collective-permute-done.75
  552.9 3.9 collective-permute-done.85
  566.3 3.6 convolution_convert_fusion.3
  572.8 9.0 shard_map.307
  594.0 14.2 %shard_map.308 = (f32[8,64,640]{2,1,0:T(8,128)}, f32[640,640]{1,0:T(8,128)}, f32[640,640]{1,0:T(8,128)}, f32[8,640]{1,0:T(8,128)}) custom-call(s32[1]{0:T(128)} %bitcast.1.scalars, f32[8,64,640]{2,1,0:T(8,128)} %get-tuple-element.42.prod, f32[8,64,640]{2,1,0:T(8,128)} %get-tuple-element.43.part, f32[16,2,640]{2,1,0:T(2,128)} %bitcast.558, ...), custom_call_target="tpu_custom_call" | custom-call | tf_op jit(solution)/shard_map/pallas_call | solution.py:127
  613.2 3.4 reshape.676
  616.6 3.4 reshape.678
  620.0 6.7 select_reduce_fusion.3
  629.8 3.5 shard_map.309
  633.3 3.8 fusion.65
  637.1 5.1 fusion.7
  652.9 4.3 concatenate.50
  674.3 21.0 %collective-permute-done.98 = bf16[26368]{0:T(1024)(128)(2,1)S(1)} collective-permute-done((bf16[26368]{0:T(1024)(128)(2,1)S(1)}, bf16[26368]{0:T(1024)(128)(2,1)S(1)}, u32[]{:S(2)}, u32[]{:S(2)}) %collective-permute-start.98) | collective-permute-done | bytes 52768 | tf_op jit(solution)/shard_map/ppermute | solution.py:46
  700.4 7.8 collective-permute-done.90
  739.2 9.4 collective-permute-done.106
  748.9 13.8 %collective-permute-done.103 = bf16[2,80,2048]{2,1,0:T(8,128)(2,1)S(1)} collective-permute-done((bf16[2,80,2048]{2,1,0:T(8,128)(2,1)}, bf16[2,80,2048]{2,1,0:T(8,128)(2,1)S(1)}, u32[]{:S(2)}, u32[]{:S(2)}) %collective-permute-start.103) | collective-permute-done | bytes 655392 | tf_op jit(solution)/shard_map/ppermute | solution.py:46
  763.7 11.7 %collective-permute-done.107 = bf16[4,64,640]{2,1,0:T(8,128)(2,1)S(1)} collective-permute-done((bf16[4,64,640]{2,1,0:T(8,128)(2,1)S(1)}, bf16[4,64,640]{2,1,0:T(8,128)(2,1)S(1)}, u32[]{:S(2)}, u32[]{:S(2)}) %collective-permute-start.107) | collective-permute-done | bytes 327712 | tf_op jit(solution)/shard_map/ppermute | solution.py:46
  775.4 3.4 collective-permute-start.104
  783.5 7.6 collective-permute-start.109
  804.8 3.5 reshape.709
  810.3 52.7 %collective-permute-done.118 = bf16[2,4,64,1536]{3,2,1,0:T(8,128)(2,1)} collective-permute-done((bf16[2,4,64,1536]{3,2,1,0:T(8,128)(2,1)}, bf16[2,4,64,1536]{3,2,1,0:T(8,128)(2,1)}, u32[]{:S(2)}, u32[]{:S(2)}) %collective-permute-start.118) | collective-permute-done | bytes 1572896 | tf_op jit(solution)/shard_map/ppermute | solution.py:46
  872.7 61.3 %collective-permute-done.119 = bf16[4,64,1536]{2,1,0:T(8,128)(2,1)S(1)} collective-permute-done((bf16[4,64,1536]{2,1,0:T(8,128)(2,1)S(1)}, bf16[4,64,1536]{2,1,0:T(8,128)(2,1)S(1)}, u32[]{:S(2)}, u32[]{:S(2)}) %collective-permute-start.119) | collective-permute-done | bytes 786464 | tf_op jit(solution)/shard_map/ppermute | solution.py:46
  939.0 11.9 %collective-permute-done.113 = bf16[192,2048]{1,0:T(8,128)(2,1)S(1)} collective-permute-done((bf16[192,2048]{1,0:T(8,128)(2,1)S(1)}, bf16[192,2048]{1,0:T(8,128)(2,1)S(1)}, u32[]{:S(2)}, u32[]{:S(2)}) %collective-permute-start.113) | collective-permute-done | bytes 786464 | tf_op jit(solution)/shard_map/ppermute | solution.py:46
  952.2 13.9 %collective-permute-done.116 = bf16[192,2048]{1,0:T(8,128)(2,1)S(1)} collective-permute-done((bf16[192,2048]{1,0:T(8,128)(2,1)S(1)}, bf16[192,2048]{1,0:T(8,128)(2,1)S(1)}, u32[]{:S(2)}, u32[]{:S(2)}) %collective-permute-start.116) | collective-permute-done | bytes 786464 | tf_op jit(solution)/shard_map/ppermute | solution.py:46
  967.5 4.2 collective-permute-done.121
  971.8 4.1 collective-permute-done.122
  975.9 3.4 reshape.727
  (676 shorter events, 391.4 us)
Async XLA Ops:
  0.7 183.1 %collective-permute-start = (bf16[128,2048]{1,0:T(8,128)(2,1)}, bf16[128,2048]{1,0:T(8,128)(2,1)}, u32[]{:S(2)}, u32[]{:S(2)}) collective-permute-start(bf16[128,2048]{1,0:T(8,128)(2,1)} %bitcast.504), channel_id=1, source_target_pairs={{0,4},{1,5},{2,6},{3,7},{4,0},{5,1},{6,2},{7,3},{8,12},{9,13},{10,... | collective-permute-start | bytes 1572872 | tf_op jit(solution)/shard_map/ppermute | solution.py:46
  1.2 185.8 %collective-permute-start.1 = (bf16[128,2048]{1,0:T(8,128)(2,1)}, bf16[128,2048]{1,0:T(8,128)(2,1)}, u32[]{:S(2)}, u32[]{:S(2)}) collective-permute-start(bf16[128,2048]{1,0:T(8,128)(2,1)} %bitcast.505), channel_id=1, source_target_pairs={{0,8},{1,9},{2,10},{3,11},{4,12},{5,13},{6,14},{7,15},{8,0},{9,1},... | collective-permute-start | bytes 1572872 | tf_op jit(solution)/shard_map/ppermute | solution.py:46
  4.0 46.0 %collective-permute-start.4 = (bf16[1,2,64]{2,1,0:T(2,128)(2,1)}, bf16[1,2,64]{2,1,0:T(2,128)(2,1)}, u32[]{:S(2)}, u32[]{:S(2)}) collective-permute-start(bf16[1,2,64]{2,1,0:T(2,128)(2,1)} %maximum_bitcast_fusion.1), channel_id=1, source_target_pairs={{0,1},{1,0},{2,3},{3,2},{4,5},{5,4},{6,7},{7,6},{8,9},{9,8},{10,11... | collective-permute-start | bytes 776 | tf_op jit(solution)/shard_map/ppermute | solution.py:46
  63.5 83.5 %collective-permute-start.10 = (bf16[80,2048]{1,0:T(8,128)(2,1)}, bf16[80,2048]{1,0:T(8,128)(2,1)}, u32[]{:S(2)}, u32[]{:S(2)}) collective-permute-start(bf16[80,2048]{1,0:T(8,128)(2,1)} %param.24), channel_id=1, source_target_pairs={{0,16},{1,17},{2,18},{3,19},{4,20},{5,21},{6,22},{7,23},{8,24},{9,... | collective-permute-start | bytes 983048 | tf_op jit(solution)/shard_map/ppermute | solution.py:46
  64.1 87.0 %collective-permute-start.11 = (bf16[80,2048]{1,0:T(8,128)(2,1)}, bf16[80,2048]{1,0:T(8,128)(2,1)}, u32[]{:S(2)}, u32[]{:S(2)}) collective-permute-start(bf16[80,2048]{1,0:T(8,128)(2,1)} %param.24), channel_id=1, source_target_pairs={{0,2},{1,3},{2,0},{3,1},{4,6},{5,7},{6,4},{7,5},{8,10},{9,11},{10,... | collective-permute-start | bytes 983048 | tf_op jit(solution)/shard_map/ppermute | solution.py:46
  109.0 18.0 %collective-permute-start.64 = (bf16[64,1536]{1,0:T(8,128)(2,1)}, bf16[64,1536]{1,0:T(8,128)(2,1)}, u32[]{:S(2)}, u32[]{:S(2)}) collective-permute-start(bf16[64,1536]{1,0:T(8,128)(2,1)} %get-tuple-element.186), channel_id=1, source_target_pairs={{0,4},{1,5},{2,6},{3,7},{4,0},{5,1},{6,2},{7,3},{8,12},{9,13},{10,... | collective-permute-start | bytes 589832 | tf_op jit(solution)/shard_map/ppermute | solution.py:46
  140.8 68.8 %collective-permute-start.13 = (bf16[80,2048]{1,0:T(8,128)(2,1)}, bf16[80,2048]{1,0:T(8,128)(2,1)S(1)}, u32[]{:S(2)}, u32[]{:S(2)}) collective-permute-start(bf16[80,2048]{1,0:T(8,128)(2,1)} %param.24), channel_id=1, source_target_pairs={{0,1},{1,0},{2,3},{3,2},{4,5},{5,4},{6,7},{7,6},{8,9},{9,8},{10,11... | collective-permute-start | bytes 983048 | tf_op jit(solution)/shard_map/ppermute | solution.py:46
  147.0 17.1 %collective-permute-start.26 = (bf16[80,2048]{1,0:T(8,128)(2,1)S(1)}, bf16[80,2048]{1,0:T(8,128)(2,1)S(1)}, u32[]{:S(2)}, u32[]{:S(2)}) collective-permute-start(bf16[80,2048]{1,0:T(8,128)(2,1)S(1)} %copy-done.44), channel_id=1, source_target_pairs={{0,16},{1,17},{2,18},{3,19},{4,20},{5,21},{6,22},{7,23},{8,24},{9,... | collective-permute-start | bytes 983048 | tf_op jit(solution)/shard_map/ppermute | solution.py:46
  151.1 17.1 %collective-permute-start.27 = (bf16[80,2048]{1,0:T(8,128)(2,1)S(1)}, bf16[80,2048]{1,0:T(8,128)(2,1)S(1)}, u32[]{:S(2)}, u32[]{:S(2)}) collective-permute-start(bf16[80,2048]{1,0:T(8,128)(2,1)S(1)} %copy-done.44), channel_id=1, source_target_pairs={{0,2},{1,3},{2,0},{3,1},{4,6},{5,7},{6,4},{7,5},{8,10},{9,11},{10,... | collective-permute-start | bytes 983048 | tf_op jit(solution)/shard_map/ppermute | solution.py:46
  164.1 16.7 %collective-permute-start.36 = (bf16[4,64,640]{2,1,0:T(8,128)(2,1)}, bf16[4,64,640]{2,1,0:T(8,128)(2,1)S(1)}, u32[]{:S(2)}, u32[]{:S(2)}) collective-permute-start(bf16[4,64,640]{2,1,0:T(8,128)(2,1)} %bitcast_dynamic-update-slice_fusion.57), channel_id=1, source_target_pairs={{0,16},{1,17},{2,18},{3,19},{4,20},{5,21},{6,22},{7,23},{8,24},{9,... | collective-permute-start | bytes 983048 | tf_op jit(solution)/shard_map/ppermute | solution.py:46
  180.8 53.1 %collective-permute-start.29 = (bf16[80,2048]{1,0:T(8,128)(2,1)S(1)}, bf16[80,2048]{1,0:T(8,128)(2,1)S(1)}, u32[]{:S(2)}, u32[]{:S(2)}) collective-permute-start(bf16[80,2048]{1,0:T(8,128)(2,1)S(1)} %copy-done.44), channel_id=1, source_target_pairs={{0,1},{1,0},{2,3},{3,2},{4,5},{5,4},{6,7},{7,6},{8,9},{9,8},{10,11... | collective-permute-start | bytes 983048 | tf_op jit(solution)/shard_map/ppermute | solution.py:46
  183.8 23.6 %collective-permute-start.78 = (bf16[128,2048]{1,0:T(8,128)(2,1)S(1)}, bf16[128,2048]{1,0:T(8,128)(2,1)S(1)}, u32[]{:S(2)}, u32[]{:S(2)}) collective-permute-start(bf16[128,2048]{1,0:T(8,128)(2,1)S(1)} %bitcast.542), channel_id=1, source_target_pairs={{0,8},{1,9},{2,10},{3,11},{4,12},{5,13},{6,14},{7,15},{8,0},{9,1},... | collective-permute-start | bytes 1572872 | tf_op jit(solution)/shard_map/ppermute | solution.py:46
  187.1 84.7 %collective-permute-start.57 = (bf16[192,2048]{1,0:T(8,128)(2,1)S(1)}, bf16[192,2048]{1,0:T(8,128)(2,1)}, u32[]{:S(2)}, u32[]{:S(2)}) collective-permute-start(bf16[192,2048]{1,0:T(8,128)(2,1)S(1)} %copy-done.31), channel_id=1, source_target_pairs={{0,16},{1,17},{2,18},{3,19},{4,20},{5,21},{6,22},{7,23},{8,24},{9,... | collective-permute-start | bytes 2359304 | tf_op jit(solution)/shard_map/ppermute | solution.py:46
  207.4 66.5 %collective-permute-start.58 = (bf16[192,2048]{1,0:T(8,128)(2,1)S(1)}, bf16[192,2048]{1,0:T(8,128)(2,1)S(1)}, u32[]{:S(2)}, u32[]{:S(2)}) collective-permute-start(bf16[192,2048]{1,0:T(8,128)(2,1)S(1)} %copy-done.31), channel_id=1, source_target_pairs={{0,2},{1,3},{2,0},{3,1},{4,6},{5,7},{6,4},{7,5},{8,10},{9,11},{10,... | collective-permute-start | bytes 2359304 | tf_op jit(solution)/shard_map/ppermute | solution.py:46
  208.8 165.0 %collective-permute-start.60 = (bf16[192,2048]{1,0:T(8,128)(2,1)S(1)}, bf16[192,2048]{1,0:T(8,128)(2,1)}, u32[]{:S(2)}, u32[]{:S(2)}) collective-permute-start(bf16[192,2048]{1,0:T(8,128)(2,1)S(1)} %copy-done.31), channel_id=1, source_target_pairs={{0,1},{1,0},{2,3},{3,2},{4,5},{5,4},{6,7},{7,6},{8,9},{9,8},{10,11... | collective-permute-start | bytes 2359304 | tf_op jit(solution)/shard_map/ppermute | solution.py:46
  213.7 19.6 %collective-permute-start.28 = (bf16[80,2048]{1,0:T(8,128)(2,1)S(1)}, bf16[80,2048]{1,0:T(8,128)(2,1)S(1)}, u32[]{:S(2)}, u32[]{:S(2)}) collective-permute-start(bf16[80,2048]{1,0:T(8,128)(2,1)S(1)} %collective-permute-done.26), channel_id=1, source_target_pairs={{0,2},{1,3},{2,0},{3,1},{4,6},{5,7},{6,4},{7,5},{8,10},{9,11},{10,... | collective-permute-start | bytes 983048 | tf_op jit(solution)/shard_map/ppermute | solution.py:46
  233.2 16.9 %collective-permute-start.39 = (bf16[4,64,640]{2,1,0:T(8,128)(2,1)}, bf16[4,64,640]{2,1,0:T(8,128)(2,1)S(1)}, u32[]{:S(2)}, u32[]{:S(2)}) collective-permute-start(bf16[4,64,640]{2,1,0:T(8,128)(2,1)} %bitcast_dynamic-update-slice_fusion.57), channel_id=1, source_target_pairs={{0,1},{1,0},{2,3},{3,2},{4,5},{5,4},{6,7},{7,6},{8,9},{9,8},{10,11... | collective-permute-start | bytes 983048 | tf_op jit(solution)/shard_map/ppermute | solution.py:46
  266.5 52.8 %collective-permute-start.50 = (bf16[192,2048]{1,0:T(8,128)(2,1)}, bf16[192,2048]{1,0:T(8,128)(2,1)S(1)}, u32[]{:S(2)}, u32[]{:S(2)}) collective-permute-start(bf16[192,2048]{1,0:T(8,128)(2,1)} %param.34), channel_id=1, source_target_pairs={{0,16},{1,17},{2,18},{3,19},{4,20},{5,21},{6,22},{7,23},{8,24},{9,... | collective-permute-start | bytes 2359304 | tf_op jit(solution)/shard_map/ppermute | solution.py:46
  270.4 50.4 %collective-permute-start.51 = (bf16[192,2048]{1,0:T(8,128)(2,1)}, bf16[192,2048]{1,0:T(8,128)(2,1)S(1)}, u32[]{:S(2)}, u32[]{:S(2)}) collective-permute-start(bf16[192,2048]{1,0:T(8,128)(2,1)} %param.34), channel_id=1, source_target_pairs={{0,2},{1,3},{2,0},{3,1},{4,6},{5,7},{6,4},{7,5},{8,10},{9,11},{10,... | collective-permute-start | bytes 2359304 | tf_op jit(solution)/shard_map/ppermute | solution.py:46
  271.8 125.4 %collective-permute-start.53 = (bf16[192,2048]{1,0:T(8,128)(2,1)}, bf16[192,2048]{1,0:T(8,128)(2,1)}, u32[]{:S(2)}, u32[]{:S(2)}) collective-permute-start(bf16[192,2048]{1,0:T(8,128)(2,1)} %param.34), channel_id=1, source_target_pairs={{0,1},{1,0},{2,3},{3,2},{4,5},{5,4},{6,7},{7,6},{8,9},{9,8},{10,11... | collective-permute-start | bytes 2359304 | tf_op jit(solution)/shard_map/ppermute | solution.py:46
  273.9 61.2 %collective-permute-start.67 = (bf16[4,64,1536]{2,1,0:T(8,128)(2,1)}, bf16[4,64,1536]{2,1,0:T(8,128)(2,1)S(1)}, u32[]{:S(2)}, u32[]{:S(2)}) collective-permute-start(bf16[4,64,1536]{2,1,0:T(8,128)(2,1)} %bitcast_dynamic-update-slice_fusion.51), channel_id=1, source_target_pairs={{0,16},{1,17},{2,18},{3,19},{4,20},{5,21},{6,22},{7,23},{8,24},{9,... | collective-permute-start | bytes 2359304 | tf_op jit(solution)/shard_map/ppermute | solution.py:46
  319.2 17.7 %collective-permute-start.68 = (bf16[4,64,1536]{2,1,0:T(8,128)(2,1)}, bf16[4,64,1536]{2,1,0:T(8,128)(2,1)S(1)}, u32[]{:S(2)}, u32[]{:S(2)}) collective-permute-start(bf16[4,64,1536]{2,1,0:T(8,128)(2,1)} %bitcast_dynamic-update-slice_fusion.51), channel_id=1, source_target_pairs={{0,2},{1,3},{2,0},{3,1},{4,6},{5,7},{6,4},{7,5},{8,10},{9,11},{10,... | collective-permute-start | bytes 2359304 | tf_op jit(solution)/shard_map/ppermute | solution.py:46
  327.0 94.2 %collective-permute-start.70 = (bf16[4,64,1536]{2,1,0:T(8,128)(2,1)}, bf16[4,64,1536]{2,1,0:T(8,128)(2,1)}, u32[]{:S(2)}, u32[]{:S(2)}) collective-permute-start(bf16[4,64,1536]{2,1,0:T(8,128)(2,1)} %bitcast_dynamic-update-slice_fusion.51), channel_id=1, source_target_pairs={{0,1},{1,0},{2,3},{3,2},{4,5},{5,4},{6,7},{7,6},{8,9},{9,8},{10,11... | collective-permute-start | bytes 2359304 | tf_op jit(solution)/shard_map/ppermute | solution.py:46
  335.1 22.6 %collective-permute-start.42 = (bf16[4,64,640]{2,1,0:T(8,128)(2,1)S(1)}, bf16[4,64,640]{2,1,0:T(8,128)(2,1)S(1)}, u32[]{:S(2)}, u32[]{:S(2)}) collective-permute-start(bf16[4,64,640]{2,1,0:T(8,128)(2,1)S(1)} %collective-permute-done.38), channel_id=1, source_target_pairs={{0,1},{1,0},{2,3},{3,2},{4,5},{5,4},{6,7},{7,6},{8,9},{9,8},{10,11... | collective-permute-start | bytes 983048 | tf_op jit(solution)/shard_map/ppermute | solution.py:46
  342.3 28.9 %collective-permute-start.59 = (bf16[192,2048]{1,0:T(8,128)(2,1)}, bf16[192,2048]{1,0:T(8,128)(2,1)}, u32[]{:S(2)}, u32[]{:S(2)}) collective-permute-start(bf16[192,2048]{1,0:T(8,128)(2,1)} %collective-permute-done.57), channel_id=1, source_target_pairs={{0,2},{1,3},{2,0},{3,1},{4,6},{5,7},{6,4},{7,5},{8,10},{9,11},{10,... | collective-permute-start | bytes 2359304 | tf_op jit(solution)/shard_map/ppermute | solution.py:46
  373.8 19.5 %collective-permute-start.52 = (bf16[192,2048]{1,0:T(8,128)(2,1)S(1)}, bf16[192,2048]{1,0:T(8,128)(2,1)S(1)}, u32[]{:S(2)}, u32[]{:S(2)}) collective-permute-start(bf16[192,2048]{1,0:T(8,128)(2,1)S(1)} %copy-done.37), channel_id=1, source_target_pairs={{0,2},{1,3},{2,0},{3,1},{4,6},{5,7},{6,4},{7,5},{8,10},{9,11},{10,... | collective-permute-start | bytes 2359304 | tf_op jit(solution)/shard_map/ppermute | solution.py:46
  376.4 23.2 %collective-permute-start.54 = (bf16[192,2048]{1,0:T(8,128)(2,1)S(1)}, bf16[192,2048]{1,0:T(8,128)(2,1)S(1)}, u32[]{:S(2)}, u32[]{:S(2)}) collective-permute-start(bf16[192,2048]{1,0:T(8,128)(2,1)S(1)} %copy-done.37), channel_id=1, source_target_pairs={{0,1},{1,0},{2,3},{3,2},{4,5},{5,4},{6,7},{7,6},{8,9},{9,8},{10,11... | collective-permute-start | bytes 2359304 | tf_op jit(solution)/shard_map/ppermute | solution.py:46
  377.8 24.4 %collective-permute-start.55 = (bf16[192,2048]{1,0:T(8,128)(2,1)S(1)}, bf16[192,2048]{1,0:T(8,128)(2,1)S(1)}, u32[]{:S(2)}, u32[]{:S(2)}) collective-permute-start(bf16[192,2048]{1,0:T(8,128)(2,1)S(1)} %copy-done.35), channel_id=1, source_target_pairs={{0,1},{1,0},{2,3},{3,2},{4,5},{5,4},{6,7},{7,6},{8,9},{9,8},{10,11... | collective-permute-start | bytes 2359304 | tf_op jit(solution)/shard_map/ppermute | solution.py:46
  397.1 21.8 %collective-permute-start.44 = (bf16[128,2048]{1,0:T(8,128)(2,1)S(1)}, bf16[128,2048]{1,0:T(8,128)(2,1)S(1)}, u32[]{:S(2)}, u32[]{:S(2)}) collective-permute-start(bf16[128,2048]{1,0:T(8,128)(2,1)S(1)} %get-tuple-element.177), channel_id=1, source_target_pairs={{0,8},{1,9},{2,10},{3,11},{4,12},{5,13},{6,14},{7,15},{8,0},{9,1},... | collective-permute-start | bytes 1572872 | tf_op jit(solution)/shard_map/ppermute | solution.py:46
  399.7 19.3 %collective-permute-start.43 = (bf16[128,2048]{1,0:T(8,128)(2,1)S(1)}, bf16[128,2048]{1,0:T(8,128)(2,1)S(1)}, u32[]{:S(2)}, u32[]{:S(2)}) collective-permute-start(bf16[128,2048]{1,0:T(8,128)(2,1)S(1)} %get-tuple-element.175), channel_id=1, source_target_pairs={{0,4},{1,5},{2,6},{3,7},{4,0},{5,1},{6,2},{7,3},{8,12},{9,13},{10,... | collective-permute-start | bytes 1572872 | tf_op jit(solution)/shard_map/ppermute | solution.py:46
  402.2 18.0 %collective-permute-start.69 = (bf16[4,64,1536]{2,1,0:T(8,128)(2,1)S(1)}, bf16[4,64,1536]{2,1,0:T(8,128)(2,1)S(1)}, u32[]{:S(2)}, u32[]{:S(2)}) collective-permute-start(bf16[4,64,1536]{2,1,0:T(8,128)(2,1)S(1)} %copy-done.41), channel_id=1, source_target_pairs={{0,2},{1,3},{2,0},{3,1},{4,6},{5,7},{6,4},{7,5},{8,10},{9,11},{10,... | collective-permute-start | bytes 2359304 | tf_op jit(solution)/shard_map/ppermute | solution.py:46
  419.0 22.7 %collective-permute-start.63 = (bf16[192,2048]{1,0:T(8,128)(2,1)}, bf16[192,2048]{1,0:T(8,128)(2,1)S(1)}, u32[]{:S(2)}, u32[]{:S(2)}) collective-permute-start(bf16[192,2048]{1,0:T(8,128)(2,1)} %collective-permute-done.59), channel_id=1, source_target_pairs={{0,1},{1,0},{2,3},{3,2},{4,5},{5,4},{6,7},{7,6},{8,9},{9,8},{10,11... | collective-permute-start | bytes 2359304 | tf_op jit(solution)/shard_map/ppermute | solution.py:46
  420.2 21.6 %collective-permute-start.56 = (bf16[192,2048]{1,0:T(8,128)(2,1)S(1)}, bf16[192,2048]{1,0:T(8,128)(2,1)S(1)}, u32[]{:S(2)}, u32[]{:S(2)}) collective-permute-start(bf16[192,2048]{1,0:T(8,128)(2,1)S(1)} %collective-permute-done.52), channel_id=1, source_target_pairs={{0,1},{1,0},{2,3},{3,2},{4,5},{5,4},{6,7},{7,6},{8,9},{9,8},{10,11... | collective-permute-start | bytes 2359304 | tf_op jit(solution)/shard_map/ppermute | solution.py:46
  421.3 18.5 %collective-permute-start.46 = (bf16[128,2048]{1,0:T(8,128)(2,1)S(1)}, bf16[128,2048]{1,0:T(8,128)(2,1)S(1)}, u32[]{:S(2)}, u32[]{:S(2)}) collective-permute-start(bf16[128,2048]{1,0:T(8,128)(2,1)S(1)} %get-tuple-element.152), channel_id=1, source_target_pairs={{0,4},{1,5},{2,6},{3,7},{4,0},{5,1},{6,2},{7,3},{8,12},{9,13},{10,... | collective-permute-start | bytes 1572872 | tf_op jit(solution)/shard_map/ppermute | solution.py:46
  427.5 24.6 %collective-permute-start.73 = (bf16[4,64,1536]{2,1,0:T(8,128)(2,1)S(1)}, bf16[4,64,1536]{2,1,0:T(8,128)(2,1)S(1)}, u32[]{:S(2)}, u32[]{:S(2)}) collective-permute-start(bf16[4,64,1536]{2,1,0:T(8,128)(2,1)S(1)} %collective-permute-done.69), channel_id=1, source_target_pairs={{0,1},{1,0},{2,3},{3,2},{4,5},{5,4},{6,7},{7,6},{8,9},{9,8},{10,11... | collective-permute-start | bytes 2359304 | tf_op jit(solution)/shard_map/ppermute | solution.py:46
  491.4 19.8 %collective-permute-start.83 = (bf16[128,2048]{1,0:T(8,128)(2,1)S(1)}, bf16[128,2048]{1,0:T(8,128)(2,1)S(1)}, u32[]{:S(2)}, u32[]{:S(2)}) collective-permute-start(bf16[128,2048]{1,0:T(8,128)(2,1)S(1)} %get-tuple-element.170), channel_id=1, source_target_pairs={{0,12},{1,13},{2,14},{3,15},{4,8},{5,9},{6,10},{7,11},{8,4},{9,5},... | collective-permute-start | bytes 1572872 | tf_op jit(solution)/shard_map/ppermute | solution.py:46
  507.5 26.1 %collective-permute-start.81 = (bf16[128,2048]{1,0:T(8,128)(2,1)S(1)}, bf16[128,2048]{1,0:T(8,128)(2,1)S(1)}, u32[]{:S(2)}, u32[]{:S(2)}) collective-permute-start(bf16[128,2048]{1,0:T(8,128)(2,1)S(1)} %get-tuple-element.169), channel_id=1, source_target_pairs={{0,4},{1,5},{2,6},{3,7},{4,0},{5,1},{6,2},{7,3},{8,12},{9,13},{10,... | collective-permute-start | bytes 1572872 | tf_op jit(solution)/shard_map/ppermute | solution.py:46
  509.0 25.1 %collective-permute-start.76 = (bf16[128,2048]{1,0:T(8,128)(2,1)S(1)}, bf16[128,2048]{1,0:T(8,128)(2,1)S(1)}, u32[]{:S(2)}, u32[]{:S(2)}) collective-permute-start(bf16[128,2048]{1,0:T(8,128)(2,1)S(1)} %get-tuple-element.173), channel_id=1, source_target_pairs={{0,12},{1,13},{2,14},{3,15},{4,8},{5,9},{6,10},{7,11},{8,4},{9,5},... | collective-permute-start | bytes 1572872 | tf_op jit(solution)/shard_map/ppermute | solution.py:46
  510.8 30.4 %collective-permute-start.75 = (bf16[128,2048]{1,0:T(8,128)(2,1)S(1)}, bf16[128,2048]{1,0:T(8,128)(2,1)S(1)}, u32[]{:S(2)}, u32[]{:S(2)}) collective-permute-start(bf16[128,2048]{1,0:T(8,128)(2,1)S(1)} %get-tuple-element.174), channel_id=1, source_target_pairs={{0,8},{1,9},{2,10},{3,11},{4,12},{5,13},{6,14},{7,15},{8,0},{9,1},... | collective-permute-start | bytes 1572872 | tf_op jit(solution)/shard_map/ppermute | solution.py:46
  511.3 30.3 %collective-permute-start.74 = (bf16[128,2048]{1,0:T(8,128)(2,1)S(1)}, bf16[128,2048]{1,0:T(8,128)(2,1)S(1)}, u32[]{:S(2)}, u32[]{:S(2)}) collective-permute-start(bf16[128,2048]{1,0:T(8,128)(2,1)S(1)} %get-tuple-element.172), channel_id=1, source_target_pairs={{0,4},{1,5},{2,6},{3,7},{4,0},{5,1},{6,2},{7,3},{8,12},{9,13},{10,... | collective-permute-start | bytes 1572872 | tf_op jit(solution)/shard_map/ppermute | solution.py:46
  522.0 199.6 %collective-permute-start.111 = (bf16[2,2,192,2048]{3,2,1,0:T(8,128)(2,1)}, bf16[2,2,192,2048]{3,2,1,0:T(8,128)(2,1)}, u32[]{:S(2)}, u32[]{:S(2)}) collective-permute-start(bf16[2,2,192,2048]{3,2,1,0:T(8,128)(2,1)} %dynamic-slice_bitcast_fusion.1), channel_id=1, source_target_pairs={{0,1},{1,0},{2,3},{3,2},{4,5},{5,4},{6,7},{7,6},{8,9},{9,8},{10,11... | collective-permute-start | bytes 9437192 | tf_op jit(solution)/shard_map/ppermute | solution.py:46
  590.2 123.2 %collective-permute-start.99 = (bf16[2,2,80,2048]{3,2,1,0:T(8,128)(2,1)}, bf16[2,2,80,2048]{3,2,1,0:T(8,128)(2,1)}, u32[]{:S(2)}, u32[]{:S(2)}) collective-permute-start(bf16[2,2,80,2048]{3,2,1,0:T(8,128)(2,1)} %dynamic-slice_bitcast_fusion.6), channel_id=1, source_target_pairs={{0,1},{1,0},{2,3},{3,2},{4,5},{5,4},{6,7},{7,6},{8,9},{9,8},{10,11... | collective-permute-start | bytes 3932168 | tf_op jit(solution)/shard_map/ppermute | solution.py:46
  642.4 19.3 %collective-permute-start.95 = (bf16[8,128]{1,0:T(8,128)(2,1)S(1)}, bf16[8,128]{1,0:T(8,128)(2,1)S(1)}, u32[]{:S(2)}, u32[]{:S(2)}) collective-permute-start(bf16[8,128]{1,0:T(8,128)(2,1)S(1)} %get-tuple-element.208), channel_id=1, source_target_pairs={{0,12},{1,13},{2,14},{3,15},{4,8},{5,9},{6,10},{7,11},{8,4},{9,5},... | collective-permute-start | bytes 6152 | tf_op jit(solution)/shard_map/ppermute | solution.py:46
  644.1 17.6 %collective-permute-start.94 = (bf16[8,128]{1,0:T(8,128)(2,1)S(1)}, bf16[8,128]{1,0:T(8,128)(2,1)S(1)}, u32[]{:S(2)}, u32[]{:S(2)}) collective-permute-start(bf16[8,128]{1,0:T(8,128)(2,1)S(1)} %get-tuple-element.209), channel_id=1, source_target_pairs={{0,8},{1,9},{2,10},{3,11},{4,12},{5,13},{6,14},{7,15},{8,0},{9,1},... | collective-permute-start | bytes 6152 | tf_op jit(solution)/shard_map/ppermute | solution.py:46
  668.2 31.7 %collective-permute-start.92 = (bf16[128,2048]{1,0:T(8,128)(2,1)}, bf16[128,2048]{1,0:T(8,128)(2,1)}, u32[]{:S(2)}, u32[]{:S(2)}) collective-permute-start(bf16[128,2048]{1,0:T(8,128)(2,1)} %get-tuple-element.167), channel_id=1, source_target_pairs={{0,12},{1,13},{2,14},{3,15},{4,8},{5,9},{6,10},{7,11},{8,4},{9,5},... | collective-permute-start | bytes 1572872 | tf_op jit(solution)/shard_map/ppermute | solution.py:46
  670.0 29.9 %collective-permute-start.91 = (bf16[128,2048]{1,0:T(8,128)(2,1)}, bf16[128,2048]{1,0:T(8,128)(2,1)}, u32[]{:S(2)}, u32[]{:S(2)}) collective-permute-start(bf16[128,2048]{1,0:T(8,128)(2,1)} %get-tuple-element.168), channel_id=1, source_target_pairs={{0,8},{1,9},{2,10},{3,11},{4,12},{5,13},{6,14},{7,15},{8,0},{9,1},... | collective-permute-start | bytes 1572872 | tf_op jit(solution)/shard_map/ppermute | solution.py:46
  671.8 23.5 %collective-permute-start.98 = (bf16[26368]{0:T(1024)(128)(2,1)S(1)}, bf16[26368]{0:T(1024)(128)(2,1)S(1)}, u32[]{:S(2)}, u32[]{:S(2)}) collective-permute-start(bf16[26368]{0:T(1024)(128)(2,1)S(1)} %dynamic-slice_reduce_fusion), channel_id=1, source_target_pairs={{0,16},{1,17},{2,18},{3,19},{4,20},{5,21},{6,22},{7,23},{8,24},{9,... | collective-permute-start | bytes 158216 | tf_op jit(solution)/shard_map/ppermute | solution.py:46
  699.9 26.9 %collective-permute-start.114 = (bf16[2,2,192,2048]{3,2,1,0:T(8,128)(2,1)}, bf16[2,2,192,2048]{3,2,1,0:T(8,128)(2,1)S(1)}, u32[]{:S(2)}, u32[]{:S(2)}) collective-permute-start(bf16[2,2,192,2048]{3,2,1,0:T(8,128)(2,1)} %dynamic-slice_bitcast_fusion), channel_id=1, source_target_pairs={{0,1},{1,0},{2,3},{3,2},{4,5},{5,4},{6,7},{7,6},{8,9},{9,8},{10,11... | collective-permute-start | bytes 9437192 | tf_op jit(solution)/shard_map/ppermute | solution.py:46
  699.9 16.9 %collective-permute-start.105 = (bf16[2,4,2,64,640]{4,3,1,0,2:T(8,128)(2,1)}, bf16[2,4,2,64,640]{4,3,1,0,2:T(8,128)(2,1)S(1)}, u32[]{:S(2)}, u32[]{:S(2)}) collective-permute-start(bf16[2,4,2,64,640]{4,3,1,0,2:T(8,128)(2,1)} %bitcast.547), channel_id=1, source_target_pairs={{0,1},{1,0},{2,3},{3,2},{4,5},{5,4},{6,7},{7,6},{8,9},{9,8},{10,11... | collective-permute-start | bytes 3932168 | tf_op jit(solution)/shard_map/ppermute | solution.py:46
  713.4 17.6 %collective-permute-start.117 = (bf16[2,4,2,64,1536]{4,3,1,0,2:T(8,128)(2,1)S(1)}, bf16[2,4,2,64,1536]{4,3,1,0,2:T(8,128)(2,1)}, u32[]{:S(2)}, u32[]{:S(2)}) collective-permute-start(bf16[2,4,2,64,1536]{4,3,1,0,2:T(8,128)(2,1)S(1)} %bitcast.525), channel_id=1, source_target_pairs={{0,1},{1,0},{2,3},{3,2},{4,5},{5,4},{6,7},{7,6},{8,9},{9,8},{10,11... | collective-permute-start | bytes 9437192 | tf_op jit(solution)/shard_map/ppermute | solution.py:46
  716.8 21.4 %collective-permute-start.100 = (bf16[2,80,2048]{2,1,0:T(8,128)(2,1)}, bf16[2,80,2048]{2,1,0:T(8,128)(2,1)S(1)}, u32[]{:S(2)}, u32[]{:S(2)}) collective-permute-start(bf16[2,80,2048]{2,1,0:T(8,128)(2,1)} %dynamic-slice_bitcast_fusion.12), channel_id=1, source_target_pairs={{0,2},{1,3},{2,0},{3,1},{4,6},{5,7},{6,4},{7,5},{8,10},{9,11},{10,... | collective-permute-start | bytes 1966088 | tf_op jit(solution)/shard_map/ppermute | solution.py:46
  718.7 29.9 %collective-permute-start.106 = (bf16[2,4,64,640]{3,2,1,0:T(8,128)(2,1)}, bf16[2,4,64,640]{3,2,1,0:T(8,128)(2,1)S(1)}, u32[]{:S(2)}, u32[]{:S(2)}) collective-permute-start(bf16[2,4,64,640]{3,2,1,0:T(8,128)(2,1)} %dynamic-slice_bitcast_fusion.10), channel_id=1, source_target_pairs={{0,2},{1,3},{2,0},{3,1},{4,6},{5,7},{6,4},{7,5},{8,10},{9,11},{10,... | collective-permute-start | bytes 1966088 | tf_op jit(solution)/shard_map/ppermute | solution.py:46
  721.6 41.1 %collective-permute-start.103 = (bf16[2,80,2048]{2,1,0:T(8,128)(2,1)}, bf16[2,80,2048]{2,1,0:T(8,128)(2,1)S(1)}, u32[]{:S(2)}, u32[]{:S(2)}) collective-permute-start(bf16[2,80,2048]{2,1,0:T(8,128)(2,1)} %dynamic-slice_bitcast_fusion.11), channel_id=1, source_target_pairs={{0,2},{1,3},{2,0},{3,1},{4,6},{5,7},{6,4},{7,5},{8,10},{9,11},{10,... | collective-permute-start | bytes 1966088 | tf_op jit(solution)/shard_map/ppermute | solution.py:46
  726.8 138.6 %collective-permute-start.112 = (bf16[2,192,2048]{2,1,0:T(8,128)(2,1)}, bf16[2,192,2048]{2,1,0:T(8,128)(2,1)}, u32[]{:S(2)}, u32[]{:S(2)}) collective-permute-start(bf16[2,192,2048]{2,1,0:T(8,128)(2,1)} %dynamic-slice_bitcast_fusion.4), channel_id=1, source_target_pairs={{0,2},{1,3},{2,0},{3,1},{4,6},{5,7},{6,4},{7,5},{8,10},{9,11},{10,... | collective-permute-start | bytes 4718600 | tf_op jit(solution)/shard_map/ppermute | solution.py:46
  730.9 139.6 %collective-permute-start.115 = (bf16[2,192,2048]{2,1,0:T(8,128)(2,1)}, bf16[2,192,2048]{2,1,0:T(8,128)(2,1)}, u32[]{:S(2)}, u32[]{:S(2)}) collective-permute-start(bf16[2,192,2048]{2,1,0:T(8,128)(2,1)} %dynamic-slice_bitcast_fusion.3), channel_id=1, source_target_pairs={{0,2},{1,3},{2,0},{3,1},{4,6},{5,7},{6,4},{7,5},{8,10},{9,11},{10,... | collective-permute-start | bytes 4718600 | tf_op jit(solution)/shard_map/ppermute | solution.py:46
  738.1 124.8 %collective-permute-start.118 = (bf16[2,4,64,1536]{3,2,1,0:T(8,128)(2,1)}, bf16[2,4,64,1536]{3,2,1,0:T(8,128)(2,1)}, u32[]{:S(2)}, u32[]{:S(2)}) collective-permute-start(bf16[2,4,64,1536]{3,2,1,0:T(8,128)(2,1)} %dynamic-slice_bitcast_fusion.2), channel_id=1, source_target_pairs={{0,2},{1,3},{2,0},{3,1},{4,6},{5,7},{6,4},{7,5},{8,10},{9,11},{10,... | collective-permute-start | bytes 4718600 | tf_op jit(solution)/shard_map/ppermute | solution.py:46
  748.6 30.3 %collective-permute-start.101 = (bf16[80,2048]{1,0:T(8,128)(2,1)S(1)}, bf16[80,2048]{1,0:T(8,128)(2,1)S(1)}, u32[]{:S(2)}, u32[]{:S(2)}) collective-permute-start(bf16[80,2048]{1,0:T(8,128)(2,1)S(1)} %dynamic-slice_bitcast_fusion.15), channel_id=1, source_target_pairs={{0,16},{1,17},{2,18},{3,19},{4,20},{5,21},{6,22},{7,23},{8,24},{9,... | collective-permute-start | bytes 983048 | tf_op jit(solution)/shard_map/ppermute | solution.py:46
  775.4 32.9 %collective-permute-start.104 = (bf16[80,2048]{1,0:T(8,128)(2,1)}, bf16[80,2048]{1,0:T(8,128)(2,1)}, u32[]{:S(2)}, u32[]{:S(2)}) collective-permute-start(bf16[80,2048]{1,0:T(8,128)(2,1)} %dynamic-slice_bitcast_fusion.14), channel_id=1, source_target_pairs={{0,16},{1,17},{2,18},{3,19},{4,20},{5,21},{6,22},{7,23},{8,24},{9,... | collective-permute-start | bytes 983048 | tf_op jit(solution)/shard_map/ppermute | solution.py:46
  865.3 68.6 %collective-permute-start.119 = (bf16[4,64,1536]{2,1,0:T(8,128)(2,1)S(1)}, bf16[4,64,1536]{2,1,0:T(8,128)(2,1)S(1)}, u32[]{:S(2)}, u32[]{:S(2)}) collective-permute-start(bf16[4,64,1536]{2,1,0:T(8,128)(2,1)S(1)} %dynamic-slice_bitcast_fusion.7), channel_id=1, source_target_pairs={{0,16},{1,17},{2,18},{3,19},{4,20},{5,21},{6,22},{7,23},{8,24},{9,... | collective-permute-start | bytes 2359304 | tf_op jit(solution)/shard_map/ppermute | solution.py:46
  867.6 83.3 %collective-permute-start.113 = (bf16[192,2048]{1,0:T(8,128)(2,1)S(1)}, bf16[192,2048]{1,0:T(8,128)(2,1)S(1)}, u32[]{:S(2)}, u32[]{:S(2)}) collective-permute-start(bf16[192,2048]{1,0:T(8,128)(2,1)S(1)} %dynamic-slice_bitcast_fusion.9), channel_id=1, source_target_pairs={{0,16},{1,17},{2,18},{3,19},{4,20},{5,21},{6,22},{7,23},{8,24},{9,... | collective-permute-start | bytes 2359304 | tf_op jit(solution)/shard_map/ppermute | solution.py:46
  872.6 93.6 %collective-permute-start.116 = (bf16[192,2048]{1,0:T(8,128)(2,1)S(1)}, bf16[192,2048]{1,0:T(8,128)(2,1)S(1)}, u32[]{:S(2)}, u32[]{:S(2)}) collective-permute-start(bf16[192,2048]{1,0:T(8,128)(2,1)S(1)} %dynamic-slice_bitcast_fusion.8), channel_id=1, source_target_pairs={{0,16},{1,17},{2,18},{3,19},{4,20},{5,21},{6,22},{7,23},{8,24},{9,... | collective-permute-start | bytes 2359304 | tf_op jit(solution)/shard_map/ppermute | solution.py:46
  934.3 33.2 %collective-permute-start.120 = (bf16[64,1536]{1,0:T(8,128)(2,1)S(1)}, bf16[64,1536]{1,0:T(8,128)(2,1)S(1)}, u32[]{:S(2)}, u32[]{:S(2)}) collective-permute-start(bf16[64,1536]{1,0:T(8,128)(2,1)S(1)} %get-tuple-element.182), channel_id=1, source_target_pairs={{0,4},{1,5},{2,6},{3,7},{4,0},{5,1},{6,2},{7,3},{8,12},{9,13},{10,... | collective-permute-start | bytes 589832 | tf_op jit(solution)/shard_map/ppermute | solution.py:46
  935.8 35.9 %collective-permute-start.121 = (bf16[64,1536]{1,0:T(8,128)(2,1)S(1)}, bf16[64,1536]{1,0:T(8,128)(2,1)S(1)}, u32[]{:S(2)}, u32[]{:S(2)}) collective-permute-start(bf16[64,1536]{1,0:T(8,128)(2,1)S(1)} %get-tuple-element.181), channel_id=1, source_target_pairs={{0,8},{1,9},{2,10},{3,11},{4,12},{5,13},{6,14},{7,15},{8,0},{9,1},... | collective-permute-start | bytes 589832 | tf_op jit(solution)/shard_map/ppermute | solution.py:46
  938.5 37.3 %collective-permute-start.122 = (bf16[64,1536]{1,0:T(8,128)(2,1)S(1)}, bf16[64,1536]{1,0:T(8,128)(2,1)S(1)}, u32[]{:S(2)}, u32[]{:S(2)}) collective-permute-start(bf16[64,1536]{1,0:T(8,128)(2,1)S(1)} %get-tuple-element.180), channel_id=1, source_target_pairs={{0,12},{1,13},{2,14},{3,15},{4,8},{5,9},{6,10},{7,11},{8,4},{9,5},... | collective-permute-start | bytes 589832 | tf_op jit(solution)/shard_map/ppermute | solution.py:46
  (134 other events, 1452.0 us)

commit v2 on v1

v2 whole, which is shorter than its diff:
```python
import functools

import jax
import jax.numpy as jnp
import numpy as np
from jax import lax
from jax.experimental import pallas as pl
from jax.experimental.pallas import tpu as pltpu
from jax.sharding import PartitionSpec as P

AXES = ("seq", "fsdp")
TAPS = 4
EPSILON = 1e-06
DECAY_SCALE = 8.0
VMEM_BYTES = 56 * 1024 * 1024
BF16 = jnp.bfloat16
F32 = jnp.float32


def device_bits(seq_count, fsdp_count, rows, block):
    low = fsdp_count
    while low * rows < block:
        low *= 2
    total = seq_count * fsdp_count
    every = [1 << k for k in reversed(range(total.bit_length() - 1))]
    return low, tuple(every)


def linear_index():
    return lax.axis_index("seq") * lax.axis_size("fsdp") + lax.axis_index("fsdp")


def bit_of(index, bit):
    return lax.rem(lax.div(index, jnp.int32(bit)), jnp.int32(2))


def number_of(index, bits):
    value = jnp.int32(0)
    for b in bits:
        value = value * 2 + bit_of(index, b)
    return value


def fence(value, *others):
    return lax.optimization_barrier((value,) + others)[0]


def trade(value, mask):
    count = lax.axis_size("seq") * lax.axis_size("fsdp")
    return lax.ppermute(value, AXES, [(i, i ^ mask) for i in range(count)])


class Streams:
    def __init__(self):
        self.last = {}

    def trade(self, value, bit):
        if bit > 1:
            if bit in self.last:
                value = fence(value, self.last[bit])
            self.last[bit] = value = trade(value, bit)
            return value
        return trade(value, bit)


def pick(value, index, axis):
    return lax.dynamic_index_in_dim(value, index, axis, keepdims=False)


def put(buffer, part, index, axis):
    return lax.dynamic_update_index_in_dim(buffer, part, index, axis)


def gather_units(own, bits, send):
    units = [(0, own)]
    for b in bits:
        units += [(mask | b, send(unit, b)) for mask, unit in units]
    return units


def copy_kernel(count, shapes, places, scalars, *refs):
    pieces, wholes, sems = refs[:count], refs[count:-1], refs[-1]
    copies = []
    for i, piece in enumerate(pieces):
        for source, which, target in places(i, scalars[0]):
            here = piece if source is None else piece.at[source]
            copies.append(
                pltpu.make_async_copy(here, wholes[which].at[target], sems.at[len(copies)])
            )
    for c in copies:
        c.start()
    for c in copies:
        c.wait()


def assemble(pieces, shapes, places, me, copies):
    where = pl.BlockSpec(memory_space=pl.ANY)
    return pl.pallas_call(
        functools.partial(copy_kernel, len(pieces), shapes, places),
        out_shape=[jax.ShapeDtypeStruct(shape, pieces[0].dtype) for shape in shapes],
        in_specs=[pl.BlockSpec(memory_space=pltpu.SMEM)] + [where] * len(pieces),
        out_specs=[pl.BlockSpec(memory_space=pltpu.VMEM)] * len(shapes),
        scratch_shapes=[pltpu.SemaphoreType.DMA((copies,))],
        compiler_params=pltpu.CompilerParams(vmem_limit_bytes=VMEM_BYTES),
    )(me.astype(jnp.int32).reshape(1), *pieces)


def stack_pieces(pieces, me):
    (whole,) = assemble(
        pieces,
        [(len(pieces),) + pieces[0].shape],
        lambda i, at: [(None, 0, i)],
        me,
        len(pieces),
    )
    return whole


def halves(value, axis, bit, me):
    mine = bit_of(me, bit)
    return pick(value, 1 - mine, axis), pick(value, mine, axis)


def scatter_bits(value, axes, bits, me, send):
    for k, (b, axis) in enumerate(zip(bits, axes)):
        away, kept = halves(value, axis, b, me)
        value = kept.astype(F32) + send(away.astype(BF16), b).astype(F32)
        if k < len(bits) - 1:
            value = value.astype(BF16)
    return value


def share_list(own, low):
    half = own.shape[-2] // 2
    one, two = trade(own, low), trade(own, 2 * low)
    three = (trade(two[..., :half, :], low), trade(one[..., half:, :], 2 * low))
    return [own, one, two, three]


def place_tokens(lists, me):
    rows, width = lists[0][0].shape
    pieces, spots = [], []
    for k, units in enumerate(lists):
        for j, unit in enumerate(units[:3]):
            pieces.append(unit)
            spots.append(pl.ds((4 * k + j) * rows, rows))
        for i, unit in enumerate(units[3]):
            pieces.append(unit)
            spots.append(pl.ds((4 * k + 3) * rows + i * (rows // 2), rows // 2))
    (whole,) = assemble(
        pieces,
        [(4 * len(lists) * rows, width)],
        lambda i, at: [(None, 0, spots[i])],
        me,
        len(pieces),
    )
    return whole


def sum_tokens(partial, low):
    total = partial[0].astype(F32)
    for j in (1, 2, 3):
        total = total + trade(partial[j], j * low).astype(F32)
    return total


def project(left, weight):
    return lax.dot_general(left, weight, (((1,), (1,)), ((), ())), preferred_element_type=F32)


def back_project(left, weight):
    return lax.dot_general(left, weight, (((1,), (0,)), ((), ())), preferred_element_type=F32)


def outer(grads, values):
    return lax.dot_general(grads, values, (((0,), (0,)), ((), ())), preferred_element_type=F32)


def inverse_rms(values):
    return lax.rsqrt(jnp.mean(values * values, axis=-1, keepdims=True) + EPSILON)


def gelu_parts(v):
    c = 0.7978845608028654
    t = jnp.tanh(c * (v + 0.044715 * v * v * v))
    act = 0.5 * v * (1.0 + t)
    slope = 0.5 * (1.0 + t) + 0.5 * v * (1.0 - t * t) * c * (1.0 + 3 * 0.044715 * v * v)
    return act, slope


def call(body, outs, scalars, arrays, scratch=()):
    return pl.pallas_call(
        body,
        out_shape=[jax.ShapeDtypeStruct(shape, kind) for shape, kind in outs],
        in_specs=[pl.BlockSpec(memory_space=pltpu.SMEM)]
        + [pl.BlockSpec(memory_space=pltpu.VMEM)] * len(arrays),
        out_specs=[pl.BlockSpec(memory_space=pltpu.VMEM)] * len(outs),
        scratch_shapes=list(scratch),
        compiler_params=pltpu.CompilerParams(vmem_limit_bytes=VMEM_BYTES),
    )(scalars, *arrays)


def block_number(scalars, n, rows, step):
    return jnp.bitwise_xor(scalars[0], (n // rows) * step)


def injection(s, speed):
    y = speed * s
    e = jnp.exp(-y)
    z = 2.0 * y
    series = 1.0 - z * (1 / 7)
    for k in (6, 5, 4, 3, 2):
        series = 1.0 - z * (1 / k) * series
    return e, jnp.sqrt(jnp.where(z < 0.35, z * series, 1.0 - e * e))


def span_scan(a, b, reverse):
    span, channels = a.shape
    within = lax.broadcasted_iota(jnp.int32, (span, channels), 0) % 8
    for k in (1, 2, 4):
        turn = span - k if reverse else k
        reached = within < 8 - k if reverse else within >= k
        a_far = jnp.where(reached, pltpu.roll(a, turn, 0), 1.0)
        b_far = jnp.where(reached, pltpu.roll(b, turn, 0), 0.0)
        b = b + a * b_far
        a = a * a_far
    count = span // 8
    order = range(count - 1, -1, -1) if reverse else range(count)
    edge = 0 if reverse else 7
    a_all, b_all = [None] * count, [None] * count
    p = jnp.ones((1, channels), F32)
    h = jnp.zeros((1, channels), F32)
    for i in order:
        a_i, b_i = a[8 * i : 8 * i + 8], b[8 * i : 8 * i + 8]
        b_all[i] = b_i + a_i * h
        a_all[i] = a_i * p
        p = a_all[i][edge : edge + 1]
        h = b_all[i][edge : edge + 1]
    return jnp.concatenate(a_all, axis=0), jnp.concatenate(b_all, axis=0), p, h


def sequence_marks(scalars, block, row, span, total_len):
    rows = row[1]
    slots = (scalars.shape[0] - 1) // rows
    place = block * span + lax.broadcasted_iota(jnp.int32, (span, 8), 0)
    column = lax.broadcasted_iota(jnp.int32, (span, 8), 1)
    other = place + jnp.where(column <= 3, -column, column - 3)
    here = jnp.full((span, 8), -1, jnp.int32)
    there = jnp.full((span, 8), -1, jnp.int32)
    first = jnp.zeros((span, 8), jnp.int32)
    offset = jnp.int32(0)
    for j in range(slots):
        length = scalars[1 + row[0] * slots + j]
        live = jnp.where(length > 0, 1, 0)
        here = here + jnp.where(place >= offset, live, 0)
        there = there + jnp.where(other >= offset, live, 0)
        first = first + jnp.where(place == offset, live, 0)
        offset = offset + length
    inside = (other >= 0) & (other < total_len)
    same = jnp.where(inside & (here == there), 1, 0)
    return jnp.where(column == 0, first, same).astype(F32)


def forward_kernel(
    rows, step, total_len, scalars, recur, halo, coef, rate_rows, gate_rows, spread, diagonal,
    conv, s_out, q_out, prod, part, ends, marks, rate_w, gate_w, pad,
):
    count, span, channels = recur.shape
    for n in range(count):
        block = block_number(scalars, n, rows, step)
        marks[n] = sequence_marks(scalars, block, (n % rows, rows), span, total_len)
    for narrow, wide in ((rate_rows, rate_w), (gate_rows, gate_w)):
        wide[...] = (back_project(narrow[...], spread[...]) * diagonal[...].astype(F32)).astype(BF16)

    def convolve(n, carry):
        block = block_number(scalars, n, rows, step)
        before = jnp.bitwise_xor(jnp.maximum(block - 1, 0), scalars[0])
        pad[4:8, :] = halo[before * rows + n % rows]
        pad[8:, :] = recur[n].astype(F32)
        total = coef[4:5, :] + coef[0:1, :] * pad[8:, :]
        for k in range(1, TAPS):
            total = total + coef[k : k + 1, :] * pad[8 - k : 8 - k + span, :] * marks[n][:, k : k + 1]
        conv[n] = total.astype(BF16)
        return carry

    lax.fori_loop(0, count, convolve, 0)
    flat = conv[...].reshape(count * span, channels)
    s_out[...] = project(flat, rate_w[...]).reshape(count, span, channels)
    q_out[...] = project(flat, gate_w[...]).reshape(count, span, channels)

    def scan(n, carry):
        s = jax.nn.sigmoid(s_out[n] + coef[5:6, :])
        q = jax.nn.sigmoid(q_out[n] + coef[6:7, :])
        s_out[n] = s
        q_out[n] = q
        e, m = injection(s, coef[7:8, :])
        decay = e * (1.0 - marks[n][:, 0:1])
        p_all, h_all, p, h = span_scan(decay, m * q * conv[n].astype(F32), False)
        prod[n] = p_all
        part[n] = h_all
        ends[n, 0:1, :] = p
        ends[n, 1:2, :] = h
        return carry

    lax.fori_loop(0, count, scan, 0)


def join(ends, into, scalars, rows, blocks, reverse):
    def lap(k, carry):
        block = blocks - 1 - k if reverse else k
        place = jnp.bitwise_xor(block, scalars[0]) * rows
        new = []
        for r in range(rows):
            into[block * rows + r] = carry[r]
            pair = ends[place + r]
            new.append(pair[0:1] * carry[r] + pair[1:2])
        return tuple(new)

    channels = into.shape[-1]
    lax.fori_loop(0, blocks, lap, (jnp.zeros((1, channels), F32),) * rows)


def state_kernel(rows, step, scalars, prod, part, ends, branch, state, mixed, came, into):
    count = prod.shape[0]
    join(ends, into, scalars, rows, into.shape[0] // rows, False)

    def finish(n, carry):
        incoming = into[block_number(scalars, n, rows, step) * rows + n % rows]
        h = part[n] + prod[n] * incoming
        came[n] = incoming
        state[n] = h
        mixed[n] = (h * gelu_parts(branch[n])[0]).astype(BF16)
        return carry

    lax.fori_loop(0, count, finish, 0)


def adjoint_kernel(
    scalars, grad_mixed, state, branch, s_in, marks, coef, grad_branch, prod, part, ends, pad
):
    count, span, channels = state.shape
    pad[span:, :] = jnp.ones((8, channels), F32)

    def scan(n, carry):
        act, slope = gelu_parts(branch[n])
        grad = grad_mixed[n]
        grad_branch[n] = (grad * state[n] * slope).astype(BF16)
        decay = jnp.exp(-coef[7:8, :] * s_in[n]) * (1.0 - marks[n][:, 0:1])
        pad[:span, :] = decay
        p_all, h_all, p, h = span_scan(pad[1 : span + 1, :], grad * act, True)
        prod[n] = p_all
        part[n] = h_all
        ends[n, 0:1, :] = decay[0:1] * p
        ends[n, 1:2, :] = decay[0:1] * h
        return carry

    lax.fori_loop(0, count, scan, 0)


def gates_kernel(
    rows, step, scalars, prod, part, ends, s_in, q_in, conv, state, came, recur, halo, marks, coef,
    rate_w, gate_w, collect, diagonal, eye, grad_conv, edges, packed, grad_rate, grad_gate, sums,
    into, pad, pad_two,
):
    count, span, channels = prod.shape
    join(ends, into, scalars, rows, into.shape[0] // rows, True)
    sums[...] = jnp.zeros((8, channels), F32)

    def terms(n, carry):
        block = block_number(scalars, n, rows, step)
        total = part[n] + prod[n] * into[block * rows + n % rows]
        pad[7:8, :] = came[n]
        pad[8:, :] = state[n]
        s, q = s_in[n], q_in[n]
        e, m = injection(s, coef[7:8, :])
        c = conv[n].astype(F32)
        first = marks[n][:, 0:1]
        grad_log = total * (pad[7 : 7 + span, :] * e * (1.0 - first) - e * e * q * c / m)
        rate = -coef[7:8, :] * s * (1.0 - s) * grad_log
        gate = total * m * c * q * (1.0 - q)
        grad_conv[n] = total * m * q
        grad_rate[pl.ds(pl.multiple_of(n * span, span), span), :] = rate.astype(BF16)
        grad_gate[pl.ds(pl.multiple_of(n * span, span), span), :] = gate.astype(BF16)
        sums[5:6, :] += jnp.sum(rate, axis=0, keepdims=True)
        sums[6:7, :] += jnp.sum(gate, axis=0, keepdims=True)
        sums[7:8, :] += jnp.sum(coef[8:9, :] * s * grad_log, axis=0, keepdims=True)
        return carry

    lax.fori_loop(0, count, terms, 0)
    through = back_project(grad_rate[...], rate_w[...]) + back_project(grad_gate[...], gate_w[...])
    grad_conv[...] += through.reshape(count, span, channels)
    flat = conv[...].reshape(count * span, channels)

    def kernel_terms(n, carry):
        block = block_number(scalars, n, rows, step)
        before = jnp.bitwise_xor(jnp.maximum(block - 1, 0), scalars[0])
        pad_two[4:8, :] = halo[before * rows + n % rows]
        pad_two[8:, :] = recur[n].astype(F32)
        grad = grad_conv[n]
        edges[n] = grad[:4].astype(BF16)
        sums[4:5, :] += jnp.sum(grad, axis=0, keepdims=True)
        sums[0:1, :] += jnp.sum(grad * pad_two[8:, :], axis=0, keepdims=True)
        for k in range(1, TAPS):
            term = grad * pad_two[8 - k : 8 - k + span, :] * marks[n][:, k : k + 1]
            sums[k : k + 1, :] += jnp.sum(term, axis=0, keepdims=True)
        return carry

    lax.fori_loop(0, count, kernel_terms, 0)
    on = diagonal[...].astype(F32)
    size = collect.shape[1] // 3
    total = back_project((outer(grad_rate[...], flat) * on).astype(BF16), collect[:, :size])
    total += back_project((outer(grad_gate[...], flat) * on).astype(BF16), collect[:, size : 2 * size])
    turned = project(eye[...], sums[...].astype(BF16))
    total += back_project(turned.astype(BF16), collect[:8, 2 * size :])
    packed[...] = total.astype(BF16)


def unconvolve_kernel(rows, step, blocks, scalars, grad_conv, halo, marks, coef, grad_recur, pad):
    count, span, channels = grad_conv.shape

    def body(n, carry):
        block = block_number(scalars, n, rows, step)
        behind = jnp.bitwise_xor(jnp.minimum(block + 1, blocks - 1), scalars[0])
        pad[:span, :] = grad_conv[n]
        pad[span : span + 4, :] = halo[behind * rows + n % rows]
        total = coef[0:1, :] * pad[:span, :]
        for k in range(1, TAPS):
            seen = marks[n][:, 3 + k : 4 + k]
            total = total + coef[k : k + 1, :] * pad[k : k + span, :] * seen
        grad_recur[n] = total.astype(BF16)
        return carry

    lax.fori_loop(0, count, body, 0)


def shards(
    block_input,
    seq_lengths,
    mixer_gain,
    branch_weight,
    recur_weight,
    conv_kernel,
    conv_bias,
    recur_gate_weight,
    recur_gate_bias,
    input_gate_weight,
    input_gate_bias,
    decay_param,
    mixer_weight,
    mlp_gain,
    gate_weight,
    up_weight,
    down_weight,
    cotangent,
):
    rows, span, width = block_input.shape
    tokens = rows * span
    seq_count, fsdp_count = lax.axis_size("seq"), lax.axis_size("fsdp")
    channel_rows = branch_weight.shape[0]
    hidden_rows = gate_weight.shape[0]
    out_rows = mixer_weight.shape[0]
    block_size = recur_gate_weight.shape[1]
    low, every = device_bits(seq_count, fsdp_count, channel_rows, block_size)
    wide = 4 * low
    tp, tp_wide = (2 * low, low), (wide, 2 * low, low)
    dp = tuple(b for b in every if b not in tp)
    dp_wide = tuple(b for b in every if b not in tp_wide)
    above, below = tuple(b for b in dp if b > low), tuple(b for b in dp if b < low)
    above_wide = tuple(b for b in above if b != wide)
    step = low // fsdp_count
    me = linear_index().astype(jnp.int32)
    seq_index = lax.axis_index("seq")
    tp_index, wide_index = number_of(me, tp), number_of(me, tp_wide)
    share, share_wide = 1 << len(dp), 1 << len(dp_wide)
    high, deep, high_wide = 1 << len(above), 1 << len(below), 1 << len(above_wide)
    channels = share * channel_rows
    hidden = share_wide * hidden_rows
    blocks = 4 * rows
    seq_dp = tuple(b for b in dp if b >= fsdp_count)
    streams = Streams()

    def across_blocks(own):
        units = sorted(gather_units(own, seq_dp, trade), key=lambda unit: unit[0])
        every_slot = jnp.stack([unit for _, unit in units])
        every_slot = every_slot.reshape((-1, step) + own.shape)
        return jnp.moveaxis(every_slot, 2, 1).reshape((seq_count,) + own.shape[1:])

    def slot_places(units, bits, arrays):
        def places(i, at):
            slot = number_of(jnp.bitwise_xor(at, units[i][0]), bits)
            if arrays == 1:
                return [(None, 0, slot)]
            return [(a, a, slot) for a in range(arrays)]

        return places

    def column_places(units, up_bits, down_bits):
        def places(i, at):
            owner = jnp.bitwise_xor(at, units[i][0])
            return [(None, 0, (number_of(owner, up_bits), slice(None), number_of(owner, down_bits)))]

        return places

    def by_rank(weight, upper, ranks):
        split = weight.reshape(weight.shape[0], upper, ranks, -1)
        return jnp.transpose(split, (2, 0, 1, 3)).reshape(ranks, weight.shape[0], -1)

    def swap_ranks(parts, index, bits):
        masks = [sum(b for k, b in enumerate(reversed(bits)) if j >> k & 1) for j in range(len(parts))]
        sent = [pick(parts, jnp.bitwise_xor(index, j), 0) for j in range(len(parts))]
        return [trade(part, mask) if mask else part for part, mask in zip(sent, masks)]

    input_own = block_input.reshape(tokens, width)
    cot_own = cotangent.reshape(tokens, width)
    input_all = place_tokens([share_list(input_own, low)], me)

    gain_columns = jnp.stack([mixer_gain, mlp_gain], axis=1)
    gain_columns = jnp.pad(gain_columns, ((0, channel_rows - out_rows), (0, 0)))
    small = jnp.concatenate(
        [
            conv_kernel,
            jnp.stack([conv_bias, recur_gate_bias, input_gate_bias, decay_param], axis=1),
            gain_columns,
            recur_gate_weight,
            input_gate_weight,
        ],
        axis=1,
    )
    for i, b in enumerate(dp):
        got = trade(small, b)
        mine = bit_of(me, b) == 0
        small = jnp.stack([jnp.where(mine, small, got), jnp.where(mine, got, small)], axis=i)
    small = small.reshape((share,) + small.shape[len(dp) :])
    gains = jnp.moveaxis(small[:, :out_rows, 8:10], 2, 0)
    gains = jnp.stack([gains] + [trade(gains, j * low) for j in (1, 2, 3)])
    gains = jnp.take(gains, jnp.bitwise_xor(tp_index, jnp.arange(4)), axis=0)
    gains = gains.reshape(4, 2, high, deep, out_rows).transpose(1, 2, 0, 3, 4).reshape(2, width)
    gain_one, gain_two = gains[0].astype(F32), gains[1].astype(F32)
    small = small.reshape(channels, -1)
    coef = small[:, :8].astype(F32).T
    decay_vec = coef[7:]
    coef = jnp.concatenate(
        [
            coef[:7],
            DECAY_SCALE * jax.nn.softplus(-decay_vec),
            DECAY_SCALE * jax.nn.sigmoid(-decay_vec),
            jnp.zeros((7, channels), F32),
        ]
    )
    rate_rows, gate_rows = small[:, 10 : 10 + block_size], small[:, 10 + block_size :]
    number = np.arange(channels)
    spread = jnp.asarray(number[None] % block_size == np.arange(block_size)[:, None], BF16)
    diagonal = jnp.asarray(number[None] // block_size == number[:, None] // block_size, BF16)
    eye = jnp.asarray(np.eye(channels), BF16)
    packed_width = -(-(2 * block_size + 8) // 128) * 128
    collect = np.zeros((channels, 3, packed_width))
    collect[number, 0, number % block_size] = 1
    collect[number, 1, block_size + number % block_size] = 1
    collect[np.arange(8), 2, 2 * block_size + np.arange(8)] = 1
    collect = jnp.asarray(collect.reshape(channels, -1), BF16)
    lengths = lax.dynamic_slice_in_dim(seq_lengths, lax.axis_index("fsdp") * rows, rows, 0)
    scalars = jnp.concatenate([seq_index.astype(jnp.int32)[None], lengths.reshape(-1)])

    units = gather_units(jnp.stack([branch_weight, recur_weight]), dp, streams.trade)
    branch_q, recur_q = assemble(
        [unit for _, unit in units],
        [(share, channel_rows, width)] * 2,
        slot_places(units, dp, 2),
        me,
        2 * share,
    )
    branch_q, recur_q = branch_q.reshape(channels, width), recur_q.reshape(channels, width)
    mixer_weight = fence(mixer_weight, input_all)
    pieces = swap_ranks(by_rank(mixer_weight, high, 4), tp_index, tp)
    (piece,) = assemble(
        pieces,
        [(4,) + pieces[0].shape],
        lambda i, at: [(None, 0, jnp.bitwise_xor(number_of(at, tp), i))],
        me,
        4,
    )
    units = gather_units(piece, dp, streams.trade)
    (mixer_q,) = assemble(
        [unit for _, unit in units],
        [(high, 4, deep, out_rows, channels)],
        column_places(units, above, below),
        me,
        share,
    )
    mixer_q = mixer_q.reshape(width, channels)

    cot_far = streams.trade(cot_own, wide)
    cot_lists = [share_list(cot_own, low), share_list(cot_far, low)]

    units = gather_units(jnp.stack([gate_weight, up_weight]), dp_wide, streams.trade)
    gate_q, up_q = assemble(
        [unit for _, unit in units],
        [(share_wide, hidden_rows, width)] * 2,
        slot_places(units, dp_wide, 2),
        me,
        2 * share_wide,
    )
    gate_q, up_q = gate_q.reshape(hidden, width), up_q.reshape(hidden, width)

    scale_one = inverse_rms(input_all.astype(F32))
    normed = (input_all.astype(F32) * scale_one * gain_one).astype(BF16)
    recur_in = project(normed, recur_q).astype(BF16).reshape(blocks, span, channels)
    edge = recur_in[:, span - 4 :].reshape(4, rows, 4, channels)
    halo = across_blocks(edge).astype(F32).reshape(seq_count * rows, 4, channels)
    branch = project(normed, branch_q).reshape(blocks, span, channels)
    shape = (blocks, span, channels)
    one = (blocks, 1, channels)
    everything = (seq_count * rows, 1, channels)
    square = (channels, channels)
    padded = (span + 8, channels)
    conv, s_val, q_val, prod, part, ends, marks, rate_wide, gate_wide = call(
        functools.partial(forward_kernel, rows, step, seq_count * span),
        [(shape, BF16)] + [(shape, F32)] * 4
        + [((blocks, 2, channels), F32), ((blocks, span, 8), F32), (square, BF16), (square, BF16)],
        scalars,
        [recur_in, halo, coef, rate_rows, gate_rows, spread, diagonal],
        [pltpu.VMEM(padded, F32)],
    )
    ends = across_blocks(ends.reshape(4, rows, 2, channels)).reshape(-1, 2, channels)
    state, mixed, came = call(
        functools.partial(state_kernel, rows, step),
        [(shape, F32), (shape, BF16), (one, F32)],
        scalars,
        [prod, part, ends, branch],
        [pltpu.VMEM(everything, F32)],
    )
    mixed_flat = mixed.reshape(4 * tokens, channels)
    mixer_part = project(mixed_flat, mixer_q).astype(BF16).reshape(4, tokens, width)
    residual = input_own.astype(F32) + sum_tokens(mixer_part, low)

    down_weight = fence(down_weight, mixed)
    pieces = swap_ranks(by_rank(down_weight, high_wide, 8), wide_index, tp_wide)
    (piece,) = assemble(
        pieces,
        [(8,) + pieces[0].shape],
        lambda i, at: [(None, 0, jnp.bitwise_xor(number_of(at, tp_wide), i))],
        me,
        8,
    )
    units = gather_units(piece, dp_wide, streams.trade)
    (down_q,) = assemble(
        [unit for _, unit in units],
        [(high_wide, 8, deep, out_rows, hidden)],
        column_places(units, above_wide, below),
        me,
        share_wide,
    )
    down_q = down_q.reshape(width, hidden)

    scale_two = inverse_rms(residual)
    unit_two = residual * scale_two
    normed_own = (unit_two * gain_two).astype(BF16)
    normed_far = streams.trade(normed_own, wide)
    normed_two = place_tokens([share_list(normed_own, low), share_list(normed_far, low)], me)
    cot_all = place_tokens(cot_lists, me)
    gate_val = project(normed_two, gate_q)
    up_val = project(normed_two, up_q)
    act, slope = gelu_parts(gate_val)
    hidden_val = (act * up_val).astype(BF16)
    grad_hidden = back_project(cot_all, down_q)
    grad_gate = (grad_hidden * up_val * slope).astype(BF16)
    grad_up = (grad_hidden * act).astype(BF16)
    grad_two_part = (back_project(grad_gate, gate_q) + back_project(grad_up, up_q)).astype(BF16)
    grad_two_part = grad_two_part.reshape(2, 4, tokens, width)
    grad_two_far = sum_tokens(grad_two_part[1], low).astype(BF16)
    grad_two = sum_tokens(grad_two_part[0], low) + trade(grad_two_far, wide).astype(F32)
    down_part = project(hidden_val, down_q).astype(BF16).reshape(2, 4, tokens, width)
    down_far = sum_tokens(down_part[1], low).astype(BF16)
    down_own = sum_tokens(down_part[0], low) + trade(down_far, wide).astype(F32)
    block_output = (residual + down_own).astype(BF16)
    scaled = grad_two * gain_two
    grad_residual = cot_own.astype(F32) + scale_two * (
        scaled - unit_two * jnp.mean(scaled * unit_two, axis=-1, keepdims=True)
    )
    gain_two_part = jnp.sum(grad_two * unit_two, axis=0)

    def row_axes(bits):
        return list(range(len(bits)))

    def row_grad(grads, values, bits):
        whole = outer(grads, values).astype(BF16)
        whole = whole.reshape((2,) * len(bits) + (-1, width))
        order = tuple(reversed(bits))
        return scatter_bits(whole, tuple(reversed(row_axes(bits))), order, me, streams.trade)

    def column_grad(grads, values, bits, ranks):
        up_bits = [b for b in bits if b > low]
        whole = outer(grads, values).astype(BF16)
        whole = whole.reshape((2,) * len(up_bits) + (ranks,) + (2,) * (len(bits) - len(up_bits)) + (out_rows, -1))
        axes = [k if b > low else k + 1 for k, b in enumerate(bits)]
        order = tuple(reversed(bits))
        return scatter_bits(whole, tuple(reversed(axes)), order, me, streams.trade).astype(BF16)

    def join_ranks(parts, index, bits, upper):
        ranks = len(parts)
        got = swap_ranks(parts, index, bits)
        count = got[0].shape[0]
        whole = jnp.zeros((ranks, count, upper, got[0].shape[1] // upper), BF16)
        for j, part in enumerate(got):
            whole = put(whole, part.reshape(count, upper, -1), jnp.bitwise_xor(index, j), 0)
        return jnp.transpose(whole, (1, 2, 0, 3)).reshape(count, -1).astype(F32)

    down_grad = column_grad(cot_all, hidden_val, dp_wide, 8)
    gate_weight_grad = row_grad(grad_gate, normed_two, dp_wide)
    up_weight_grad = row_grad(grad_up, normed_two, dp_wide)

    grad_mix_own = fence(grad_residual.astype(BF16), gate_weight_grad, down_grad)
    grad_mix = place_tokens([share_list(grad_mix_own, low)], me)
    grad_mixed = back_project(grad_mix, mixer_q).reshape(shape)
    grad_branch, prod_back, part_back, ends_back = call(
        adjoint_kernel,
        [(shape, BF16), (shape, F32), (shape, F32), ((blocks, 2, channels), F32)],
        scalars,
        [grad_mixed, state, branch, s_val, marks, coef],
        [pltpu.VMEM(padded, F32)],
    )
    ends_back = across_blocks(ends_back.reshape(4, rows, 2, channels)).reshape(-1, 2, channels)
    ends_back = fence(ends_back, up_weight_grad, block_output)
    down_weight_grad = join_ranks(down_grad.reshape(8, out_rows, hidden), wide_index, tp_wide, high_wide)
    mixer_grad = column_grad(grad_mix, mixed_flat, dp, 4)
    grad_branch = grad_branch.reshape(4 * tokens, channels)
    branch_weight_grad = row_grad(grad_branch, normed, dp)
    packed_shape = (channels, packed_width)
    grad_conv, edge_back, packed = call(
        functools.partial(gates_kernel, rows, step),
        [(shape, F32), ((blocks, 4, channels), BF16), (packed_shape, BF16)],
        scalars,
        [
            prod_back, part_back, ends_back, s_val, q_val, conv, state, came, recur_in, halo,
            marks, coef, rate_wide, gate_wide, collect, diagonal, eye,
        ],
        [
            pltpu.VMEM((4 * tokens, channels), BF16),
            pltpu.VMEM((4 * tokens, channels), BF16),
            pltpu.VMEM((8, channels), F32),
            pltpu.VMEM(everything, F32),
            pltpu.VMEM(padded, F32),
            pltpu.VMEM(padded, F32),
        ],
    )
    edge_back = edge_back.reshape(4, rows, 4, channels)
    halo_back = across_blocks(edge_back).astype(F32).reshape(seq_count * rows, 4, channels)
    halo_back = fence(halo_back, down_weight_grad)
    (grad_recur,) = call(
        functools.partial(unconvolve_kernel, rows, step, seq_count),
        [(shape, BF16)],
        scalars,
        [grad_conv, halo_back, marks, coef],
        [pltpu.VMEM(padded, F32)],
    )
    grad_recur = grad_recur.reshape(4 * tokens, channels)
    grad_normed_part = back_project(grad_branch, branch_q) + back_project(grad_recur, recur_q)
    grad_normed_sent = grad_normed_part.astype(BF16)
    gain_one_part = jnp.sum(grad_normed_sent.astype(F32) * input_all.astype(F32) * scale_one, axis=0)
    grad_normed_sent = fence(grad_normed_sent.reshape(4, tokens, width), mixer_grad)
    grad_normed = sum_tokens(grad_normed_sent, low)
    own_scale = scale_one[:tokens]
    unit_one = input_own.astype(F32) * own_scale
    scaled_one = grad_normed * gain_one
    input_grad = (
        grad_residual
        + own_scale
        * (scaled_one - unit_one * jnp.mean(scaled_one * unit_one, axis=-1, keepdims=True))
    ).astype(BF16)
    mixer_weight_grad = join_ranks(mixer_grad.reshape(4, out_rows, channels), tp_index, tp, high)
    recur_weight_grad = row_grad(grad_recur, normed, dp)

    packed = packed.reshape((2,) * len(dp) + (channel_rows, packed_width))
    order = tuple(reversed(dp))
    axes = tuple(reversed(row_axes(dp)))
    packed = scatter_bits(packed, axes, order, me, trade)
    gain_parts = jnp.stack([gain_one_part, gain_two_part]).reshape(2, high, 4, deep, -1)
    gain_parts = gain_parts.transpose(2, 1, 3, 0, 4).reshape(4, share, -1).astype(BF16)
    gain_sum = pick(gain_parts, tp_index, 0).astype(F32)
    for j in (1, 2, 3):
        sent = pick(gain_parts, jnp.bitwise_xor(tp_index, j), 0)
        gain_sum = gain_sum + trade(sent, j * low).astype(F32)
    gain_sum = gain_sum.astype(BF16).reshape((2,) * len(dp) + (-1,))
    gain_grads = scatter_bits(gain_sum, axes, order, me, trade).reshape(2, -1)
    numbers = packed[:, 2 * block_size : 2 * block_size + 8]
    return (
        block_output.reshape(rows, span, width),
        input_grad.reshape(rows, span, width),
        gain_grads[0],
        branch_weight_grad,
        recur_weight_grad,
        numbers[:, :TAPS],
        numbers[:, 4],
        packed[:, :block_size],
        numbers[:, 5],
        packed[:, block_size : 2 * block_size],
        numbers[:, 6],
        numbers[:, 7],
        mixer_weight_grad,
        gain_grads[1],
        gate_weight_grad,
        up_weight_grad,
        down_weight_grad,
    )


def solution(mesh):
    tokens, spread, table = P("fsdp", "seq", None), P(AXES), P(AXES, None)
    in_specs = (
        tokens, P(), spread, table, table, table, spread, table, spread, table, spread, spread,
        table, spread, table, table, table, tokens,
    )
    out_specs = (
        tokens, tokens, spread, table, table, table, spread, table, spread, table, spread, spread,
        table, spread, table, table, table,
    )
    return jax.shard_map(shards, mesh=mesh, in_specs=in_specs, out_specs=out_specs, check_vma=False)
```

time: 998 us -> 783 us (0.78)
  waiting for transfers between devices: 457 us -> 296 us
  local copies, waits for them, and re-layouts: 203 us -> 125 us
  Pallas kernels: 42.1 us -> 81.1 us
  other arithmetic: 59.3 us -> 39.2 us
    ppermute x123 -> x120, waiting for transfers between devices: 457 us -> 296 us  [trade(): return lax.ppermute(value, AXES, [(i, i ^ mask) for i in range(count)])]
    reshape x24 -> x3, local copies, waits for them, and re-layouts: 47.7 us -> 0.76 us  [the longest x1 0.39 us: by_rank(): split = weight.reshape(weight.shape[0], upper, ranks, -1)]
    pallas_call x0 -> x10, Pallas kernels: none -> 35.8 us  [assemble(): pl.pallas_call(functools.partial(copy_kernel, len(pieces), shapes, places...]
    dynamic_update_slice x17 -> x0, local copies, waits for them, and re-layouts: 16.1 us -> none  [gather_columns(): lax.dynamic_update_slice(whole, got[None, :, None], (number_of(owner, hig...]
    dynamic_update_slice x52 -> x12, local copies, waits for them, and re-layouts: 38.2 us -> 53.5 us  [put(): return lax.dynamic_update_index_in_dim(buffer, part, index, axis)]
    unnamed x183 -> x225, local copies, waits for them, and re-layouts: 24 us -> 10.9 us
    another operation x24 -> x5, local copies, waits for them, and re-layouts: 17 us -> 4.91 us  [the longest x4 3.07 us: shards(): jnp.stack([conv_bias, recur_gate_bias, input_gate_bias, decay_param], axi...]
    squeeze x22 -> x18, local copies, waits for them, and re-layouts: 16.8 us -> 6.78 us  [pick(): return lax.dynamic_index_in_dim(value, index, axis, keepdims=False)]
  transfers between devices with their start and end apart: 123 -> 120, of which waited for: 62 -> 48; matrix products, arithmetic and copies ran while one was open for 30% -> 25% of each run, Pallas kernels for 4% -> 10%
where the time goes in v2:
time: 783 us; the launch traced here: 768 us
  waiting for transfers between devices  296 us (38%)
  starting transfers between devices  140 us (18%)
  local copies, waits for them, and re-layouts  125 us (16%)
  matrix products  85.1 us (11%)
  Pallas kernels  81.1 us (10%)
  other arithmetic  39.2 us (5%)
    ppermute x120, waiting for transfers between devices, trade(): return lax.ppermute(value, AXES, [(i, i ^ mask) for i in range(count)])  296 us
    ppermute x120, starting transfers between devices, trade(): return lax.ppermute(value, AXES, [(i, i ^ mask) for i in range(count)])  140 us
    dynamic_update_slice x12, local copies, waits for them, and re-layouts, put(): return lax.dynamic_update_index_in_dim(buffer, part, index, axis)  53.5 us
    pallas_call x5, Pallas kernels, call(): pl.pallas_call(body, out_shape=[jax.ShapeDtypeStruct(shape, kind) for sha...  45.3 us
    dot_general x6, matrix products, back_project(): lax.dot_general(left, weight, (((1,), (0,)), ((), ())), preferred_element...  36.8 us
    pallas_call x10, Pallas kernels, assemble(): pl.pallas_call(functools.partial(copy_kernel, len(pieces), shapes, places...  35.8 us
    dot_general x6, matrix products, project(): lax.dot_general(left, weight, (((1,), (1,)), ((), ())), preferred_element...  27.7 us
    dot_general x6, matrix products, outer(): lax.dot_general(grads, values, (((0,), (0,)), ((), ())), preferred_elemen...  20.6 us
  transfers between devices with their start and end apart: 120, of which 48 were waited for; matrix products, arithmetic and copies ran while one was open for 25% of the time, Pallas kernels for 10%

profile of v2, /device:TPU:20, one launch (start us, length us, event | category | flops | bytes accessed | tf_op | source)
XLA Modules:
  0.0 768.3 jit_solution(11388877218519118672)
XLA Ops:
  15.0 20.8 %collective-permute-done.4 = bf16[80,330]{1,0:T(8,128)(2,1)S(1)} collective-permute-done((bf16[80,330]{1,0:T(8,128)(2,1)S(1)}, bf16[80,330]{1,0:T(8,128)(2,1)S(1)}, u32[]{:S(2)}, u32[]{:S(2)}) %collective-permute-start.4) | collective-permute-done | bytes 52832 | tf_op jit(solution)/shard_map/ppermute | solution.py:50
  36.4 4.3 collective-permute-done.5
  42.8 3.5 collective-permute-start.8
  61.8 3.8 collective-permute-done.2.refs_3_
  83.3 3.4 collective-permute-done.19.refs_1_
  92.1 4.9 shard_map.342
  97.1 3.7 convolution_convert_fusion.8
  106.6 13.1 %shard_map.343 = (bf16[8,64,640]{2,1,0:T(8,128)(2,1)}, f32[8,64,640]{2,1,0:T(8,128)}, f32[8,64,640]{2,1,0:T(8,128)}, f32[8,64,640]{2,1,0:T(8,128)}, f32[8,64,640...) custom-call(s32[5]{0:T(128)} %pad_add_fusion.scalars, ...), custom_call_target="tpu_custom_call" | custom-call | tf_op jit(solution)/shard_map/pallas_call | solution.py:192
  128.4 4.1 shard_map.344
  134.1 12.8 %collective-permute-done.36.refs_5_ = bf16[128,2048]{1,0:T(8,128)(2,1)} collective-permute-done((bf16[128,2048]{1,0:T(8,128)(2,1)S(1)}, bf16[128,2048]{1,0:T(8,128)(2,1)}, u32[]{:S(2)}, u32[]{:S(2)}) %collective-permute-start.36) | collective-permute-done | bytes 524320 | tf_op jit(solution)/shard_map/ppermute | solution.py:50
  146.9 3.5 collective-permute-start.67
  155.7 3.6 convolution_convert_fusion.7
  163.0 4.8 collective-permute-done.67.refs_7_
  177.7 10.4 %collective-permute-done.29 = bf16[128,2048]{1,0:T(8,128)(2,1)} collective-permute-done((bf16[128,2048]{1,0:T(8,128)(2,1)}, bf16[128,2048]{1,0:T(8,128)(2,1)}, u32[]{:S(2)}, u32[]{:S(2)}) %collective-permute-start.29) | collective-permute-done | bytes 524320 | tf_op jit(solution)/shard_map/ppermute | solution.py:50
  202.2 7.1 collective-permute-done.48.refs_4_
  211.4 3.4 collective-permute-start.37
  214.8 9.8 %collective-permute-done.50.refs_6_ = bf16[64,768]{1,0:T(8,128)(2,1)S(1)} collective-permute-done((bf16[64,768]{1,0:T(8,128)(2,1)S(1)}, bf16[64,768]{1,0:T(8,128)(2,1)S(1)}, u32[]{:S(2)}, u32[]{:S(2)}) %collective-permute-start.50) | collective-permute-done | bytes 98336 | tf_op jit(solution)/shard_map/ppermute | solution.py:50
  224.6 4.1 collective-permute-done.51.refs_7_
  229.4 18.2 %collective-permute-done.69.refs_9_ = bf16[64,2048]{1,0:T(8,128)(2,1)} collective-permute-done((bf16[64,2048]{1,0:T(8,128)(2,1)S(1)}, bf16[64,2048]{1,0:T(8,128)(2,1)}, u32[]{:S(2)}, u32[]{:S(2)}) %collective-permute-start.69) | collective-permute-done | bytes 262176 | tf_op jit(solution)/shard_map/ppermute | solution.py:50
  255.2 7.3 collective-permute-done.32.refs_1_
  266.1 3.9 collective-permute-done.38.refs_6_
  280.5 4.3 shard_map.351
  285.5 4.2 shard_map.347
  289.9 5.8 shard_map.348
  295.7 7.0 fusion.59
  302.7 3.7 shard_map.350
  306.4 14.1 %fusion.60 = f32[1024,768]{1,0:T(8,128)S(1)} fusion(bf16[1024,2048]{1,0:T(8,128)(2,1)S(1)} %copy-done.18, bf16[2048,768]{1,0:T(8,128)(2,1)} %bitcast.382), kind=kOutput, calls=%fused_computation.235 | convolution fusion | flops 3221225472 | bytes 10485760 | tf_op jit(solution)/shard_map/dot_general | solution.py:172
  320.6 6.9 fusion.11
  327.5 5.3 convolution_convert_fusion.2
  332.9 3.7 convolution_convert_fusion
  336.6 3.7 convolution_convert_fusion.1
  340.3 5.7 fusion.61
  346.0 3.7 convolution_convert_fusion.3
  349.7 6.1 add_convert_fusion
  362.3 9.7 %collective-permute-done.75 = bf16[128,2048]{1,0:T(8,128)(2,1)S(1)} collective-permute-done((bf16[128,2048]{1,0:T(8,128)(2,1)S(1)}, bf16[128,2048]{1,0:T(8,128)(2,1)S(1)}, u32[]{:S(2)}, u32[]{:S(2)}) %collective-permute-start.75) | collective-permute-done | bytes 524320 | tf_op jit(solution)/shard_map/ppermute | solution.py:50
  372.5 9.8 %collective-permute-done.74 = bf16[128,2048]{1,0:T(8,128)(2,1)S(1)} collective-permute-done((bf16[128,2048]{1,0:T(8,128)(2,1)S(1)}, bf16[128,2048]{1,0:T(8,128)(2,1)S(1)}, u32[]{:S(2)}, u32[]{:S(2)}) %collective-permute-start.74) | collective-permute-done | bytes 524320 | tf_op jit(solution)/shard_map/ppermute | solution.py:50
  384.7 9.8 %collective-permute-done.60 = bf16[128,2048]{1,0:T(8,128)(2,1)S(1)} collective-permute-done((bf16[128,2048]{1,0:T(8,128)(2,1)S(1)}, bf16[128,2048]{1,0:T(8,128)(2,1)S(1)}, u32[]{:S(2)}, u32[]{:S(2)}) %collective-permute-start.60) | collective-permute-done | bytes 524320 | tf_op jit(solution)/shard_map/ppermute | solution.py:50
  394.6 9.9 %collective-permute-done.59 = bf16[128,2048]{1,0:T(8,128)(2,1)S(1)} collective-permute-done((bf16[128,2048]{1,0:T(8,128)(2,1)S(1)}, bf16[128,2048]{1,0:T(8,128)(2,1)S(1)}, u32[]{:S(2)}, u32[]{:S(2)}) %collective-permute-start.59) | collective-permute-done | bytes 524320 | tf_op jit(solution)/shard_map/ppermute | solution.py:50
  407.6 20.4 %collective-permute-done.70 = bf16[128,2048]{1,0:T(8,128)(2,1)S(1)} collective-permute-done((bf16[128,2048]{1,0:T(8,128)(2,1)S(1)}, bf16[128,2048]{1,0:T(8,128)(2,1)S(1)}, u32[]{:S(2)}, u32[]{:S(2)}) %collective-permute-start.70) | collective-permute-done | bytes 524320 | tf_op jit(solution)/shard_map/ppermute | solution.py:50
  434.5 18.8 %collective-permute-done.76 = bf16[128,2048]{1,0:T(8,128)(2,1)S(1)} collective-permute-done((bf16[128,2048]{1,0:T(8,128)(2,1)S(1)}, bf16[128,2048]{1,0:T(8,128)(2,1)S(1)}, u32[]{:S(2)}, u32[]{:S(2)}) %collective-permute-start.76) | collective-permute-done | bytes 524320 | tf_op jit(solution)/shard_map/ppermute | solution.py:50
  460.2 15.0 %collective-permute-done.79 = bf16[8,64,768]{2,1,0:T(8,128)(2,1)S(1)} collective-permute-done((bf16[8,64,768]{2,1,0:T(8,128)(2,1)S(1)}, bf16[8,64,768]{2,1,0:T(8,128)(2,1)S(1)}, u32[]{:S(2)}, u32[]{:S(2)}) %collective-permute-start.79) | collective-permute-done | bytes 786464 | tf_op jit(solution)/shard_map/ppermute | solution.py:50
  476.5 5.3 collective-permute-done.61
  483.8 11.4 %collective-permute-done.80 = bf16[192,2048]{1,0:T(8,128)(2,1)S(1)} collective-permute-done((bf16[192,2048]{1,0:T(8,128)(2,1)S(1)}, bf16[192,2048]{1,0:T(8,128)(2,1)S(1)}, u32[]{:S(2)}, u32[]{:S(2)}) %collective-permute-start.80) | collective-permute-done | bytes 786464 | tf_op jit(solution)/shard_map/ppermute | solution.py:50
  502.7 9.0 %collective-permute-done.82.refs_2_ = bf16[128,2048]{1,0:T(8,128)(2,1)} collective-permute-done((bf16[128,2048]{1,0:T(8,128)(2,1)}, bf16[128,2048]{1,0:T(8,128)(2,1)}, u32[]{:S(2)}, u32[]{:S(2)}) %collective-permute-start.82) | collective-permute-done | bytes 524320 | tf_op jit(solution)/shard_map/ppermute | solution.py:50
  528.5 4.7 dynamic_update_slice.38
  544.0 4.7 dynamic_update_slice.39
  548.6 4.7 dynamic_update_slice.40
  553.3 4.7 dynamic_update_slice.41
  558.0 4.7 dynamic_update_slice.42
  562.7 4.7 dynamic_update_slice.43
  567.4 4.7 dynamic_update_slice.44
  572.1 5.1 dynamic_update_slice.45
  584.4 4.5 fusion.62.grad_mixed
  588.9 9.1 %shard_map.353 = (bf16[8,64,640]{2,1,0:T(8,128)(2,1)}, f32[8,64,640]{2,1,0:T(8,128)}, f32[8,64,640]{2,1,0:T(8,128)}, f32[8,2,640]{2,1,0:T(2,128)}) custom-call(s32[5]{0:T(128)} %pad_add_fusion.scalars, f32[8,64,640]{2,1,0:T(8,128)} %fusion.62.grad_mixed, f32[8,64,640]{2,1,0:T(8,128)} %get-tuple-element.84.state, f32[8,64,640]{2,1,0:T(8,128)} %fusion.58.branch, ...), custom_call_target="tpu_custom_call" | custom-call | tf_op jit(solution)/shard_map/pallas_call | solution.py:192
  610.8 15.4 %shard_map.354 = (f32[8,64,640]{2,1,0:T(8,128)}, bf16[8,4,640]{2,1,0:T(4,128)(2,1)}, bf16[640,384]{1,0:T(8,128)(2,1)}) custom-call(s32[5]{0:T(128)} %pad_add_fusion.scalars, f32[8,64,640]{2,1,0:T(8,128)} %get-tuple-element.88.prod, f32[8,64,640]{2,1,0:T(8,128)} %get-tuple-element.89.part, f32[16,2,640]{2,1,0:T(2,128)} %bitcast.411, ...), custom_call_target="tpu_custom_call" | custom-call | tf_op jit(solution)/shard_map/pallas_call | solution.py:192
  632.1 3.7 shard_map.355
  674.9 10.6 %collective-permute-done.97 = bf16[2,4,64,640]{3,2,1,0:T(8,128)(2,1)S(1)} collective-permute-done((bf16[2,4,64,640]{3,2,1,0:T(8,128)(2,1)S(1)}, bf16[2,4,64,640]{3,2,1,0:T(8,128)(2,1)S(1)}, u32[]{:S(2)}, u32[]{:S(2)}) %collective-permute-start.97) | collective-permute-done | bytes 655392 | tf_op jit(solution)/shard_map/ppermute | solution.py:50
  692.5 6.8 collective-permute-done.98
  706.8 3.9 dynamic_update_slice.46
  715.4 3.9 dynamic_update_slice.47
  721.1 3.9 dynamic_update_slice.48
  726.7 4.1 dynamic_update_slice.49
  745.7 7.3 collective-permute-done.112
  755.0 12.2 %collective-permute-done.113 = bf16[80,2048]{1,0:T(8,128)(2,1)S(1)} collective-permute-done((bf16[80,2048]{1,0:T(8,128)(2,1)S(1)}, bf16[80,2048]{1,0:T(8,128)(2,1)S(1)}, u32[]{:S(2)}, u32[]{:S(2)}) %collective-permute-start.113) | collective-permute-done | bytes 327712 | tf_op jit(solution)/shard_map/ppermute | solution.py:50
  (602 shorter events, 298.7 us)
Async XLA Ops:
  0.7 56.1 %collective-permute-start.1 = (bf16[128,2048]{1,0:T(8,128)(2,1)}, bf16[128,2048]{1,0:T(8,128)(2,1)S(1)}, u32[]{:S(2)}, u32[]{:S(2)}) collective-permute-start(bf16[128,2048]{1,0:T(8,128)(2,1)} %bitcast.366), channel_id=1, source_target_pairs={{0,8},{1,9},{2,10},{3,11},{4,12},{5,13},{6,14},{7,15},{8,0},{9,1},... | collective-permute-start | bytes 1572872 | tf_op jit(solution)/shard_map/ppermute | solution.py:50
  2.3 56.0 %collective-permute-start = (bf16[128,2048]{1,0:T(8,128)(2,1)}, bf16[128,2048]{1,0:T(8,128)(2,1)S(1)}, u32[]{:S(2)}, u32[]{:S(2)}) collective-permute-start(bf16[128,2048]{1,0:T(8,128)(2,1)} %bitcast.367), channel_id=1, source_target_pairs={{0,4},{1,5},{2,6},{3,7},{4,0},{5,1},{6,2},{7,3},{8,12},{9,13},{10,... | collective-permute-start | bytes 1572872 | tf_op jit(solution)/shard_map/ppermute | solution.py:50
  4.0 56.5 %collective-permute-start.11 = (bf16[2,80,2048]{2,1,0:T(8,128)(2,1)S(1)}, bf16[2,80,2048]{2,1,0:T(8,128)(2,1)}, u32[]{:S(2)}, u32[]{:S(2)}) collective-permute-start(bf16[2,80,2048]{2,1,0:T(8,128)(2,1)S(1)} %pad_maximum_fusion.1.refs_0_), channel_id=1, source_target_pairs={{0,2},{1,3},{2,0},{3,1},{4,6},{5,7},{6,4},{7,5},{8,10},{9,11},{10,... | collective-permute-start | bytes 1966088 | tf_op jit(solution)/shard_map/ppermute | solution.py:50
  5.5 54.9 %collective-permute-start.10 = (bf16[2,80,2048]{2,1,0:T(8,128)(2,1)S(1)}, bf16[2,80,2048]{2,1,0:T(8,128)(2,1)}, u32[]{:S(2)}, u32[]{:S(2)}) collective-permute-start(bf16[2,80,2048]{2,1,0:T(8,128)(2,1)S(1)} %pad_maximum_fusion.1.refs_0_), channel_id=1, source_target_pairs={{0,16},{1,17},{2,18},{3,19},{4,20},{5,21},{6,22},{7,23},{8,24},{9,... | collective-permute-start | bytes 1966088 | tf_op jit(solution)/shard_map/ppermute | solution.py:50
  11.5 24.3 %collective-permute-start.4 = (bf16[80,330]{1,0:T(8,128)(2,1)S(1)}, bf16[80,330]{1,0:T(8,128)(2,1)S(1)}, u32[]{:S(2)}, u32[]{:S(2)}) collective-permute-start(bf16[80,330]{1,0:T(8,128)(2,1)S(1)} %concatenate.12), channel_id=1, source_target_pairs={{0,16},{1,17},{2,18},{3,19},{4,20},{5,21},{6,22},{7,23},{8,24},{9,... | collective-permute-start | bytes 158408 | tf_op jit(solution)/shard_map/ppermute | solution.py:50
  56.1 34.6 %collective-permute-start.13 = (bf16[2,80,2048]{2,1,0:T(8,128)(2,1)S(1)}, bf16[2,80,2048]{2,1,0:T(8,128)(2,1)}, u32[]{:S(2)}, u32[]{:S(2)}) collective-permute-start(bf16[2,80,2048]{2,1,0:T(8,128)(2,1)S(1)} %pad_maximum_fusion.1.refs_0_), channel_id=1, source_target_pairs={{0,1},{1,0},{2,3},{3,2},{4,5},{5,4},{6,7},{7,6},{8,9},{9,8},{10,11... | collective-permute-start | bytes 1966088 | tf_op jit(solution)/shard_map/ppermute | solution.py:50
  60.4 19.1 %collective-permute-start.12 = (bf16[2,80,2048]{2,1,0:T(8,128)(2,1)}, bf16[2,80,2048]{2,1,0:T(8,128)(2,1)}, u32[]{:S(2)}, u32[]{:S(2)}) collective-permute-start(bf16[2,80,2048]{2,1,0:T(8,128)(2,1)} %collective-permute-done.10.refs_1_), channel_id=1, source_target_pairs={{0,2},{1,3},{2,0},{3,1},{4,6},{5,7},{6,4},{7,5},{8,10},{9,11},{10,... | collective-permute-start | bytes 1966088 | tf_op jit(solution)/shard_map/ppermute | solution.py:50
  61.8 29.5 %collective-permute-start.15 = (bf16[2,80,2048]{2,1,0:T(8,128)(2,1)}, bf16[2,80,2048]{2,1,0:T(8,128)(2,1)}, u32[]{:S(2)}, u32[]{:S(2)}) collective-permute-start(bf16[2,80,2048]{2,1,0:T(8,128)(2,1)} %collective-permute-done.11.refs_2_), channel_id=1, source_target_pairs={{0,1},{1,0},{2,3},{3,2},{4,5},{5,4},{6,7},{7,6},{8,9},{9,8},{10,11... | collective-permute-start | bytes 1966088 | tf_op jit(solution)/shard_map/ppermute | solution.py:50
  65.6 25.7 %collective-permute-start.14 = (bf16[2,80,2048]{2,1,0:T(8,128)(2,1)}, bf16[2,80,2048]{2,1,0:T(8,128)(2,1)}, u32[]{:S(2)}, u32[]{:S(2)}) collective-permute-start(bf16[2,80,2048]{2,1,0:T(8,128)(2,1)} %collective-permute-done.10.refs_1_), channel_id=1, source_target_pairs={{0,1},{1,0},{2,3},{3,2},{4,5},{5,4},{6,7},{7,6},{8,9},{9,8},{10,11... | collective-permute-start | bytes 1966088 | tf_op jit(solution)/shard_map/ppermute | solution.py:50
  103.0 21.2 %collective-permute-start.24 = (bf16[4,64,640]{2,1,0:T(8,128)(2,1)S(1)}, bf16[4,64,640]{2,1,0:T(8,128)(2,1)}, u32[]{:S(2)}, u32[]{:S(2)}) collective-permute-start(bf16[4,64,640]{2,1,0:T(8,128)(2,1)S(1)} %collective-permute-done.22.refs_1_), channel_id=1, source_target_pairs={{0,2},{1,3},{2,0},{3,1},{4,6},{5,7},{6,4},{7,5},{8,10},{9,11},{10,... | collective-permute-start | bytes 983048 | tf_op jit(solution)/shard_map/ppermute | solution.py:50
  122.3 24.6 %collective-permute-start.36 = (bf16[128,2048]{1,0:T(8,128)(2,1)S(1)}, bf16[128,2048]{1,0:T(8,128)(2,1)}, u32[]{:S(2)}, u32[]{:S(2)}) collective-permute-start(bf16[128,2048]{1,0:T(8,128)(2,1)S(1)} %bitcast.372), channel_id=1, source_target_pairs={{0,16},{1,17},{2,18},{3,19},{4,20},{5,21},{6,22},{7,23},{8,24},{9,... | collective-permute-start | bytes 1572872 | tf_op jit(solution)/shard_map/ppermute | solution.py:50
  124.2 26.3 %collective-permute-start.27 = (bf16[4,64,640]{2,1,0:T(8,128)(2,1)}, bf16[4,64,640]{2,1,0:T(8,128)(2,1)S(1)}, u32[]{:S(2)}, u32[]{:S(2)}) collective-permute-start(bf16[4,64,640]{2,1,0:T(8,128)(2,1)} %copy-done.52), channel_id=1, source_target_pairs={{0,1},{1,0},{2,3},{3,2},{4,5},{5,4},{6,7},{7,6},{8,9},{9,8},{10,11... | collective-permute-start | bytes 983048 | tf_op jit(solution)/shard_map/ppermute | solution.py:50
  124.8 26.1 %collective-permute-start.28 = (bf16[4,64,640]{2,1,0:T(8,128)(2,1)}, bf16[4,64,640]{2,1,0:T(8,128)(2,1)S(1)}, u32[]{:S(2)}, u32[]{:S(2)}) collective-permute-start(bf16[4,64,640]{2,1,0:T(8,128)(2,1)} %collective-permute-done.24.refs_3_), channel_id=1, source_target_pairs={{0,1},{1,0},{2,3},{3,2},{4,5},{5,4},{6,7},{7,6},{8,9},{9,8},{10,11... | collective-permute-start | bytes 983048 | tf_op jit(solution)/shard_map/ppermute | solution.py:50
  132.5 28.1 %collective-permute-start.63 = (bf16[128,2048]{1,0:T(8,128)(2,1)S(1)}, bf16[128,2048]{1,0:T(8,128)(2,1)S(1)}, u32[]{:S(2)}, u32[]{:S(2)}) collective-permute-start(bf16[128,2048]{1,0:T(8,128)(2,1)S(1)} %bitcast.373), channel_id=1, source_target_pairs={{0,8},{1,9},{2,10},{3,11},{4,12},{5,13},{6,14},{7,15},{8,0},{9,1},... | collective-permute-start | bytes 1572872 | tf_op jit(solution)/shard_map/ppermute | solution.py:50
  133.0 29.1 %collective-permute-start.62 = (bf16[128,2048]{1,0:T(8,128)(2,1)S(1)}, bf16[128,2048]{1,0:T(8,128)(2,1)S(1)}, u32[]{:S(2)}, u32[]{:S(2)}) collective-permute-start(bf16[128,2048]{1,0:T(8,128)(2,1)S(1)} %bitcast.374), channel_id=1, source_target_pairs={{0,4},{1,5},{2,6},{3,7},{4,0},{5,1},{6,2},{7,3},{8,12},{9,13},{10,... | collective-permute-start | bytes 1572872 | tf_op jit(solution)/shard_map/ppermute | solution.py:50
  146.9 20.8 %collective-permute-start.67 = (bf16[128,2048]{1,0:T(8,128)(2,1)}, bf16[128,2048]{1,0:T(8,128)(2,1)}, u32[]{:S(2)}, u32[]{:S(2)}) collective-permute-start(bf16[128,2048]{1,0:T(8,128)(2,1)} %collective-permute-done.36.refs_5_), channel_id=1, source_target_pairs={{0,8},{1,9},{2,10},{3,11},{4,12},{5,13},{6,14},{7,15},{8,0},{9,1},... | collective-permute-start | bytes 1572872 | tf_op jit(solution)/shard_map/ppermute | solution.py:50
  150.5 25.1 %collective-permute-start.66 = (bf16[128,2048]{1,0:T(8,128)(2,1)}, bf16[128,2048]{1,0:T(8,128)(2,1)}, u32[]{:S(2)}, u32[]{:S(2)}) collective-permute-start(bf16[128,2048]{1,0:T(8,128)(2,1)} %collective-permute-done.36.refs_5_), channel_id=1, source_target_pairs={{0,4},{1,5},{2,6},{3,7},{4,0},{5,1},{6,2},{7,3},{8,12},{9,13},{10,... | collective-permute-start | bytes 1572872 | tf_op jit(solution)/shard_map/ppermute | solution.py:50
  151.0 77.8 %collective-permute-start.42 = (bf16[2,192,2048]{2,1,0:T(8,128)(2,1)}, bf16[2,192,2048]{2,1,0:T(8,128)(2,1)}, u32[]{:S(2)}, u32[]{:S(2)}) collective-permute-start(bf16[2,192,2048]{2,1,0:T(8,128)(2,1)} %pad_maximum_fusion.refs_0_), channel_id=1, source_target_pairs={{0,2},{1,3},{2,0},{3,1},{4,6},{5,7},{6,4},{7,5},{8,10},{9,11},{10,... | collective-permute-start | bytes 4718600 | tf_op jit(solution)/shard_map/ppermute | solution.py:50
  160.6 27.4 %collective-permute-start.29 = (bf16[128,2048]{1,0:T(8,128)(2,1)}, bf16[128,2048]{1,0:T(8,128)(2,1)}, u32[]{:S(2)}, u32[]{:S(2)}) collective-permute-start(bf16[128,2048]{1,0:T(8,128)(2,1)} %get-tuple-element.195), channel_id=1, source_target_pairs={{0,4},{1,5},{2,6},{3,7},{4,0},{5,1},{6,2},{7,3},{8,12},{9,13},{10,... | collective-permute-start | bytes 1572872 | tf_op jit(solution)/shard_map/ppermute | solution.py:50
  163.0 25.1 %collective-permute-start.31 = (bf16[128,2048]{1,0:T(8,128)(2,1)}, bf16[128,2048]{1,0:T(8,128)(2,1)}, u32[]{:S(2)}, u32[]{:S(2)}) collective-permute-start(bf16[128,2048]{1,0:T(8,128)(2,1)} %get-tuple-element.196), channel_id=1, source_target_pairs={{0,12},{1,13},{2,14},{3,15},{4,8},{5,9},{6,10},{7,11},{8,4},{9,5},... | collective-permute-start | bytes 1572872 | tf_op jit(solution)/shard_map/ppermute | solution.py:50
  167.7 22.5 %collective-permute-start.30 = (bf16[128,2048]{1,0:T(8,128)(2,1)}, bf16[128,2048]{1,0:T(8,128)(2,1)}, u32[]{:S(2)}, u32[]{:S(2)}) collective-permute-start(bf16[128,2048]{1,0:T(8,128)(2,1)} %get-tuple-element.197), channel_id=1, source_target_pairs={{0,8},{1,9},{2,10},{3,11},{4,12},{5,13},{6,14},{7,15},{8,0},{9,1},... | collective-permute-start | bytes 1572872 | tf_op jit(solution)/shard_map/ppermute | solution.py:50
  175.6 19.2 %collective-permute-start.64 = (bf16[64,2048]{1,0:T(8,128)(2,1)S(1)}, bf16[64,2048]{1,0:T(8,128)(2,1)S(1)}, u32[]{:S(2)}, u32[]{:S(2)}) collective-permute-start(bf16[64,2048]{1,0:T(8,128)(2,1)S(1)} %slice.304), channel_id=1, source_target_pairs={{0,4},{1,5},{2,6},{3,7},{4,0},{5,1},{6,2},{7,3},{8,12},{9,13},{10,... | collective-permute-start | bytes 786440 | tf_op jit(solution)/shard_map/ppermute | solution.py:50
  199.3 25.3 %collective-permute-start.50 = (bf16[64,768]{1,0:T(8,128)(2,1)S(1)}, bf16[64,768]{1,0:T(8,128)(2,1)S(1)}, u32[]{:S(2)}, u32[]{:S(2)}) collective-permute-start(bf16[64,768]{1,0:T(8,128)(2,1)S(1)} %bitcast.419), channel_id=1, source_target_pairs={{0,24},{1,25},{2,26},{3,27},{4,28},{5,29},{6,30},{7,31},{8,16},{9,... | collective-permute-start | bytes 294920 | tf_op jit(solution)/shard_map/ppermute | solution.py:50
  201.0 27.6 %collective-permute-start.51 = (bf16[64,768]{1,0:T(8,128)(2,1)S(1)}, bf16[64,768]{1,0:T(8,128)(2,1)S(1)}, u32[]{:S(2)}, u32[]{:S(2)}) collective-permute-start(bf16[64,768]{1,0:T(8,128)(2,1)S(1)} %bitcast.418), channel_id=1, source_target_pairs={{0,28},{1,29},{2,30},{3,31},{4,24},{5,25},{6,26},{7,27},{8,20},{9,... | collective-permute-start | bytes 294920 | tf_op jit(solution)/shard_map/ppermute | solution.py:50
  209.3 19.4 %collective-permute-start.68 = (bf16[64,2048]{1,0:T(8,128)(2,1)S(1)}, bf16[64,2048]{1,0:T(8,128)(2,1)S(1)}, u32[]{:S(2)}, u32[]{:S(2)}) collective-permute-start(bf16[64,2048]{1,0:T(8,128)(2,1)S(1)} %slice.306), channel_id=1, source_target_pairs={{0,4},{1,5},{2,6},{3,7},{4,0},{5,1},{6,2},{7,3},{8,12},{9,13},{10,... | collective-permute-start | bytes 786440 | tf_op jit(solution)/shard_map/ppermute | solution.py:50
  211.4 38.1 %collective-permute-start.37 = (bf16[128,2048]{1,0:T(8,128)(2,1)S(1)}, bf16[128,2048]{1,0:T(8,128)(2,1)S(1)}, u32[]{:S(2)}, u32[]{:S(2)}) collective-permute-start(bf16[128,2048]{1,0:T(8,128)(2,1)S(1)} %multiply_convert_fusion.2.refs_0_), channel_id=1, source_target_pairs={{0,16},{1,17},{2,18},{3,19},{4,20},{5,21},{6,22},{7,23},{8,24},{9,... | collective-permute-start | bytes 1572872 | tf_op jit(solution)/shard_map/ppermute | solution.py:50
  224.6 27.5 %collective-permute-start.33 = (bf16[128,2048]{1,0:T(8,128)(2,1)S(1)}, bf16[128,2048]{1,0:T(8,128)(2,1)S(1)}, u32[]{:S(2)}, u32[]{:S(2)}) collective-permute-start(bf16[128,2048]{1,0:T(8,128)(2,1)S(1)} %multiply_convert_fusion.2.refs_0_), channel_id=1, source_target_pairs={{0,8},{1,9},{2,10},{3,11},{4,12},{5,13},{6,14},{7,15},{8,0},{9,1},... | collective-permute-start | bytes 1572872 | tf_op jit(solution)/shard_map/ppermute | solution.py:50
  228.7 19.0 %collective-permute-start.69 = (bf16[64,2048]{1,0:T(8,128)(2,1)S(1)}, bf16[64,2048]{1,0:T(8,128)(2,1)}, u32[]{:S(2)}, u32[]{:S(2)}) collective-permute-start(bf16[64,2048]{1,0:T(8,128)(2,1)S(1)} %slice.307), channel_id=1, source_target_pairs={{0,8},{1,9},{2,10},{3,11},{4,12},{5,13},{6,14},{7,15},{8,0},{9,1},... | collective-permute-start | bytes 786440 | tf_op jit(solution)/shard_map/ppermute | solution.py:50
  228.7 61.2 %collective-permute-start.43 = (bf16[2,192,2048]{2,1,0:T(8,128)(2,1)}, bf16[2,192,2048]{2,1,0:T(8,128)(2,1)}, u32[]{:S(2)}, u32[]{:S(2)}) collective-permute-start(bf16[2,192,2048]{2,1,0:T(8,128)(2,1)} %pad_maximum_fusion.refs_0_), channel_id=1, source_target_pairs={{0,1},{1,0},{2,3},{3,2},{4,5},{5,4},{6,7},{7,6},{8,9},{9,8},{10,11... | collective-permute-start | bytes 4718600 | tf_op jit(solution)/shard_map/ppermute | solution.py:50
  228.8 61.1 %collective-permute-start.44 = (bf16[2,192,2048]{2,1,0:T(8,128)(2,1)}, bf16[2,192,2048]{2,1,0:T(8,128)(2,1)}, u32[]{:S(2)}, u32[]{:S(2)}) collective-permute-start(bf16[2,192,2048]{2,1,0:T(8,128)(2,1)} %collective-permute-done.42.refs_1_), channel_id=1, source_target_pairs={{0,1},{1,0},{2,3},{3,2},{4,5},{5,4},{6,7},{7,6},{8,9},{9,8},{10,11... | collective-permute-start | bytes 4718600 | tf_op jit(solution)/shard_map/ppermute | solution.py:50
  252.1 18.0 %collective-permute-start.38 = (bf16[128,2048]{1,0:T(8,128)(2,1)S(1)}, bf16[128,2048]{1,0:T(8,128)(2,1)S(1)}, u32[]{:S(2)}, u32[]{:S(2)}) collective-permute-start(bf16[128,2048]{1,0:T(8,128)(2,1)S(1)} %collective-permute-done.37.refs_5_), channel_id=1, source_target_pairs={{0,4},{1,5},{2,6},{3,7},{4,0},{5,1},{6,2},{7,3},{8,12},{9,13},{10,... | collective-permute-start | bytes 1572872 | tf_op jit(solution)/shard_map/ppermute | solution.py:50
  262.5 27.3 %collective-permute-start.52 = (bf16[8,64,768]{2,1,0:T(8,128)(2,1)}, bf16[8,64,768]{2,1,0:T(8,128)(2,1)}, u32[]{:S(2)}, u32[]{:S(2)}) collective-permute-start(bf16[8,64,768]{2,1,0:T(8,128)(2,1)} %shard_map.349.refs_0_), channel_id=1, source_target_pairs={{0,2},{1,3},{2,0},{3,1},{4,6},{5,7},{6,4},{7,5},{8,10},{9,11},{10,... | collective-permute-start | bytes 2359304 | tf_op jit(solution)/shard_map/ppermute | solution.py:50
  284.8 17.8 %collective-permute-start.53 = (bf16[8,64,768]{2,1,0:T(8,128)(2,1)S(1)}, bf16[8,64,768]{2,1,0:T(8,128)(2,1)}, u32[]{:S(2)}, u32[]{:S(2)}) collective-permute-start(bf16[8,64,768]{2,1,0:T(8,128)(2,1)S(1)} %copy-done.21), channel_id=1, source_target_pairs={{0,1},{1,0},{2,3},{3,2},{4,5},{5,4},{6,7},{7,6},{8,9},{9,8},{10,11... | collective-permute-start | bytes 2359304 | tf_op jit(solution)/shard_map/ppermute | solution.py:50
  358.1 24.2 %collective-permute-start.74 = (bf16[128,2048]{1,0:T(8,128)(2,1)S(1)}, bf16[128,2048]{1,0:T(8,128)(2,1)S(1)}, u32[]{:S(2)}, u32[]{:S(2)}) collective-permute-start(bf16[128,2048]{1,0:T(8,128)(2,1)S(1)} %get-tuple-element.174), channel_id=1, source_target_pairs={{0,8},{1,9},{2,10},{3,11},{4,12},{5,13},{6,14},{7,15},{8,0},{9,1},... | collective-permute-start | bytes 1572872 | tf_op jit(solution)/shard_map/ppermute | solution.py:50
  358.2 26.1 %collective-permute-start.73 = (bf16[128,2048]{1,0:T(8,128)(2,1)S(1)}, bf16[128,2048]{1,0:T(8,128)(2,1)S(1)}, u32[]{:S(2)}, u32[]{:S(2)}) collective-permute-start(bf16[128,2048]{1,0:T(8,128)(2,1)S(1)} %get-tuple-element.175), channel_id=1, source_target_pairs={{0,4},{1,5},{2,6},{3,7},{4,0},{5,1},{6,2},{7,3},{8,12},{9,13},{10,... | collective-permute-start | bytes 1572872 | tf_op jit(solution)/shard_map/ppermute | solution.py:50
  360.2 34.4 %collective-permute-start.60 = (bf16[128,2048]{1,0:T(8,128)(2,1)S(1)}, bf16[128,2048]{1,0:T(8,128)(2,1)S(1)}, u32[]{:S(2)}, u32[]{:S(2)}) collective-permute-start(bf16[128,2048]{1,0:T(8,128)(2,1)S(1)} %get-tuple-element.179), channel_id=1, source_target_pairs={{0,12},{1,13},{2,14},{3,15},{4,8},{5,9},{6,10},{7,11},{8,4},{9,5},... | collective-permute-start | bytes 1572872 | tf_op jit(solution)/shard_map/ppermute | solution.py:50
  362.0 42.4 %collective-permute-start.59 = (bf16[128,2048]{1,0:T(8,128)(2,1)S(1)}, bf16[128,2048]{1,0:T(8,128)(2,1)S(1)}, u32[]{:S(2)}, u32[]{:S(2)}) collective-permute-start(bf16[128,2048]{1,0:T(8,128)(2,1)S(1)} %get-tuple-element.180), channel_id=1, source_target_pairs={{0,8},{1,9},{2,10},{3,11},{4,12},{5,13},{6,14},{7,15},{8,0},{9,1},... | collective-permute-start | bytes 1572872 | tf_op jit(solution)/shard_map/ppermute | solution.py:50
  372.1 34.8 %collective-permute-start.58 = (bf16[128,2048]{1,0:T(8,128)(2,1)S(1)}, bf16[128,2048]{1,0:T(8,128)(2,1)S(1)}, u32[]{:S(2)}, u32[]{:S(2)}) collective-permute-start(bf16[128,2048]{1,0:T(8,128)(2,1)S(1)} %get-tuple-element.181), channel_id=1, source_target_pairs={{0,4},{1,5},{2,6},{3,7},{4,0},{5,1},{6,2},{7,3},{8,12},{9,13},{10,... | collective-permute-start | bytes 1572872 | tf_op jit(solution)/shard_map/ppermute | solution.py:50
  382.2 45.7 %collective-permute-start.70 = (bf16[128,2048]{1,0:T(8,128)(2,1)S(1)}, bf16[128,2048]{1,0:T(8,128)(2,1)S(1)}, u32[]{:S(2)}, u32[]{:S(2)}) collective-permute-start(bf16[128,2048]{1,0:T(8,128)(2,1)S(1)} %get-tuple-element.172), channel_id=1, source_target_pairs={{0,4},{1,5},{2,6},{3,7},{4,0},{5,1},{6,2},{7,3},{8,12},{9,13},{10,... | collective-permute-start | bytes 1572872 | tf_op jit(solution)/shard_map/ppermute | solution.py:50
  384.3 71.7 %collective-permute-start.78 = (bf16[8,2,64,768]{3,2,0,1:T(8,128)(2,1)S(1)}, bf16[8,2,64,768]{3,2,0,1:T(8,128)(2,1)S(1)}, u32[]{:S(2)}, u32[]{:S(2)}) collective-permute-start(bf16[8,2,64,768]{3,2,0,1:T(8,128)(2,1)S(1)} %bitcast.398), channel_id=1, source_target_pairs={{0,1},{1,0},{2,3},{3,2},{4,5},{5,4},{6,7},{7,6},{8,9},{9,8},{10,11... | collective-permute-start | bytes 4718600 | tf_op jit(solution)/shard_map/ppermute | solution.py:50
  394.6 63.3 %collective-permute-start.77 = (bf16[2,192,2048]{2,1,0:T(8,128)(2,1)S(1)}, bf16[2,192,2048]{2,1,0:T(8,128)(2,1)S(1)}, u32[]{:S(2)}, u32[]{:S(2)}) collective-permute-start(bf16[2,192,2048]{2,1,0:T(8,128)(2,1)S(1)} %dynamic-slice_bitcast_fusion.1), channel_id=1, source_target_pairs={{0,1},{1,0},{2,3},{3,2},{4,5},{5,4},{6,7},{7,6},{8,9},{9,8},{10,11... | collective-permute-start | bytes 4718600 | tf_op jit(solution)/shard_map/ppermute | solution.py:50
  404.5 27.9 %collective-permute-start.72 = (bf16[128,2048]{1,0:T(8,128)(2,1)S(1)}, bf16[128,2048]{1,0:T(8,128)(2,1)S(1)}, u32[]{:S(2)}, u32[]{:S(2)}) collective-permute-start(bf16[128,2048]{1,0:T(8,128)(2,1)S(1)} %get-tuple-element.176), channel_id=1, source_target_pairs={{0,12},{1,13},{2,14},{3,15},{4,8},{5,9},{6,10},{7,11},{8,4},{9,5},... | collective-permute-start | bytes 1572872 | tf_op jit(solution)/shard_map/ppermute | solution.py:50
  406.9 25.6 %collective-permute-start.71 = (bf16[128,2048]{1,0:T(8,128)(2,1)S(1)}, bf16[128,2048]{1,0:T(8,128)(2,1)S(1)}, u32[]{:S(2)}, u32[]{:S(2)}) collective-permute-start(bf16[128,2048]{1,0:T(8,128)(2,1)S(1)} %get-tuple-element.177), channel_id=1, source_target_pairs={{0,8},{1,9},{2,10},{3,11},{4,12},{5,13},{6,14},{7,15},{8,0},{9,1},... | collective-permute-start | bytes 1572872 | tf_op jit(solution)/shard_map/ppermute | solution.py:50
  427.9 25.4 %collective-permute-start.76 = (bf16[128,2048]{1,0:T(8,128)(2,1)S(1)}, bf16[128,2048]{1,0:T(8,128)(2,1)S(1)}, u32[]{:S(2)}, u32[]{:S(2)}) collective-permute-start(bf16[128,2048]{1,0:T(8,128)(2,1)S(1)} %add_convert_fusion.2), channel_id=1, source_target_pairs={{0,16},{1,17},{2,18},{3,19},{4,20},{5,21},{6,22},{7,23},{8,24},{9,... | collective-permute-start | bytes 1572872 | tf_op jit(solution)/shard_map/ppermute | solution.py:50
  432.3 42.9 %collective-permute-start.55 = (bf16[128,2048]{1,0:T(8,128)(2,1)S(1)}, bf16[128,2048]{1,0:T(8,128)(2,1)S(1)}, u32[]{:S(2)}, u32[]{:S(2)}) collective-permute-start(bf16[128,2048]{1,0:T(8,128)(2,1)S(1)} %get-tuple-element.178), channel_id=1, source_target_pairs={{0,4},{1,5},{2,6},{3,7},{4,0},{5,1},{6,2},{7,3},{8,12},{9,13},{10,... | collective-permute-start | bytes 1572872 | tf_op jit(solution)/shard_map/ppermute | solution.py:50
  432.4 44.0 %collective-permute-start.57 = (bf16[128,2048]{1,0:T(8,128)(2,1)S(1)}, bf16[128,2048]{1,0:T(8,128)(2,1)S(1)}, u32[]{:S(2)}, u32[]{:S(2)}) collective-permute-start(bf16[128,2048]{1,0:T(8,128)(2,1)S(1)} %get-tuple-element.182), channel_id=1, source_target_pairs={{0,12},{1,13},{2,14},{3,15},{4,8},{5,9},{6,10},{7,11},{8,4},{9,5},... | collective-permute-start | bytes 1572872 | tf_op jit(solution)/shard_map/ppermute | solution.py:50
  453.3 23.1 %collective-permute-start.56 = (bf16[128,2048]{1,0:T(8,128)(2,1)S(1)}, bf16[128,2048]{1,0:T(8,128)(2,1)S(1)}, u32[]{:S(2)}, u32[]{:S(2)}) collective-permute-start(bf16[128,2048]{1,0:T(8,128)(2,1)S(1)} %get-tuple-element.183), channel_id=1, source_target_pairs={{0,8},{1,9},{2,10},{3,11},{4,12},{5,13},{6,14},{7,15},{8,0},{9,1},... | collective-permute-start | bytes 1572872 | tf_op jit(solution)/shard_map/ppermute | solution.py:50
  456.6 18.7 %collective-permute-start.79 = (bf16[8,64,768]{2,1,0:T(8,128)(2,1)S(1)}, bf16[8,64,768]{2,1,0:T(8,128)(2,1)S(1)}, u32[]{:S(2)}, u32[]{:S(2)}) collective-permute-start(bf16[8,64,768]{2,1,0:T(8,128)(2,1)S(1)} %dynamic-slice_bitcast_fusion.3), channel_id=1, source_target_pairs={{0,2},{1,3},{2,0},{3,1},{4,6},{5,7},{6,4},{7,5},{8,10},{9,11},{10,... | collective-permute-start | bytes 2359304 | tf_op jit(solution)/shard_map/ppermute | solution.py:50
  457.9 23.8 %collective-permute-start.61 = (bf16[128,2048]{1,0:T(8,128)(2,1)S(1)}, bf16[128,2048]{1,0:T(8,128)(2,1)S(1)}, u32[]{:S(2)}, u32[]{:S(2)}) collective-permute-start(bf16[128,2048]{1,0:T(8,128)(2,1)S(1)} %add_convert_fusion.4), channel_id=1, source_target_pairs={{0,16},{1,17},{2,18},{3,19},{4,20},{5,21},{6,22},{7,23},{8,24},{9,... | collective-permute-start | bytes 1572872 | tf_op jit(solution)/shard_map/ppermute | solution.py:50
  475.2 43.5 %collective-permute-start.86 = (bf16[2,192,2048]{2,1,0:T(8,128)(2,1)}, bf16[2,192,2048]{2,1,0:T(8,128)(2,1)}, u32[]{:S(2)}, u32[]{:S(2)}) collective-permute-start(bf16[2,192,2048]{2,1,0:T(8,128)(2,1)} %dynamic-slice_bitcast_fusion), channel_id=1, source_target_pairs={{0,1},{1,0},{2,3},{3,2},{4,5},{5,4},{6,7},{7,6},{8,9},{9,8},{10,11... | collective-permute-start | bytes 4718600 | tf_op jit(solution)/shard_map/ppermute | solution.py:50
  475.2 20.0 %collective-permute-start.80 = (bf16[192,2048]{1,0:T(8,128)(2,1)S(1)}, bf16[192,2048]{1,0:T(8,128)(2,1)S(1)}, u32[]{:S(2)}, u32[]{:S(2)}) collective-permute-start(bf16[192,2048]{1,0:T(8,128)(2,1)S(1)} %dynamic-slice_bitcast_fusion.4), channel_id=1, source_target_pairs={{0,2},{1,3},{2,0},{3,1},{4,6},{5,7},{6,4},{7,5},{8,10},{9,11},{10,... | collective-permute-start | bytes 2359304 | tf_op jit(solution)/shard_map/ppermute | solution.py:50
  498.9 20.6 %collective-permute-start.95 = (bf16[64,768]{1,0:T(8,128)(2,1)}, bf16[64,768]{1,0:T(8,128)(2,1)}, u32[]{:S(2)}, u32[]{:S(2)}) collective-permute-start(bf16[64,768]{1,0:T(8,128)(2,1)} %get-tuple-element.200), channel_id=1, source_target_pairs={{0,28},{1,29},{2,30},{3,31},{4,24},{5,25},{6,26},{7,27},{8,20},{9,... | collective-permute-start | bytes 294920 | tf_op jit(solution)/shard_map/ppermute | solution.py:50
  502.7 20.2 %collective-permute-start.94 = (bf16[64,768]{1,0:T(8,128)(2,1)S(1)}, bf16[64,768]{1,0:T(8,128)(2,1)S(1)}, u32[]{:S(2)}, u32[]{:S(2)}) collective-permute-start(bf16[64,768]{1,0:T(8,128)(2,1)S(1)} %get-tuple-element.201), channel_id=1, source_target_pairs={{0,24},{1,25},{2,26},{3,27},{4,28},{5,29},{6,30},{7,31},{8,16},{9,... | collective-permute-start | bytes 294920 | tf_op jit(solution)/shard_map/ppermute | solution.py:50
  518.7 62.8 %collective-permute-start.83 = (bf16[64,2048]{1,0:T(8,128)(2,1)}, bf16[64,2048]{1,0:T(8,128)(2,1)}, u32[]{:S(2)}, u32[]{:S(2)}) collective-permute-start(bf16[64,2048]{1,0:T(8,128)(2,1)} %slice.316), channel_id=1, source_target_pairs={{0,4},{1,5},{2,6},{3,7},{4,0},{5,1},{6,2},{7,3},{8,12},{9,13},{10,... | collective-permute-start | bytes 786440 | tf_op jit(solution)/shard_map/ppermute | solution.py:50
  519.5 62.0 %collective-permute-start.84 = (bf16[64,2048]{1,0:T(8,128)(2,1)}, bf16[64,2048]{1,0:T(8,128)(2,1)}, u32[]{:S(2)}, u32[]{:S(2)}) collective-permute-start(bf16[64,2048]{1,0:T(8,128)(2,1)} %slice.317), channel_id=1, source_target_pairs={{0,8},{1,9},{2,10},{3,11},{4,12},{5,13},{6,14},{7,15},{8,0},{9,1},... | collective-permute-start | bytes 786440 | tf_op jit(solution)/shard_map/ppermute | solution.py:50
  580.1 28.7 %collective-permute-start.87 = (bf16[192,2048]{1,0:T(8,128)(2,1)S(1)}, bf16[192,2048]{1,0:T(8,128)(2,1)S(1)}, u32[]{:S(2)}, u32[]{:S(2)}) collective-permute-start(bf16[192,2048]{1,0:T(8,128)(2,1)S(1)} %copy-done.45), channel_id=1, source_target_pairs={{0,2},{1,3},{2,0},{3,1},{4,6},{5,7},{6,4},{7,5},{8,10},{9,11},{10,... | collective-permute-start | bytes 2359304 | tf_op jit(solution)/shard_map/ppermute | solution.py:50
  606.0 66.2 %collective-permute-start.108 = (bf16[2,2,80,2048]{3,2,0,1:T(8,128)(2,1)}, bf16[2,2,80,2048]{3,2,0,1:T(8,128)(2,1)}, u32[]{:S(2)}, u32[]{:S(2)}) collective-permute-start(bf16[2,2,80,2048]{3,2,0,1:T(8,128)(2,1)} %bitcast.349), channel_id=1, source_target_pairs={{0,1},{1,0},{2,3},{3,2},{4,5},{5,4},{6,7},{7,6},{8,9},{9,8},{10,11... | collective-permute-start | bytes 3932168 | tf_op jit(solution)/shard_map/ppermute | solution.py:50
  628.8 39.9 %collective-permute-start.96 = (bf16[2,4,2,64,640]{4,3,1,0,2:T(8,128)(2,1)}, bf16[2,4,2,64,640]{4,3,1,0,2:T(8,128)(2,1)}, u32[]{:S(2)}, u32[]{:S(2)}) collective-permute-start(bf16[2,4,2,64,640]{4,3,1,0,2:T(8,128)(2,1)} %bitcast.350), channel_id=1, source_target_pairs={{0,1},{1,0},{2,3},{3,2},{4,5},{5,4},{6,7},{7,6},{8,9},{9,8},{10,11... | collective-permute-start | bytes 3932168 | tf_op jit(solution)/shard_map/ppermute | solution.py:50
  654.9 33.3 %collective-permute-start.111 = (bf16[2,2,80,2048]{3,2,0,1:T(8,128)(2,1)}, bf16[2,2,80,2048]{3,2,0,1:T(8,128)(2,1)}, u32[]{:S(2)}, u32[]{:S(2)}) collective-permute-start(bf16[2,2,80,2048]{3,2,0,1:T(8,128)(2,1)} %bitcast.348), channel_id=1, source_target_pairs={{0,1},{1,0},{2,3},{3,2},{4,5},{5,4},{6,7},{7,6},{8,9},{9,8},{10,11... | collective-permute-start | bytes 3932168 | tf_op jit(solution)/shard_map/ppermute | solution.py:50
  691.1 43.2 %collective-permute-start.109 = (bf16[2,80,2048]{2,1,0:T(8,128)(2,1)}, bf16[2,80,2048]{2,1,0:T(8,128)(2,1)}, u32[]{:S(2)}, u32[]{:S(2)}) collective-permute-start(bf16[2,80,2048]{2,1,0:T(8,128)(2,1)} %dynamic-slice_bitcast_fusion.6), channel_id=1, source_target_pairs={{0,2},{1,3},{2,0},{3,1},{4,6},{5,7},{6,4},{7,5},{8,10},{9,11},{10,... | collective-permute-start | bytes 1966088 | tf_op jit(solution)/shard_map/ppermute | solution.py:50
  700.1 24.8 %collective-permute-start.119 = (bf16[64,640]{1,0:T(8,128)(2,1)}, bf16[64,640]{1,0:T(8,128)(2,1)}, u32[]{:S(2)}, u32[]{:S(2)}) collective-permute-start(bf16[64,640]{1,0:T(8,128)(2,1)} %get-tuple-element.222), channel_id=1, source_target_pairs={{0,12},{1,13},{2,14},{3,15},{4,8},{5,9},{6,10},{7,11},{8,4},{9,5},... | collective-permute-start | bytes 245768 | tf_op jit(solution)/shard_map/ppermute | solution.py:50
  706.1 34.3 %collective-permute-start.99 = (bf16[128,2048]{1,0:T(8,128)(2,1)}, bf16[128,2048]{1,0:T(8,128)(2,1)}, u32[]{:S(2)}, u32[]{:S(2)}) collective-permute-start(bf16[128,2048]{1,0:T(8,128)(2,1)} %get-tuple-element.192), channel_id=1, source_target_pairs={{0,4},{1,5},{2,6},{3,7},{4,0},{5,1},{6,2},{7,3},{8,12},{9,13},{10,... | collective-permute-start | bytes 1572872 | tf_op jit(solution)/shard_map/ppermute | solution.py:50
  710.7 29.7 %collective-permute-start.101 = (bf16[128,2048]{1,0:T(8,128)(2,1)}, bf16[128,2048]{1,0:T(8,128)(2,1)}, u32[]{:S(2)}, u32[]{:S(2)}) collective-permute-start(bf16[128,2048]{1,0:T(8,128)(2,1)} %get-tuple-element.193), channel_id=1, source_target_pairs={{0,12},{1,13},{2,14},{3,15},{4,8},{5,9},{6,10},{7,11},{8,4},{9,5},... | collective-permute-start | bytes 1572872 | tf_op jit(solution)/shard_map/ppermute | solution.py:50
  719.3 21.2 %collective-permute-start.100 = (bf16[128,2048]{1,0:T(8,128)(2,1)}, bf16[128,2048]{1,0:T(8,128)(2,1)}, u32[]{:S(2)}, u32[]{:S(2)}) collective-permute-start(bf16[128,2048]{1,0:T(8,128)(2,1)} %get-tuple-element.194), channel_id=1, source_target_pairs={{0,8},{1,9},{2,10},{3,11},{4,12},{5,13},{6,14},{7,15},{8,0},{9,1},... | collective-permute-start | bytes 1572872 | tf_op jit(solution)/shard_map/ppermute | solution.py:50
  (160 other events, 2267.1 us)

commit v3 on v2

--- a/solution.py
+++ b/solution.py
@@ -1,4 +1,5 @@
 import functools
+import math
 
 import jax
 import jax.numpy as jnp
@@ -45,6 +46,10 @@
     return lax.optimization_barrier((value,) + others)[0]
 
 
+def fence_all(values, *others):
+    return list(lax.optimization_barrier(tuple(values) + others)[: len(values)])
+
+
 def trade(value, mask):
     count = lax.axis_size("seq") * lax.axis_size("fsdp")
     return lax.ppermute(value, AXES, [(i, i ^ mask) for i in range(count)])
@@ -71,11 +76,16 @@
     return lax.dynamic_update_index_in_dim(buffer, part, index, axis)
 
 
-def gather_units(own, bits, send):
-    units = [(0, own)]
+def gather_units(owns, bits, send):
+    lists = [[(0, own)] for own in owns]
     for b in bits:
-        units += [(mask | b, send(unit, b)) for mask, unit in units]
-    return units
+        fresh = [[] for _ in owns]
+        for k in range(len(lists[0])):
+            for units, new in zip(lists, fresh):
+                mask, unit = units[k]
+                new.append((mask | b, send(unit, b)))
+        lists = [units + new for units, new in zip(lists, fresh)]
+    return lists
 
 
 def copy_kernel(count, shapes, places, scalars, *refs):
@@ -102,18 +112,10 @@
         out_specs=[pl.BlockSpec(memory_space=pltpu.VMEM)] * len(shapes),
         scratch_shapes=[pltpu.SemaphoreType.DMA((copies,))],
         compiler_params=pltpu.CompilerParams(vmem_limit_bytes=VMEM_BYTES),
+        cost_estimate=pl.CostEstimate(
+            flops=0, bytes_accessed=4 * sum(piece.size for piece in pieces), transcendentals=0
+        ),
     )(me.astype(jnp.int32).reshape(1), *pieces)
-
-
-def stack_pieces(pieces, me):
-    (whole,) = assemble(
-        pieces,
-        [(len(pieces),) + pieces[0].shape],
-        lambda i, at: [(None, 0, i)],
-        me,
-        len(pieces),
-    )
-    return whole
 
 
 def halves(value, axis, bit, me):
@@ -121,47 +123,108 @@
     return pick(value, 1 - mine, axis), pick(value, mine, axis)
 
 
-def scatter_bits(value, axes, bits, me, send):
-    for k, (b, axis) in enumerate(zip(bits, axes)):
-        away, kept = halves(value, axis, b, me)
-        value = kept.astype(F32) + send(away.astype(BF16), b).astype(F32)
-        if k < len(bits) - 1:
-            value = value.astype(BF16)
-    return value
+class Reduction:
+    def __init__(self, value, axes, bits, me):
+        self.kept, self.got, self.me = value, None, me
+        self.left = list(zip(axes, bits))
+
+    def send(self, *after):
+        value = self.total(*after).astype(BF16)
+        axis, bit = self.left.pop()
+        away, self.kept = halves(value, axis, bit, self.me)
+        self.got = trade(away, bit)
+        return away
+
+    def send_to(self, count, *after):
+        while len(self.left) > count:
+            away = self.send(*after)
+        return away
+
+    def total(self, *after):
+        if self.got is None:
+            return self.kept
+        return self.kept.astype(F32) + fence(self.got, *after).astype(F32)
+
+
+def reduce_rows(whole, bits, me):
+    whole = whole.astype(BF16).reshape((2,) * len(bits) + (whole.shape[0] >> len(bits), -1))
+    return Reduction(whole, range(len(bits)), bits, me)
+
+
+def reduce_columns(whole, bits, ranks, low, me):
+    above = sum(b > low for b in bits)
+    split = (2,) * above + (ranks,) + (2,) * (len(bits) - above)
+    rows = whole.shape[0] // (ranks << len(bits))
+    whole = whole.astype(BF16).reshape(split + (rows, whole.shape[1]))
+    return Reduction(whole, [k if b > low else k + 1 for k, b in enumerate(bits)], bits, me)
 
 
 def share_list(own, low):
     half = own.shape[-2] // 2
     one, two = trade(own, low), trade(own, 2 * low)
     three = (trade(two[..., :half, :], low), trade(one[..., half:, :], 2 * low))
-    return [own, one, two, three]
-
-
-def place_tokens(lists, me):
-    rows, width = lists[0][0].shape
-    pieces, spots = [], []
-    for k, units in enumerate(lists):
-        for j, unit in enumerate(units[:3]):
-            pieces.append(unit)
-            spots.append(pl.ds((4 * k + j) * rows, rows))
-        for i, unit in enumerate(units[3]):
-            pieces.append(unit)
-            spots.append(pl.ds((4 * k + 3) * rows + i * (rows // 2), rows // 2))
-    (whole,) = assemble(
-        pieces,
-        [(4 * len(lists) * rows, width)],
-        lambda i, at: [(None, 0, spots[i])],
-        me,
-        len(pieces),
-    )
+    return [own, one, two, *three]
+
+
+def share_direct(own, low):
+    return [own] + [trade(own, j * low) for j in (1, 2, 3)]
+
+
+def place_tokens(units, low, me):
+    rows, width = units[0].shape
+    pieces = list(units)
+
+    def places(i, at):
+        slot = jnp.bitwise_xor(number_of(at, (2 * low, low)), min(i, 3))
+        start = pl.multiple_of(slot * rows + (rows // 2 if i == 4 else 0), rows // 2)
+        return [(None, 0, pl.ds(start, pieces[i].shape[0]))]
+
+    (whole,) = assemble(pieces, [(4 * rows, width)], places, me, len(pieces))
     return whole
 
 
-def sum_tokens(partial, low):
-    total = partial[0].astype(F32)
-    for j in (1, 2, 3):
-        total = total + trade(partial[j], j * low).astype(F32)
-    return total
+def groups_of(bits, count):
+    inside = [0]
+    for b in bits:
+        inside = [i | k for i in inside for k in (0, b)]
+    return [[first | i for i in inside] for first in range(count) if not first & sum(bits)]
+
+
+def line_of(bits):
+    fsdp_count, count = lax.axis_size("fsdp"), lax.axis_size("seq") * lax.axis_size("fsdp")
+    if sum(bits) == fsdp_count - 1:
+        return {"axis_name": "fsdp"}
+    if sum(bits) == count - 1:
+        return {"axis_name": AXES}
+    return {"axis_name": AXES, "axis_index_groups": groups_of(bits, count)}
+
+
+def gather_along(own, bits, axis):
+    return lax.all_gather(own, axis=axis, tiled=True, **line_of(bits))
+
+
+def scatter_along(partial, bits, axis):
+    return lax.psum_scatter(partial, scatter_dimension=axis, tiled=True, **line_of(bits))
+
+
+def pair_up(own, bits, me, *pins):
+    value = own
+    for i, b in enumerate(bits):
+        got = fence(trade(value, b), *pins)
+        mine = bit_of(me, b) == 0
+        value = jnp.stack([jnp.where(mine, value, got), jnp.where(mine, got, value)], axis=i)
+    return value.reshape((1 << len(bits),) + own.shape)
+
+
+def exchange(parts, step):
+    ranks, count = parts.shape[0], lax.axis_size("seq")
+    inside = [r * step for r in range(ranks)]
+    groups = [[b + i for i in inside] for b in range(count) if not b & ((ranks - 1) * step)]
+    return lax.all_to_all(parts, "seq", 0, 0, axis_index_groups=groups, tiled=True)
+
+
+def sum_tokens(partial, step):
+    return jnp.sum(exchange(partial, step).astype(F32), axis=0)
 
 
 def project(left, weight):
@@ -188,7 +251,9 @@
     return act, slope
 
 
-def call(body, outs, scalars, arrays, scratch=()):
+def call(body, outs, scalars, arrays, scratch=(), passes=1):
+    sizes = [array.size * array.dtype.itemsize for array in arrays]
+    sizes += [math.prod(shape) * jnp.dtype(kind).itemsize for shape, kind in outs]
     return pl.pallas_call(
         body,
         out_shape=[jax.ShapeDtypeStruct(shape, kind) for shape, kind in outs],
@@ -197,6 +262,9 @@
         out_specs=[pl.BlockSpec(memory_space=pltpu.VMEM)] * len(outs),
         scratch_shapes=list(scratch),
         compiler_params=pltpu.CompilerParams(vmem_limit_bytes=VMEM_BYTES),
+        cost_estimate=pl.CostEstimate(
+            flops=0, bytes_accessed=passes * sum(sizes), transcendentals=0
+        ),
     )(scalars, *arrays)
 
 
@@ -266,9 +334,13 @@
     conv, s_out, q_out, prod, part, ends, marks, rate_w, gate_w, pad,
 ):
     count, span, channels = recur.shape
-    for n in range(count):
+
+    def mark(n, carry):
         block = block_number(scalars, n, rows, step)
         marks[n] = sequence_marks(scalars, block, (n % rows, rows), span, total_len)
+        return carry
+
+    lax.fori_loop(0, count, mark, 0)
     for narrow, wide in ((rate_rows, rate_w), (gate_rows, gate_w)):
         wide[...] = (back_project(narrow[...], spread[...]) * diagonal[...].astype(F32)).astype(BF16)
 
@@ -431,6 +503,82 @@
         return carry
 
     lax.fori_loop(0, count, body, 0)
+
+
+def forward_backward_kernel(
+    tokens, cot, gate_w, up_w, down_w, down, grad, hidden, grad_gate, grad_up, down_sum, grad_sum
+):
+    step = pl.program_id(0)
+    gate_val = project(tokens[...], gate_w[...])
+    up_val = project(tokens[...], up_w[...])
+    act, slope = gelu_parts(gate_val)
+    hidden_val = (act * up_val).astype(BF16)
+    hidden[...] = hidden_val
+    grad_hidden = back_project(cot[...], down_w[...])
+    gate_part = (grad_hidden * up_val * slope).astype(BF16)
+    up_part = (grad_hidden * act).astype(BF16)
+    grad_gate[...] = gate_part
+    grad_up[...] = up_part
+
+    @pl.when(step == 0)
+    def _():
+        grad_sum[...] = jnp.zeros(grad_sum.shape, F32)
+        down_sum[...] = jnp.zeros(down_sum.shape, F32)
+
+    grad_sum[...] += back_project(gate_part, gate_w[...]) + back_project(up_part, up_w[...])
+    down_sum[...] += project(hidden_val, down_w[...])
+
+    @pl.when(step == pl.num_programs(0) - 1)
+    def _():
+        grad[...] = grad_sum[...].astype(BF16)
+        down[...] = down_sum[...].astype(BF16)
+
+
+def pack_kernel(taps, bias, rate_bias, gate_bias, decay, gain_one, gain_two, rate_w, gate_w, packed):
+    count, size = rate_w.shape
+    packed[...] = jnp.zeros(packed.shape, F32)
+    packed[:count, :size] = rate_w[...].astype(F32)
+    packed[:count, size : 2 * size] = gate_w[...].astype(F32)
+    first = packed.shape[0] - 16
+    packed[first : first + TAPS, :count] = taps[...].astype(F32).T
+    for i, row in enumerate((bias, rate_bias, gate_bias, decay, gain_one, gain_two)):
+        packed[first + TAPS + i : first + TAPS + i + 1, : row.shape[1]] = row[...].astype(F32)
+
+
+def lay_kernel(ranks, upper, me, *refs):
+    pieces, whole = refs[:-1], refs[-1]
+    for i, piece in enumerate(pieces):
+        rank = jnp.bitwise_xor(me[0], i)
+        size = piece.shape[1] // upper
+        for u in range(upper):
+            start = pl.multiple_of((u * ranks + rank) * size, 128)
+            whole[:, pl.ds(start, size)] = piece[:, u * size : (u + 1) * size].astype(F32)
+
+
+def feed_forward(tokens, cot, gate_w, up_w, down_w):
+    count, width = tokens.shape
+    units = gate_w.shape[0]
+    tile = 256
+    whole = pl.BlockSpec((count, width), lambda i: (0, 0))
+    row_tile = pl.BlockSpec((tile, width), lambda i: (i, 0))
+    column_tile = pl.BlockSpec((count, tile), lambda i: (0, i))
+    return pl.pallas_call(
+        forward_backward_kernel,
+        grid=(units // tile,),
+        out_shape=[jax.ShapeDtypeStruct((count, width), BF16)] * 2
+        + [jax.ShapeDtypeStruct((count, units), BF16)] * 3,
+        in_specs=[whole, whole, row_tile, row_tile, pl.BlockSpec((width, tile), lambda i: (0, i))],
+        out_specs=[whole, whole] + [column_tile] * 3,
+        scratch_shapes=[pltpu.VMEM((count, width), F32)] * 2,
+        compiler_params=pltpu.CompilerParams(
+            dimension_semantics=("arbitrary",), vmem_limit_bytes=VMEM_BYTES
+        ),
+        cost_estimate=pl.CostEstimate(
+            flops=12 * count * width * units,
+            bytes_accessed=2 * (4 * count * width + 3 * width * units + 3 * count * units),
+            transcendentals=count * units,
+        ),
+    )(tokens, cot, gate_w, up_w, down_w)
 
 
 def shards(
@@ -456,6 +604,7 @@
     rows, span, width = block_input.shape
     tokens = rows * span
     seq_count, fsdp_count = lax.axis_size("seq"), lax.axis_size("fsdp")
+    device_count = seq_count * fsdp_count
     channel_rows = branch_weight.shape[0]
     hidden_rows = gate_weight.shape[0]
     out_rows = mixer_weight.shape[0]
@@ -470,7 +619,7 @@
     step = low // fsdp_count
     me = linear_index().astype(jnp.int32)
     seq_index = lax.axis_index("seq")
-    tp_index, wide_index = number_of(me, tp), number_of(me, tp_wide)
+    tp_index = number_of(me, tp)
     share, share_wide = 1 << len(dp), 1 << len(dp_wide)
     high, deep, high_wide = 1 << len(above), 1 << len(below), 1 << len(above_wide)
     channels = share * channel_rows
@@ -480,64 +629,82 @@
     streams = Streams()
 
     def across_blocks(own):
-        units = sorted(gather_units(own, seq_dp, trade), key=lambda unit: unit[0])
+        units = sorted(gather_units([own], seq_dp, trade)[0], key=lambda unit: unit[0])
         every_slot = jnp.stack([unit for _, unit in units])
         every_slot = every_slot.reshape((-1, step) + own.shape)
         return jnp.moveaxis(every_slot, 2, 1).reshape((seq_count,) + own.shape[1:])
 
-    def slot_places(units, bits, arrays):
+    def place_rows(units):
         def places(i, at):
-            slot = number_of(jnp.bitwise_xor(at, units[i][0]), bits)
-            if arrays == 1:
-                return [(None, 0, slot)]
-            return [(a, a, slot) for a in range(arrays)]
-
-        return places
-
-    def column_places(units, up_bits, down_bits):
+            return [(None, 0, number_of(jnp.bitwise_xor(at, units[i][0]), dp))]
+
+        one = units[0][1].shape
+        pieces = [unit for _, unit in units]
+        (whole,) = assemble(pieces, [(len(units),) + one], places, me, len(units))
+        return whole.reshape(-1, one[1])
+
+    def place_columns(units):
         def places(i, at):
             owner = jnp.bitwise_xor(at, units[i][0])
-            return [(None, 0, (number_of(owner, up_bits), slice(None), number_of(owner, down_bits)))]
-
-        return places
+            return [(None, 0, (number_of(owner, above), slice(None), number_of(owner, below)))]
+
+        ranks, one = units[0][1].shape[0], units[0][1].shape[1:]
+        pieces = [unit for _, unit in units]
+        (whole,) = assemble(pieces, [(high, ranks, deep) + one], places, me, len(units))
+        return whole.reshape(-1, one[1])
 
     def by_rank(weight, upper, ranks):
         split = weight.reshape(weight.shape[0], upper, ranks, -1)
         return jnp.transpose(split, (2, 0, 1, 3)).reshape(ranks, weight.shape[0], -1)
 
-    def swap_ranks(parts, index, bits):
-        masks = [sum(b for k, b in enumerate(reversed(bits)) if j >> k & 1) for j in range(len(parts))]
-        sent = [pick(parts, jnp.bitwise_xor(index, j), 0) for j in range(len(parts))]
-        return [trade(part, mask) if mask else part for part, mask in zip(sent, masks)]
-
     input_own = block_input.reshape(tokens, width)
     cot_own = cotangent.reshape(tokens, width)
-    input_all = place_tokens([share_list(input_own, low)], me)
-
-    gain_columns = jnp.stack([mixer_gain, mlp_gain], axis=1)
-    gain_columns = jnp.pad(gain_columns, ((0, channel_rows - out_rows), (0, 0)))
-    small = jnp.concatenate(
-        [
-            conv_kernel,
-            jnp.stack([conv_bias, recur_gate_bias, input_gate_bias, decay_param], axis=1),
-            gain_columns,
-            recur_gate_weight,
-            input_gate_weight,
-        ],
-        axis=1,
-    )
+    packed_width = -(-(2 * block_size + 8) // 128) * 128
+    extra = -(-channel_rows // 16) * 16
+    small = pl.pallas_call(
+        pack_kernel,
+        out_shape=jax.ShapeDtypeStruct((extra + 16, packed_width), F32),
+        compiler_params=pltpu.CompilerParams(vmem_limit_bytes=VMEM_BYTES),
+    )(
+        conv_kernel,
+        *(v[None] for v in (conv_bias, recur_gate_bias, input_gate_bias, decay_param)),
+        mixer_gain[None],
+        mlp_gain[None],
+        recur_gate_weight,
+        input_gate_weight,
+    ).astype(BF16)
+    one = small.shape
     for i, b in enumerate(dp):
         got = trade(small, b)
+        if i == 0:
+            first_got = got
         mine = bit_of(me, b) == 0
         small = jnp.stack([jnp.where(mine, small, got), jnp.where(mine, got, small)], axis=i)
-    small = small.reshape((share,) + small.shape[len(dp) :])
-    gains = jnp.moveaxis(small[:, :out_rows, 8:10], 2, 0)
-    gains = jnp.stack([gains] + [trade(gains, j * low) for j in (1, 2, 3)])
-    gains = jnp.take(gains, jnp.bitwise_xor(tp_index, jnp.arange(4)), axis=0)
-    gains = gains.reshape(4, 2, high, deep, out_rows).transpose(1, 2, 0, 3, 4).reshape(2, width)
+    small = small.reshape((share,) + one)
+    gains = small[:, extra + TAPS + 4 : extra + TAPS + 6, :out_rows].reshape(high, deep, 2, out_rows)
+    for i, b in enumerate(tp):
+        got = trade(gains, b)
+        mine = bit_of(me, b) == 0
+        gains = jnp.stack([jnp.where(mine, gains, got), jnp.where(mine, got, gains)], axis=i + 1)
+    last_got = got
+    gains = jnp.moveaxis(gains, 4, 0).reshape(2, width)
     gain_one, gain_two = gains[0].astype(F32), gains[1].astype(F32)
-    small = small.reshape(channels, -1)
-    coef = small[:, :8].astype(F32).T
+    numbers = jnp.moveaxis(small[:, extra : extra + TAPS + 4, :channel_rows], 1, 0)
+    numbers = numbers.reshape(TAPS + 4, channels).astype(F32)
+    gate_rows = small[:, :channel_rows, : 2 * block_size].reshape(channels, -1)
+
+    input_list = share_list(input_own, low)
+    recur_units, branch_units = gather_units(
+        [fence(recur_weight, first_got), branch_weight], dp, streams.trade
+    )
+    input_all = place_tokens(input_list, low, me)
+    piece = exchange(fence(by_rank(mixer_weight, high, 4), *input_list[1:]), step)
+    (mixer_units,) = gather_units([piece], dp, streams.trade)
+    recur_q, branch_q = place_rows(recur_units), place_rows(branch_units)
+    mixer_q = place_columns(mixer_units)
+    cot_near_list = share_direct(fence(cot_own, input_all), low)
+
+    coef = numbers
     decay_vec = coef[7:]
     coef = jnp.concatenate(
         [
@@ -547,67 +714,33 @@
             jnp.zeros((7, channels), F32),
         ]
     )
-    rate_rows, gate_rows = small[:, 10 : 10 + block_size], small[:, 10 + block_size :]
+    rate_rows, gate_rows = gate_rows[:, :block_size], gate_rows[:, block_size:]
     number = np.arange(channels)
     spread = jnp.asarray(number[None] % block_size == np.arange(block_size)[:, None], BF16)
     diagonal = jnp.asarray(number[None] // block_size == number[:, None] // block_size, BF16)
     eye = jnp.asarray(np.eye(channels), BF16)
-    packed_width = -(-(2 * block_size + 8) // 128) * 128
     collect = np.zeros((channels, 3, packed_width))
     collect[number, 0, number % block_size] = 1
     collect[number, 1, block_size + number % block_size] = 1
     collect[np.arange(8), 2, 2 * block_size + np.arange(8)] = 1
     collect = jnp.asarray(collect.reshape(channels, -1), BF16)
     lengths = lax.dynamic_slice_in_dim(seq_lengths, lax.axis_index("fsdp") * rows, rows, 0)
-    scalars = jnp.concatenate([seq_index.astype(jnp.int32)[None], lengths.reshape(-1)])
-
-    units = gather_units(jnp.stack([branch_weight, recur_weight]), dp, streams.trade)
-    branch_q, recur_q = assemble(
-        [unit for _, unit in units],
-        [(share, channel_rows, width)] * 2,
-        slot_places(units, dp, 2),
-        me,
-        2 * share,
-    )
-    branch_q, recur_q = branch_q.reshape(channels, width), recur_q.reshape(channels, width)
-    mixer_weight = fence(mixer_weight, input_all)
-    pieces = swap_ranks(by_rank(mixer_weight, high, 4), tp_index, tp)
-    (piece,) = assemble(
-        pieces,
-        [(4,) + pieces[0].shape],
-        lambda i, at: [(None, 0, jnp.bitwise_xor(number_of(at, tp), i))],
-        me,
-        4,
-    )
-    units = gather_units(piece, dp, streams.trade)
-    (mixer_q,) = assemble(
-        [unit for _, unit in units],
-        [(high, 4, deep, out_rows, channels)],
-        column_places(units, above, below),
-        me,
-        share,
-    )
-    mixer_q = mixer_q.reshape(width, channels)
-
-    cot_far = streams.trade(cot_own, wide)
-    cot_lists = [share_list(cot_own, low), share_list(cot_far, low)]
-
-    units = gather_units(jnp.stack([gate_weight, up_weight]), dp_wide, streams.trade)
-    gate_q, up_q = assemble(
-        [unit for _, unit in units],
-        [(share_wide, hidden_rows, width)] * 2,
-        slot_places(units, dp_wide, 2),
-        me,
-        2 * share_wide,
-    )
-    gate_q, up_q = gate_q.reshape(hidden, width), up_q.reshape(hidden, width)
+    base = seq_index.astype(jnp.int32) - tp_index * step
+    scalars = jnp.concatenate([base[None], lengths.reshape(-1)])
+
+    def join_ranks(parts, upper):
+        got = exchange(parts, step)
+        got = got.reshape(got.shape[:2] + (upper, -1))
+        return jnp.transpose(got, (1, 2, 0, 3)).reshape(got.shape[1], -1).astype(F32)
 
     scale_one = inverse_rms(input_all.astype(F32))
     normed = (input_all.astype(F32) * scale_one * gain_one).astype(BF16)
-    recur_in = project(normed, recur_q).astype(BF16).reshape(blocks, span, channels)
-    edge = recur_in[:, span - 4 :].reshape(4, rows, 4, channels)
-    halo = across_blocks(edge).astype(F32).reshape(seq_count * rows, 4, channels)
-    branch = project(normed, branch_q).reshape(blocks, span, channels)
+    recur_in = project(normed, recur_q).astype(BF16)
+    edge = recur_in.reshape(blocks, span, channels)[:, span - 4 :].reshape(4, rows, 4, channels)
+    halo = across_blocks(edge)
+    cot_far = trade(fence(cot_own, halo), wide)
+    halo = halo.astype(F32).reshape(seq_count * rows, 4, channels)
+    recur_in = recur_in.reshape(blocks, span, channels)
     shape = (blocks, span, channels)
     one = (blocks, 1, channels)
     everything = (seq_count * rows, 1, channels)
@@ -620,111 +753,98 @@
         scalars,
         [recur_in, halo, coef, rate_rows, gate_rows, spread, diagonal],
         [pltpu.VMEM(padded, F32)],
-    )
-    ends = across_blocks(ends.reshape(4, rows, 2, channels)).reshape(-1, 2, channels)
+        4,
+    )
+    ends_all = across_blocks(ends.reshape(4, rows, 2, channels)).reshape(-1, 2, channels)
+    branch = project(normed, fence(branch_q, ends)).reshape(blocks, span, channels)
+    ends = fence(ends_all, branch)
     state, mixed, came = call(
         functools.partial(state_kernel, rows, step),
         [(shape, F32), (shape, BF16), (one, F32)],
         scalars,
         [prod, part, ends, branch],
         [pltpu.VMEM(everything, F32)],
-    )
+        2,
+    )
+    cot_far_list = share_direct(fence(cot_far, mixed), low)
+    down_piece = exchange(fence(by_rank(down_weight, high_wide, 8), mixed), step)
+    gate_pair, up_pair, down_pair = (
+        pair_up(fence(weight, recur_q), above_wide, me)
+        for weight in (gate_weight, up_weight, down_piece)
+    )
+    gate_q = gather_along(gate_pair, below, 1).reshape(hidden, width)
+    up_q = gather_along(up_pair, below, 1).reshape(hidden, width)
+    down_q = gather_along(down_pair, below, 2).reshape(width, hidden)
     mixed_flat = mixed.reshape(4 * tokens, channels)
+    cot_near = place_tokens(fence_all(cot_near_list, mixed), low, me)
     mixer_part = project(mixed_flat, mixer_q).astype(BF16).reshape(4, tokens, width)
-    residual = input_own.astype(F32) + sum_tokens(mixer_part, low)
-
-    down_weight = fence(down_weight, mixed)
-    pieces = swap_ranks(by_rank(down_weight, high_wide, 8), wide_index, tp_wide)
-    (piece,) = assemble(
-        pieces,
-        [(8,) + pieces[0].shape],
-        lambda i, at: [(None, 0, jnp.bitwise_xor(number_of(at, tp_wide), i))],
-        me,
-        8,
-    )
-    units = gather_units(piece, dp_wide, streams.trade)
-    (down_q,) = assemble(
-        [unit for _, unit in units],
-        [(high_wide, 8, deep, out_rows, hidden)],
-        column_places(units, above_wide, below),
-        me,
-        share_wide,
-    )
-    down_q = down_q.reshape(width, hidden)
+    residual = input_own.astype(F32) + sum_tokens(mixer_part, step)
+
 
     scale_two = inverse_rms(residual)
     unit_two = residual * scale_two
     normed_own = (unit_two * gain_two).astype(BF16)
-    normed_far = streams.trade(normed_own, wide)
-    normed_two = place_tokens([share_list(normed_own, low), share_list(normed_far, low)], me)
-    cot_all = place_tokens(cot_lists, me)
-    gate_val = project(normed_two, gate_q)
-    up_val = project(normed_two, up_q)
-    act, slope = gelu_parts(gate_val)
-    hidden_val = (act * up_val).astype(BF16)
-    grad_hidden = back_project(cot_all, down_q)
-    grad_gate = (grad_hidden * up_val * slope).astype(BF16)
-    grad_up = (grad_hidden * act).astype(BF16)
-    grad_two_part = (back_project(grad_gate, gate_q) + back_project(grad_up, up_q)).astype(BF16)
-    grad_two_part = grad_two_part.reshape(2, 4, tokens, width)
-    grad_two_far = sum_tokens(grad_two_part[1], low).astype(BF16)
-    grad_two = sum_tokens(grad_two_part[0], low) + trade(grad_two_far, wide).astype(F32)
-    down_part = project(hidden_val, down_q).astype(BF16).reshape(2, 4, tokens, width)
-    down_far = sum_tokens(down_part[1], low).astype(BF16)
-    down_own = sum_tokens(down_part[0], low) + trade(down_far, wide).astype(F32)
-    block_output = (residual + down_own).astype(BF16)
+    normed_far = trade(normed_own, wide)
+    near_list = share_direct(normed_own, low)
+    far_list = share_direct(fence(normed_far, *near_list[1:]), low)
+    near = place_tokens(near_list, low, me)
+    cot_far = place_tokens(fence_all(cot_far_list, normed_own), low, me)
+    near_out = feed_forward(near, cot_near, gate_q, up_q, down_q)
+    ranks_shape = (4, tokens, width)
+    far = place_tokens(far_list, low, me)
+    far_out = feed_forward(far, cot_far, gate_q, up_q, down_q)
+    grad_far_parts = exchange(far_out[1].reshape(ranks_shape), step)
+
+    def finish(partial, bits):
+        partial = partial.reshape((2,) * len(bits) + partial.shape[1:])
+        grad = Reduction(partial, range(len(bits)), bits, me)
+        if bits:
+            grad.send_to(0)
+        return grad.total()
+
+    def both(one, two, k):
+        return outer(one[k], near) + outer(two[k], far)
+
+    down_grad = outer(cot_near, near_out[2]) + outer(cot_far, far_out[2])
+    down_grad = down_grad.astype(BF16).reshape(high_wide, 8, -1, hidden)
+    grad_far_parts = fence(grad_far_parts, down_grad)
+    down_grad = finish(scatter_along(down_grad, below, 2), above_wide).reshape(8, out_rows, hidden)
+    grad_two_far = jnp.sum(grad_far_parts.astype(F32), axis=0).astype(BF16)
+    grad_two_near = sum_tokens(fence(near_out[1], grad_two_far).reshape(ranks_shape), step)
+    grad_two = grad_two_near + trade(grad_two_far, wide).astype(F32)
     scaled = grad_two * gain_two
     grad_residual = cot_own.astype(F32) + scale_two * (
         scaled - unit_two * jnp.mean(scaled * unit_two, axis=-1, keepdims=True)
     )
     gain_two_part = jnp.sum(grad_two * unit_two, axis=0)
 
-    def row_axes(bits):
-        return list(range(len(bits)))
-
-    def row_grad(grads, values, bits):
-        whole = outer(grads, values).astype(BF16)
-        whole = whole.reshape((2,) * len(bits) + (-1, width))
-        order = tuple(reversed(bits))
-        return scatter_bits(whole, tuple(reversed(row_axes(bits))), order, me, streams.trade)
-
-    def column_grad(grads, values, bits, ranks):
-        up_bits = [b for b in bits if b > low]
-        whole = outer(grads, values).astype(BF16)
-        whole = whole.reshape((2,) * len(up_bits) + (ranks,) + (2,) * (len(bits) - len(up_bits)) + (out_rows, -1))
-        axes = [k if b > low else k + 1 for k, b in enumerate(bits)]
-        order = tuple(reversed(bits))
-        return scatter_bits(whole, tuple(reversed(axes)), order, me, streams.trade).astype(BF16)
-
-    def join_ranks(parts, index, bits, upper):
-        ranks = len(parts)
-        got = swap_ranks(parts, index, bits)
-        count = got[0].shape[0]
-        whole = jnp.zeros((ranks, count, upper, got[0].shape[1] // upper), BF16)
-        for j, part in enumerate(got):
-            whole = put(whole, part.reshape(count, upper, -1), jnp.bitwise_xor(index, j), 0)
-        return jnp.transpose(whole, (1, 2, 0, 3)).reshape(count, -1).astype(F32)
-
-    down_grad = column_grad(cot_all, hidden_val, dp_wide, 8)
-    gate_weight_grad = row_grad(grad_gate, normed_two, dp_wide)
-    up_weight_grad = row_grad(grad_up, normed_two, dp_wide)
-
-    grad_mix_own = fence(grad_residual.astype(BF16), gate_weight_grad, down_grad)
-    grad_mix = place_tokens([share_list(grad_mix_own, low)], me)
+    grad_mix_own = grad_residual.astype(BF16)
+    grad_mix_list = share_list(grad_mix_own, low)
+    late = [fence_all(out[3:], grad_mix_own) for out in (near_out, far_out)]
+    gate_grad = both(*late, 0).astype(BF16).reshape(high_wide, -1, width)
+    up_grad = both(*late, 1).astype(BF16).reshape(high_wide, -1, width)
+    down_far = fence(far_out[0].reshape(ranks_shape), grad_mix_list[1], grad_mix_list[2])
+    down_far = exchange(down_far, step)
+    down_parts = fence(down_grad, grad_mix_own).reshape(2, 4, out_rows, hidden)
+    down_sent, down_kept = halves(down_parts, 0, wide, me)
+    down_got = trade(down_sent, wide)
+    grad_mix = place_tokens(fence_all(grad_mix_list, gate_grad, up_grad, down_got), low, me)
+    gate_grad = finish(scatter_along(gate_grad, below, 1), above_wide)
+    up_grad = finish(scatter_along(up_grad, below, 1), above_wide)
     grad_mixed = back_project(grad_mix, mixer_q).reshape(shape)
-    grad_branch, prod_back, part_back, ends_back = call(
+    grad_branch, prod_back, part_back, own_ends = call(
         adjoint_kernel,
         [(shape, BF16), (shape, F32), (shape, F32), ((blocks, 2, channels), F32)],
         scalars,
         [grad_mixed, state, branch, s_val, marks, coef],
         [pltpu.VMEM(padded, F32)],
-    )
-    ends_back = across_blocks(ends_back.reshape(4, rows, 2, channels)).reshape(-1, 2, channels)
-    ends_back = fence(ends_back, up_weight_grad, block_output)
-    down_weight_grad = join_ranks(down_grad.reshape(8, out_rows, hidden), wide_index, tp_wide, high_wide)
-    mixer_grad = column_grad(grad_mix, mixed_flat, dp, 4)
+        3,
+    )
+    ends_back = across_blocks(own_ends.reshape(4, rows, 2, channels)).reshape(-1, 2, channels)
     grad_branch = grad_branch.reshape(4 * tokens, channels)
-    branch_weight_grad = row_grad(grad_branch, normed, dp)
+    branch_grad = reduce_rows(outer(grad_branch, normed), dp, me)
+    mixer_grad = reduce_columns(outer(fence(grad_mix, own_ends), mixed_flat), dp, 4, low, me)
+    ends_back = fence(ends_back, branch_grad.send(), mixer_grad.send())
     packed_shape = (channels, packed_width)
     grad_conv, edge_back, packed = call(
         functools.partial(gates_kernel, rows, step),
@@ -742,24 +862,38 @@
             pltpu.VMEM(padded, F32),
             pltpu.VMEM(padded, F32),
         ],
+        4,
     )
     edge_back = edge_back.reshape(4, rows, 4, channels)
-    halo_back = across_blocks(edge_back).astype(F32).reshape(seq_count * rows, 4, channels)
-    halo_back = fence(halo_back, down_weight_grad)
+    down_far = jnp.sum(fence(down_far, edge_back).astype(F32), axis=0).astype(BF16)
+    down_far_own = trade(down_far, wide)
+    down_near = fence(near_out[0].reshape(ranks_shape), edge_back)
+    down_near = [pick(down_near, jnp.bitwise_xor(tp_index, j), 0) for j in range(4)]
+    down_near[1:] = [trade(down_near[j], j * low) for j in (1, 2, 3)]
+    halo_back = across_blocks(edge_back)
+    last = len(dp)
+    aways = [grad.send_to(last - 2, edge_back) for grad in (mixer_grad, branch_grad)]
+    halo_back = fence(halo_back, *aways, down_far)
+    halo_back = halo_back.astype(F32).reshape(seq_count * rows, 4, channels)
     (grad_recur,) = call(
         functools.partial(unconvolve_kernel, rows, step, seq_count),
         [(shape, BF16)],
         scalars,
         [grad_conv, halo_back, marks, coef],
         [pltpu.VMEM(padded, F32)],
+        4,
     )
     grad_recur = grad_recur.reshape(4 * tokens, channels)
+    recur_grad = reduce_rows(outer(grad_recur, normed), dp, me)
+    grad_recur = fence(grad_recur, recur_grad.send())
     grad_normed_part = back_project(grad_branch, branch_q) + back_project(grad_recur, recur_q)
     grad_normed_sent = grad_normed_part.astype(BF16)
+    aways = [grad.send_to(0, grad_recur) for grad in (mixer_grad, branch_grad)]
+    aways.append(recur_grad.send_to(last - 2, grad_normed_sent))
+    grad_normed_sent = fence(grad_normed_sent, *aways, down_far_own)
     gain_one_part = jnp.sum(grad_normed_sent.astype(F32) * input_all.astype(F32) * scale_one, axis=0)
-    grad_normed_sent = fence(grad_normed_sent.reshape(4, tokens, width), mixer_grad)
-    grad_normed = sum_tokens(grad_normed_sent, low)
-    own_scale = scale_one[:tokens]
+    grad_normed = sum_tokens(grad_normed_sent.reshape(ranks_shape), step)
+    own_scale = inverse_rms(input_own.astype(F32))
     unit_one = input_own.astype(F32) * own_scale
     scaled_one = grad_normed * gain_one
     input_grad = (
@@ -767,21 +901,38 @@
         + own_scale
         * (scaled_one - unit_one * jnp.mean(scaled_one * unit_one, axis=-1, keepdims=True))
     ).astype(BF16)
-    mixer_weight_grad = join_ranks(mixer_grad.reshape(4, out_rows, channels), tp_index, tp, high)
-    recur_weight_grad = row_grad(grad_recur, normed, dp)
-
-    packed = packed.reshape((2,) * len(dp) + (channel_rows, packed_width))
-    order = tuple(reversed(dp))
-    axes = tuple(reversed(row_axes(dp)))
-    packed = scatter_bits(packed, axes, order, me, trade)
-    gain_parts = jnp.stack([gain_one_part, gain_two_part]).reshape(2, high, 4, deep, -1)
-    gain_parts = gain_parts.transpose(2, 1, 3, 0, 4).reshape(4, share, -1).astype(BF16)
-    gain_sum = pick(gain_parts, tp_index, 0).astype(F32)
-    for j in (1, 2, 3):
-        sent = pick(gain_parts, jnp.bitwise_xor(tp_index, j), 0)
-        gain_sum = gain_sum + trade(sent, j * low).astype(F32)
-    gain_sum = gain_sum.astype(BF16).reshape((2,) * len(dp) + (-1,))
-    gain_grads = scatter_bits(gain_sum, axes, order, me, trade).reshape(2, -1)
+    packed = reduce_rows(fence(packed, grad_normed_sent), dp, me)
+    packed_sent = packed.send_to(last - 2)
+    sent = recur_grad.send_to(0, packed_sent)
+    packed_sent = packed.send_to(0, sent)
+    down_got, down_kept = fence_all([down_got, down_kept], packed_sent)
+    down_pieces = []
+    for j in range(4):
+        peer = jnp.bitwise_xor(tp_index, j)
+        pair = jnp.stack([pick(down_kept, peer, 0), pick(down_got, peer, 0)])
+        down_pieces.append(trade(pair, j * low) if j else pair)
+    down_sum = sum(fence(part, packed_sent).astype(F32) for part in down_near + [down_far_own])
+    block_output = (residual + down_sum).astype(BF16)
+    branch_weight_grad = branch_grad.total(block_output)
+    own_half = number_of(me, (wide,))
+    flat_pieces = [pair[h] for h in range(2) for pair in down_pieces]
+    down_weight_grad = pl.pallas_call(
+        functools.partial(lay_kernel, 8, high_wide),
+        out_shape=jax.ShapeDtypeStruct((out_rows, 8 * hidden), F32),
+        in_specs=[pl.BlockSpec(memory_space=pltpu.SMEM)]
+        + [pl.BlockSpec(memory_space=pltpu.VMEM)] * len(flat_pieces),
+        out_specs=pl.BlockSpec(memory_space=pltpu.VMEM),
+        compiler_params=pltpu.CompilerParams(vmem_limit_bytes=VMEM_BYTES),
+    )((own_half * 4 + tp_index).reshape(1), *flat_pieces)
+    recur_weight_grad = recur_grad.total(branch_weight_grad)
+    packed = packed.total(branch_weight_grad)
+    mixer_grad = mixer_grad.total(branch_weight_grad).astype(BF16).reshape(4, out_rows, channels)
+    mixer_weight_grad = join_ranks(fence(mixer_grad, grad_normed), high)
+
+    gain_parts = jnp.stack([gain_one_part, gain_two_part]).astype(BF16)
+    gain_parts = jnp.moveaxis(gain_parts.reshape(2, device_count, out_rows), 1, 0)
+    gain_parts = lax.all_to_all(fence(gain_parts, grad_normed), AXES, 0, 0, tiled=True)
+    gain_grads = jnp.sum(gain_parts.astype(F32), axis=0)
     numbers = packed[:, 2 * block_size : 2 * block_size + 8]
     return (
         block_output.reshape(rows, span, width),
@@ -798,8 +949,8 @@
         numbers[:, 7],
         mixer_weight_grad,
         gain_grads[1],
-        gate_weight_grad,
-        up_weight_grad,
+        gate_grad.reshape(hidden_rows, width).astype(F32),
+        up_grad.reshape(hidden_rows, width).astype(F32),
         down_weight_grad,
     )
 

time: 783 us -> 696 us (0.89)
  local copies, waits for them, and re-layouts: 125 us -> 44.2 us
  Pallas kernels: 81.1 us -> 122 us
  matrix products: 85.1 us -> 50.2 us
  starting transfers between devices: 140 us -> 114 us
  other arithmetic: 39.2 us -> 52.5 us
  between operations: 2.79 us -> 16 us
  waiting for transfers between devices: 296 us -> 285 us
    ppermute x120 -> x73, waiting for transfers between devices: 296 us -> 220 us  [trade(): return lax.ppermute(value, AXES, [(i, i ^ mask) for i in range(count)])]
    ppermute x120 -> x73, starting transfers between devices: 140 us -> 67.7 us  [trade(): return lax.ppermute(value, AXES, [(i, i ^ mask) for i in range(count)])]
    all_to_all x0 -> x9, waiting for transfers between devices: none -> 64.9 us  [the longest x8 64.9 us: exchange(): lax.all_to_all(parts, 'seq', 0, 0, axis_index_groups=groups, tiled=True)]
    dynamic_update_slice x12 -> x0, local copies, waits for them, and re-layouts: 53.5 us -> none  [put(): return lax.dynamic_update_index_in_dim(buffer, part, index, axis)]
    pallas_call x0 -> x4, Pallas kernels: none -> 47.6 us  [the longest x2 43.5 us: feed_forward(): pl.pallas_call(forward_backward_kernel, grid=(units // tile,), out_shape=...]
    all_to_all x0 -> x9, starting transfers between devices: none -> 45.9 us  [the longest x8 42 us: exchange(): lax.all_to_all(parts, 'seq', 0, 0, axis_index_groups=groups, tiled=True)]
    dot_general x6 -> x3, matrix products: 36.8 us -> 8.11 us  [back_project(): lax.dot_general(left, weight, (((1,), (0,)), ((), ())), preferred_element...]
    broadcast_in_dim x14 -> x0, local copies, waits for them, and re-layouts: 17.9 us -> none  [the longest x12 16.8 us: put(): return lax.dynamic_update_index_in_dim(buffer, part, index, axis)]
  transfers between devices with their start and end apart: 120 -> 88, of which waited for: 48 -> 36; matrix products, arithmetic and copies ran while one was open for 25% -> 19% of each run, Pallas kernels for 10% -> 17%
where the time goes in v3:
time: 696 us; the launch traced here: 684 us
  waiting for transfers between devices  285 us (41%)
  Pallas kernels  122 us (18%)
  starting transfers between devices  114 us (16%)
  other arithmetic  52.5 us (8%)
  matrix products  50.2 us (7%)
  local copies, waits for them, and re-layouts  44.2 us (6%)
  between operations  16 us (2%)
    ppermute x73, waiting for transfers between devices, trade(): return lax.ppermute(value, AXES, [(i, i ^ mask) for i in range(count)])  220 us
    ppermute x73, starting transfers between devices, trade(): return lax.ppermute(value, AXES, [(i, i ^ mask) for i in range(count)])  67.7 us
    all_to_all x8, waiting for transfers between devices, exchange(): lax.all_to_all(parts, 'seq', 0, 0, axis_index_groups=groups, tiled=True)  64.9 us
    pallas_call x5, Pallas kernels, call(): pl.pallas_call(body, out_shape=[jax.ShapeDtypeStruct(shape, kind) for sha...  46.5 us
    pallas_call x2, Pallas kernels, feed_forward(): pl.pallas_call(forward_backward_kernel, grid=(units // tile,), out_shape=...  43.5 us
    all_to_all x8, starting transfers between devices, exchange(): lax.all_to_all(parts, 'seq', 0, 0, axis_index_groups=groups, tiled=True)  42 us
    dot_general x9, matrix products, outer(): lax.dot_general(grads, values, (((0,), (0,)), ((), ())), preferred_elemen...  28.3 us
    pallas_call x9, Pallas kernels, assemble(): pl.pallas_call(functools.partial(copy_kernel, len(pieces), shapes, places...  27.4 us
  transfers between devices with their start and end apart: 88, of which 36 were waited for; matrix products, arithmetic and copies ran while one was open for 19% of the time, Pallas kernels for 17%

profile of v3, /device:TPU:20, one launch (start us, length us, event | category | flops | bytes accessed | tf_op | source)
XLA Modules:
  0.0 684.0 jit_solution(14600879339798435162)
XLA Ops:
  11.6 4.9 collective-permute-done.4
  19.8 5.3 collective-permute-done.10.refs_2_
  26.6 4.7 collective-permute-done.9.refs_1_
  35.2 5.1 collective-permute-done.12.refs_3_
  42.6 3.3 shard_map.343
  47.7 4.4 collective-permute-done.5
  53.4 5.1 collective-permute-start.1
  63.8 14.1 %collective-permute-done.7 = bf16[2,4,2,64]{3,1,0,2:T(4,128)(2,1)S(1)} collective-permute-done((bf16[2,4,2,64]{3,1,0,2:T(4,128)(2,1)S(1)}, bf16[2,4,2,64]{3,1,0,2:T(4,128)(2,1)S(1)}, u32[]{:S(2)}, u32[]{:S(2)}) %collective-permute-start.7) | collective-permute-done | bytes 2080 | tf_op jit(solution)/shard_map/ppermute | solution.py:55
  85.3 3.3 collective-permute-done.2.refs_3_
  90.6 2.9 shard_map.341
  95.6 4.4 all-to-all-start
  101.3 4.2 convolution_convert_fusion.4
  106.9 7.8 %collective-permute-done.20.refs_3_ = bf16[80,2048]{1,0:T(8,128)(2,1)S(1)} collective-permute-done((bf16[80,2048]{1,0:T(8,128)(2,1)S(1)}, bf16[80,2048]{1,0:T(8,128)(2,1)S(1)}, u32[]{:S(2)}, u32[]{:S(2)}) %collective-permute-start.20) | collective-permute-done | bytes 327712 | tf_op jit(solution)/shard_map/ppermute | solution.py:55
  115.4 12.8 %shard_map.344 = (bf16[8,64,640]{2,1,0:T(8,128)(2,1)}, f32[8,64,640]{2,1,0:T(8,128)}, f32[8,64,640]{2,1,0:T(8,128)}, f32[8,64,640]{2,1,0:T(8,128)}, f32[8,64,640...) custom-call(s32[5]{0:T(128)} %pad_add_fusion.scalars, ...), custom_call_target="tpu_custom_call" | custom-call | bytes 39550976 | tf_op jit(solution)/shard_map/pallas_call | solution.py:257
  129.9 3.5 collective-permute-done.18
  135.8 3.2 shard_map.345
  139.0 4.6 fusion.29
  143.7 4.1 shard_map.346
  147.8 7.1 %all-to-all-start.2 = ((bf16[8,64,768]{2,1,0:T(8,128)(2,1)}), bf16[8,64,768]{2,1,0:T(8,128)(2,1)S(1)}, u32[]{:S(2)}, u32[]{:S(2)}) async-start(bf16[8,64,768]{2,1,0:T(8,128)(2,1)} %bitcast.258), calls=%async_computation.2 | async-start | bytes 1572864 | tf_op jit(solution)/shard_map/all_to_all | solution.py:223
  157.0 6.6 collective-permute-done.27.refs_3_
  166.0 3.2 shard_map.347
  169.2 4.9 convolution_convert_fusion.3
  175.0 5.0 all-to-all-start.1
  181.5 32.8 %all-to-all-done.1 = bf16[4,128,2048]{2,1,0:T(8,128)(2,1)} async-done(((bf16[4,128,2048]{2,1,0:T(8,128)(2,1)}), bf16[4,128,2048]{2,1,0:T(8,128)(2,1)}, u32[]{:S(2)}, u32[]{:S(2)}) %all-to-all-start.1) | async-done | bytes 2097184 | tf_op jit(solution)/shard_map/all_to_all | solution.py:223
  223.4 10.1 %collective-permute-done.32.refs_1_ = bf16[128,2048]{1,0:T(8,128)(2,1)S(1)} collective-permute-done((bf16[128,2048]{1,0:T(8,128)(2,1)S(1)}, bf16[128,2048]{1,0:T(8,128)(2,1)S(1)}, u32[]{:S(2)}, u32[]{:S(2)}) %collective-permute-start.32) | collective-permute-done | bytes 524320 | tf_op jit(solution)/shard_map/ppermute | solution.py:55
  234.4 9.1 %collective-permute-done.33.refs_2_ = bf16[128,2048]{1,0:T(8,128)(2,1)S(1)} collective-permute-done((bf16[128,2048]{1,0:T(8,128)(2,1)S(1)}, bf16[128,2048]{1,0:T(8,128)(2,1)S(1)}, u32[]{:S(2)}, u32[]{:S(2)}) %collective-permute-start.33) | collective-permute-done | bytes 524320 | tf_op jit(solution)/shard_map/ppermute | solution.py:55
  243.5 3.6 collective-permute-start.45
  247.1 7.6 %collective-permute-done.34.refs_3_ = bf16[128,2048]{1,0:T(8,128)(2,1)S(1)} collective-permute-done((bf16[128,2048]{1,0:T(8,128)(2,1)S(1)}, bf16[128,2048]{1,0:T(8,128)(2,1)S(1)}, u32[]{:S(2)}, u32[]{:S(2)}) %collective-permute-start.34) | collective-permute-done | bytes 524320 | tf_op jit(solution)/shard_map/ppermute | solution.py:55
  260.0 6.5 collective-permute-done.44.refs_2_
  268.2 10.7 %collective-permute-done.45.refs_3_ = bf16[128,2048]{1,0:T(8,128)(2,1)S(1)} collective-permute-done((bf16[128,2048]{1,0:T(8,128)(2,1)}, bf16[128,2048]{1,0:T(8,128)(2,1)S(1)}, u32[]{:S(2)}, u32[]{:S(2)}) %collective-permute-start.45) | collective-permute-done | bytes 524320 | tf_op jit(solution)/shard_map/ppermute | solution.py:55
  280.9 3.0 shard_map.352.cot
  284.5 4.5 collective-permute-done.40.refs_2_
  289.0 12.4 %collective-permute-done.41.refs_3_ = bf16[128,2048]{1,0:T(8,128)(2,1)S(1)} collective-permute-done((bf16[128,2048]{1,0:T(8,128)(2,1)S(1)}, bf16[128,2048]{1,0:T(8,128)(2,1)S(1)}, u32[]{:S(2)}, u32[]{:S(2)}) %collective-permute-start.41) | collective-permute-done | bytes 524320 | tf_op jit(solution)/shard_map/ppermute | solution.py:55
  302.2 2.9 shard_map.351.tokens
  305.1 21.8 %shard_map.353 = (bf16[512,2048]{1,0:T(8,128)(2,1)}, bf16[512,2048]{1,0:T(8,128)(2,1)}, bf16[512,768]{1,0:T(8,128)(2,1)}, bf16[512,768]{1,0:T(8,128)(2,1)}, bf16[512,768]{1,0:T(8,128)(2,1)}) custom-call(bf16[512,2048]{1,0:T(8,128)(2,1)} %shard_map.351.tokens, bf16[512,2048]{1,0:T(8,128)(2,1)} %shard_map.352.cot, ...), custom_call_target="tpu_custom_call" | custom-call | flops 9663676416 | bytes 20185088 | tf_op jit(solution)/shard_map/pallas_call | solution.py:565
  326.9 4.8 all-to-all-start.3
  335.7 3.0 shard_map.348.tokens
  338.7 3.6 fusion.35
  342.3 21.7 %shard_map.350 = (bf16[512,2048]{1,0:T(8,128)(2,1)}, bf16[512,2048]{1,0:T(8,128)(2,1)}, bf16[512,768]{1,0:T(8,128)(2,1)}, bf16[512,768]{1,0:T(8,128)(2,1)}, bf16[512,768]{1,0:T(8,128)(2,1)}) custom-call(bf16[512,2048]{1,0:T(8,128)(2,1)} %shard_map.348.tokens, bf16[512,2048]{1,0:T(8,128)(2,1)} %shard_map.349.cot, ...), custom_call_target="tpu_custom_call" | custom-call | flops 9663676416 | bytes 20185088 | tf_op jit(solution)/shard_map/pallas_call | solution.py:565
  364.1 5.3 add_convert_fusion.2
  371.4 4.5 all-to-all-start.4
  378.2 29.2 %all-to-all-done.4 = bf16[4,128,2048]{2,1,0:T(8,128)(2,1)} async-done(((bf16[4,128,2048]{2,1,0:T(8,128)(2,1)}), bf16[4,128,2048]{2,1,0:T(8,128)(2,1)}, u32[]{:S(2)}, u32[]{:S(2)}) %all-to-all-start.4) | async-done | bytes 2097184 | tf_op jit(solution)/shard_map/all_to_all | solution.py:223
  414.6 3.7 fusion.5
  423.7 3.9 fusion.37
  427.5 11.1 %collective-permute-done.48.refs_2_ = bf16[128,2048]{1,0:T(8,128)(2,1)S(1)} collective-permute-done((bf16[128,2048]{1,0:T(8,128)(2,1)S(1)}, bf16[128,2048]{1,0:T(8,128)(2,1)S(1)}, u32[]{:S(2)}, u32[]{:S(2)}) %collective-permute-start.48) | collective-permute-done | bytes 524320 | tf_op jit(solution)/shard_map/ppermute | solution.py:55
  443.7 3.7 fusion.6
  447.4 4.8 all-to-all-start.5
  452.9 3.2 shard_map.354
  456.1 4.4 fusion.38.grad_mixed
  460.5 9.2 %shard_map.355 = (bf16[8,64,640]{2,1,0:T(8,128)(2,1)}, f32[8,64,640]{2,1,0:T(8,128)}, f32[8,64,640]{2,1,0:T(8,128)}, f32[8,2,640]{2,1,0:T(2,128)}) custom-call(s32[5]{0:T(128)} %pad_add_fusion.scalars, f32[8,64,640]{2,1,0:T(8,128)} %fusion.38.grad_mixed, f32[8,64,640]{2,1,0:T(8,128)} %get-tuple-element.164.state, f32[8,64,640]{2,1,0:T(8,128)} %bitcast.269, ...), custom_call_target="tpu_custom_call" | custom-call | bytes 25853952 | tf_op jit(solution)/shard_map/pallas_call | solution.py:257
  479.9 3.9 collective-permute-done.52
  484.5 16.6 %shard_map.356 = (f32[8,64,640]{2,1,0:T(8,128)}, bf16[8,4,640]{2,1,0:T(4,128)(2,1)}, bf16[640,384]{1,0:T(8,128)(2,1)}) custom-call(s32[5]{0:T(128)} %pad_add_fusion.scalars, f32[8,64,640]{2,1,0:T(8,128)} %get-tuple-element.167.prod, f32[8,64,640]{2,1,0:T(8,128)} %get-tuple-element.168.part, f32[16,2,640]{2,1,0:T(2,128)} %bitcast.309, ...), custom_call_target="tpu_custom_call" | custom-call | bytes 59129856 | tf_op jit(solution)/shard_map/pallas_call | solution.py:257
  516.6 2.9 reduce_sum.134
  521.3 3.8 shard_map.357
  528.2 4.3 collective-permute-done.56
  534.6 11.5 %collective-permute-done.57 = bf16[2,80,2048]{2,1,0:T(8,128)(2,1)} collective-permute-done((bf16[2,80,2048]{2,1,0:T(8,128)(2,1)}, bf16[2,80,2048]{2,1,0:T(8,128)(2,1)}, u32[]{:S(2)}, u32[]{:S(2)}) %collective-permute-start.57) | collective-permute-done | bytes 655392 | tf_op jit(solution)/shard_map/ppermute | solution.py:55
  555.4 13.4 %collective-permute-done.59 = bf16[128,2048]{1,0:T(8,128)(2,1)S(1)} collective-permute-done((bf16[128,2048]{1,0:T(8,128)(2,1)S(1)}, bf16[128,2048]{1,0:T(8,128)(2,1)S(1)}, u32[]{:S(2)}, u32[]{:S(2)}) %collective-permute-start.59) | collective-permute-done | bytes 524320 | tf_op jit(solution)/shard_map/ppermute | solution.py:55
  571.7 7.1 %all-to-all-start.6 = ((bf16[4,128,2048]{2,1,0:T(8,128)(2,1)}), bf16[4,128,2048]{2,1,0:T(8,128)(2,1)}, u32[]{:S(2)}, u32[]{:S(2)}) async-start(bf16[4,128,2048]{2,1,0:T(8,128)(2,1)} %bitcast.267), calls=%async_computation.7 | async-start | bytes 4194304 | tf_op jit(solution)/shard_map/all_to_all | solution.py:223
  595.4 11.4 %collective-permute-done.70 = bf16[2,64,768]{2,1,0:T(8,128)(2,1)S(1)} collective-permute-done((bf16[2,64,768]{2,1,0:T(8,128)(2,1)S(1)}, bf16[2,64,768]{2,1,0:T(8,128)(2,1)S(1)}, u32[]{:S(2)}, u32[]{:S(2)}) %collective-permute-start.70) | collective-permute-done | bytes 196640 | tf_op jit(solution)/shard_map/ppermute | solution.py:55
  607.5 23.8 %collective-permute-done.71 = bf16[2,64,768]{2,1,0:T(8,128)(2,1)S(1)} collective-permute-done((bf16[2,64,768]{2,1,0:T(8,128)(2,1)S(1)}, bf16[2,64,768]{2,1,0:T(8,128)(2,1)S(1)}, u32[]{:S(2)}, u32[]{:S(2)}) %collective-permute-start.71) | collective-permute-done | bytes 196640 | tf_op jit(solution)/shard_map/ppermute | solution.py:55
  632.0 6.9 %collective-permute-done.72 = bf16[2,64,768]{2,1,0:T(8,128)(2,1)S(1)} collective-permute-done((bf16[2,64,768]{2,1,0:T(8,128)(2,1)S(1)}, bf16[2,64,768]{2,1,0:T(8,128)(2,1)S(1)}, u32[]{:S(2)}, u32[]{:S(2)}) %collective-permute-start.72) | collective-permute-done | bytes 196640 | tf_op jit(solution)/shard_map/ppermute | solution.py:55
  650.1 4.0 all-to-all-start.7
  654.1 3.9 fusion.17
  664.4 4.3 all-to-all-start.8
  (474 shorter events, 184.7 us)
Async XLA Ops:
  7.2 297.9 %all-gather.7.cloned.1.call-start = ((), (), s32[]{:S(2)}) async-start(), calls=%async_computation.15 | async-start | bytes 3932160 | tf_op jit(solution)/shard_map/all_gather | solution.py:203
  18.0 13.3 %collective-permute-start.9 = (bf16[80,2048]{1,0:T(8,128)(2,1)}, bf16[80,2048]{1,0:T(8,128)(2,1)S(1)}, u32[]{:S(2)}, u32[]{:S(2)}) collective-permute-start(bf16[80,2048]{1,0:T(8,128)(2,1)} %refs_0_.1), channel_id=1, source_target_pairs={{0,16},{1,17},{2,18},{3,19},{4,20},{5,21},{6,22},{7,23},{8,24},{9,... | collective-permute-start | bytes 983048 | tf_op jit(solution)/shard_map/ppermute | solution.py:55
  46.0 259.1 %all-gather.9.cloned.1.call-start = ((), (), s32[]{:S(2)}) async-start(), calls=%async_computation.16 | async-start | bytes 3932160 | tf_op jit(solution)/shard_map/all_gather | solution.py:203
  52.9 30.5 %collective-permute-start = (bf16[128,2048]{1,0:T(8,128)(2,1)S(1)}, bf16[128,2048]{1,0:T(8,128)(2,1)S(1)}, u32[]{:S(2)}, u32[]{:S(2)}) collective-permute-start(bf16[128,2048]{1,0:T(8,128)(2,1)S(1)} %bitcast.264), channel_id=1, source_target_pairs={{0,4},{1,5},{2,6},{3,7},{4,0},{5,1},{6,2},{7,3},{8,12},{9,13},{10,... | collective-permute-start | bytes 1572872 | tf_op jit(solution)/shard_map/ppermute | solution.py:55
  53.4 28.3 %collective-permute-start.1 = (bf16[128,2048]{1,0:T(8,128)(2,1)S(1)}, bf16[128,2048]{1,0:T(8,128)(2,1)S(1)}, u32[]{:S(2)}, u32[]{:S(2)}) collective-permute-start(bf16[128,2048]{1,0:T(8,128)(2,1)S(1)} %bitcast.265), channel_id=1, source_target_pairs={{0,8},{1,9},{2,10},{3,11},{4,12},{5,13},{6,14},{7,15},{8,0},{9,1},... | collective-permute-start | bytes 1572872 | tf_op jit(solution)/shard_map/ppermute | solution.py:55
  58.6 76.0 %collective-permute-start.21 = (bf16[80,2048]{1,0:T(8,128)(2,1)S(1)}, bf16[80,2048]{1,0:T(8,128)(2,1)}, u32[]{:S(2)}, u32[]{:S(2)}) collective-permute-start(bf16[80,2048]{1,0:T(8,128)(2,1)S(1)} %copy-done.60), channel_id=1, source_target_pairs={{0,1},{1,0},{2,3},{3,2},{4,5},{5,4},{6,7},{7,6},{8,9},{9,8},{10,11... | collective-permute-start | bytes 983048 | tf_op jit(solution)/shard_map/ppermute | solution.py:55
  61.2 38.8 %collective-permute-start.19 = (bf16[80,2048]{1,0:T(8,128)(2,1)S(1)}, bf16[80,2048]{1,0:T(8,128)(2,1)S(1)}, u32[]{:S(2)}, u32[]{:S(2)}) collective-permute-start(bf16[80,2048]{1,0:T(8,128)(2,1)S(1)} %copy-done.60), channel_id=1, source_target_pairs={{0,16},{1,17},{2,18},{3,19},{4,20},{5,21},{6,22},{7,23},{8,24},{9,... | collective-permute-start | bytes 983048 | tf_op jit(solution)/shard_map/ppermute | solution.py:55
  62.5 15.5 %collective-permute-start.7 = (bf16[2,4,2,64]{3,1,0,2:T(4,128)(2,1)S(1)}, bf16[2,4,2,64]{3,1,0,2:T(4,128)(2,1)S(1)}, u32[]{:S(2)}, u32[]{:S(2)}) collective-permute-start(bf16[2,4,2,64]{3,1,0,2:T(4,128)(2,1)S(1)} %copy.114), channel_id=1, source_target_pairs={{0,8},{1,9},{2,10},{3,11},{4,12},{5,13},{6,14},{7,15},{8,0},{9,1},... | collective-permute-start | bytes 6152 | tf_op jit(solution)/shard_map/ppermute | solution.py:55
  95.6 34.4 %all-to-all-start = ((bf16[4,64,640]{2,1,0:T(8,128)(2,1)}), bf16[4,64,640]{2,1,0:T(8,128)(2,1)S(1)}, u32[]{:S(2)}, u32[]{:S(2)}) async-start(bf16[4,64,640]{2,1,0:T(8,128)(2,1)} %reshape.349), calls=%async_computation | async-start | bytes 655360 | tf_op jit(solution)/shard_map/all_to_all | solution.py:223
  100.1 14.6 %collective-permute-start.20 = (bf16[80,2048]{1,0:T(8,128)(2,1)S(1)}, bf16[80,2048]{1,0:T(8,128)(2,1)S(1)}, u32[]{:S(2)}, u32[]{:S(2)}) collective-permute-start(bf16[80,2048]{1,0:T(8,128)(2,1)S(1)} %collective-permute-done.19.refs_1_), channel_id=1, source_target_pairs={{0,2},{1,3},{2,0},{3,1},{4,6},{5,7},{6,4},{7,5},{8,10},{9,11},{10,... | collective-permute-start | bytes 983048 | tf_op jit(solution)/shard_map/ppermute | solution.py:55
  106.4 28.7 %collective-permute-start.22 = (bf16[80,2048]{1,0:T(8,128)(2,1)S(1)}, bf16[80,2048]{1,0:T(8,128)(2,1)S(1)}, u32[]{:S(2)}, u32[]{:S(2)}) collective-permute-start(bf16[80,2048]{1,0:T(8,128)(2,1)S(1)} %collective-permute-done.19.refs_1_), channel_id=1, source_target_pairs={{0,1},{1,0},{2,3},{3,2},{4,5},{5,4},{6,7},{7,6},{8,9},{9,8},{10,11... | collective-permute-start | bytes 983048 | tf_op jit(solution)/shard_map/ppermute | solution.py:55
  106.4 28.7 %collective-permute-start.23 = (bf16[80,2048]{1,0:T(8,128)(2,1)S(1)}, bf16[80,2048]{1,0:T(8,128)(2,1)}, u32[]{:S(2)}, u32[]{:S(2)}) collective-permute-start(bf16[80,2048]{1,0:T(8,128)(2,1)S(1)} %copy-done.62), channel_id=1, source_target_pairs={{0,1},{1,0},{2,3},{3,2},{4,5},{5,4},{6,7},{7,6},{8,9},{9,8},{10,11... | collective-permute-start | bytes 983048 | tf_op jit(solution)/shard_map/ppermute | solution.py:55
  114.7 20.5 %collective-permute-start.24 = (bf16[80,2048]{1,0:T(8,128)(2,1)S(1)}, bf16[80,2048]{1,0:T(8,128)(2,1)}, u32[]{:S(2)}, u32[]{:S(2)}) collective-permute-start(bf16[80,2048]{1,0:T(8,128)(2,1)S(1)} %collective-permute-done.20.refs_3_), channel_id=1, source_target_pairs={{0,1},{1,0},{2,3},{3,2},{4,5},{5,4},{6,7},{7,6},{8,9},{9,8},{10,11... | collective-permute-start | bytes 983048 | tf_op jit(solution)/shard_map/ppermute | solution.py:55
  133.4 21.5 %collective-permute-start.25 = (bf16[4,64,640]{2,1,0:T(8,128)(2,1)S(1)}, bf16[4,64,640]{2,1,0:T(8,128)(2,1)S(1)}, u32[]{:S(2)}, u32[]{:S(2)}) collective-permute-start(bf16[4,64,640]{2,1,0:T(8,128)(2,1)S(1)} %all-to-all-done.refs_0_), channel_id=1, source_target_pairs={{0,16},{1,17},{2,18},{3,19},{4,20},{5,21},{6,22},{7,23},{8,24},{9,... | collective-permute-start | bytes 983048 | tf_op jit(solution)/shard_map/ppermute | solution.py:55
  134.6 20.4 %collective-permute-start.26 = (bf16[4,64,640]{2,1,0:T(8,128)(2,1)S(1)}, bf16[4,64,640]{2,1,0:T(8,128)(2,1)S(1)}, u32[]{:S(2)}, u32[]{:S(2)}) collective-permute-start(bf16[4,64,640]{2,1,0:T(8,128)(2,1)S(1)} %all-to-all-done.refs_0_), channel_id=1, source_target_pairs={{0,2},{1,3},{2,0},{3,1},{4,6},{5,7},{6,4},{7,5},{8,10},{9,11},{10,... | collective-permute-start | bytes 983048 | tf_op jit(solution)/shard_map/ppermute | solution.py:55
  147.8 26.4 %all-to-all-start.2 = ((bf16[8,64,768]{2,1,0:T(8,128)(2,1)}), bf16[8,64,768]{2,1,0:T(8,128)(2,1)S(1)}, u32[]{:S(2)}, u32[]{:S(2)}) async-start(bf16[8,64,768]{2,1,0:T(8,128)(2,1)} %bitcast.258), calls=%async_computation.2 | async-start | bytes 1572864 | tf_op jit(solution)/shard_map/all_to_all | solution.py:223
  175.0 39.3 %all-to-all-start.1 = ((bf16[4,128,2048]{2,1,0:T(8,128)(2,1)}), bf16[4,128,2048]{2,1,0:T(8,128)(2,1)}, u32[]{:S(2)}, u32[]{:S(2)}) async-start(bf16[4,128,2048]{2,1,0:T(8,128)(2,1)} %bitcast.294), calls=%async_computation.1 | async-start | bytes 4194304 | tf_op jit(solution)/shard_map/all_to_all | solution.py:223
  180.0 125.1 %all-gather.11.cloned.1.call-start = ((), (), s32[]{:S(2)}) async-start(), calls=%async_computation.17 | async-start | bytes 3932160 | tf_op jit(solution)/shard_map/all_gather | solution.py:203
  180.7 42.1 %collective-permute-start.42 = (bf16[128,2048]{1,0:T(8,128)(2,1)S(1)}, bf16[128,2048]{1,0:T(8,128)(2,1)}, u32[]{:S(2)}, u32[]{:S(2)}) collective-permute-start(bf16[128,2048]{1,0:T(8,128)(2,1)S(1)} %bitcast.287), channel_id=1, source_target_pairs={{0,16},{1,17},{2,18},{3,19},{4,20},{5,21},{6,22},{7,23},{8,24},{9,... | collective-permute-start | bytes 1572872 | tf_op jit(solution)/shard_map/ppermute | solution.py:55
  217.0 16.5 %collective-permute-start.32 = (bf16[128,2048]{1,0:T(8,128)(2,1)S(1)}, bf16[128,2048]{1,0:T(8,128)(2,1)S(1)}, u32[]{:S(2)}, u32[]{:S(2)}) collective-permute-start(bf16[128,2048]{1,0:T(8,128)(2,1)S(1)} %multiply_convert_fusion.refs_0_), channel_id=1, source_target_pairs={{0,4},{1,5},{2,6},{3,7},{4,0},{5,1},{6,2},{7,3},{8,12},{9,13},{10,... | collective-permute-start | bytes 1572872 | tf_op jit(solution)/shard_map/ppermute | solution.py:55
  217.4 26.1 %collective-permute-start.33 = (bf16[128,2048]{1,0:T(8,128)(2,1)S(1)}, bf16[128,2048]{1,0:T(8,128)(2,1)S(1)}, u32[]{:S(2)}, u32[]{:S(2)}) collective-permute-start(bf16[128,2048]{1,0:T(8,128)(2,1)S(1)} %multiply_convert_fusion.refs_0_), channel_id=1, source_target_pairs={{0,8},{1,9},{2,10},{3,11},{4,12},{5,13},{6,14},{7,15},{8,0},{9,1},... | collective-permute-start | bytes 1572872 | tf_op jit(solution)/shard_map/ppermute | solution.py:55
  219.9 34.8 %collective-permute-start.34 = (bf16[128,2048]{1,0:T(8,128)(2,1)S(1)}, bf16[128,2048]{1,0:T(8,128)(2,1)S(1)}, u32[]{:S(2)}, u32[]{:S(2)}) collective-permute-start(bf16[128,2048]{1,0:T(8,128)(2,1)S(1)} %multiply_convert_fusion.refs_0_), channel_id=1, source_target_pairs={{0,12},{1,13},{2,14},{3,15},{4,8},{5,9},{6,10},{7,11},{8,4},{9,5},... | collective-permute-start | bytes 1572872 | tf_op jit(solution)/shard_map/ppermute | solution.py:55
  221.0 34.2 %collective-permute-start.38 = (bf16[128,2048]{1,0:T(8,128)(2,1)S(1)}, bf16[128,2048]{1,0:T(8,128)(2,1)S(1)}, u32[]{:S(2)}, u32[]{:S(2)}) collective-permute-start(bf16[128,2048]{1,0:T(8,128)(2,1)S(1)} %multiply_convert_fusion.refs_0_), channel_id=1, source_target_pairs={{0,16},{1,17},{2,18},{3,19},{4,20},{5,21},{6,22},{7,23},{8,24},{9,... | collective-permute-start | bytes 1572872 | tf_op jit(solution)/shard_map/ppermute | solution.py:55
  222.8 35.9 %collective-permute-start.43 = (bf16[128,2048]{1,0:T(8,128)(2,1)}, bf16[128,2048]{1,0:T(8,128)(2,1)S(1)}, u32[]{:S(2)}, u32[]{:S(2)}) collective-permute-start(bf16[128,2048]{1,0:T(8,128)(2,1)} %collective-permute-done.42.refs_0_), channel_id=1, source_target_pairs={{0,4},{1,5},{2,6},{3,7},{4,0},{5,1},{6,2},{7,3},{8,12},{9,13},{10,... | collective-permute-start | bytes 1572872 | tf_op jit(solution)/shard_map/ppermute | solution.py:55
  233.5 32.9 %collective-permute-start.44 = (bf16[128,2048]{1,0:T(8,128)(2,1)}, bf16[128,2048]{1,0:T(8,128)(2,1)S(1)}, u32[]{:S(2)}, u32[]{:S(2)}) collective-permute-start(bf16[128,2048]{1,0:T(8,128)(2,1)} %collective-permute-done.42.refs_0_), channel_id=1, source_target_pairs={{0,8},{1,9},{2,10},{3,11},{4,12},{5,13},{6,14},{7,15},{8,0},{9,1},... | collective-permute-start | bytes 1572872 | tf_op jit(solution)/shard_map/ppermute | solution.py:55
  243.5 35.4 %collective-permute-start.45 = (bf16[128,2048]{1,0:T(8,128)(2,1)}, bf16[128,2048]{1,0:T(8,128)(2,1)S(1)}, u32[]{:S(2)}, u32[]{:S(2)}) collective-permute-start(bf16[128,2048]{1,0:T(8,128)(2,1)} %collective-permute-done.42.refs_0_), channel_id=1, source_target_pairs={{0,12},{1,13},{2,14},{3,15},{4,8},{5,9},{6,10},{7,11},{8,4},{9,5},... | collective-permute-start | bytes 1572872 | tf_op jit(solution)/shard_map/ppermute | solution.py:55
  255.3 28.6 %collective-permute-start.39 = (bf16[128,2048]{1,0:T(8,128)(2,1)S(1)}, bf16[128,2048]{1,0:T(8,128)(2,1)S(1)}, u32[]{:S(2)}, u32[]{:S(2)}) collective-permute-start(bf16[128,2048]{1,0:T(8,128)(2,1)S(1)} %collective-permute-done.38.refs_0_), channel_id=1, source_target_pairs={{0,4},{1,5},{2,6},{3,7},{4,0},{5,1},{6,2},{7,3},{8,12},{9,13},{10,... | collective-permute-start | bytes 1572872 | tf_op jit(solution)/shard_map/ppermute | solution.py:55
  256.7 32.3 %collective-permute-start.40 = (bf16[128,2048]{1,0:T(8,128)(2,1)S(1)}, bf16[128,2048]{1,0:T(8,128)(2,1)S(1)}, u32[]{:S(2)}, u32[]{:S(2)}) collective-permute-start(bf16[128,2048]{1,0:T(8,128)(2,1)S(1)} %collective-permute-done.38.refs_0_), channel_id=1, source_target_pairs={{0,8},{1,9},{2,10},{3,11},{4,12},{5,13},{6,14},{7,15},{8,0},{9,1},... | collective-permute-start | bytes 1572872 | tf_op jit(solution)/shard_map/ppermute | solution.py:55
  258.8 42.6 %collective-permute-start.41 = (bf16[128,2048]{1,0:T(8,128)(2,1)S(1)}, bf16[128,2048]{1,0:T(8,128)(2,1)S(1)}, u32[]{:S(2)}, u32[]{:S(2)}) collective-permute-start(bf16[128,2048]{1,0:T(8,128)(2,1)S(1)} %collective-permute-done.38.refs_0_), channel_id=1, source_target_pairs={{0,12},{1,13},{2,14},{3,15},{4,8},{5,9},{6,10},{7,11},{8,4},{9,5},... | collective-permute-start | bytes 1572872 | tf_op jit(solution)/shard_map/ppermute | solution.py:55
  266.5 65.6 %collective-permute-start.35 = (bf16[128,2048]{1,0:T(8,128)(2,1)S(1)}, bf16[128,2048]{1,0:T(8,128)(2,1)}, u32[]{:S(2)}, u32[]{:S(2)}) collective-permute-start(bf16[128,2048]{1,0:T(8,128)(2,1)S(1)} %bitcast.288), channel_id=1, source_target_pairs={{0,4},{1,5},{2,6},{3,7},{4,0},{5,1},{6,2},{7,3},{8,12},{9,13},{10,... | collective-permute-start | bytes 1572872 | tf_op jit(solution)/shard_map/ppermute | solution.py:55
  278.9 53.1 %collective-permute-start.36 = (bf16[128,2048]{1,0:T(8,128)(2,1)S(1)}, bf16[128,2048]{1,0:T(8,128)(2,1)}, u32[]{:S(2)}, u32[]{:S(2)}) collective-permute-start(bf16[128,2048]{1,0:T(8,128)(2,1)S(1)} %bitcast.289), channel_id=1, source_target_pairs={{0,8},{1,9},{2,10},{3,11},{4,12},{5,13},{6,14},{7,15},{8,0},{9,1},... | collective-permute-start | bytes 1572872 | tf_op jit(solution)/shard_map/ppermute | solution.py:55
  283.9 48.2 %collective-permute-start.37 = (bf16[128,2048]{1,0:T(8,128)(2,1)S(1)}, bf16[128,2048]{1,0:T(8,128)(2,1)S(1)}, u32[]{:S(2)}, u32[]{:S(2)}) collective-permute-start(bf16[128,2048]{1,0:T(8,128)(2,1)S(1)} %bitcast.290), channel_id=1, source_target_pairs={{0,12},{1,13},{2,14},{3,15},{4,8},{5,9},{6,10},{7,11},{8,4},{9,5},... | collective-permute-start | bytes 1572872 | tf_op jit(solution)/shard_map/ppermute | solution.py:55
  326.9 42.5 %all-to-all-start.3 = ((bf16[4,128,2048]{2,1,0:T(8,128)(2,1)}), bf16[4,128,2048]{2,1,0:T(8,128)(2,1)}, u32[]{:S(2)}, u32[]{:S(2)}) async-start(bf16[4,128,2048]{2,1,0:T(8,128)(2,1)} %bitcast.292), calls=%async_computation.3 | async-start | bytes 4194304 | tf_op jit(solution)/shard_map/all_to_all | solution.py:223
  331.6 89.6 %reduce-scatter.4.cloned.1.call-start = ((), (), s32[]{:S(2)}) async-start(), calls=%async_computation.12 | async-start | bytes 3932160 | tf_op jit(solution)/shard_map/reduce_scatter | solution.py:207
  371.4 36.0 %all-to-all-start.4 = ((bf16[4,128,2048]{2,1,0:T(8,128)(2,1)}), bf16[4,128,2048]{2,1,0:T(8,128)(2,1)}, u32[]{:S(2)}, u32[]{:S(2)}) async-start(bf16[4,128,2048]{2,1,0:T(8,128)(2,1)} %bitcast.293), calls=%async_computation.4 | async-start | bytes 4194304 | tf_op jit(solution)/shard_map/all_to_all | solution.py:223
  375.9 266.1 %reduce-scatter.6.cloned.1.call-start = ((), (), s32[]{:S(2)}) async-start(), calls=%async_computation.13 | async-start | bytes 3932160 | tf_op jit(solution)/shard_map/reduce_scatter | solution.py:207
  376.1 33.4 %collective-permute-start.46 = (bf16[128,2048]{1,0:T(8,128)(2,1)S(1)}, bf16[128,2048]{1,0:T(8,128)(2,1)S(1)}, u32[]{:S(2)}, u32[]{:S(2)}) collective-permute-start(bf16[128,2048]{1,0:T(8,128)(2,1)S(1)} %reduce_sum.131), channel_id=1, source_target_pairs={{0,16},{1,17},{2,18},{3,19},{4,20},{5,21},{6,22},{7,23},{8,24},{9,... | collective-permute-start | bytes 1572872 | tf_op jit(solution)/shard_map/ppermute | solution.py:55
  418.4 22.7 %collective-permute-start.47 = (bf16[128,2048]{1,0:T(8,128)(2,1)S(1)}, bf16[128,2048]{1,0:T(8,128)(2,1)S(1)}, u32[]{:S(2)}, u32[]{:S(2)}) collective-permute-start(bf16[128,2048]{1,0:T(8,128)(2,1)S(1)} %get-tuple-element.159.refs_0_), channel_id=1, source_target_pairs={{0,4},{1,5},{2,6},{3,7},{4,0},{5,1},{6,2},{7,3},{8,12},{9,13},{10,... | collective-permute-start | bytes 1572872 | tf_op jit(solution)/shard_map/ppermute | solution.py:55
  418.8 19.9 %collective-permute-start.48 = (bf16[128,2048]{1,0:T(8,128)(2,1)S(1)}, bf16[128,2048]{1,0:T(8,128)(2,1)S(1)}, u32[]{:S(2)}, u32[]{:S(2)}) collective-permute-start(bf16[128,2048]{1,0:T(8,128)(2,1)S(1)} %get-tuple-element.159.refs_0_), channel_id=1, source_target_pairs={{0,8},{1,9},{2,10},{3,11},{4,12},{5,13},{6,14},{7,15},{8,0},{9,1},... | collective-permute-start | bytes 1572872 | tf_op jit(solution)/shard_map/ppermute | solution.py:55
  423.3 28.8 %collective-permute-start.51 = (bf16[4,64,768]{2,1,0:T(8,128)(2,1)}, bf16[4,64,768]{2,1,0:T(8,128)(2,1)S(1)}, u32[]{:S(2)}, u32[]{:S(2)}) collective-permute-start(bf16[4,64,768]{2,1,0:T(8,128)(2,1)} %get-tuple-element.313), channel_id=1, source_target_pairs={{0,16},{1,17},{2,18},{3,19},{4,20},{5,21},{6,22},{7,23},{8,24},{9,... | collective-permute-start | bytes 1179656 | tf_op jit(solution)/shard_map/ppermute | solution.py:55
  439.4 12.8 %collective-permute-start.49 = (bf16[64,2048]{1,0:T(8,128)(2,1)}, bf16[64,2048]{1,0:T(8,128)(2,1)}, u32[]{:S(2)}, u32[]{:S(2)}) collective-permute-start(bf16[64,2048]{1,0:T(8,128)(2,1)} %slice.141), channel_id=1, source_target_pairs={{0,4},{1,5},{2,6},{3,7},{4,0},{5,1},{6,2},{7,3},{8,12},{9,13},{10,... | collective-permute-start | bytes 786440 | tf_op jit(solution)/shard_map/ppermute | solution.py:55
  441.1 11.1 %collective-permute-start.50 = (bf16[64,2048]{1,0:T(8,128)(2,1)S(1)}, bf16[64,2048]{1,0:T(8,128)(2,1)S(1)}, u32[]{:S(2)}, u32[]{:S(2)}) collective-permute-start(bf16[64,2048]{1,0:T(8,128)(2,1)S(1)} %slice.142), channel_id=1, source_target_pairs={{0,8},{1,9},{2,10},{3,11},{4,12},{5,13},{6,14},{7,15},{8,0},{9,1},... | collective-permute-start | bytes 786440 | tf_op jit(solution)/shard_map/ppermute | solution.py:55
  447.4 69.3 %all-to-all-start.5 = ((bf16[4,128,2048]{2,1,0:T(8,128)(2,1)}), bf16[4,128,2048]{2,1,0:T(8,128)(2,1)}, u32[]{:S(2)}, u32[]{:S(2)}) async-start(bf16[4,128,2048]{2,1,0:T(8,128)(2,1)} %bitcast.291), calls=%async_computation.6 | async-start | bytes 4194304 | tf_op jit(solution)/shard_map/all_to_all | solution.py:223
  452.1 192.3 %reduce-scatter.8.cloned.1.call-start = ((), (), s32[]{:S(2)}) async-start(), calls=%async_computation.14 | async-start | bytes 3932160 | tf_op jit(solution)/shard_map/reduce_scatter | solution.py:207
  472.9 34.3 %collective-permute-start.54 = (bf16[2,4,2,64,640]{4,3,2,1,0:T(8,128)(2,1)}, bf16[2,4,2,64,640]{4,3,2,1,0:T(8,128)(2,1)S(1)}, u32[]{:S(2)}, u32[]{:S(2)}) collective-permute-start(bf16[2,4,2,64,640]{4,3,2,1,0:T(8,128)(2,1)} %dynamic-slice_bitcast_fusion), channel_id=1, source_target_pairs={{0,1},{1,0},{2,3},{3,2},{4,5},{5,4},{6,7},{7,6},{8,9},{9,8},{10,11... | collective-permute-start | bytes 3932168 | tf_op jit(solution)/shard_map/ppermute | solution.py:55
  478.9 29.4 %collective-permute-start.55 = (bf16[2,2,80,2048]{3,2,0,1:T(8,128)(2,1)}, bf16[2,2,80,2048]{3,2,0,1:T(8,128)(2,1)}, u32[]{:S(2)}, u32[]{:S(2)}) collective-permute-start(bf16[2,2,80,2048]{3,2,0,1:T(8,128)(2,1)} %bitcast.256), channel_id=1, source_target_pairs={{0,1},{1,0},{2,3},{3,2},{4,5},{5,4},{6,7},{7,6},{8,9},{9,8},{10,11... | collective-permute-start | bytes 3932168 | tf_op jit(solution)/shard_map/ppermute | solution.py:55
  502.6 88.7 %collective-permute-start.65 = (bf16[128,2048]{1,0:T(8,128)(2,1)}, bf16[128,2048]{1,0:T(8,128)(2,1)}, u32[]{:S(2)}, u32[]{:S(2)}) collective-permute-start(bf16[128,2048]{1,0:T(8,128)(2,1)} %get-tuple-element.309), channel_id=1, source_target_pairs={{0,12},{1,13},{2,14},{3,15},{4,8},{5,9},{6,10},{7,11},{8,4},{9,5},... | collective-permute-start | bytes 1572872 | tf_op jit(solution)/shard_map/ppermute | solution.py:55
  504.4 88.3 %collective-permute-start.64 = (bf16[128,2048]{1,0:T(8,128)(2,1)}, bf16[128,2048]{1,0:T(8,128)(2,1)}, u32[]{:S(2)}, u32[]{:S(2)}) collective-permute-start(bf16[128,2048]{1,0:T(8,128)(2,1)} %get-tuple-element.310), channel_id=1, source_target_pairs={{0,8},{1,9},{2,10},{3,11},{4,12},{5,13},{6,14},{7,15},{8,0},{9,1},... | collective-permute-start | bytes 1572872 | tf_op jit(solution)/shard_map/ppermute | solution.py:55
  506.3 88.0 %collective-permute-start.63 = (bf16[128,2048]{1,0:T(8,128)(2,1)}, bf16[128,2048]{1,0:T(8,128)(2,1)}, u32[]{:S(2)}, u32[]{:S(2)}) collective-permute-start(bf16[128,2048]{1,0:T(8,128)(2,1)} %get-tuple-element.311), channel_id=1, source_target_pairs={{0,4},{1,5},{2,6},{3,7},{4,0},{5,1},{6,2},{7,3},{8,12},{9,13},{10,... | collective-permute-start | bytes 1572872 | tf_op jit(solution)/shard_map/ppermute | solution.py:55
  510.9 21.6 %collective-permute-start.56 = (bf16[2,4,64,640]{3,2,1,0:T(8,128)(2,1)}, bf16[2,4,64,640]{3,2,1,0:T(8,128)(2,1)S(1)}, u32[]{:S(2)}, u32[]{:S(2)}) collective-permute-start(bf16[2,4,64,640]{3,2,1,0:T(8,128)(2,1)} %dynamic-slice_bitcast_fusion.3), channel_id=1, source_target_pairs={{0,2},{1,3},{2,0},{3,1},{4,6},{5,7},{6,4},{7,5},{8,10},{9,11},{10,... | collective-permute-start | bytes 1966088 | tf_op jit(solution)/shard_map/ppermute | solution.py:55
  516.2 30.0 %collective-permute-start.57 = (bf16[2,80,2048]{2,1,0:T(8,128)(2,1)}, bf16[2,80,2048]{2,1,0:T(8,128)(2,1)}, u32[]{:S(2)}, u32[]{:S(2)}) collective-permute-start(bf16[2,80,2048]{2,1,0:T(8,128)(2,1)} %dynamic-slice_bitcast_fusion.2), channel_id=1, source_target_pairs={{0,2},{1,3},{2,0},{3,1},{4,6},{5,7},{6,4},{7,5},{8,10},{9,11},{10,... | collective-permute-start | bytes 1966088 | tf_op jit(solution)/shard_map/ppermute | solution.py:55
  533.3 20.1 %collective-permute-start.58 = (bf16[2,2,80,2048]{3,2,0,1:T(8,128)(2,1)S(1)}, bf16[2,2,80,2048]{3,2,0,1:T(8,128)(2,1)S(1)}, u32[]{:S(2)}, u32[]{:S(2)}) collective-permute-start(bf16[2,2,80,2048]{3,2,0,1:T(8,128)(2,1)S(1)} %bitcast.301), channel_id=1, source_target_pairs={{0,1},{1,0},{2,3},{3,2},{4,5},{5,4},{6,7},{7,6},{8,9},{9,8},{10,11... | collective-permute-start | bytes 3932168 | tf_op jit(solution)/shard_map/ppermute | solution.py:55
  546.2 22.6 %collective-permute-start.59 = (bf16[128,2048]{1,0:T(8,128)(2,1)S(1)}, bf16[128,2048]{1,0:T(8,128)(2,1)S(1)}, u32[]{:S(2)}, u32[]{:S(2)}) collective-permute-start(bf16[128,2048]{1,0:T(8,128)(2,1)S(1)} %copy-done.55), channel_id=1, source_target_pairs={{0,16},{1,17},{2,18},{3,19},{4,20},{5,21},{6,22},{7,23},{8,24},{9,... | collective-permute-start | bytes 1572872 | tf_op jit(solution)/shard_map/ppermute | solution.py:55
  554.8 29.1 %collective-permute-start.62 = (bf16[2,80,2048]{2,1,0:T(8,128)(2,1)}, bf16[2,80,2048]{2,1,0:T(8,128)(2,1)}, u32[]{:S(2)}, u32[]{:S(2)}) collective-permute-start(bf16[2,80,2048]{2,1,0:T(8,128)(2,1)} %dynamic-slice_bitcast_fusion.1), channel_id=1, source_target_pairs={{0,2},{1,3},{2,0},{3,1},{4,6},{5,7},{6,4},{7,5},{8,10},{9,11},{10,... | collective-permute-start | bytes 1966088 | tf_op jit(solution)/shard_map/ppermute | solution.py:55
  570.4 11.2 %collective-permute-start.60 = (bf16[2,2,80,384]{3,2,0,1:T(8,128)(2,1)}, bf16[2,2,80,384]{3,2,0,1:T(8,128)(2,1)}, u32[]{:S(2)}, u32[]{:S(2)}) collective-permute-start(bf16[2,2,80,384]{3,2,0,1:T(8,128)(2,1)} %bitcast.260), channel_id=1, source_target_pairs={{0,1},{1,0},{2,3},{3,2},{4,5},{5,4},{6,7},{7,6},{8,9},{9,8},{10,11... | collective-permute-start | bytes 737288 | tf_op jit(solution)/shard_map/ppermute | solution.py:55
  571.7 75.3 %all-to-all-start.6 = ((bf16[4,128,2048]{2,1,0:T(8,128)(2,1)}), bf16[4,128,2048]{2,1,0:T(8,128)(2,1)}, u32[]{:S(2)}, u32[]{:S(2)}) async-start(bf16[4,128,2048]{2,1,0:T(8,128)(2,1)} %bitcast.267), calls=%async_computation.7 | async-start | bytes 4194304 | tf_op jit(solution)/shard_map/all_to_all | solution.py:223
  581.6 76.4 %collective-permute-start.66 = (bf16[80,2048]{1,0:T(8,128)(2,1)}, bf16[80,2048]{1,0:T(8,128)(2,1)}, u32[]{:S(2)}, u32[]{:S(2)}) collective-permute-start(bf16[80,2048]{1,0:T(8,128)(2,1)} %dynamic-slice_bitcast_fusion.11), channel_id=1, source_target_pairs={{0,16},{1,17},{2,18},{3,19},{4,20},{5,21},{6,22},{7,23},{8,24},{9,... | collective-permute-start | bytes 983048 | tf_op jit(solution)/shard_map/ppermute | solution.py:55
  589.2 72.6 %collective-permute-start.69 = (bf16[4,64,640]{2,1,0:T(8,128)(2,1)}, bf16[4,64,640]{2,1,0:T(8,128)(2,1)}, u32[]{:S(2)}, u32[]{:S(2)}) collective-permute-start(bf16[4,64,640]{2,1,0:T(8,128)(2,1)} %dynamic-slice_bitcast_fusion.12), channel_id=1, source_target_pairs={{0,16},{1,17},{2,18},{3,19},{4,20},{5,21},{6,22},{7,23},{8,24},{9,... | collective-permute-start | bytes 983048 | tf_op jit(solution)/shard_map/ppermute | solution.py:55
  591.3 68.6 %collective-permute-start.67 = (bf16[80,2048]{1,0:T(8,128)(2,1)}, bf16[80,2048]{1,0:T(8,128)(2,1)}, u32[]{:S(2)}, u32[]{:S(2)}) collective-permute-start(bf16[80,2048]{1,0:T(8,128)(2,1)} %dynamic-slice_bitcast_fusion.10), channel_id=1, source_target_pairs={{0,16},{1,17},{2,18},{3,19},{4,20},{5,21},{6,22},{7,23},{8,24},{9,... | collective-permute-start | bytes 983048 | tf_op jit(solution)/shard_map/ppermute | solution.py:55
  592.8 67.1 %collective-permute-start.68 = (bf16[80,384]{1,0:T(8,128)(2,1)}, bf16[80,384]{1,0:T(8,128)(2,1)}, u32[]{:S(2)}, u32[]{:S(2)}) collective-permute-start(bf16[80,384]{1,0:T(8,128)(2,1)} %dynamic-slice_bitcast_fusion.16), channel_id=1, source_target_pairs={{0,16},{1,17},{2,18},{3,19},{4,20},{5,21},{6,22},{7,23},{8,24},{9,... | collective-permute-start | bytes 184328 | tf_op jit(solution)/shard_map/ppermute | solution.py:55
  595.0 11.8 %collective-permute-start.70 = (bf16[2,64,768]{2,1,0:T(8,128)(2,1)S(1)}, bf16[2,64,768]{2,1,0:T(8,128)(2,1)S(1)}, u32[]{:S(2)}, u32[]{:S(2)}) collective-permute-start(bf16[2,64,768]{2,1,0:T(8,128)(2,1)S(1)} %pad_maximum_fusion.2), channel_id=1, source_target_pairs={{0,4},{1,5},{2,6},{3,7},{4,0},{5,1},{6,2},{7,3},{8,12},{9,13},{10,... | collective-permute-start | bytes 589832 | tf_op jit(solution)/shard_map/ppermute | solution.py:55
  606.8 24.5 %collective-permute-start.71 = (bf16[2,64,768]{2,1,0:T(8,128)(2,1)S(1)}, bf16[2,64,768]{2,1,0:T(8,128)(2,1)S(1)}, u32[]{:S(2)}, u32[]{:S(2)}) collective-permute-start(bf16[2,64,768]{2,1,0:T(8,128)(2,1)S(1)} %pad_maximum_fusion.3), channel_id=1, source_target_pairs={{0,8},{1,9},{2,10},{3,11},{4,12},{5,13},{6,14},{7,15},{8,0},{9,1},... | collective-permute-start | bytes 589832 | tf_op jit(solution)/shard_map/ppermute | solution.py:55
  650.1 14.3 %all-to-all-start.7 = ((bf16[32,2,64]{2,1,0:T(2,128)(2,1)}), bf16[32,2,64]{2,1,0:T(2,128)(2,1)S(1)}, u32[]{:S(2)}, u32[]{:S(2)}) async-start(bf16[32,2,64]{2,1,0:T(2,128)(2,1)} %copy.127), calls=%async_computation.8 | async-start | bytes 32768 | tf_op jit(solution)/shard_map/all_to_all | solution.py:934
  664.4 9.9 %all-to-all-start.8 = ((bf16[4,64,640]{2,1,0:T(8,128)(2,1)}), bf16[4,64,640]{2,1,0:T(8,128)(2,1)S(1)}, u32[]{:S(2)}, u32[]{:S(2)}) async-start(bf16[4,64,640]{2,1,0:T(8,128)(2,1)} %fusion.23), calls=%async_computation.9 | async-start | bytes 655360 | tf_op jit(solution)/shard_map/all_to_all | solution.py:223
  (124 other events, 1476.8 us)
Sparse Core Ops, SparseCore 0:
  46.1 32.8 all-gather.6
  80.6 34.8 all-gather.8
  183.0 29.4 all-gather.10
  369.5 39.1 reduce-scatter.3
  418.5 39.7 reduce-scatter.5
  480.0 43.7 reduce-scatter.7

commit v4 on v3

--- a/solution.py
+++ b/solution.py
@@ -505,80 +505,37 @@
     lax.fori_loop(0, count, body, 0)
 
 
-def forward_backward_kernel(
-    tokens, cot, gate_w, up_w, down_w, down, grad, hidden, grad_gate, grad_up, down_sum, grad_sum
-):
-    step = pl.program_id(0)
-    gate_val = project(tokens[...], gate_w[...])
-    up_val = project(tokens[...], up_w[...])
-    act, slope = gelu_parts(gate_val)
-    hidden_val = (act * up_val).astype(BF16)
-    hidden[...] = hidden_val
-    grad_hidden = back_project(cot[...], down_w[...])
-    gate_part = (grad_hidden * up_val * slope).astype(BF16)
-    up_part = (grad_hidden * act).astype(BF16)
-    grad_gate[...] = gate_part
-    grad_up[...] = up_part
-
-    @pl.when(step == 0)
-    def _():
-        grad_sum[...] = jnp.zeros(grad_sum.shape, F32)
-        down_sum[...] = jnp.zeros(down_sum.shape, F32)
-
-    grad_sum[...] += back_project(gate_part, gate_w[...]) + back_project(up_part, up_w[...])
-    down_sum[...] += project(hidden_val, down_w[...])
-
-    @pl.when(step == pl.num_programs(0) - 1)
-    def _():
-        grad[...] = grad_sum[...].astype(BF16)
-        down[...] = down_sum[...].astype(BF16)
-
-
-def pack_kernel(taps, bias, rate_bias, gate_bias, decay, gain_one, gain_two, rate_w, gate_w, packed):
+def pack_kernel(taps, bias, rate_bias, gate_bias, decay, gains, rate_w, gate_w, packed):
     count, size = rate_w.shape
     packed[...] = jnp.zeros(packed.shape, F32)
     packed[:count, :size] = rate_w[...].astype(F32)
     packed[:count, size : 2 * size] = gate_w[...].astype(F32)
     first = packed.shape[0] - 16
     packed[first : first + TAPS, :count] = taps[...].astype(F32).T
-    for i, row in enumerate((bias, rate_bias, gate_bias, decay, gain_one, gain_two)):
-        packed[first + TAPS + i : first + TAPS + i + 1, : row.shape[1]] = row[...].astype(F32)
-
-
-def lay_kernel(ranks, upper, me, *refs):
+    for i, row in enumerate((bias, rate_bias, gate_bias, decay)):
+        packed[first + TAPS + i : first + TAPS + i + 1, :count] = row[...].astype(F32)
+    packed[first + 8 :, : gains.shape[1]] = gains[...].astype(F32)
+
+
+def lay_kernel(ranks, upper, half, *refs):
     pieces, whole = refs[:-1], refs[-1]
     for i, piece in enumerate(pieces):
-        rank = jnp.bitwise_xor(me[0], i)
+        rank = jnp.bitwise_xor(half[0], i // ranks) * ranks + i % ranks
         size = piece.shape[1] // upper
         for u in range(upper):
-            start = pl.multiple_of((u * ranks + rank) * size, 128)
+            start = pl.multiple_of((u * 2 * ranks + rank) * size, 128)
             whole[:, pl.ds(start, size)] = piece[:, u * size : (u + 1) * size].astype(F32)
 
 
 def feed_forward(tokens, cot, gate_w, up_w, down_w):
-    count, width = tokens.shape
-    units = gate_w.shape[0]
-    tile = 256
-    whole = pl.BlockSpec((count, width), lambda i: (0, 0))
-    row_tile = pl.BlockSpec((tile, width), lambda i: (i, 0))
-    column_tile = pl.BlockSpec((count, tile), lambda i: (0, i))
-    return pl.pallas_call(
-        forward_backward_kernel,
-        grid=(units // tile,),
-        out_shape=[jax.ShapeDtypeStruct((count, width), BF16)] * 2
-        + [jax.ShapeDtypeStruct((count, units), BF16)] * 3,
-        in_specs=[whole, whole, row_tile, row_tile, pl.BlockSpec((width, tile), lambda i: (0, i))],
-        out_specs=[whole, whole] + [column_tile] * 3,
-        scratch_shapes=[pltpu.VMEM((count, width), F32)] * 2,
-        compiler_params=pltpu.CompilerParams(
-            dimension_semantics=("arbitrary",), vmem_limit_bytes=VMEM_BYTES
-        ),
-        cost_estimate=pl.CostEstimate(
-            flops=12 * count * width * units,
-            bytes_accessed=2 * (4 * count * width + 3 * width * units + 3 * count * units),
-            transcendentals=count * units,
-        ),
-    )(tokens, cot, gate_w, up_w, down_w)
+    act, slope = gelu_parts(project(tokens, gate_w))
+    up_val = project(tokens, up_w)
+    hidden = (act * up_val).astype(BF16)
+    grad_hidden = back_project(cot, down_w)
+    grad_gate = (grad_hidden * up_val * slope).astype(BF16)
+    grad_up = (grad_hidden * act).astype(BF16)
+    grad = (back_project(grad_gate, gate_w) + back_project(grad_up, up_w)).astype(BF16)
+    return grad, hidden, grad_gate, grad_up
 
 
 def shards(
@@ -659,6 +616,16 @@
 
     input_own = block_input.reshape(tokens, width)
     cot_own = cotangent.reshape(tokens, width)
+    half = tokens // 2
+
+    def stacked(value, bit, axis, *pins):
+        got = fence(trade(value, bit), *pins)
+        mine = bit_of(me, bit) == 0
+        return jnp.stack([jnp.where(mine, value, got), jnp.where(mine, got, value)], axis=axis), got
+
+    gains = jnp.stack([mixer_gain, mlp_gain])
+    for i, b in enumerate(tp):
+        gains, gains_got = stacked(gains, b, i)
     packed_width = -(-(2 * block_size + 8) // 128) * 128
     extra = -(-channel_rows // 16) * 16
     small = pl.pallas_call(
@@ -668,41 +635,35 @@
     )(
         conv_kernel,
         *(v[None] for v in (conv_bias, recur_gate_bias, input_gate_bias, decay_param)),
-        mixer_gain[None],
-        mlp_gain[None],
+        gains.reshape(8, out_rows),
         recur_gate_weight,
         input_gate_weight,
     ).astype(BF16)
-    one = small.shape
+    small_shape = small.shape
+    recur_pair = pair_up(recur_weight, above, me, small)
+    recur_q = gather_along(recur_pair, below, 1).reshape(channels, width)
+    one, two = (trade(fence(input_own, recur_pair), mask) for mask in (low, 2 * low))
+    small = fence(small, recur_pair)
     for i, b in enumerate(dp):
-        got = trade(small, b)
+        small, small_got = stacked(small, b, i)
         if i == 0:
-            first_got = got
-        mine = bit_of(me, b) == 0
-        small = jnp.stack([jnp.where(mine, small, got), jnp.where(mine, got, small)], axis=i)
-    small = small.reshape((share,) + one)
-    gains = small[:, extra + TAPS + 4 : extra + TAPS + 6, :out_rows].reshape(high, deep, 2, out_rows)
-    for i, b in enumerate(tp):
-        got = trade(gains, b)
-        mine = bit_of(me, b) == 0
-        gains = jnp.stack([jnp.where(mine, gains, got), jnp.where(mine, got, gains)], axis=i + 1)
-    last_got = got
-    gains = jnp.moveaxis(gains, 4, 0).reshape(2, width)
+            first_got = small_got
+    three = [trade(two[:half], low), trade(one[half:], 2 * low)]
+    piece = exchange(fence(by_rank(mixer_weight, high, 4), recur_pair), step)
+    branch_pair = pair_up(fence(branch_weight, first_got), above, me, piece, small_got, *three)
+    branch_q = gather_along(branch_pair, below, 1).reshape(channels, width)
+    down_piece = exchange(fence(by_rank(down_weight, high_wide, 8), piece), step)
+    mixer_pair = pair_up(fence(piece, branch_pair), above, me, down_piece)
+    mixer_q = gather_along(mixer_pair, below, 2).reshape(width, channels)
+    small = small.reshape((share,) + small_shape)
+    gains = small[:, extra + 8 :, :out_rows].reshape(high, deep, 4, 2, out_rows)
+    gains = gains.transpose(3, 0, 2, 1, 4).reshape(2, width)
     gain_one, gain_two = gains[0].astype(F32), gains[1].astype(F32)
-    numbers = jnp.moveaxis(small[:, extra : extra + TAPS + 4, :channel_rows], 1, 0)
+    numbers = jnp.moveaxis(small[:, extra : extra + 8, :channel_rows], 1, 0)
     numbers = numbers.reshape(TAPS + 4, channels).astype(F32)
     gate_rows = small[:, :channel_rows, : 2 * block_size].reshape(channels, -1)
-
-    input_list = share_list(input_own, low)
-    recur_units, branch_units = gather_units(
-        [fence(recur_weight, first_got), branch_weight], dp, streams.trade
-    )
-    input_all = place_tokens(input_list, low, me)
-    piece = exchange(fence(by_rank(mixer_weight, high, 4), *input_list[1:]), step)
-    (mixer_units,) = gather_units([piece], dp, streams.trade)
-    recur_q, branch_q = place_rows(recur_units), place_rows(branch_units)
-    mixer_q = place_columns(mixer_units)
-    cot_near_list = share_direct(fence(cot_own, input_all), low)
+    input_all = place_tokens([input_own, one, two, *three], low, me)
+    cot_near_list = share_direct(fence(cot_own, three[0]), low)
 
     coef = numbers
     decay_vec = coef[7:]
@@ -756,7 +717,8 @@
         4,
     )
     ends_all = across_blocks(ends.reshape(4, rows, 2, channels)).reshape(-1, 2, channels)
-    branch = project(normed, fence(branch_q, ends)).reshape(blocks, span, channels)
+    branch = project(normed, fence(branch_q, ends, *cot_near_list[1:], cot_far))
+    branch = branch.reshape(blocks, span, channels)
     ends = fence(ends_all, branch)
     state, mixed, came = call(
         functools.partial(state_kernel, rows, step),
@@ -766,10 +728,8 @@
         [pltpu.VMEM(everything, F32)],
         2,
     )
-    cot_far_list = share_direct(fence(cot_far, mixed), low)
-    down_piece = exchange(fence(by_rank(down_weight, high_wide, 8), mixed), step)
     gate_pair, up_pair, down_pair = (
-        pair_up(fence(weight, recur_q), above_wide, me)
+        pair_up(fence(weight, mixer_pair), above_wide, me)
         for weight in (gate_weight, up_weight, down_piece)
     )
     gate_q = gather_along(gate_pair, below, 1).reshape(hidden, width)
@@ -778,7 +738,9 @@
     mixed_flat = mixed.reshape(4 * tokens, channels)
     cot_near = place_tokens(fence_all(cot_near_list, mixed), low, me)
     mixer_part = project(mixed_flat, mixer_q).astype(BF16).reshape(4, tokens, width)
-    residual = input_own.astype(F32) + sum_tokens(mixer_part, step)
+    cot_far_list = share_direct(fence(cot_far, mixer_part), low)
+    mixer_parts = fence(exchange(mixer_part, step), *cot_far_list[1:])
+    residual = input_own.astype(F32) + jnp.sum(mixer_parts.astype(F32), axis=0)
 
 
     scale_two = inverse_rms(residual)
@@ -786,14 +748,14 @@
     normed_own = (unit_two * gain_two).astype(BF16)
     normed_far = trade(normed_own, wide)
     near_list = share_direct(normed_own, low)
-    far_list = share_direct(fence(normed_far, *near_list[1:]), low)
+    far_list = share_direct(normed_far, low)
     near = place_tokens(near_list, low, me)
     cot_far = place_tokens(fence_all(cot_far_list, normed_own), low, me)
     near_out = feed_forward(near, cot_near, gate_q, up_q, down_q)
     ranks_shape = (4, tokens, width)
-    far = place_tokens(far_list, low, me)
+    far = place_tokens(fence_all(far_list, near_out[0]), low, me)
     far_out = feed_forward(far, cot_far, gate_q, up_q, down_q)
-    grad_far_parts = exchange(far_out[1].reshape(ranks_shape), step)
+    grad_far_parts = exchange(far_out[0].reshape(ranks_shape), step)
 
     def finish(partial, bits):
         partial = partial.reshape((2,) * len(bits) + partial.shape[1:])
@@ -805,12 +767,13 @@
     def both(one, two, k):
         return outer(one[k], near) + outer(two[k], far)
 
-    down_grad = outer(cot_near, near_out[2]) + outer(cot_far, far_out[2])
+    down_grad = outer(cot_near, near_out[1]) + outer(cot_far, far_out[1])
     down_grad = down_grad.astype(BF16).reshape(high_wide, 8, -1, hidden)
     grad_far_parts = fence(grad_far_parts, down_grad)
     down_grad = finish(scatter_along(down_grad, below, 2), above_wide).reshape(8, out_rows, hidden)
     grad_two_far = jnp.sum(grad_far_parts.astype(F32), axis=0).astype(BF16)
-    grad_two_near = sum_tokens(fence(near_out[1], grad_two_far).reshape(ranks_shape), step)
+    grad_near_parts = exchange(fence(near_out[0], grad_two_far).reshape(ranks_shape), step)
+    grad_two_near = jnp.sum(grad_near_parts.astype(F32), axis=0)
     grad_two = grad_two_near + trade(grad_two_far, wide).astype(F32)
     scaled = grad_two * gain_two
     grad_residual = cot_own.astype(F32) + scale_two * (
@@ -820,15 +783,15 @@
 
     grad_mix_own = grad_residual.astype(BF16)
     grad_mix_list = share_list(grad_mix_own, low)
-    late = [fence_all(out[3:], grad_mix_own) for out in (near_out, far_out)]
+    down_far = project(fence(far_out[1], grad_mix_own), down_q).astype(BF16)
+    late = [fence_all(out[2:], grad_mix_own) for out in (near_out, far_out)]
     gate_grad = both(*late, 0).astype(BF16).reshape(high_wide, -1, width)
     up_grad = both(*late, 1).astype(BF16).reshape(high_wide, -1, width)
-    down_far = fence(far_out[0].reshape(ranks_shape), grad_mix_list[1], grad_mix_list[2])
-    down_far = exchange(down_far, step)
+    down_far_parts = exchange(fence(down_far, *grad_mix_list[1:3]).reshape(ranks_shape), step)
     down_parts = fence(down_grad, grad_mix_own).reshape(2, 4, out_rows, hidden)
     down_sent, down_kept = halves(down_parts, 0, wide, me)
     down_got = trade(down_sent, wide)
-    grad_mix = place_tokens(fence_all(grad_mix_list, gate_grad, up_grad, down_got), low, me)
+    grad_mix = place_tokens(fence_all(grad_mix_list, down_got, gate_grad, up_grad, down_far), low, me)
     gate_grad = finish(scatter_along(gate_grad, below, 1), above_wide)
     up_grad = finish(scatter_along(up_grad, below, 1), above_wide)
     grad_mixed = back_project(grad_mix, mixer_q).reshape(shape)
@@ -842,9 +805,12 @@
     )
     ends_back = across_blocks(own_ends.reshape(4, rows, 2, channels)).reshape(-1, 2, channels)
     grad_branch = grad_branch.reshape(4 * tokens, channels)
-    branch_grad = reduce_rows(outer(grad_branch, normed), dp, me)
-    mixer_grad = reduce_columns(outer(fence(grad_mix, own_ends), mixed_flat), dp, 4, low, me)
-    ends_back = fence(ends_back, branch_grad.send(), mixer_grad.send())
+    mixer_grad = outer(fence(grad_mix, own_ends), mixed_flat).astype(BF16)
+    mixer_grad = mixer_grad.reshape(high, 4, -1, channels)
+    down_far = jnp.sum(fence(down_far_parts, own_ends).astype(F32), axis=0).astype(BF16)
+    ends_back = fence(ends_back, mixer_grad, down_far)
+    mixer_grad = scatter_along(mixer_grad, below, 2)
+    down_far_own = trade(down_far, wide)
     packed_shape = (channels, packed_width)
     grad_conv, edge_back, packed = call(
         functools.partial(gates_kernel, rows, step),
@@ -865,15 +831,15 @@
         4,
     )
     edge_back = edge_back.reshape(4, rows, 4, channels)
-    down_far = jnp.sum(fence(down_far, edge_back).astype(F32), axis=0).astype(BF16)
-    down_far_own = trade(down_far, wide)
-    down_near = fence(near_out[0].reshape(ranks_shape), edge_back)
+    down_near = project(fence(near_out[1], own_ends), down_q).astype(BF16).reshape(ranks_shape)
+    down_near = fence(down_near, edge_back)
     down_near = [pick(down_near, jnp.bitwise_xor(tp_index, j), 0) for j in range(4)]
     down_near[1:] = [trade(down_near[j], j * low) for j in (1, 2, 3)]
     halo_back = across_blocks(edge_back)
     last = len(dp)
-    aways = [grad.send_to(last - 2, edge_back) for grad in (mixer_grad, branch_grad)]
-    halo_back = fence(halo_back, *aways, down_far)
+    branch_grad = outer(fence(grad_branch, edge_back), normed).astype(BF16).reshape(high, -1, width)
+    halo_back = fence(halo_back, down_far_own, branch_grad)
+    branch_grad = scatter_along(branch_grad, below, 1)
     halo_back = halo_back.astype(F32).reshape(seq_count * rows, 4, channels)
     (grad_recur,) = call(
         functools.partial(unconvolve_kernel, rows, step, seq_count),
@@ -888,9 +854,9 @@
     grad_recur = fence(grad_recur, recur_grad.send())
     grad_normed_part = back_project(grad_branch, branch_q) + back_project(grad_recur, recur_q)
     grad_normed_sent = grad_normed_part.astype(BF16)
-    aways = [grad.send_to(0, grad_recur) for grad in (mixer_grad, branch_grad)]
-    aways.append(recur_grad.send_to(last - 2, grad_normed_sent))
-    grad_normed_sent = fence(grad_normed_sent, *aways, down_far_own)
+    recur_sent = recur_grad.send_to(last - 2, grad_normed_sent)
+    packed = reduce_rows(fence(packed, grad_recur), dp, me)
+    grad_normed_sent = fence(grad_normed_sent, recur_sent, packed.send())
     gain_one_part = jnp.sum(grad_normed_sent.astype(F32) * input_all.astype(F32) * scale_one, axis=0)
     grad_normed = sum_tokens(grad_normed_sent.reshape(ranks_shape), step)
     own_scale = inverse_rms(input_own.astype(F32))
@@ -901,37 +867,38 @@
         + own_scale
         * (scaled_one - unit_one * jnp.mean(scaled_one * unit_one, axis=-1, keepdims=True))
     ).astype(BF16)
-    packed = reduce_rows(fence(packed, grad_normed_sent), dp, me)
-    packed_sent = packed.send_to(last - 2)
-    sent = recur_grad.send_to(0, packed_sent)
+    def halve(partial):
+        partial = fence(partial, grad_normed).reshape((2,) * len(above) + partial.shape[1:])
+        return Reduction(partial, range(len(above)), above, me)
+
+    mixer_grad, branch_grad = halve(mixer_grad), halve(branch_grad)
+    mixer_sent = mixer_grad.send_to(0)
+    recur_sent = recur_grad.send_to(0, grad_normed, mixer_sent)
+    sent = branch_grad.send_to(0, recur_sent)
     packed_sent = packed.send_to(0, sent)
-    down_got, down_kept = fence_all([down_got, down_kept], packed_sent)
-    down_pieces = []
-    for j in range(4):
-        peer = jnp.bitwise_xor(tp_index, j)
-        pair = jnp.stack([pick(down_kept, peer, 0), pick(down_got, peer, 0)])
-        down_pieces.append(trade(pair, j * low) if j else pair)
-    down_sum = sum(fence(part, packed_sent).astype(F32) for part in down_near + [down_far_own])
-    block_output = (residual + down_sum).astype(BF16)
-    branch_weight_grad = branch_grad.total(block_output)
+    pair = jnp.stack([fence(part, packed_sent) for part in (down_kept, down_got)], axis=1)
+    pair = exchange(pair, step)
     own_half = number_of(me, (wide,))
-    flat_pieces = [pair[h] for h in range(2) for pair in down_pieces]
+    flat_pieces = [pair[j, h] for h in range(2) for j in range(4)]
     down_weight_grad = pl.pallas_call(
-        functools.partial(lay_kernel, 8, high_wide),
+        functools.partial(lay_kernel, 4, high_wide),
         out_shape=jax.ShapeDtypeStruct((out_rows, 8 * hidden), F32),
         in_specs=[pl.BlockSpec(memory_space=pltpu.SMEM)]
         + [pl.BlockSpec(memory_space=pltpu.VMEM)] * len(flat_pieces),
         out_specs=pl.BlockSpec(memory_space=pltpu.VMEM),
         compiler_params=pltpu.CompilerParams(vmem_limit_bytes=VMEM_BYTES),
-    )((own_half * 4 + tp_index).reshape(1), *flat_pieces)
-    recur_weight_grad = recur_grad.total(branch_weight_grad)
-    packed = packed.total(branch_weight_grad)
-    mixer_grad = mixer_grad.total(branch_weight_grad).astype(BF16).reshape(4, out_rows, channels)
-    mixer_weight_grad = join_ranks(fence(mixer_grad, grad_normed), high)
+    )(own_half.reshape(1), *flat_pieces)
+    mixer_rows = mixer_grad.total(sent).astype(BF16).reshape(4, out_rows, channels)
+    mixer_weight_grad = join_ranks(mixer_rows, high)
+    down_sum = sum(fence(part, mixer_rows).astype(F32) for part in down_near + [down_far_own])
+    block_output = (residual + down_sum).astype(BF16)
+    recur_weight_grad = recur_grad.total(mixer_rows)
+    branch_weight_grad = branch_grad.total(recur_weight_grad)
+    packed = packed.total(recur_weight_grad)
 
     gain_parts = jnp.stack([gain_one_part, gain_two_part]).astype(BF16)
     gain_parts = jnp.moveaxis(gain_parts.reshape(2, device_count, out_rows), 1, 0)
-    gain_parts = lax.all_to_all(fence(gain_parts, grad_normed), AXES, 0, 0, tiled=True)
+    gain_parts = lax.all_to_all(fence(gain_parts, sent), AXES, 0, 0, tiled=True)
     gain_grads = jnp.sum(gain_parts.astype(F32), axis=0)
     numbers = packed[:, 2 * block_size : 2 * block_size + 8]
     return (

time: 696 us -> 637 us (0.915)
  Pallas kernels: 122 us -> 67.1 us
  matrix products: 50.2 us -> 105 us
  waiting for transfers between devices: 285 us -> 232 us
    ppermute x73 -> x48, waiting for transfers between devices: 220 us -> 159 us  [trade(): return lax.ppermute(value, AXES, [(i, i ^ mask) for i in range(count)])]
    pallas_call x3 -> x1, Pallas kernels: 45.9 us -> 2.46 us  [shards(): pl.pallas_call(functools.partial(lay_kernel, 4, high_wide), out_shape=jax...]
    dot_general x3 -> x9, matrix products: 13.8 us -> 41.6 us  [project(): lax.dot_general(left, weight, (((1,), (1,)), ((), ())), preferred_element...]
    dot_general x3 -> x9, matrix products: 8.11 us -> 34.4 us  [back_project(): lax.dot_general(left, weight, (((1,), (0,)), ((), ())), preferred_element...]
    ppermute x73 -> x48, starting transfers between devices: 67.7 us -> 53 us  [trade(): return lax.ppermute(value, AXES, [(i, i ^ mask) for i in range(count)])]
    all_to_all x8 -> x9, starting transfers between devices: 42 us -> 55.8 us  [exchange(): lax.all_to_all(parts, 'seq', 0, 0, axis_index_groups=groups, tiled=True)]
    all_to_all x1, waiting for transfers between devices: 0.01 us -> 12.9 us  [shards(): gain_parts = lax.all_to_all(fence(gain_parts, sent), AXES, 0, 0, tiled=True)]
    pallas_call x9 -> x6, Pallas kernels: 27.4 us -> 17.6 us  [assemble(): pl.pallas_call(functools.partial(copy_kernel, len(pieces), shapes, places...]
  transfers between devices with their start and end apart: 88 -> 69, of which waited for: 36 -> 25; matrix products, arithmetic and copies ran while one was open for 19% -> 28% of each run, Pallas kernels for 17% -> 10%
where the time goes in v4:
time: 637 us; the launch traced here: 627 us
  waiting for transfers between devices  232 us (36%)
  starting transfers between devices  115 us (18%)
  matrix products  105 us (16%)
  Pallas kernels  67.1 us (11%)
  other arithmetic  50 us (8%)
  local copies, waits for them, and re-layouts  43 us (7%)
  between operations  15.4 us (2%)
    ppermute x48, waiting for transfers between devices, trade(): return lax.ppermute(value, AXES, [(i, i ^ mask) for i in range(count)])  159 us
    all_to_all x9, waiting for transfers between devices, exchange(): lax.all_to_all(parts, 'seq', 0, 0, axis_index_groups=groups, tiled=True)  59.5 us
    all_to_all x9, starting transfers between devices, exchange(): lax.all_to_all(parts, 'seq', 0, 0, axis_index_groups=groups, tiled=True)  55.8 us
    ppermute x48, starting transfers between devices, trade(): return lax.ppermute(value, AXES, [(i, i ^ mask) for i in range(count)])  53 us
    pallas_call x5, Pallas kernels, call(): pl.pallas_call(body, out_shape=[jax.ShapeDtypeStruct(shape, kind) for sha...  45.4 us
    dot_general x9, matrix products, project(): lax.dot_general(left, weight, (((1,), (1,)), ((), ())), preferred_element...  41.6 us
    dot_general x9, matrix products, back_project(): lax.dot_general(left, weight, (((1,), (0,)), ((), ())), preferred_element...  34.4 us
    dot_general x9, matrix products, outer(): lax.dot_general(grads, values, (((0,), (0,)), ((), ())), preferred_elemen...  28.9 us
  transfers between devices with their start and end apart: 69, of which 25 were waited for; matrix products, arithmetic and copies ran while one was open for 28% of the time, Pallas kernels for 10%

profile of v4, /device:TPU:20, one launch (start us, length us, event | category | flops | bytes accessed | tf_op | source)
XLA Modules:
  0.0 627.3 jit_solution(11814129626591131273)
XLA Ops:
  10.0 6.9 %collective-permute-done.1 = bf16[2,64]{1,0:T(2,128)(2,1)S(1)} collective-permute-done((bf16[2,64]{1,0:T(2,128)(2,1)S(1)}, bf16[2,64]{1,0:T(2,128)(2,1)S(1)}, u32[]{:S(2)}, u32[]{:S(2)}) %collective-permute-start.1) | collective-permute-done | bytes 288 | tf_op jit(solution)/shard_map/ppermute | solution.py:55
  27.2 4.6 collective-permute-done.7
  38.1 4.9 all-to-all-start
  44.7 8.2 %collective-permute-done.4.refs_2_ = bf16[128,2048]{1,0:T(8,128)(2,1)S(1)} collective-permute-done((bf16[128,2048]{1,0:T(8,128)(2,1)S(1)}, bf16[128,2048]{1,0:T(8,128)(2,1)S(1)}, u32[]{:S(2)}, u32[]{:S(2)}) %collective-permute-start.4) | collective-permute-done | bytes 524320 | tf_op jit(solution)/shard_map/ppermute | solution.py:55
  54.1 3.0 collective-permute-start.6
  60.2 3.1 collective-permute-done.6.refs_4_
  67.7 6.3 %all-to-all-start.1 = ((bf16[8,64,768]{2,1,0:T(8,128)(2,1)}), bf16[8,64,768]{2,1,0:T(8,128)(2,1)S(1)}, u32[]{:S(2)}, u32[]{:S(2)}) async-start(bf16[8,64,768]{2,1,0:T(8,128)(2,1)} %copy.117), calls=%async_computation.1 | async-start | bytes 1572864 | tf_op jit(solution)/shard_map/all_to_all | solution.py:223
  74.5 28.6 %collective-permute-done.17 = bf16[4,64,640]{2,1,0:T(8,128)(2,1)S(1)} collective-permute-done((bf16[4,64,640]{2,1,0:T(8,128)(2,1)S(1)}, bf16[4,64,640]{2,1,0:T(8,128)(2,1)S(1)}, u32[]{:S(2)}, u32[]{:S(2)}) %collective-permute-start.17) | collective-permute-done | bytes 327712 | tf_op jit(solution)/shard_map/ppermute | solution.py:55
  105.8 3.4 collective-permute-start.16
  120.5 3.6 convolution_convert_fusion.6
  125.0 17.9 %collective-permute-done.10 = bf16[4,2,4,640]{3,2,1,0:T(4,128)(2,1)S(1)} collective-permute-done((bf16[4,2,4,640]{3,2,1,0:T(4,128)(2,1)S(1)}, bf16[4,2,4,640]{3,2,1,0:T(4,128)(2,1)S(1)}, u32[]{:S(2)}, u32[]{:S(2)}) %collective-permute-start.10) | collective-permute-done | bytes 40992 | tf_op jit(solution)/shard_map/ppermute | solution.py:55
  143.6 12.8 %shard_map.343 = (bf16[8,64,640]{2,1,0:T(8,128)(2,1)}, f32[8,64,640]{2,1,0:T(8,128)}, f32[8,64,640]{2,1,0:T(8,128)}, f32[8,64,640]{2,1,0:T(8,128)}, f32[8,64,640...) custom-call(s32[5]{0:T(128)} %pad_add_fusion.scalars, ...), custom_call_target="tpu_custom_call" | custom-call | bytes 39550976 | tf_op jit(solution)/shard_map/pallas_call | solution.py:257
  156.5 5.1 collective-permute-done.11
  163.1 4.7 fusion.43
  167.7 4.3 shard_map.344
  172.1 5.2 convolution_convert_fusion.5
  177.3 5.0 all-to-all-start.2
  182.9 3.0 shard_map.346
  192.0 2.9 fusion.50
  195.0 21.9 %collective-permute-done.18.refs_1_ = bf16[128,2048]{1,0:T(8,128)(2,1)S(1)} collective-permute-done((bf16[128,2048]{1,0:T(8,128)(2,1)}, bf16[128,2048]{1,0:T(8,128)(2,1)S(1)}, u32[]{:S(2)}, u32[]{:S(2)}) %collective-permute-start.18) | collective-permute-done | bytes 524320 | tf_op jit(solution)/shard_map/ppermute | solution.py:55
  219.3 7.2 %collective-permute-done.20.refs_3_ = bf16[128,2048]{1,0:T(8,128)(2,1)} collective-permute-done((bf16[128,2048]{1,0:T(8,128)(2,1)}, bf16[128,2048]{1,0:T(8,128)(2,1)}, u32[]{:S(2)}, u32[]{:S(2)}) %collective-permute-start.20) | collective-permute-done | bytes 524320 | tf_op jit(solution)/shard_map/ppermute | solution.py:55
  238.2 4.5 fusion.52
  242.8 25.4 %collective-permute-done.24.refs_0_ = bf16[128,2048]{1,0:T(8,128)(2,1)S(1)} collective-permute-done((bf16[128,2048]{1,0:T(8,128)(2,1)S(1)}, bf16[128,2048]{1,0:T(8,128)(2,1)S(1)}, u32[]{:S(2)}, u32[]{:S(2)}) %collective-permute-start.24) | collective-permute-done | bytes 524320 | tf_op jit(solution)/shard_map/ppermute | solution.py:55
  268.2 3.5 collective-permute-start.27
  273.3 2.9 shard_map.345
  276.3 5.5 fusion.49
  281.8 6.3 %multiply_convert_fusion.3 = (bf16[512,768]{1,0:T(8,128)(2,1)S(1)}, bf16[512,768]{1,0:T(8,128)(2,1)S(1)}, bf16[512,768]{1,0:T(8,128)(2,1)S(1)}) fusion(f32[512,768]{1,0:T(8,128)} %fusion.49, f32[512,768]{1,0:T(8,128)} %fusion.50, bf16[512,2048]{1,0:T(8,128)(2,1)} %shard_map.345, bf16[768,2048]{1,0:T(8,128)(2,1)} %all-gather.18.cloned.1.call-done), kind=kOutput, calls=%fused_computation.48 | convolution fusion | flops 1620443136 | bytes 10747904 | tf_op jit(solution)/shard_map/dot_general | solution.py:231
  290.9 3.4 add_convert_fusion.5
  295.0 3.0 shard_map.348
  298.0 4.5 fusion.53
  302.6 2.9 multiply_convert_fusion.1
  308.2 3.2 add_convert_fusion.4
  311.4 4.4 all-to-all-start.3
  315.9 3.6 fusion.55
  319.5 3.5 add_convert_fusion.2
  323.1 10.7 %all-to-all-done.3 = bf16[4,128,2048]{2,1,0:T(8,128)(2,1)} async-done(((bf16[4,128,2048]{2,1,0:T(8,128)(2,1)}), bf16[4,128,2048]{2,1,0:T(8,128)(2,1)}, u32[]{:S(2)}, u32[]{:S(2)}) %all-to-all-start.3) | async-done | bytes 2097184 | tf_op jit(solution)/shard_map/all_to_all | solution.py:223
  335.8 5.0 all-to-all-start.4
  342.0 31.0 %all-to-all-done.4 = bf16[4,128,2048]{2,1,0:T(8,128)(2,1)} async-done(((bf16[4,128,2048]{2,1,0:T(8,128)(2,1)}), bf16[4,128,2048]{2,1,0:T(8,128)(2,1)}, u32[]{:S(2)}, u32[]{:S(2)}) %all-to-all-start.4) | async-done | bytes 2097184 | tf_op jit(solution)/shard_map/all_to_all | solution.py:223
  380.2 3.5 fusion.5
  384.8 3.6 fusion.57
  388.4 3.5 fusion.6
  398.3 13.3 %collective-permute-done.30.refs_2_ = bf16[128,2048]{1,0:T(8,128)(2,1)S(1)} collective-permute-done((bf16[128,2048]{1,0:T(8,128)(2,1)S(1)}, bf16[128,2048]{1,0:T(8,128)(2,1)S(1)}, u32[]{:S(2)}, u32[]{:S(2)}) %collective-permute-start.30) | collective-permute-done | bytes 524320 | tf_op jit(solution)/shard_map/ppermute | solution.py:55
  415.0 5.1 convolution_convert_fusion.4
  420.1 6.4 %all-to-all-start.5 = ((bf16[4,128,2048]{2,1,0:T(8,128)(2,1)}), bf16[4,128,2048]{2,1,0:T(8,128)(2,1)}, u32[]{:S(2)}, u32[]{:S(2)}) async-start(bf16[4,128,2048]{2,1,0:T(8,128)(2,1)} %bitcast.302), calls=%async_computation.6 | async-start | bytes 4194304 | tf_op jit(solution)/shard_map/all_to_all | solution.py:223
  427.2 3.2 shard_map.349
  430.4 4.8 fusion.58.grad_mixed
  435.2 9.1 %shard_map.350 = (bf16[8,64,640]{2,1,0:T(8,128)(2,1)}, f32[8,64,640]{2,1,0:T(8,128)}, f32[8,64,640]{2,1,0:T(8,128)}, f32[8,2,640]{2,1,0:T(2,128)}) custom-call(s32[5]{0:T(128)} %pad_add_fusion.scalars, f32[8,64,640]{2,1,0:T(8,128)} %fusion.58.grad_mixed, f32[8,64,640]{2,1,0:T(8,128)} %get-tuple-element.153.state, f32[8,64,640]{2,1,0:T(8,128)} %bitcast.279, ...), custom_call_target="tpu_custom_call" | custom-call | bytes 25853952 | tf_op jit(solution)/shard_map/pallas_call | solution.py:257
  444.3 3.4 convolution_convert_fusion.2
  454.6 15.5 %shard_map.351 = (f32[8,64,640]{2,1,0:T(8,128)}, bf16[8,4,640]{2,1,0:T(4,128)(2,1)}, bf16[640,384]{1,0:T(8,128)(2,1)}) custom-call(s32[5]{0:T(128)} %pad_add_fusion.scalars, f32[8,64,640]{2,1,0:T(8,128)} %get-tuple-element.158.prod, f32[8,64,640]{2,1,0:T(8,128)} %get-tuple-element.159.part, f32[16,2,640]{2,1,0:T(2,128)} %bitcast.316, ...), custom_call_target="tpu_custom_call" | custom-call | bytes 59129856 | tf_op jit(solution)/shard_map/pallas_call | solution.py:257
  470.2 3.3 convolution_convert_fusion.1
  476.1 3.6 shard_map.352
  483.9 5.6 fusion.59
  491.4 6.4 %add_convert_fusion.3 = bf16[512,2048]{1,0:T(8,128)(2,1)} fusion(f32[512,2048]{1,0:T(8,128)} %fusion.59, bf16[512,640]{1,0:T(8,128)(2,1)} %bitcast.311, bf16[640,2048]{1,0:T(8,128)(2,1)} %bitcast.343), kind=kOutput, calls=%fused_computation.12 | convolution fusion | flops 1344274432 | bytes 9568256 | tf_op jit(solution)/shard_map/dot_general | solution.py:235
  500.7 14.3 %all-to-all-start.6 = ((bf16[4,128,2048]{2,1,0:T(8,128)(2,1)}), bf16[4,128,2048]{2,1,0:T(8,128)(2,1)}, u32[]{:S(2)}, u32[]{:S(2)}) async-start(bf16[4,128,2048]{2,1,0:T(8,128)(2,1)} %bitcast.277), calls=%async_computation.8 | async-start | bytes 4194304 | tf_op jit(solution)/shard_map/all_to_all | solution.py:223
  515.8 3.8 convolution_convert_fusion.3
  530.2 10.8 %all-to-all-done.6 = bf16[4,128,2048]{2,1,0:T(8,128)(2,1)} async-done(((bf16[4,128,2048]{2,1,0:T(8,128)(2,1)}), bf16[4,128,2048]{2,1,0:T(8,128)(2,1)}, u32[]{:S(2)}, u32[]{:S(2)}) %all-to-all-start.6) | async-done | bytes 2097184 | tf_op jit(solution)/shard_map/all_to_all | solution.py:223
  544.9 5.8 collective-permute-done.43
  556.6 4.9 all-to-all-start.7
  563.9 12.9 %all-to-all-done.7 = bf16[32,2,64]{2,1,0:T(2,128)(2,1)S(1)} async-done(((bf16[32,2,64]{2,1,0:T(2,128)(2,1)}), bf16[32,2,64]{2,1,0:T(2,128)(2,1)S(1)}, u32[]{:S(2)}, u32[]{:S(2)}) %all-to-all-start.7) | async-done | bytes 8224 | tf_op jit(solution)/shard_map/all_to_all | solution.py:901
  577.4 3.3 collective-permute-start.42
  582.6 4.3 all-to-all-start.8
  587.4 4.0 fusion.27
  595.5 6.0 all-to-all-done.8
  601.5 5.2 all-to-all-start.9
  (392 shorter events, 160.5 us)
Async XLA Ops:
  7.2 113.3 %all-gather.10.cloned.1.call-start = ((), (), s32[]{:S(2)}) async-start(), calls=%async_computation.15 | async-start | bytes 3276800 | tf_op jit(solution)/shard_map/all_gather | solution.py:203
  7.2 17.2 %collective-permute-start = (bf16[80,2048]{1,0:T(8,128)(2,1)}, bf16[80,2048]{1,0:T(8,128)(2,1)S(1)}, u32[]{:S(2)}, u32[]{:S(2)}) collective-permute-start(bf16[80,2048]{1,0:T(8,128)(2,1)} %param.26), channel_id=1, source_target_pairs={{0,16},{1,17},{2,18},{3,19},{4,20},{5,21},{6,22},{7,23},{8,24},{9,... | collective-permute-start | bytes 983048 | tf_op jit(solution)/shard_map/ppermute | solution.py:55
  8.3 8.6 %collective-permute-start.1 = (bf16[2,64]{1,0:T(2,128)(2,1)S(1)}, bf16[2,64]{1,0:T(2,128)(2,1)S(1)}, u32[]{:S(2)}, u32[]{:S(2)}) collective-permute-start(bf16[2,64]{1,0:T(2,128)(2,1)S(1)} %pad_maximum_fusion.13), channel_id=1, source_target_pairs={{0,8},{1,9},{2,10},{3,11},{4,12},{5,13},{6,14},{7,15},{8,0},{9,1},... | collective-permute-start | bytes 776 | tf_op jit(solution)/shard_map/ppermute | solution.py:55
  31.9 11.7 %collective-permute-start.8 = (bf16[2,96,384]{2,1,0:T(8,128)(2,1)S(1)}, bf16[2,96,384]{2,1,0:T(8,128)(2,1)}, u32[]{:S(2)}, u32[]{:S(2)}) collective-permute-start(bf16[2,96,384]{2,1,0:T(8,128)(2,1)S(1)} %pad_maximum_fusion.6), channel_id=1, source_target_pairs={{0,2},{1,3},{2,0},{3,1},{4,6},{5,7},{6,4},{7,5},{8,10},{9,11},{10,... | collective-permute-start | bytes 442376 | tf_op jit(solution)/shard_map/ppermute | solution.py:55
  33.5 19.4 %collective-permute-start.4 = (bf16[128,2048]{1,0:T(8,128)(2,1)S(1)}, bf16[128,2048]{1,0:T(8,128)(2,1)S(1)}, u32[]{:S(2)}, u32[]{:S(2)}) collective-permute-start(bf16[128,2048]{1,0:T(8,128)(2,1)S(1)} %bitcast.274), channel_id=1, source_target_pairs={{0,8},{1,9},{2,10},{3,11},{4,12},{5,13},{6,14},{7,15},{8,0},{9,1},... | collective-permute-start | bytes 1572872 | tf_op jit(solution)/shard_map/ppermute | solution.py:55
  35.9 18.2 %collective-permute-start.3 = (bf16[128,2048]{1,0:T(8,128)(2,1)S(1)}, bf16[128,2048]{1,0:T(8,128)(2,1)S(1)}, u32[]{:S(2)}, u32[]{:S(2)}) collective-permute-start(bf16[128,2048]{1,0:T(8,128)(2,1)S(1)} %bitcast.275), channel_id=1, source_target_pairs={{0,4},{1,5},{2,6},{3,7},{4,0},{5,1},{6,2},{7,3},{8,12},{9,13},{10,... | collective-permute-start | bytes 1572872 | tf_op jit(solution)/shard_map/ppermute | solution.py:55
  38.1 21.3 %all-to-all-start = ((bf16[4,64,640]{2,1,0:T(8,128)(2,1)}), bf16[4,64,640]{2,1,0:T(8,128)(2,1)S(1)}, u32[]{:S(2)}, u32[]{:S(2)}) async-start(bf16[4,64,640]{2,1,0:T(8,128)(2,1)} %reshape.339), calls=%async_computation | async-start | bytes 655360 | tf_op jit(solution)/shard_map/all_to_all | solution.py:223
  43.1 120.0 %all-gather.12.cloned.1.call-start = ((), (), s32[]{:S(2)}) async-start(), calls=%async_computation.16 | async-start | bytes 3276800 | tf_op jit(solution)/shard_map/all_gather | solution.py:203
  43.1 16.4 %collective-permute-start.12 = (bf16[80,2048]{1,0:T(8,128)(2,1)S(1)}, bf16[80,2048]{1,0:T(8,128)(2,1)}, u32[]{:S(2)}, u32[]{:S(2)}) collective-permute-start(bf16[80,2048]{1,0:T(8,128)(2,1)S(1)} %copy-done.51), channel_id=1, source_target_pairs={{0,16},{1,17},{2,18},{3,19},{4,20},{5,21},{6,22},{7,23},{8,24},{9,... | collective-permute-start | bytes 983048 | tf_op jit(solution)/shard_map/ppermute | solution.py:55
  44.6 12.5 %collective-permute-start.9 = (bf16[2,2,96,384]{3,2,0,1:T(8,128)(2,1)S(1)}, bf16[2,2,96,384]{3,2,0,1:T(8,128)(2,1)S(1)}, u32[]{:S(2)}, u32[]{:S(2)}) collective-permute-start(bf16[2,2,96,384]{3,2,0,1:T(8,128)(2,1)S(1)} %pad_maximum_fusion.5), channel_id=1, source_target_pairs={{0,1},{1,0},{2,3},{3,2},{4,5},{5,4},{6,7},{7,6},{8,9},{9,8},{10,11... | collective-permute-start | bytes 884744 | tf_op jit(solution)/shard_map/ppermute | solution.py:55
  53.6 6.6 %collective-permute-start.5 = (bf16[64,2048]{1,0:T(8,128)(2,1)}, bf16[64,2048]{1,0:T(8,128)(2,1)S(1)}, u32[]{:S(2)}, u32[]{:S(2)}) collective-permute-start(bf16[64,2048]{1,0:T(8,128)(2,1)} %slice.137), channel_id=1, source_target_pairs={{0,4},{1,5},{2,6},{3,7},{4,0},{5,1},{6,2},{7,3},{8,12},{9,13},{10,... | collective-permute-start | bytes 786440 | tf_op jit(solution)/shard_map/ppermute | solution.py:55
  54.1 9.2 %collective-permute-start.6 = (bf16[64,2048]{1,0:T(8,128)(2,1)S(1)}, bf16[64,2048]{1,0:T(8,128)(2,1)S(1)}, u32[]{:S(2)}, u32[]{:S(2)}) collective-permute-start(bf16[64,2048]{1,0:T(8,128)(2,1)S(1)} %slice.138), channel_id=1, source_target_pairs={{0,8},{1,9},{2,10},{3,11},{4,12},{5,13},{6,14},{7,15},{8,0},{9,1},... | collective-permute-start | bytes 786440 | tf_op jit(solution)/shard_map/ppermute | solution.py:55
  67.7 35.5 %all-to-all-start.1 = ((bf16[8,64,768]{2,1,0:T(8,128)(2,1)}), bf16[8,64,768]{2,1,0:T(8,128)(2,1)S(1)}, u32[]{:S(2)}, u32[]{:S(2)}) async-start(bf16[8,64,768]{2,1,0:T(8,128)(2,1)} %copy.117), calls=%async_computation.1 | async-start | bytes 1572864 | tf_op jit(solution)/shard_map/all_to_all | solution.py:223
  74.0 98.1 %all-gather.14.cloned.1.call-start = ((), (), s32[]{:S(2)}) async-start(), calls=%async_computation.17 | async-start | bytes 3276800 | tf_op jit(solution)/shard_map/all_gather | solution.py:203
  74.0 29.2 %collective-permute-start.17 = (bf16[4,64,640]{2,1,0:T(8,128)(2,1)S(1)}, bf16[4,64,640]{2,1,0:T(8,128)(2,1)S(1)}, u32[]{:S(2)}, u32[]{:S(2)}) collective-permute-start(bf16[4,64,640]{2,1,0:T(8,128)(2,1)S(1)} %all-to-all-done), channel_id=1, source_target_pairs={{0,16},{1,17},{2,18},{3,19},{4,20},{5,21},{6,22},{7,23},{8,24},{9,... | collective-permute-start | bytes 983048 | tf_op jit(solution)/shard_map/ppermute | solution.py:55
  104.2 85.3 %all-gather.20.cloned.1.call-start = ((), (), s32[]{:S(2)}) async-start(), calls=%async_computation.25 | async-start | bytes 3932160 | tf_op jit(solution)/shard_map/all_gather | solution.py:203
  105.6 170.7 %all-gather.16.cloned.1.call-start = ((), (), s32[]{:S(2)}) async-start(), calls=%async_computation.23 | async-start | bytes 3932160 | tf_op jit(solution)/shard_map/all_gather | solution.py:203
  105.8 57.2 %collective-permute-start.16 = (bf16[128,2048]{1,0:T(8,128)(2,1)S(1)}, bf16[128,2048]{1,0:T(8,128)(2,1)}, u32[]{:S(2)}, u32[]{:S(2)}) collective-permute-start(bf16[128,2048]{1,0:T(8,128)(2,1)S(1)} %bitcast.297), channel_id=1, source_target_pairs={{0,16},{1,17},{2,18},{3,19},{4,20},{5,21},{6,22},{7,23},{8,24},{9,... | collective-permute-start | bytes 1572872 | tf_op jit(solution)/shard_map/ppermute | solution.py:55
  111.9 51.1 %collective-permute-start.13 = (bf16[128,2048]{1,0:T(8,128)(2,1)S(1)}, bf16[128,2048]{1,0:T(8,128)(2,1)}, u32[]{:S(2)}, u32[]{:S(2)}) collective-permute-start(bf16[128,2048]{1,0:T(8,128)(2,1)S(1)} %bitcast.298), channel_id=1, source_target_pairs={{0,4},{1,5},{2,6},{3,7},{4,0},{5,1},{6,2},{7,3},{8,12},{9,13},{10,... | collective-permute-start | bytes 1572872 | tf_op jit(solution)/shard_map/ppermute | solution.py:55
  112.6 50.4 %collective-permute-start.14 = (bf16[128,2048]{1,0:T(8,128)(2,1)S(1)}, bf16[128,2048]{1,0:T(8,128)(2,1)}, u32[]{:S(2)}, u32[]{:S(2)}) collective-permute-start(bf16[128,2048]{1,0:T(8,128)(2,1)S(1)} %bitcast.299), channel_id=1, source_target_pairs={{0,8},{1,9},{2,10},{3,11},{4,12},{5,13},{6,14},{7,15},{8,0},{9,1},... | collective-permute-start | bytes 1572872 | tf_op jit(solution)/shard_map/ppermute | solution.py:55
  112.6 50.4 %collective-permute-start.15 = (bf16[128,2048]{1,0:T(8,128)(2,1)S(1)}, bf16[128,2048]{1,0:T(8,128)(2,1)}, u32[]{:S(2)}, u32[]{:S(2)}) collective-permute-start(bf16[128,2048]{1,0:T(8,128)(2,1)S(1)} %bitcast.300), channel_id=1, source_target_pairs={{0,12},{1,13},{2,14},{3,15},{4,8},{5,9},{6,10},{7,11},{8,4},{9,5},... | collective-permute-start | bytes 1572872 | tf_op jit(solution)/shard_map/ppermute | solution.py:55
  124.2 18.7 %collective-permute-start.10 = (bf16[4,2,4,640]{3,2,1,0:T(4,128)(2,1)S(1)}, bf16[4,2,4,640]{3,2,1,0:T(4,128)(2,1)S(1)}, u32[]{:S(2)}, u32[]{:S(2)}) collective-permute-start(bf16[4,2,4,640]{3,2,1,0:T(4,128)(2,1)S(1)} %bitcast.319), channel_id=1, source_target_pairs={{0,16},{1,17},{2,18},{3,19},{4,20},{5,21},{6,22},{7,23},{8,24},{9,... | collective-permute-start | bytes 122888 | tf_op jit(solution)/shard_map/ppermute | solution.py:55
  177.3 49.2 %all-to-all-start.2 = ((bf16[4,128,2048]{2,1,0:T(8,128)(2,1)}), bf16[4,128,2048]{2,1,0:T(8,128)(2,1)}, u32[]{:S(2)}, u32[]{:S(2)}) async-start(bf16[4,128,2048]{2,1,0:T(8,128)(2,1)} %bitcast.49), calls=%async_computation.2 | async-start | bytes 4194304 | tf_op jit(solution)/shard_map/all_to_all | solution.py:223
  182.3 99.5 %all-gather.18.cloned.1.call-start = ((), (), s32[]{:S(2)}) async-start(), calls=%async_computation.24 | async-start | bytes 3932160 | tf_op jit(solution)/shard_map/all_gather | solution.py:203
  185.9 30.9 %collective-permute-start.18 = (bf16[128,2048]{1,0:T(8,128)(2,1)}, bf16[128,2048]{1,0:T(8,128)(2,1)S(1)}, u32[]{:S(2)}, u32[]{:S(2)}) collective-permute-start(bf16[128,2048]{1,0:T(8,128)(2,1)} %collective-permute-done.16.refs_0_), channel_id=1, source_target_pairs={{0,4},{1,5},{2,6},{3,7},{4,0},{5,1},{6,2},{7,3},{8,12},{9,13},{10,... | collective-permute-start | bytes 1572872 | tf_op jit(solution)/shard_map/ppermute | solution.py:55
  186.0 33.2 %collective-permute-start.19 = (bf16[128,2048]{1,0:T(8,128)(2,1)}, bf16[128,2048]{1,0:T(8,128)(2,1)S(1)}, u32[]{:S(2)}, u32[]{:S(2)}) collective-permute-start(bf16[128,2048]{1,0:T(8,128)(2,1)} %collective-permute-done.16.refs_0_), channel_id=1, source_target_pairs={{0,8},{1,9},{2,10},{3,11},{4,12},{5,13},{6,14},{7,15},{8,0},{9,1},... | collective-permute-start | bytes 1572872 | tf_op jit(solution)/shard_map/ppermute | solution.py:55
  188.0 38.5 %collective-permute-start.20 = (bf16[128,2048]{1,0:T(8,128)(2,1)}, bf16[128,2048]{1,0:T(8,128)(2,1)}, u32[]{:S(2)}, u32[]{:S(2)}) collective-permute-start(bf16[128,2048]{1,0:T(8,128)(2,1)} %collective-permute-done.16.refs_0_), channel_id=1, source_target_pairs={{0,12},{1,13},{2,14},{3,15},{4,8},{5,9},{6,10},{7,11},{8,4},{9,5},... | collective-permute-start | bytes 1572872 | tf_op jit(solution)/shard_map/ppermute | solution.py:55
  229.9 38.4 %collective-permute-start.21 = (bf16[128,2048]{1,0:T(8,128)(2,1)S(1)}, bf16[128,2048]{1,0:T(8,128)(2,1)S(1)}, u32[]{:S(2)}, u32[]{:S(2)}) collective-permute-start(bf16[128,2048]{1,0:T(8,128)(2,1)S(1)} %multiply_convert_fusion.4.refs_0_), channel_id=1, source_target_pairs={{0,4},{1,5},{2,6},{3,7},{4,0},{5,1},{6,2},{7,3},{8,12},{9,13},{10,... | collective-permute-start | bytes 1572872 | tf_op jit(solution)/shard_map/ppermute | solution.py:55
  231.4 40.3 %collective-permute-start.22 = (bf16[128,2048]{1,0:T(8,128)(2,1)S(1)}, bf16[128,2048]{1,0:T(8,128)(2,1)S(1)}, u32[]{:S(2)}, u32[]{:S(2)}) collective-permute-start(bf16[128,2048]{1,0:T(8,128)(2,1)S(1)} %multiply_convert_fusion.4.refs_0_), channel_id=1, source_target_pairs={{0,8},{1,9},{2,10},{3,11},{4,12},{5,13},{6,14},{7,15},{8,0},{9,1},... | collective-permute-start | bytes 1572872 | tf_op jit(solution)/shard_map/ppermute | solution.py:55
  231.9 39.8 %collective-permute-start.23 = (bf16[128,2048]{1,0:T(8,128)(2,1)S(1)}, bf16[128,2048]{1,0:T(8,128)(2,1)S(1)}, u32[]{:S(2)}, u32[]{:S(2)}) collective-permute-start(bf16[128,2048]{1,0:T(8,128)(2,1)S(1)} %multiply_convert_fusion.4.refs_0_), channel_id=1, source_target_pairs={{0,12},{1,13},{2,14},{3,15},{4,8},{5,9},{6,10},{7,11},{8,4},{9,5},... | collective-permute-start | bytes 1572872 | tf_op jit(solution)/shard_map/ppermute | solution.py:55
  233.4 34.8 %collective-permute-start.24 = (bf16[128,2048]{1,0:T(8,128)(2,1)S(1)}, bf16[128,2048]{1,0:T(8,128)(2,1)S(1)}, u32[]{:S(2)}, u32[]{:S(2)}) collective-permute-start(bf16[128,2048]{1,0:T(8,128)(2,1)S(1)} %multiply_convert_fusion.4.refs_0_), channel_id=1, source_target_pairs={{0,16},{1,17},{2,18},{3,19},{4,20},{5,21},{6,22},{7,23},{8,24},{9,... | collective-permute-start | bytes 1572872 | tf_op jit(solution)/shard_map/ppermute | solution.py:55
  268.2 26.0 %collective-permute-start.25 = (bf16[128,2048]{1,0:T(8,128)(2,1)S(1)}, bf16[128,2048]{1,0:T(8,128)(2,1)S(1)}, u32[]{:S(2)}, u32[]{:S(2)}) collective-permute-start(bf16[128,2048]{1,0:T(8,128)(2,1)S(1)} %collective-permute-done.24.refs_0_), channel_id=1, source_target_pairs={{0,4},{1,5},{2,6},{3,7},{4,0},{5,1},{6,2},{7,3},{8,12},{9,13},{10,... | collective-permute-start | bytes 1572872 | tf_op jit(solution)/shard_map/ppermute | solution.py:55
  268.2 26.0 %collective-permute-start.26 = (bf16[128,2048]{1,0:T(8,128)(2,1)S(1)}, bf16[128,2048]{1,0:T(8,128)(2,1)}, u32[]{:S(2)}, u32[]{:S(2)}) collective-permute-start(bf16[128,2048]{1,0:T(8,128)(2,1)S(1)} %collective-permute-done.24.refs_0_), channel_id=1, source_target_pairs={{0,8},{1,9},{2,10},{3,11},{4,12},{5,13},{6,14},{7,15},{8,0},{9,1},... | collective-permute-start | bytes 1572872 | tf_op jit(solution)/shard_map/ppermute | solution.py:55
  268.2 26.0 %collective-permute-start.27 = (bf16[128,2048]{1,0:T(8,128)(2,1)S(1)}, bf16[128,2048]{1,0:T(8,128)(2,1)}, u32[]{:S(2)}, u32[]{:S(2)}) collective-permute-start(bf16[128,2048]{1,0:T(8,128)(2,1)S(1)} %collective-permute-done.24.refs_0_), channel_id=1, source_target_pairs={{0,12},{1,13},{2,14},{3,15},{4,8},{5,9},{6,10},{7,11},{8,4},{9,5},... | collective-permute-start | bytes 1572872 | tf_op jit(solution)/shard_map/ppermute | solution.py:55
  311.4 22.4 %all-to-all-start.3 = ((bf16[4,128,2048]{2,1,0:T(8,128)(2,1)}), bf16[4,128,2048]{2,1,0:T(8,128)(2,1)}, u32[]{:S(2)}, u32[]{:S(2)}) async-start(bf16[4,128,2048]{2,1,0:T(8,128)(2,1)} %bitcast.303), calls=%async_computation.3 | async-start | bytes 4194304 | tf_op jit(solution)/shard_map/all_to_all | solution.py:223
  315.8 78.9 %reduce-scatter.6.cloned.1.call-start = ((), (), s32[]{:S(2)}) async-start(), calls=%async_computation.18 | async-start | bytes 3932160 | tf_op jit(solution)/shard_map/reduce_scatter | solution.py:207
  335.8 37.2 %all-to-all-start.4 = ((bf16[4,128,2048]{2,1,0:T(8,128)(2,1)}), bf16[4,128,2048]{2,1,0:T(8,128)(2,1)}, u32[]{:S(2)}, u32[]{:S(2)}) async-start(bf16[4,128,2048]{2,1,0:T(8,128)(2,1)} %bitcast.301), calls=%async_computation.4 | async-start | bytes 4194304 | tf_op jit(solution)/shard_map/all_to_all | solution.py:223
  340.8 184.4 %reduce-scatter.12.cloned.1.call-start = ((), (), s32[]{:S(2)}) async-start(), calls=%async_computation.21 | async-start | bytes 3932160 | tf_op jit(solution)/shard_map/reduce_scatter | solution.py:207
  341.2 33.9 %collective-permute-start.28 = (bf16[128,2048]{1,0:T(8,128)(2,1)S(1)}, bf16[128,2048]{1,0:T(8,128)(2,1)S(1)}, u32[]{:S(2)}, u32[]{:S(2)}) collective-permute-start(bf16[128,2048]{1,0:T(8,128)(2,1)S(1)} %reduce_sum.131), channel_id=1, source_target_pairs={{0,16},{1,17},{2,18},{3,19},{4,20},{5,21},{6,22},{7,23},{8,24},{9,... | collective-permute-start | bytes 1572872 | tf_op jit(solution)/shard_map/ppermute | solution.py:55
  383.7 144.0 %reduce-scatter.14.cloned.1.call-start = ((), (), s32[]{:S(2)}) async-start(), calls=%async_computation.22 | async-start | bytes 3932160 | tf_op jit(solution)/shard_map/reduce_scatter | solution.py:207
  391.9 19.7 %collective-permute-start.30 = (bf16[128,2048]{1,0:T(8,128)(2,1)S(1)}, bf16[128,2048]{1,0:T(8,128)(2,1)S(1)}, u32[]{:S(2)}, u32[]{:S(2)}) collective-permute-start(bf16[128,2048]{1,0:T(8,128)(2,1)S(1)} %get-tuple-element.148.refs_0_), channel_id=1, source_target_pairs={{0,8},{1,9},{2,10},{3,11},{4,12},{5,13},{6,14},{7,15},{8,0},{9,1},... | collective-permute-start | bytes 1572872 | tf_op jit(solution)/shard_map/ppermute | solution.py:55
  394.4 18.0 %collective-permute-start.29 = (bf16[128,2048]{1,0:T(8,128)(2,1)S(1)}, bf16[128,2048]{1,0:T(8,128)(2,1)S(1)}, u32[]{:S(2)}, u32[]{:S(2)}) collective-permute-start(bf16[128,2048]{1,0:T(8,128)(2,1)S(1)} %get-tuple-element.148.refs_0_), channel_id=1, source_target_pairs={{0,4},{1,5},{2,6},{3,7},{4,0},{5,1},{6,2},{7,3},{8,12},{9,13},{10,... | collective-permute-start | bytes 1572872 | tf_op jit(solution)/shard_map/ppermute | solution.py:55
  396.9 29.6 %collective-permute-start.33 = (bf16[4,64,768]{2,1,0:T(8,128)(2,1)}, bf16[4,64,768]{2,1,0:T(8,128)(2,1)S(1)}, u32[]{:S(2)}, u32[]{:S(2)}) collective-permute-start(bf16[4,64,768]{2,1,0:T(8,128)(2,1)} %get-tuple-element.330), channel_id=1, source_target_pairs={{0,16},{1,17},{2,18},{3,19},{4,20},{5,21},{6,22},{7,23},{8,24},{9,... | collective-permute-start | bytes 1179656 | tf_op jit(solution)/shard_map/ppermute | solution.py:55
  412.4 14.1 %collective-permute-start.31 = (bf16[64,2048]{1,0:T(8,128)(2,1)}, bf16[64,2048]{1,0:T(8,128)(2,1)}, u32[]{:S(2)}, u32[]{:S(2)}) collective-permute-start(bf16[64,2048]{1,0:T(8,128)(2,1)} %slice.149), channel_id=1, source_target_pairs={{0,4},{1,5},{2,6},{3,7},{4,0},{5,1},{6,2},{7,3},{8,12},{9,13},{10,... | collective-permute-start | bytes 786440 | tf_op jit(solution)/shard_map/ppermute | solution.py:55
  412.4 14.1 %collective-permute-start.32 = (bf16[64,2048]{1,0:T(8,128)(2,1)S(1)}, bf16[64,2048]{1,0:T(8,128)(2,1)S(1)}, u32[]{:S(2)}, u32[]{:S(2)}) collective-permute-start(bf16[64,2048]{1,0:T(8,128)(2,1)S(1)} %slice.150), channel_id=1, source_target_pairs={{0,8},{1,9},{2,10},{3,11},{4,12},{5,13},{6,14},{7,15},{8,0},{9,1},... | collective-permute-start | bytes 786440 | tf_op jit(solution)/shard_map/ppermute | solution.py:55
  420.1 28.6 %all-to-all-start.5 = ((bf16[4,128,2048]{2,1,0:T(8,128)(2,1)}), bf16[4,128,2048]{2,1,0:T(8,128)(2,1)}, u32[]{:S(2)}, u32[]{:S(2)}) async-start(bf16[4,128,2048]{2,1,0:T(8,128)(2,1)} %bitcast.302), calls=%async_computation.6 | async-start | bytes 4194304 | tf_op jit(solution)/shard_map/all_to_all | solution.py:223
  426.5 116.6 %reduce-scatter.8.cloned.1.call-start = ((), (), s32[]{:S(2)}) async-start(), calls=%async_computation.19 | async-start | bytes 3276800 | tf_op jit(solution)/shard_map/reduce_scatter | solution.py:207
  447.7 106.6 %reduce-scatter.10.cloned.1.call-start = ((), (), s32[]{:S(2)}) async-start(), calls=%async_computation.20 | async-start | bytes 3276800 | tf_op jit(solution)/shard_map/reduce_scatter | solution.py:207
  450.7 24.7 %collective-permute-start.36 = (bf16[128,2048]{1,0:T(8,128)(2,1)S(1)}, bf16[128,2048]{1,0:T(8,128)(2,1)}, u32[]{:S(2)}, u32[]{:S(2)}) collective-permute-start(bf16[128,2048]{1,0:T(8,128)(2,1)S(1)} %reduce_sum.134), channel_id=1, source_target_pairs={{0,16},{1,17},{2,18},{3,19},{4,20},{5,21},{6,22},{7,23},{8,24},{9,... | collective-permute-start | bytes 1572872 | tf_op jit(solution)/shard_map/ppermute | solution.py:55
  483.9 13.9 %collective-permute-start.37 = (bf16[2,2,80,2048]{3,2,0,1:T(8,128)(2,1)}, bf16[2,2,80,2048]{3,2,0,1:T(8,128)(2,1)}, u32[]{:S(2)}, u32[]{:S(2)}) collective-permute-start(bf16[2,2,80,2048]{3,2,0,1:T(8,128)(2,1)} %bitcast.267), channel_id=1, source_target_pairs={{0,1},{1,0},{2,3},{3,2},{4,5},{5,4},{6,7},{7,6},{8,9},{9,8},{10,11... | collective-permute-start | bytes 3932168 | tf_op jit(solution)/shard_map/ppermute | solution.py:55
  500.7 40.3 %all-to-all-start.6 = ((bf16[4,128,2048]{2,1,0:T(8,128)(2,1)}), bf16[4,128,2048]{2,1,0:T(8,128)(2,1)}, u32[]{:S(2)}, u32[]{:S(2)}) async-start(bf16[4,128,2048]{2,1,0:T(8,128)(2,1)} %bitcast.277), calls=%async_computation.8 | async-start | bytes 4194304 | tf_op jit(solution)/shard_map/all_to_all | solution.py:223
  520.9 66.0 %collective-permute-start.41 = (bf16[128,2048]{1,0:T(8,128)(2,1)}, bf16[128,2048]{1,0:T(8,128)(2,1)}, u32[]{:S(2)}, u32[]{:S(2)}) collective-permute-start(bf16[128,2048]{1,0:T(8,128)(2,1)} %get-tuple-element.318), channel_id=1, source_target_pairs={{0,12},{1,13},{2,14},{3,15},{4,8},{5,9},{6,10},{7,11},{8,4},{9,5},... | collective-permute-start | bytes 1572872 | tf_op jit(solution)/shard_map/ppermute | solution.py:55
  523.5 63.8 %collective-permute-start.40 = (bf16[128,2048]{1,0:T(8,128)(2,1)}, bf16[128,2048]{1,0:T(8,128)(2,1)}, u32[]{:S(2)}, u32[]{:S(2)}) collective-permute-start(bf16[128,2048]{1,0:T(8,128)(2,1)} %get-tuple-element.319), channel_id=1, source_target_pairs={{0,8},{1,9},{2,10},{3,11},{4,12},{5,13},{6,14},{7,15},{8,0},{9,1},... | collective-permute-start | bytes 1572872 | tf_op jit(solution)/shard_map/ppermute | solution.py:55
  523.5 63.8 %collective-permute-start.39 = (bf16[128,2048]{1,0:T(8,128)(2,1)}, bf16[128,2048]{1,0:T(8,128)(2,1)}, u32[]{:S(2)}, u32[]{:S(2)}) collective-permute-start(bf16[128,2048]{1,0:T(8,128)(2,1)} %get-tuple-element.320), channel_id=1, source_target_pairs={{0,4},{1,5},{2,6},{3,7},{4,0},{5,1},{6,2},{7,3},{8,12},{9,13},{10,... | collective-permute-start | bytes 1572872 | tf_op jit(solution)/shard_map/ppermute | solution.py:55
  524.4 37.1 %collective-permute-start.45 = (bf16[2,2,80,384]{3,2,0,1:T(8,128)(2,1)}, bf16[2,2,80,384]{3,2,0,1:T(8,128)(2,1)}, u32[]{:S(2)}, u32[]{:S(2)}) collective-permute-start(bf16[2,2,80,384]{3,2,0,1:T(8,128)(2,1)} %bitcast.269), channel_id=1, source_target_pairs={{0,1},{1,0},{2,3},{3,2},{4,5},{5,4},{6,7},{7,6},{8,9},{9,8},{10,11... | collective-permute-start | bytes 737288 | tf_op jit(solution)/shard_map/ppermute | solution.py:55
  524.4 26.4 %collective-permute-start.43 = (bf16[2,80,2048]{2,1,0:T(8,128)(2,1)S(1)}, bf16[2,80,2048]{2,1,0:T(8,128)(2,1)}, u32[]{:S(2)}, u32[]{:S(2)}) collective-permute-start(bf16[2,80,2048]{2,1,0:T(8,128)(2,1)S(1)} %dynamic-slice_bitcast_fusion), channel_id=1, source_target_pairs={{0,2},{1,3},{2,0},{3,1},{4,6},{5,7},{6,4},{7,5},{8,10},{9,11},{10,... | collective-permute-start | bytes 1966088 | tf_op jit(solution)/shard_map/ppermute | solution.py:55
  550.8 26.6 %collective-permute-start.38 = (bf16[4,64,640]{2,1,0:T(8,128)(2,1)}, bf16[4,64,640]{2,1,0:T(8,128)(2,1)}, u32[]{:S(2)}, u32[]{:S(2)}) collective-permute-start(bf16[4,64,640]{2,1,0:T(8,128)(2,1)} %dynamic-slice_bitcast_fusion.9), channel_id=1, source_target_pairs={{0,16},{1,17},{2,18},{3,19},{4,20},{5,21},{6,22},{7,23},{8,24},{9,... | collective-permute-start | bytes 983048 | tf_op jit(solution)/shard_map/ppermute | solution.py:55
  556.6 20.2 %all-to-all-start.7 = ((bf16[32,2,64]{2,1,0:T(2,128)(2,1)}), bf16[32,2,64]{2,1,0:T(2,128)(2,1)S(1)}, u32[]{:S(2)}, u32[]{:S(2)}) async-start(bf16[32,2,64]{2,1,0:T(2,128)(2,1)} %copy.123), calls=%async_computation.10 | async-start | bytes 32768 | tf_op jit(solution)/shard_map/all_to_all | solution.py:901
  561.6 29.9 %collective-permute-start.44 = (bf16[80,2048]{1,0:T(8,128)(2,1)}, bf16[80,2048]{1,0:T(8,128)(2,1)}, u32[]{:S(2)}, u32[]{:S(2)}) collective-permute-start(bf16[80,2048]{1,0:T(8,128)(2,1)} %dynamic-slice_bitcast_fusion.7), channel_id=1, source_target_pairs={{0,16},{1,17},{2,18},{3,19},{4,20},{5,21},{6,22},{7,23},{8,24},{9,... | collective-permute-start | bytes 983048 | tf_op jit(solution)/shard_map/ppermute | solution.py:55
  577.4 33.5 %collective-permute-start.42 = (bf16[80,2048]{1,0:T(8,128)(2,1)}, bf16[80,2048]{1,0:T(8,128)(2,1)}, u32[]{:S(2)}, u32[]{:S(2)}) collective-permute-start(bf16[80,2048]{1,0:T(8,128)(2,1)} %dynamic-slice_bitcast_fusion.8), channel_id=1, source_target_pairs={{0,16},{1,17},{2,18},{3,19},{4,20},{5,21},{6,22},{7,23},{8,24},{9,... | collective-permute-start | bytes 983048 | tf_op jit(solution)/shard_map/ppermute | solution.py:55
  582.6 18.9 %all-to-all-start.8 = ((bf16[4,64,640]{2,1,0:T(8,128)(2,1)}), bf16[4,64,640]{2,1,0:T(8,128)(2,1)}, u32[]{:S(2)}, u32[]{:S(2)}) async-start(bf16[4,64,640]{2,1,0:T(8,128)(2,1)} %fusion.33), calls=%async_computation.11 | async-start | bytes 655360 | tf_op jit(solution)/shard_map/all_to_all | solution.py:223
  586.9 5.7 collective-permute-start.46
  592.7 16.0 %collective-permute-start.47 = (bf16[80,384]{1,0:T(8,128)(2,1)S(1)}, bf16[80,384]{1,0:T(8,128)(2,1)S(1)}, u32[]{:S(2)}, u32[]{:S(2)}) collective-permute-start(bf16[80,384]{1,0:T(8,128)(2,1)S(1)} %dynamic-slice_bitcast_fusion.11), channel_id=1, source_target_pairs={{0,16},{1,17},{2,18},{3,19},{4,20},{5,21},{6,22},{7,23},{8,24},{9,... | collective-permute-start | bytes 184328 | tf_op jit(solution)/shard_map/ppermute | solution.py:55
  601.5 15.7 %all-to-all-start.9 = ((bf16[4,2,64,768]{3,2,1,0:T(8,128)(2,1)}), bf16[4,2,64,768]{3,2,1,0:T(8,128)(2,1)S(1)}, u32[]{:S(2)}, u32[]{:S(2)}) async-start(bf16[4,2,64,768]{3,2,1,0:T(8,128)(2,1)} %pad_maximum_fusion), calls=%async_computation.14 | async-start | bytes 1572864 | tf_op jit(solution)/shard_map/all_to_all | solution.py:223
  (79 other events, 699.5 us)
Sparse Core Ops, SparseCore 0:
  26.6 26.8 all-gather.9
  65.5 25.8 all-gather.11
  104.3 26.6 all-gather.13
  133.0 28.5 all-gather.19
  162.9 28.5 all-gather.15
  192.9 28.5 all-gather.17
  323.2 37.8 reduce-scatter.5
  383.8 38.9 reduce-scatter.11
  425.3 37.9 reduce-scatter.13
  465.8 34.6 reduce-scatter.7
  503.1 43.8 reduce-scatter.9

commit v5 on v4

--- a/solution.py
+++ b/solution.py
@@ -86,6 +86,16 @@
                 new.append((mask | b, send(unit, b)))
         lists = [units + new for units, new in zip(lists, fresh)]
     return lists
+
+
+def expand(units, bits):
+    for b in bits:
+        units = units + [(mask | b, trade(unit, b)) for mask, unit in units]
+    return units
+
+
+def pin_units(units, *others):
+    return list(zip([mask for mask, _ in units], fence_all([unit for _, unit in units], *others)))
 
 
 def copy_kernel(count, shapes, places, scalars, *refs):
@@ -194,6 +204,8 @@
     fsdp_count, count = lax.axis_size("fsdp"), lax.axis_size("seq") * lax.axis_size("fsdp")
     if sum(bits) == fsdp_count - 1:
         return {"axis_name": "fsdp"}
+    if sum(bits) == count - fsdp_count:
+        return {"axis_name": "seq"}
     if sum(bits) == count - 1:
         return {"axis_name": AXES}
     return {"axis_name": AXES, "axis_index_groups": groups_of(bits, count)}
@@ -591,9 +603,9 @@
         every_slot = every_slot.reshape((-1, step) + own.shape)
         return jnp.moveaxis(every_slot, 2, 1).reshape((seq_count,) + own.shape[1:])
 
-    def place_rows(units):
+    def place_rows(units, bits):
         def places(i, at):
-            return [(None, 0, number_of(jnp.bitwise_xor(at, units[i][0]), dp))]
+            return [(None, 0, number_of(jnp.bitwise_xor(at, units[i][0]), bits))]
 
         one = units[0][1].shape
         pieces = [unit for _, unit in units]
@@ -640,9 +652,9 @@
         input_gate_weight,
     ).astype(BF16)
     small_shape = small.shape
-    recur_pair = pair_up(recur_weight, above, me, small)
+    one, two = (trade(fence(input_own, gains_got), mask) for mask in (low, 2 * low))
+    recur_pair = pair_up(recur_weight, above, me, small, one, two)
     recur_q = gather_along(recur_pair, below, 1).reshape(channels, width)
-    one, two = (trade(fence(input_own, recur_pair), mask) for mask in (low, 2 * low))
     small = fence(small, recur_pair)
     for i, b in enumerate(dp):
         small, small_got = stacked(small, b, i)
@@ -652,8 +664,10 @@
     piece = exchange(fence(by_rank(mixer_weight, high, 4), recur_pair), step)
     branch_pair = pair_up(fence(branch_weight, first_got), above, me, piece, small_got, *three)
     branch_q = gather_along(branch_pair, below, 1).reshape(channels, width)
-    down_piece = exchange(fence(by_rank(down_weight, high_wide, 8), piece), step)
-    mixer_pair = pair_up(fence(piece, branch_pair), above, me, down_piece)
+    mixer_pair = pair_up(fence(piece, branch_pair), above, me)
+    cot_all = gather_along(fence(cot_own, mixer_pair)[None], tp_wide, 0)
+    own_half = number_of(me, (wide,))
+    cot_all = cot_all.reshape(2, 4 * tokens, width)
     mixer_q = gather_along(mixer_pair, below, 2).reshape(width, channels)
     small = small.reshape((share,) + small_shape)
     gains = small[:, extra + 8 :, :out_rows].reshape(high, deep, 4, 2, out_rows)
@@ -663,7 +677,6 @@
     numbers = numbers.reshape(TAPS + 4, channels).astype(F32)
     gate_rows = small[:, :channel_rows, : 2 * block_size].reshape(channels, -1)
     input_all = place_tokens([input_own, one, two, *three], low, me)
-    cot_near_list = share_direct(fence(cot_own, three[0]), low)
 
     coef = numbers
     decay_vec = coef[7:]
@@ -699,8 +712,8 @@
     recur_in = project(normed, recur_q).astype(BF16)
     edge = recur_in.reshape(blocks, span, channels)[:, span - 4 :].reshape(4, rows, 4, channels)
     halo = across_blocks(edge)
-    cot_far = trade(fence(cot_own, halo), wide)
     halo = halo.astype(F32).reshape(seq_count * rows, 4, channels)
+    down_piece = exchange(fence(by_rank(down_weight, high_wide, 8), halo), step)
     recur_in = recur_in.reshape(blocks, span, channels)
     shape = (blocks, span, channels)
     one = (blocks, 1, channels)
@@ -717,8 +730,9 @@
         4,
     )
     ends_all = across_blocks(ends.reshape(4, rows, 2, channels)).reshape(-1, 2, channels)
-    branch = project(normed, fence(branch_q, ends, *cot_near_list[1:], cot_far))
+    branch = project(normed, fence(branch_q, ends))
     branch = branch.reshape(blocks, span, channels)
+    down_piece = fence(down_piece, ends_all)
     ends = fence(ends_all, branch)
     state, mixed, came = call(
         functools.partial(state_kernel, rows, step),
@@ -728,18 +742,14 @@
         [pltpu.VMEM(everything, F32)],
         2,
     )
-    gate_pair, up_pair, down_pair = (
-        pair_up(fence(weight, mixer_pair), above_wide, me)
-        for weight in (gate_weight, up_weight, down_piece)
-    )
-    gate_q = gather_along(gate_pair, below, 1).reshape(hidden, width)
-    up_q = gather_along(up_pair, below, 1).reshape(hidden, width)
+    down_pair = pair_up(fence(down_piece, cot_own), above_wide, me)
     down_q = gather_along(down_pair, below, 2).reshape(width, hidden)
     mixed_flat = mixed.reshape(4 * tokens, channels)
-    cot_near = place_tokens(fence_all(cot_near_list, mixed), low, me)
-    mixer_part = project(mixed_flat, mixer_q).astype(BF16).reshape(4, tokens, width)
-    cot_far_list = share_direct(fence(cot_far, mixer_part), low)
-    mixer_parts = fence(exchange(mixer_part, step), *cot_far_list[1:])
+    mixer_part = project(fence(mixed_flat, down_piece), mixer_q).astype(BF16).reshape(4, tokens, width)
+    gate_units = expand([(0, fence(gate_weight, mixed))], dp_wide)
+    up_units = expand([(0, fence(up_weight, mixed))], dp_wide)
+    gate_q, up_q = place_rows(gate_units, dp_wide), place_rows(up_units, dp_wide)
+    mixer_parts = fence(exchange(mixer_part, step), gate_q, up_q)
     residual = input_own.astype(F32) + jnp.sum(mixer_parts.astype(F32), axis=0)
 
 
@@ -750,12 +760,14 @@
     near_list = share_direct(normed_own, low)
     far_list = share_direct(normed_far, low)
     near = place_tokens(near_list, low, me)
-    cot_far = place_tokens(fence_all(cot_far_list, normed_own), low, me)
+    cot_all = fence(cot_all, normed_own)
+    cot_near, cot_far = pick(cot_all, own_half, 0), pick(cot_all, 1 - own_half, 0)
     near_out = feed_forward(near, cot_near, gate_q, up_q, down_q)
     ranks_shape = (4, tokens, width)
     far = place_tokens(fence_all(far_list, near_out[0]), low, me)
     far_out = feed_forward(far, cot_far, gate_q, up_q, down_q)
-    grad_far_parts = exchange(far_out[0].reshape(ranks_shape), step)
+    grad_two_near = sum_tokens(near_out[0].reshape(ranks_shape), step)
+    grad_far_parts = exchange(fence(far_out[0], grad_two_near).reshape(ranks_shape), step)
 
     def finish(partial, bits):
         partial = partial.reshape((2,) * len(bits) + partial.shape[1:])
@@ -772,8 +784,6 @@
     grad_far_parts = fence(grad_far_parts, down_grad)
     down_grad = finish(scatter_along(down_grad, below, 2), above_wide).reshape(8, out_rows, hidden)
     grad_two_far = jnp.sum(grad_far_parts.astype(F32), axis=0).astype(BF16)
-    grad_near_parts = exchange(fence(near_out[0], grad_two_far).reshape(ranks_shape), step)
-    grad_two_near = jnp.sum(grad_near_parts.astype(F32), axis=0)
     grad_two = grad_two_near + trade(grad_two_far, wide).astype(F32)
     scaled = grad_two * gain_two
     grad_residual = cot_own.astype(F32) + scale_two * (
@@ -838,7 +848,8 @@
     halo_back = across_blocks(edge_back)
     last = len(dp)
     branch_grad = outer(fence(grad_branch, edge_back), normed).astype(BF16).reshape(high, -1, width)
-    halo_back = fence(halo_back, down_far_own, branch_grad)
+    first_part = back_project(grad_branch, branch_q)
+    halo_back = fence(halo_back, down_far_own, branch_grad, first_part)
     branch_grad = scatter_along(branch_grad, below, 1)
     halo_back = halo_back.astype(F32).reshape(seq_count * rows, 4, channels)
     (grad_recur,) = call(
@@ -852,7 +863,7 @@
     grad_recur = grad_recur.reshape(4 * tokens, channels)
     recur_grad = reduce_rows(outer(grad_recur, normed), dp, me)
     grad_recur = fence(grad_recur, recur_grad.send())
-    grad_normed_part = back_project(grad_branch, branch_q) + back_project(grad_recur, recur_q)
+    grad_normed_part = first_part + back_project(grad_recur, recur_q)
     grad_normed_sent = grad_normed_part.astype(BF16)
     recur_sent = recur_grad.send_to(last - 2, grad_normed_sent)
     packed = reduce_rows(fence(packed, grad_recur), dp, me)
@@ -878,7 +889,6 @@
     packed_sent = packed.send_to(0, sent)
     pair = jnp.stack([fence(part, packed_sent) for part in (down_kept, down_got)], axis=1)
     pair = exchange(pair, step)
-    own_half = number_of(me, (wide,))
     flat_pieces = [pair[j, h] for h in range(2) for j in range(4)]
     down_weight_grad = pl.pallas_call(
         functools.partial(lay_kernel, 4, high_wide),

time: 637 us -> 622 us (0.976)
  waiting for transfers between devices: 232 us -> 197 us
  blocking collectives: 0 us -> 28.6 us
  starting transfers between devices: 115 us -> 107 us
    all_to_all x9 -> x8, waiting for transfers between devices: 59.5 us -> 16.5 us  [exchange(): lax.all_to_all(parts, 'seq', 0, 0, axis_index_groups=groups, tiled=True)]
    all_to_all x0 -> x1, blocking collectives: none -> 28.6 us  [exchange(): lax.all_to_all(parts, 'seq', 0, 0, axis_index_groups=groups, tiled=True)]
    all_gather x6 -> x5, waiting for transfers between devices: 0.07 us -> 19.4 us  [gather_along(): return lax.all_gather(own, axis=axis, tiled=True, **line_of(bits))]
    all_to_all x9 -> x8, starting transfers between devices: 55.8 us -> 43.6 us  [exchange(): lax.all_to_all(parts, 'seq', 0, 0, axis_index_groups=groups, tiled=True)]
    ppermute x48 -> x47, waiting for transfers between devices: 159 us -> 150 us  [trade(): return lax.ppermute(value, AXES, [(i, i ^ mask) for i in range(count)])]
    ppermute x48 -> x47, starting transfers between devices: 53 us -> 57.5 us  [trade(): return lax.ppermute(value, AXES, [(i, i ^ mask) for i in range(count)])]
    unnamed x151 -> x155, local copies, waits for them, and re-layouts: 12.9 us -> 14.9 us
  transfers between devices with their start and end apart: 69 -> 66, of which waited for: 25 -> 24; matrix products, arithmetic and copies ran while one was open for 28% -> 29% of each run, Pallas kernels for 10% -> 11%
where the time goes in v5:
time: 622 us; the launch traced here: 614 us
  waiting for transfers between devices  197 us (32%)
  starting transfers between devices  107 us (17%)
  matrix products  103 us (17%)
  Pallas kernels  69 us (11%)
  other arithmetic  48.6 us (8%)
  local copies, waits for them, and re-layouts  45.4 us (7%)
  blocking collectives  28.6 us (5%)
  between operations  15.7 us (3%)
    ppermute x47, waiting for transfers between devices, trade(): return lax.ppermute(value, AXES, [(i, i ^ mask) for i in range(count)])  150 us
    ppermute x47, starting transfers between devices, trade(): return lax.ppermute(value, AXES, [(i, i ^ mask) for i in range(count)])  57.5 us
    pallas_call x5, Pallas kernels, call(): pl.pallas_call(body, out_shape=[jax.ShapeDtypeStruct(shape, kind) for sha...  45.5 us
    all_to_all x8, starting transfers between devices, exchange(): lax.all_to_all(parts, 'seq', 0, 0, axis_index_groups=groups, tiled=True)  43.6 us
    dot_general x9, matrix products, project(): lax.dot_general(left, weight, (((1,), (1,)), ((), ())), preferred_element...  38 us
    dot_general x9, matrix products, back_project(): lax.dot_general(left, weight, (((1,), (0,)), ((), ())), preferred_element...  34.8 us
    dot_general x9, matrix products, outer(): lax.dot_general(grads, values, (((0,), (0,)), ((), ())), preferred_elemen...  29.7 us
    all_to_all x1, blocking collectives, exchange(): lax.all_to_all(parts, 'seq', 0, 0, axis_index_groups=groups, tiled=True)  28.6 us
  transfers between devices with their start and end apart: 66, of which 24 were waited for; matrix products, arithmetic and copies ran while one was open for 29% of the time, Pallas kernels for 11%

profile of v5, /device:TPU:20, one launch (start us, length us, event | category | flops | bytes accessed | tf_op | source)
XLA Modules:
  0.0 614.4 jit_solution(15789530493581231985)
XLA Ops:
  22.9 11.7 %collective-permute-done.6 = bf16[80,2048]{1,0:T(8,128)(2,1)S(1)} collective-permute-done((bf16[80,2048]{1,0:T(8,128)(2,1)}, bf16[80,2048]{1,0:T(8,128)(2,1)S(1)}, u32[]{:S(2)}, u32[]{:S(2)}) %collective-permute-start.6) | collective-permute-done | bytes 327712 | tf_op jit(solution)/shard_map/ppermute | solution.py:55
  37.1 5.1 collective-permute-done.7
  45.5 5.0 all-to-all-start
  54.0 6.8 %collective-permute-done.4.refs_3_ = bf16[64,2048]{1,0:T(8,128)(2,1)S(1)} collective-permute-done((bf16[64,2048]{1,0:T(8,128)(2,1)S(1)}, bf16[64,2048]{1,0:T(8,128)(2,1)S(1)}, u32[]{:S(2)}, u32[]{:S(2)}) %collective-permute-start.4) | collective-permute-done | bytes 262176 | tf_op jit(solution)/shard_map/ppermute | solution.py:55
  60.8 5.3 collective-permute-done.5.refs_4_
  67.5 14.0 %collective-permute-done.13 = bf16[4,64,640]{2,1,0:T(8,128)(2,1)S(1)} collective-permute-done((bf16[4,64,640]{2,1,0:T(8,128)(2,1)S(1)}, bf16[4,64,640]{2,1,0:T(8,128)(2,1)S(1)}, u32[]{:S(2)}, u32[]{:S(2)}) %collective-permute-start.13) | collective-permute-done | bytes 327712 | tf_op jit(solution)/shard_map/ppermute | solution.py:55
  91.1 3.6 convolution_convert_fusion.6
  95.5 3.4 collective-permute-start.10
  102.8 8.7 %all-to-all-start.1 = ((bf16[8,64,768]{2,1,0:T(8,128)(2,1)}), bf16[8,64,768]{2,1,0:T(8,128)(2,1)S(1)}, u32[]{:S(2)}, u32[]{:S(2)}) async-start(bf16[8,64,768]{2,1,0:T(8,128)(2,1)} %copy.117), calls=%async_computation.1 | async-start | bytes 1572864 | tf_op jit(solution)/shard_map/all_to_all | solution.py:235
  114.6 12.8 %shard_map.343 = (bf16[8,64,640]{2,1,0:T(8,128)(2,1)}, f32[8,64,640]{2,1,0:T(8,128)}, f32[8,64,640]{2,1,0:T(8,128)}, f32[8,64,640]{2,1,0:T(8,128)}, f32[8,64,640...) custom-call(s32[5]{0:T(128)} %pad_add_fusion.scalars, ...), custom_call_target="tpu_custom_call" | custom-call | bytes 39550976 | tf_op jit(solution)/shard_map/pallas_call | solution.py:269
  128.0 4.6 collective-permute-done.11
  134.1 4.7 fusion.58
  138.7 4.1 shard_map.344
  142.9 5.1 convolution_convert_fusion.5
  148.0 4.6 all-to-all-start.2
  156.2 18.8 %collective-permute-done.14.refs_1_ = bf16[192,2048]{1,0:T(8,128)(2,1)} collective-permute-done((bf16[192,2048]{1,0:T(8,128)(2,1)}, bf16[192,2048]{1,0:T(8,128)(2,1)}, u32[]{:S(2)}, u32[]{:S(2)}) %collective-permute-start.14) | collective-permute-done | bytes 786464 | tf_op jit(solution)/shard_map/ppermute | solution.py:55
  175.5 11.9 %collective-permute-done.17.refs_1_ = bf16[192,2048]{1,0:T(8,128)(2,1)S(1)} collective-permute-done((bf16[192,2048]{1,0:T(8,128)(2,1)}, bf16[192,2048]{1,0:T(8,128)(2,1)S(1)}, u32[]{:S(2)}, u32[]{:S(2)}) %collective-permute-start.17) | collective-permute-done | bytes 786464 | tf_op jit(solution)/shard_map/ppermute | solution.py:55
  187.5 3.7 shard_map.345
  191.3 3.6 shard_map.346
  202.5 3.4 collective-permute-start.22
  205.9 16.5 %all-gather.14.cloned.1.call-done = bf16[1024,2048]{1,0:T(8,128)(2,1)} async-done(((bf16[128,2048]{1,0:T(8,128)(2,1)}), bf16[1024,2048]{1,0:T(8,128)(2,1)}) %all-gather.14.cloned.1.call-update) | async-done | bytes 4194320 | tf_op jit(solution)/shard_map/all_gather | solution.py:215
  222.4 7.8 %collective-permute-done.23.refs_0_ = bf16[128,2048]{1,0:T(8,128)(2,1)S(1)} collective-permute-done((bf16[128,2048]{1,0:T(8,128)(2,1)S(1)}, bf16[128,2048]{1,0:T(8,128)(2,1)S(1)}, u32[]{:S(2)}, u32[]{:S(2)}) %collective-permute-start.23) | collective-permute-done | bytes 524320 | tf_op jit(solution)/shard_map/ppermute | solution.py:55
  234.9 10.1 %collective-permute-done.22.refs_3_ = bf16[128,2048]{1,0:T(8,128)(2,1)} collective-permute-done((bf16[128,2048]{1,0:T(8,128)(2,1)S(1)}, bf16[128,2048]{1,0:T(8,128)(2,1)}, u32[]{:S(2)}, u32[]{:S(2)}) %collective-permute-start.22) | collective-permute-done | bytes 524320 | tf_op jit(solution)/shard_map/ppermute | solution.py:55
  247.8 4.6 fusion.64
  262.1 3.6 multiply_convert_fusion.3
  268.2 3.2 add_convert_fusion.5
  271.4 4.9 all-to-all-start.3
  276.6 4.5 fusion.9
  281.0 4.5 fusion.11
  286.3 3.2 shard_map.348
  289.6 3.6 fusion.66
  293.2 3.8 fusion.32
  297.0 3.5 add_convert_fusion.2
  301.7 3.9 fusion.67
  305.5 3.1 add_convert_fusion.4
  311.4 28.6 %all_to_all.50 = bf16[4,128,2048]{2,1,0:T(8,128)(2,1)} all-to-all(bf16[4,128,2048]{2,1,0:T(8,128)(2,1)S(1)} %bitcast.318), channel_id=1, replica_groups={{0,4,8,12},{16,20,24,28},{1,5,9,13},{17,21,25,29},{2,6,10,14},{18,22,26..., dimensions={0} | all-to-all | bytes 4194304 | tf_op jit(solution)/shard_map/all_to_all | solution.py:235
  342.6 21.5 %collective-permute-done.27 = bf16[128,2048]{1,0:T(8,128)(2,1)S(1)} collective-permute-done((bf16[128,2048]{1,0:T(8,128)(2,1)S(1)}, bf16[128,2048]{1,0:T(8,128)(2,1)S(1)}, u32[]{:S(2)}, u32[]{:S(2)}) %collective-permute-start.27) | collective-permute-done | bytes 524320 | tf_op jit(solution)/shard_map/ppermute | solution.py:55
  368.6 3.5 fusion.5
  373.3 3.6 fusion.69
  376.9 3.5 fusion.6
  380.4 3.6 collective-permute-start.29
  387.6 13.2 %collective-permute-done.29.refs_2_ = bf16[128,2048]{1,0:T(8,128)(2,1)S(1)} collective-permute-done((bf16[128,2048]{1,0:T(8,128)(2,1)S(1)}, bf16[128,2048]{1,0:T(8,128)(2,1)S(1)}, u32[]{:S(2)}, u32[]{:S(2)}) %collective-permute-start.29) | collective-permute-done | bytes 524320 | tf_op jit(solution)/shard_map/ppermute | solution.py:55
  406.9 5.1 convolution_convert_fusion.4
  412.0 4.4 all-to-all-start.5
  420.4 4.6 fusion.70.grad_mixed
  425.0 9.1 %shard_map.350 = (bf16[8,64,640]{2,1,0:T(8,128)(2,1)}, f32[8,64,640]{2,1,0:T(8,128)}, f32[8,64,640]{2,1,0:T(8,128)}, f32[8,2,640]{2,1,0:T(2,128)}) custom-call(s32[5]{0:T(128)} %pad_add_fusion.scalars, f32[8,64,640]{2,1,0:T(8,128)} %fusion.70.grad_mixed, f32[8,64,640]{2,1,0:T(8,128)} %get-tuple-element.139.state, f32[8,64,640]{2,1,0:T(8,128)} %bitcast.287, ...), custom_call_target="tpu_custom_call" | custom-call | bytes 25853952 | tf_op jit(solution)/shard_map/pallas_call | solution.py:269
  434.1 3.3 convolution_convert_fusion.2
  438.6 5.6 fusion.71
  449.5 15.5 %shard_map.351 = (f32[8,64,640]{2,1,0:T(8,128)}, bf16[8,4,640]{2,1,0:T(4,128)(2,1)}, bf16[640,384]{1,0:T(8,128)(2,1)}) custom-call(s32[5]{0:T(128)} %pad_add_fusion.scalars, f32[8,64,640]{2,1,0:T(8,128)} %get-tuple-element.144.prod, f32[8,64,640]{2,1,0:T(8,128)} %get-tuple-element.145.part, f32[16,2,640]{2,1,0:T(2,128)} %bitcast.330, ...), custom_call_target="tpu_custom_call" | custom-call | bytes 59129856 | tf_op jit(solution)/shard_map/pallas_call | solution.py:269
  465.5 3.2 convolution_convert_fusion.1
  468.7 3.2 collective-permute-done.34
  472.6 3.9 shard_map.352
  482.6 6.4 %add_convert_fusion.3 = bf16[512,2048]{1,0:T(8,128)(2,1)} fusion(f32[512,2048]{1,0:T(8,128)} %fusion.71, bf16[512,640]{1,0:T(8,128)(2,1)} %bitcast.325, bf16[640,2048]{1,0:T(8,128)(2,1)} %bitcast.361), kind=kOutput, calls=%fused_computation.12 | convolution fusion | flops 1344274432 | bytes 9568256 | tf_op jit(solution)/shard_map/dot_general | solution.py:247
  491.9 5.3 all-to-all-start.6
  498.0 3.9 convolution_convert_fusion.3
  513.8 9.5 %all-to-all-done.6 = bf16[4,128,2048]{2,1,0:T(8,128)(2,1)} async-done(((bf16[4,128,2048]{2,1,0:T(8,128)(2,1)}), bf16[4,128,2048]{2,1,0:T(8,128)(2,1)}, u32[]{:S(2)}, u32[]{:S(2)}) %all-to-all-start.6) | async-done | bytes 2097184 | tf_op jit(solution)/shard_map/all_to_all | solution.py:235
  527.3 8.7 %collective-permute-done.42 = bf16[2,80,2048]{2,1,0:T(8,128)(2,1)} collective-permute-done((bf16[2,80,2048]{2,1,0:T(8,128)(2,1)S(1)}, bf16[2,80,2048]{2,1,0:T(8,128)(2,1)}, u32[]{:S(2)}, u32[]{:S(2)}) %collective-permute-start.42) | collective-permute-done | bytes 655392 | tf_op jit(solution)/shard_map/ppermute | solution.py:55
  536.1 4.8 collective-permute-start.37
  546.2 4.9 all-to-all-start.7
  553.4 10.6 %all-to-all-done.7 = bf16[32,2,64]{2,1,0:T(2,128)(2,1)S(1)} async-done(((bf16[32,2,64]{2,1,0:T(2,128)(2,1)}), bf16[32,2,64]{2,1,0:T(2,128)(2,1)S(1)}, u32[]{:S(2)}, u32[]{:S(2)}) %all-to-all-start.7) | async-done | bytes 8224 | tf_op jit(solution)/shard_map/all_to_all | solution.py:911
  569.5 5.3 all-to-all-start.8
  576.2 4.0 fusion.38
  582.3 6.0 all-to-all-done.8
  588.3 5.2 all-to-all-start.9
  (391 shorter events, 166.9 us)
Async XLA Ops:
  7.2 83.2 %all-gather.8.cloned.1.call-start = ((), (), s32[]{:S(2)}) async-start(), calls=%async_computation.15 | async-start | bytes 3276800 | tf_op jit(solution)/shard_map/all_gather | solution.py:215
  12.2 3.6 collective-permute-start.1
  15.9 18.7 %collective-permute-start.2 = (bf16[128,2048]{1,0:T(8,128)(2,1)}, bf16[128,2048]{1,0:T(8,128)(2,1)S(1)}, u32[]{:S(2)}, u32[]{:S(2)}) collective-permute-start(bf16[128,2048]{1,0:T(8,128)(2,1)} %bitcast.281), channel_id=1, source_target_pairs={{0,4},{1,5},{2,6},{3,7},{4,0},{5,1},{6,2},{7,3},{8,12},{9,13},{10,... | collective-permute-start | bytes 1572872 | tf_op jit(solution)/shard_map/ppermute | solution.py:55
  16.4 18.2 %collective-permute-start.3 = (bf16[128,2048]{1,0:T(8,128)(2,1)}, bf16[128,2048]{1,0:T(8,128)(2,1)S(1)}, u32[]{:S(2)}, u32[]{:S(2)}) collective-permute-start(bf16[128,2048]{1,0:T(8,128)(2,1)} %bitcast.282), channel_id=1, source_target_pairs={{0,8},{1,9},{2,10},{3,11},{4,12},{5,13},{6,14},{7,15},{8,0},{9,1},... | collective-permute-start | bytes 1572872 | tf_op jit(solution)/shard_map/ppermute | solution.py:55
  17.9 16.6 %collective-permute-start.6 = (bf16[80,2048]{1,0:T(8,128)(2,1)}, bf16[80,2048]{1,0:T(8,128)(2,1)S(1)}, u32[]{:S(2)}, u32[]{:S(2)}) collective-permute-start(bf16[80,2048]{1,0:T(8,128)(2,1)} %param.26), channel_id=1, source_target_pairs={{0,16},{1,17},{2,18},{3,19},{4,20},{5,21},{6,22},{7,23},{8,24},{9,... | collective-permute-start | bytes 983048 | tf_op jit(solution)/shard_map/ppermute | solution.py:55
  36.8 5.4 collective-permute-start.7
  42.2 9.1 %collective-permute-start.8 = (bf16[2,96,384]{2,1,0:T(8,128)(2,1)S(1)}, bf16[2,96,384]{2,1,0:T(8,128)(2,1)S(1)}, u32[]{:S(2)}, u32[]{:S(2)}) collective-permute-start(bf16[2,96,384]{2,1,0:T(8,128)(2,1)S(1)} %pad_maximum_fusion.6), channel_id=1, source_target_pairs={{0,2},{1,3},{2,0},{3,1},{4,6},{5,7},{6,4},{7,5},{8,10},{9,11},{10,... | collective-permute-start | bytes 442376 | tf_op jit(solution)/shard_map/ppermute | solution.py:55
  45.5 20.6 %all-to-all-start = ((bf16[4,64,640]{2,1,0:T(8,128)(2,1)}), bf16[4,64,640]{2,1,0:T(8,128)(2,1)S(1)}, u32[]{:S(2)}, u32[]{:S(2)}) async-start(bf16[4,64,640]{2,1,0:T(8,128)(2,1)} %reshape.336), calls=%async_computation | async-start | bytes 655360 | tf_op jit(solution)/shard_map/all_to_all | solution.py:235
  50.5 83.6 %all-gather.10.cloned.1.call-start = ((), (), s32[]{:S(2)}) async-start(), calls=%async_computation.16 | async-start | bytes 3276800 | tf_op jit(solution)/shard_map/all_gather | solution.py:215
  50.5 15.6 %collective-permute-start.12 = (bf16[80,2048]{1,0:T(8,128)(2,1)S(1)}, bf16[80,2048]{1,0:T(8,128)(2,1)S(1)}, u32[]{:S(2)}, u32[]{:S(2)}) collective-permute-start(bf16[80,2048]{1,0:T(8,128)(2,1)S(1)} %copy-done.49), channel_id=1, source_target_pairs={{0,16},{1,17},{2,18},{3,19},{4,20},{5,21},{6,22},{7,23},{8,24},{9,... | collective-permute-start | bytes 983048 | tf_op jit(solution)/shard_map/ppermute | solution.py:55
  51.5 9.3 %collective-permute-start.4 = (bf16[64,2048]{1,0:T(8,128)(2,1)S(1)}, bf16[64,2048]{1,0:T(8,128)(2,1)S(1)}, u32[]{:S(2)}, u32[]{:S(2)}) collective-permute-start(bf16[64,2048]{1,0:T(8,128)(2,1)S(1)} %slice.137), channel_id=1, source_target_pairs={{0,4},{1,5},{2,6},{3,7},{4,0},{5,1},{6,2},{7,3},{8,12},{9,13},{10,... | collective-permute-start | bytes 786440 | tf_op jit(solution)/shard_map/ppermute | solution.py:55
  51.7 14.4 %collective-permute-start.5 = (bf16[64,2048]{1,0:T(8,128)(2,1)S(1)}, bf16[64,2048]{1,0:T(8,128)(2,1)S(1)}, u32[]{:S(2)}, u32[]{:S(2)}) collective-permute-start(bf16[64,2048]{1,0:T(8,128)(2,1)S(1)} %slice.138), channel_id=1, source_target_pairs={{0,8},{1,9},{2,10},{3,11},{4,12},{5,13},{6,14},{7,15},{8,0},{9,1},... | collective-permute-start | bytes 786440 | tf_op jit(solution)/shard_map/ppermute | solution.py:55
  67.1 75.8 %all-gather.12.cloned.1.call-start = ((), (), s32[]{:S(2)}) async-start(), calls=%async_computation.17 | async-start | bytes 3276800 | tf_op jit(solution)/shard_map/all_gather | solution.py:215
  67.1 14.4 %collective-permute-start.13 = (bf16[4,64,640]{2,1,0:T(8,128)(2,1)S(1)}, bf16[4,64,640]{2,1,0:T(8,128)(2,1)S(1)}, u32[]{:S(2)}, u32[]{:S(2)}) collective-permute-start(bf16[4,64,640]{2,1,0:T(8,128)(2,1)S(1)} %all-to-all-done), channel_id=1, source_target_pairs={{0,16},{1,17},{2,18},{3,19},{4,20},{5,21},{6,22},{7,23},{8,24},{9,... | collective-permute-start | bytes 983048 | tf_op jit(solution)/shard_map/ppermute | solution.py:55
  82.6 139.8 %all-gather.14.cloned.1.call-start = ((), (), s32[]{:S(2)}) async-start(), calls=%async_computation.23 | async-start | bytes 4718592 | tf_op jit(solution)/shard_map/all_gather | solution.py:215
  95.5 5.5 collective-permute-start.10
  102.8 40.0 %all-to-all-start.1 = ((bf16[8,64,768]{2,1,0:T(8,128)(2,1)}), bf16[8,64,768]{2,1,0:T(8,128)(2,1)S(1)}, u32[]{:S(2)}, u32[]{:S(2)}) async-start(bf16[8,64,768]{2,1,0:T(8,128)(2,1)} %copy.117), calls=%async_computation.1 | async-start | bytes 1572864 | tf_op jit(solution)/shard_map/all_to_all | solution.py:235
  127.4 5.2 collective-permute-start.11
  148.0 47.0 %all-to-all-start.2 = ((bf16[4,128,2048]{2,1,0:T(8,128)(2,1)}), bf16[4,128,2048]{2,1,0:T(8,128)(2,1)S(1)}, u32[]{:S(2)}, u32[]{:S(2)}) async-start(bf16[4,128,2048]{2,1,0:T(8,128)(2,1)} %bitcast.314), calls=%async_computation.2 | async-start | bytes 4194304 | tf_op jit(solution)/shard_map/all_to_all | solution.py:235
  152.6 102.8 %all-gather.16.cloned.1.call-start = ((), (), s32[]{:S(2)}) async-start(), calls=%async_computation.24 | async-start | bytes 3932160 | tf_op jit(solution)/shard_map/all_gather | solution.py:215
  154.1 20.9 %collective-permute-start.14 = (bf16[192,2048]{1,0:T(8,128)(2,1)}, bf16[192,2048]{1,0:T(8,128)(2,1)}, u32[]{:S(2)}, u32[]{:S(2)}) collective-permute-start(bf16[192,2048]{1,0:T(8,128)(2,1)} %refs_0_), channel_id=1, source_target_pairs={{0,2},{1,3},{2,0},{3,1},{4,6},{5,7},{6,4},{7,5},{8,10},{9,11},{10,... | collective-permute-start | bytes 2359304 | tf_op jit(solution)/shard_map/ppermute | solution.py:55
  155.1 32.3 %collective-permute-start.17 = (bf16[192,2048]{1,0:T(8,128)(2,1)}, bf16[192,2048]{1,0:T(8,128)(2,1)S(1)}, u32[]{:S(2)}, u32[]{:S(2)}) collective-permute-start(bf16[192,2048]{1,0:T(8,128)(2,1)} %refs_0_.1), channel_id=1, source_target_pairs={{0,2},{1,3},{2,0},{3,1},{4,6},{5,7},{6,4},{7,5},{8,10},{9,11},{10,... | collective-permute-start | bytes 2359304 | tf_op jit(solution)/shard_map/ppermute | solution.py:55
  156.2 31.3 %collective-permute-start.15 = (bf16[192,2048]{1,0:T(8,128)(2,1)}, bf16[192,2048]{1,0:T(8,128)(2,1)}, u32[]{:S(2)}, u32[]{:S(2)}) collective-permute-start(bf16[192,2048]{1,0:T(8,128)(2,1)} %refs_0_), channel_id=1, source_target_pairs={{0,1},{1,0},{2,3},{3,2},{4,5},{5,4},{6,7},{7,6},{8,9},{9,8},{10,11... | collective-permute-start | bytes 2359304 | tf_op jit(solution)/shard_map/ppermute | solution.py:55
  174.9 12.5 %collective-permute-start.16 = (bf16[192,2048]{1,0:T(8,128)(2,1)}, bf16[192,2048]{1,0:T(8,128)(2,1)}, u32[]{:S(2)}, u32[]{:S(2)}) collective-permute-start(bf16[192,2048]{1,0:T(8,128)(2,1)} %collective-permute-done.14.refs_1_), channel_id=1, source_target_pairs={{0,1},{1,0},{2,3},{3,2},{4,5},{5,4},{6,7},{7,6},{8,9},{9,8},{10,11... | collective-permute-start | bytes 2359304 | tf_op jit(solution)/shard_map/ppermute | solution.py:55
  174.9 16.3 %collective-permute-start.18 = (bf16[192,2048]{1,0:T(8,128)(2,1)}, bf16[192,2048]{1,0:T(8,128)(2,1)}, u32[]{:S(2)}, u32[]{:S(2)}) collective-permute-start(bf16[192,2048]{1,0:T(8,128)(2,1)} %refs_0_.1), channel_id=1, source_target_pairs={{0,1},{1,0},{2,3},{3,2},{4,5},{5,4},{6,7},{7,6},{8,9},{9,8},{10,11... | collective-permute-start | bytes 2359304 | tf_op jit(solution)/shard_map/ppermute | solution.py:55
  187.4 3.9 collective-permute-start.19
  199.7 30.5 %collective-permute-start.23 = (bf16[128,2048]{1,0:T(8,128)(2,1)S(1)}, bf16[128,2048]{1,0:T(8,128)(2,1)S(1)}, u32[]{:S(2)}, u32[]{:S(2)}) collective-permute-start(bf16[128,2048]{1,0:T(8,128)(2,1)S(1)} %multiply_convert_fusion.4.refs_0_), channel_id=1, source_target_pairs={{0,16},{1,17},{2,18},{3,19},{4,20},{5,21},{6,22},{7,23},{8,24},{9,... | collective-permute-start | bytes 1572872 | tf_op jit(solution)/shard_map/ppermute | solution.py:55
  202.4 32.4 %collective-permute-start.20 = (bf16[128,2048]{1,0:T(8,128)(2,1)S(1)}, bf16[128,2048]{1,0:T(8,128)(2,1)}, u32[]{:S(2)}, u32[]{:S(2)}) collective-permute-start(bf16[128,2048]{1,0:T(8,128)(2,1)S(1)} %multiply_convert_fusion.4.refs_0_), channel_id=1, source_target_pairs={{0,4},{1,5},{2,6},{3,7},{4,0},{5,1},{6,2},{7,3},{8,12},{9,13},{10,... | collective-permute-start | bytes 1572872 | tf_op jit(solution)/shard_map/ppermute | solution.py:55
  202.4 32.4 %collective-permute-start.21 = (bf16[128,2048]{1,0:T(8,128)(2,1)S(1)}, bf16[128,2048]{1,0:T(8,128)(2,1)}, u32[]{:S(2)}, u32[]{:S(2)}) collective-permute-start(bf16[128,2048]{1,0:T(8,128)(2,1)S(1)} %multiply_convert_fusion.4.refs_0_), channel_id=1, source_target_pairs={{0,8},{1,9},{2,10},{3,11},{4,12},{5,13},{6,14},{7,15},{8,0},{9,1},... | collective-permute-start | bytes 1572872 | tf_op jit(solution)/shard_map/ppermute | solution.py:55
  202.5 42.4 %collective-permute-start.22 = (bf16[128,2048]{1,0:T(8,128)(2,1)S(1)}, bf16[128,2048]{1,0:T(8,128)(2,1)}, u32[]{:S(2)}, u32[]{:S(2)}) collective-permute-start(bf16[128,2048]{1,0:T(8,128)(2,1)S(1)} %multiply_convert_fusion.4.refs_0_), channel_id=1, source_target_pairs={{0,12},{1,13},{2,14},{3,15},{4,8},{5,9},{6,10},{7,11},{8,4},{9,5},... | collective-permute-start | bytes 1572872 | tf_op jit(solution)/shard_map/ppermute | solution.py:55
  230.2 55.3 %collective-permute-start.24 = (bf16[128,2048]{1,0:T(8,128)(2,1)S(1)}, bf16[128,2048]{1,0:T(8,128)(2,1)S(1)}, u32[]{:S(2)}, u32[]{:S(2)}) collective-permute-start(bf16[128,2048]{1,0:T(8,128)(2,1)S(1)} %collective-permute-done.23.refs_0_), channel_id=1, source_target_pairs={{0,4},{1,5},{2,6},{3,7},{4,0},{5,1},{6,2},{7,3},{8,12},{9,13},{10,... | collective-permute-start | bytes 1572872 | tf_op jit(solution)/shard_map/ppermute | solution.py:55
  232.0 53.6 %collective-permute-start.25 = (bf16[128,2048]{1,0:T(8,128)(2,1)S(1)}, bf16[128,2048]{1,0:T(8,128)(2,1)}, u32[]{:S(2)}, u32[]{:S(2)}) collective-permute-start(bf16[128,2048]{1,0:T(8,128)(2,1)S(1)} %collective-permute-done.23.refs_0_), channel_id=1, source_target_pairs={{0,8},{1,9},{2,10},{3,11},{4,12},{5,13},{6,14},{7,15},{8,0},{9,1},... | collective-permute-start | bytes 1572872 | tf_op jit(solution)/shard_map/ppermute | solution.py:55
  234.9 50.7 %collective-permute-start.26 = (bf16[128,2048]{1,0:T(8,128)(2,1)S(1)}, bf16[128,2048]{1,0:T(8,128)(2,1)}, u32[]{:S(2)}, u32[]{:S(2)}) collective-permute-start(bf16[128,2048]{1,0:T(8,128)(2,1)S(1)} %collective-permute-done.23.refs_0_), channel_id=1, source_target_pairs={{0,12},{1,13},{2,14},{3,15},{4,8},{5,9},{6,10},{7,11},{8,4},{9,5},... | collective-permute-start | bytes 1572872 | tf_op jit(solution)/shard_map/ppermute | solution.py:55
  271.4 37.3 %all-to-all-start.3 = ((bf16[4,128,2048]{2,1,0:T(8,128)(2,1)}), bf16[4,128,2048]{2,1,0:T(8,128)(2,1)}, u32[]{:S(2)}, u32[]{:S(2)}) async-start(bf16[4,128,2048]{2,1,0:T(8,128)(2,1)} %bitcast.316), calls=%async_computation.3 | async-start | bytes 4194304 | tf_op jit(solution)/shard_map/all_to_all | solution.py:235
  276.3 109.1 %reduce-scatter.6.cloned.1.call-start = ((), (), s32[]{:S(2)}) async-start(), calls=%async_computation.18 | async-start | bytes 3932160 | tf_op jit(solution)/shard_map/reduce_scatter | solution.py:219
  300.6 208.3 %reduce-scatter.12.cloned.1.call-start = ((), (), s32[]{:S(2)}) async-start(), calls=%async_computation.21 | async-start | bytes 3932160 | tf_op jit(solution)/shard_map/reduce_scatter | solution.py:219
  342.0 22.1 %collective-permute-start.27 = (bf16[128,2048]{1,0:T(8,128)(2,1)S(1)}, bf16[128,2048]{1,0:T(8,128)(2,1)S(1)}, u32[]{:S(2)}, u32[]{:S(2)}) collective-permute-start(bf16[128,2048]{1,0:T(8,128)(2,1)S(1)} %reduce_sum.132), channel_id=1, source_target_pairs={{0,16},{1,17},{2,18},{3,19},{4,20},{5,21},{6,22},{7,23},{8,24},{9,... | collective-permute-start | bytes 1572872 | tf_op jit(solution)/shard_map/ppermute | solution.py:55
  372.2 139.2 %reduce-scatter.14.cloned.1.call-start = ((), (), s32[]{:S(2)}) async-start(), calls=%async_computation.22 | async-start | bytes 3932160 | tf_op jit(solution)/shard_map/reduce_scatter | solution.py:219
  380.4 20.4 %collective-permute-start.29 = (bf16[128,2048]{1,0:T(8,128)(2,1)S(1)}, bf16[128,2048]{1,0:T(8,128)(2,1)S(1)}, u32[]{:S(2)}, u32[]{:S(2)}) collective-permute-start(bf16[128,2048]{1,0:T(8,128)(2,1)S(1)} %get-tuple-element.134.refs_0_), channel_id=1, source_target_pairs={{0,8},{1,9},{2,10},{3,11},{4,12},{5,13},{6,14},{7,15},{8,0},{9,1},... | collective-permute-start | bytes 1572872 | tf_op jit(solution)/shard_map/ppermute | solution.py:55
  384.0 20.3 %collective-permute-start.28 = (bf16[128,2048]{1,0:T(8,128)(2,1)S(1)}, bf16[128,2048]{1,0:T(8,128)(2,1)S(1)}, u32[]{:S(2)}, u32[]{:S(2)}) collective-permute-start(bf16[128,2048]{1,0:T(8,128)(2,1)S(1)} %get-tuple-element.134.refs_0_), channel_id=1, source_target_pairs={{0,4},{1,5},{2,6},{3,7},{4,0},{5,1},{6,2},{7,3},{8,12},{9,13},{10,... | collective-permute-start | bytes 1572872 | tf_op jit(solution)/shard_map/ppermute | solution.py:55
  387.6 28.9 %collective-permute-start.32 = (bf16[4,64,768]{2,1,0:T(8,128)(2,1)}, bf16[4,64,768]{2,1,0:T(8,128)(2,1)S(1)}, u32[]{:S(2)}, u32[]{:S(2)}) collective-permute-start(bf16[4,64,768]{2,1,0:T(8,128)(2,1)} %get-tuple-element.316), channel_id=1, source_target_pairs={{0,16},{1,17},{2,18},{3,19},{4,20},{5,21},{6,22},{7,23},{8,24},{9,... | collective-permute-start | bytes 1179656 | tf_op jit(solution)/shard_map/ppermute | solution.py:55
  401.6 15.0 %collective-permute-start.30 = (bf16[64,2048]{1,0:T(8,128)(2,1)}, bf16[64,2048]{1,0:T(8,128)(2,1)}, u32[]{:S(2)}, u32[]{:S(2)}) collective-permute-start(bf16[64,2048]{1,0:T(8,128)(2,1)} %slice.149), channel_id=1, source_target_pairs={{0,4},{1,5},{2,6},{3,7},{4,0},{5,1},{6,2},{7,3},{8,12},{9,13},{10,... | collective-permute-start | bytes 786440 | tf_op jit(solution)/shard_map/ppermute | solution.py:55
  404.3 12.2 %collective-permute-start.31 = (bf16[64,2048]{1,0:T(8,128)(2,1)S(1)}, bf16[64,2048]{1,0:T(8,128)(2,1)S(1)}, u32[]{:S(2)}, u32[]{:S(2)}) collective-permute-start(bf16[64,2048]{1,0:T(8,128)(2,1)S(1)} %slice.150), channel_id=1, source_target_pairs={{0,8},{1,9},{2,10},{3,11},{4,12},{5,13},{6,14},{7,15},{8,0},{9,1},... | collective-permute-start | bytes 786440 | tf_op jit(solution)/shard_map/ppermute | solution.py:55
  412.0 32.2 %all-to-all-start.5 = ((bf16[4,128,2048]{2,1,0:T(8,128)(2,1)}), bf16[4,128,2048]{2,1,0:T(8,128)(2,1)}, u32[]{:S(2)}, u32[]{:S(2)}) async-start(bf16[4,128,2048]{2,1,0:T(8,128)(2,1)} %bitcast.315), calls=%async_computation.6 | async-start | bytes 4194304 | tf_op jit(solution)/shard_map/all_to_all | solution.py:235
  416.4 109.0 %reduce-scatter.8.cloned.1.call-start = ((), (), s32[]{:S(2)}) async-start(), calls=%async_computation.19 | async-start | bytes 3276800 | tf_op jit(solution)/shard_map/reduce_scatter | solution.py:219
  437.4 106.4 %reduce-scatter.10.cloned.1.call-start = ((), (), s32[]{:S(2)}) async-start(), calls=%async_computation.20 | async-start | bytes 3276800 | tf_op jit(solution)/shard_map/reduce_scatter | solution.py:219
  438.2 10.7 %collective-permute-start.33 = (f32[4,2,2,640]{3,2,1,0:T(2,128)S(1)}, f32[4,2,2,640]{3,2,1,0:T(2,128)S(1)}, u32[]{:S(2)}, u32[]{:S(2)}) collective-permute-start(f32[4,2,2,640]{3,2,1,0:T(2,128)S(1)} %bitcast.337), channel_id=1, source_target_pairs={{0,16},{1,17},{2,18},{3,19},{4,20},{5,21},{6,22},{7,23},{8,24},{9,... | collective-permute-start | bytes 122888 | tf_op jit(solution)/shard_map/ppermute | solution.py:55
  446.3 25.7 %collective-permute-start.35 = (bf16[128,2048]{1,0:T(8,128)(2,1)S(1)}, bf16[128,2048]{1,0:T(8,128)(2,1)}, u32[]{:S(2)}, u32[]{:S(2)}) collective-permute-start(bf16[128,2048]{1,0:T(8,128)(2,1)S(1)} %reduce_sum.134), channel_id=1, source_target_pairs={{0,16},{1,17},{2,18},{3,19},{4,20},{5,21},{6,22},{7,23},{8,24},{9,... | collective-permute-start | bytes 1572872 | tf_op jit(solution)/shard_map/ppermute | solution.py:55
  465.0 6.8 %collective-permute-start.34 = (bf16[4,2,4,640]{3,2,1,0:T(4,128)(2,1)}, bf16[4,2,4,640]{3,2,1,0:T(4,128)(2,1)S(1)}, u32[]{:S(2)}, u32[]{:S(2)}) collective-permute-start(bf16[4,2,4,640]{3,2,1,0:T(4,128)(2,1)} %bitcast.339), channel_id=1, source_target_pairs={{0,16},{1,17},{2,18},{3,19},{4,20},{5,21},{6,22},{7,23},{8,24},{9,... | collective-permute-start | bytes 122888 | tf_op jit(solution)/shard_map/ppermute | solution.py:55
  480.7 8.3 %collective-permute-start.36 = (bf16[2,2,80,2048]{3,2,0,1:T(8,128)(2,1)}, bf16[2,2,80,2048]{3,2,0,1:T(8,128)(2,1)}, u32[]{:S(2)}, u32[]{:S(2)}) collective-permute-start(bf16[2,2,80,2048]{3,2,0,1:T(8,128)(2,1)} %bitcast.276), channel_id=1, source_target_pairs={{0,1},{1,0},{2,3},{3,2},{4,5},{5,4},{6,7},{7,6},{8,9},{9,8},{10,11... | collective-permute-start | bytes 3932168 | tf_op jit(solution)/shard_map/ppermute | solution.py:55
  491.9 31.4 %all-to-all-start.6 = ((bf16[4,128,2048]{2,1,0:T(8,128)(2,1)}), bf16[4,128,2048]{2,1,0:T(8,128)(2,1)}, u32[]{:S(2)}, u32[]{:S(2)}) async-start(bf16[4,128,2048]{2,1,0:T(8,128)(2,1)} %bitcast.285), calls=%async_computation.8 | async-start | bytes 4194304 | tf_op jit(solution)/shard_map/all_to_all | solution.py:235
  503.3 71.5 %collective-permute-start.40 = (bf16[128,2048]{1,0:T(8,128)(2,1)}, bf16[128,2048]{1,0:T(8,128)(2,1)}, u32[]{:S(2)}, u32[]{:S(2)}) collective-permute-start(bf16[128,2048]{1,0:T(8,128)(2,1)} %get-tuple-element.304), channel_id=1, source_target_pairs={{0,12},{1,13},{2,14},{3,15},{4,8},{5,9},{6,10},{7,11},{8,4},{9,5},... | collective-permute-start | bytes 1572872 | tf_op jit(solution)/shard_map/ppermute | solution.py:55
  504.9 71.3 %collective-permute-start.39 = (bf16[128,2048]{1,0:T(8,128)(2,1)}, bf16[128,2048]{1,0:T(8,128)(2,1)}, u32[]{:S(2)}, u32[]{:S(2)}) collective-permute-start(bf16[128,2048]{1,0:T(8,128)(2,1)} %get-tuple-element.305), channel_id=1, source_target_pairs={{0,8},{1,9},{2,10},{3,11},{4,12},{5,13},{6,14},{7,15},{8,0},{9,1},... | collective-permute-start | bytes 1572872 | tf_op jit(solution)/shard_map/ppermute | solution.py:55
  505.1 71.1 %collective-permute-start.38 = (bf16[128,2048]{1,0:T(8,128)(2,1)}, bf16[128,2048]{1,0:T(8,128)(2,1)}, u32[]{:S(2)}, u32[]{:S(2)}) collective-permute-start(bf16[128,2048]{1,0:T(8,128)(2,1)} %get-tuple-element.306), channel_id=1, source_target_pairs={{0,4},{1,5},{2,6},{3,7},{4,0},{5,1},{6,2},{7,3},{8,12},{9,13},{10,... | collective-permute-start | bytes 1572872 | tf_op jit(solution)/shard_map/ppermute | solution.py:55
  506.8 44.3 %collective-permute-start.44 = (bf16[2,2,80,384]{3,2,0,1:T(8,128)(2,1)}, bf16[2,2,80,384]{3,2,0,1:T(8,128)(2,1)}, u32[]{:S(2)}, u32[]{:S(2)}) collective-permute-start(bf16[2,2,80,384]{3,2,0,1:T(8,128)(2,1)} %bitcast.278), channel_id=1, source_target_pairs={{0,1},{1,0},{2,3},{3,2},{4,5},{5,4},{6,7},{7,6},{8,9},{9,8},{10,11... | collective-permute-start | bytes 737288 | tf_op jit(solution)/shard_map/ppermute | solution.py:55
  506.8 29.3 %collective-permute-start.42 = (bf16[2,80,2048]{2,1,0:T(8,128)(2,1)S(1)}, bf16[2,80,2048]{2,1,0:T(8,128)(2,1)}, u32[]{:S(2)}, u32[]{:S(2)}) collective-permute-start(bf16[2,80,2048]{2,1,0:T(8,128)(2,1)S(1)} %dynamic-slice_bitcast_fusion), channel_id=1, source_target_pairs={{0,2},{1,3},{2,0},{3,1},{4,6},{5,7},{6,4},{7,5},{8,10},{9,11},{10,... | collective-permute-start | bytes 1966088 | tf_op jit(solution)/shard_map/ppermute | solution.py:55
  536.1 28.5 %collective-permute-start.37 = (bf16[4,64,640]{2,1,0:T(8,128)(2,1)}, bf16[4,64,640]{2,1,0:T(8,128)(2,1)}, u32[]{:S(2)}, u32[]{:S(2)}) collective-permute-start(bf16[4,64,640]{2,1,0:T(8,128)(2,1)} %dynamic-slice_bitcast_fusion.9), channel_id=1, source_target_pairs={{0,16},{1,17},{2,18},{3,19},{4,20},{5,21},{6,22},{7,23},{8,24},{9,... | collective-permute-start | bytes 983048 | tf_op jit(solution)/shard_map/ppermute | solution.py:55
  546.2 17.8 %all-to-all-start.7 = ((bf16[32,2,64]{2,1,0:T(2,128)(2,1)}), bf16[32,2,64]{2,1,0:T(2,128)(2,1)S(1)}, u32[]{:S(2)}, u32[]{:S(2)}) async-start(bf16[32,2,64]{2,1,0:T(2,128)(2,1)} %copy.123), calls=%async_computation.10 | async-start | bytes 32768 | tf_op jit(solution)/shard_map/all_to_all | solution.py:911
  551.1 29.2 %collective-permute-start.43 = (bf16[80,2048]{1,0:T(8,128)(2,1)}, bf16[80,2048]{1,0:T(8,128)(2,1)}, u32[]{:S(2)}, u32[]{:S(2)}) collective-permute-start(bf16[80,2048]{1,0:T(8,128)(2,1)} %dynamic-slice_bitcast_fusion.7), channel_id=1, source_target_pairs={{0,16},{1,17},{2,18},{3,19},{4,20},{5,21},{6,22},{7,23},{8,24},{9,... | collective-permute-start | bytes 983048 | tf_op jit(solution)/shard_map/ppermute | solution.py:55
  564.6 33.1 %collective-permute-start.41 = (bf16[80,2048]{1,0:T(8,128)(2,1)}, bf16[80,2048]{1,0:T(8,128)(2,1)}, u32[]{:S(2)}, u32[]{:S(2)}) collective-permute-start(bf16[80,2048]{1,0:T(8,128)(2,1)} %dynamic-slice_bitcast_fusion.8), channel_id=1, source_target_pairs={{0,16},{1,17},{2,18},{3,19},{4,20},{5,21},{6,22},{7,23},{8,24},{9,... | collective-permute-start | bytes 983048 | tf_op jit(solution)/shard_map/ppermute | solution.py:55
  569.5 18.9 %all-to-all-start.8 = ((bf16[4,64,640]{2,1,0:T(8,128)(2,1)}), bf16[4,64,640]{2,1,0:T(8,128)(2,1)}, u32[]{:S(2)}, u32[]{:S(2)}) async-start(bf16[4,64,640]{2,1,0:T(8,128)(2,1)} %fusion.44), calls=%async_computation.11 | async-start | bytes 655360 | tf_op jit(solution)/shard_map/all_to_all | solution.py:235
  574.8 5.5 collective-permute-start.45
  580.3 15.1 %collective-permute-start.46 = (bf16[80,384]{1,0:T(8,128)(2,1)S(1)}, bf16[80,384]{1,0:T(8,128)(2,1)S(1)}, u32[]{:S(2)}, u32[]{:S(2)}) collective-permute-start(bf16[80,384]{1,0:T(8,128)(2,1)S(1)} %dynamic-slice_bitcast_fusion.11), channel_id=1, source_target_pairs={{0,16},{1,17},{2,18},{3,19},{4,20},{5,21},{6,22},{7,23},{8,24},{9,... | collective-permute-start | bytes 184328 | tf_op jit(solution)/shard_map/ppermute | solution.py:55
  588.3 15.6 %all-to-all-start.9 = ((bf16[4,2,64,768]{3,2,1,0:T(8,128)(2,1)}), bf16[4,2,64,768]{3,2,1,0:T(8,128)(2,1)S(1)}, u32[]{:S(2)}, u32[]{:S(2)}) async-start(bf16[4,2,64,768]{3,2,1,0:T(8,128)(2,1)} %pad_maximum_fusion), calls=%async_computation.14 | async-start | bytes 1572864 | tf_op jit(solution)/shard_map/all_to_all | solution.py:235
  (78 other events, 676.0 us)
Sparse Core Ops, SparseCore 0:
  36.9 26.6 all-gather.7
  67.2 26.9 all-gather.9
  95.7 25.5 all-gather.11
  123.3 99.0 all-gather.13
  223.8 31.4 all-gather.15
  300.7 37.9 reduce-scatter.5
  372.3 40.0 reduce-scatter.11
  414.9 37.9 reduce-scatter.13
  455.6 34.6 reduce-scatter.7
  492.7 46.4 reduce-scatter.9

commit v6 on v5

--- a/solution.py
+++ b/solution.py
@@ -278,6 +278,17 @@
             flops=0, bytes_accessed=passes * sum(sizes), transcendentals=0
         ),
     )(scalars, *arrays)
+
+
+LANES = 128
+
+
+def lane_groups(channels):
+    return [slice(c, c + LANES) for c in range(0, channels, LANES)]
+
+
+def column(marks, n, k):
+    return jnp.broadcast_to(marks[n][:, k : k + 1], (marks.shape[1], LANES))
 
 
 def block_number(scalars, n, rows, step):
@@ -359,12 +370,14 @@
     def convolve(n, carry):
         block = block_number(scalars, n, rows, step)
         before = jnp.bitwise_xor(jnp.maximum(block - 1, 0), scalars[0])
-        pad[4:8, :] = halo[before * rows + n % rows]
-        pad[8:, :] = recur[n].astype(F32)
-        total = coef[4:5, :] + coef[0:1, :] * pad[8:, :]
-        for k in range(1, TAPS):
-            total = total + coef[k : k + 1, :] * pad[8 - k : 8 - k + span, :] * marks[n][:, k : k + 1]
-        conv[n] = total.astype(BF16)
+        same = [column(marks, n, k) for k in range(1, TAPS)]
+        for at in lane_groups(channels):
+            pad[4:8, at] = halo[before * rows + n % rows, :, at]
+            pad[8:, at] = recur[n, :, at].astype(F32)
+            total = coef[4:5, at] + coef[0:1, at] * pad[8:, at]
+            for k in range(1, TAPS):
+                total = total + coef[k : k + 1, at] * pad[8 - k : 8 - k + span, at] * same[k - 1]
+            conv[n, :, at] = total.astype(BF16)
         return carry
 
     lax.fori_loop(0, count, convolve, 0)
@@ -373,17 +386,19 @@
     q_out[...] = project(flat, gate_w[...]).reshape(count, span, channels)
 
     def scan(n, carry):
-        s = jax.nn.sigmoid(s_out[n] + coef[5:6, :])
-        q = jax.nn.sigmoid(q_out[n] + coef[6:7, :])
-        s_out[n] = s
-        q_out[n] = q
-        e, m = injection(s, coef[7:8, :])
-        decay = e * (1.0 - marks[n][:, 0:1])
-        p_all, h_all, p, h = span_scan(decay, m * q * conv[n].astype(F32), False)
-        prod[n] = p_all
-        part[n] = h_all
-        ends[n, 0:1, :] = p
-        ends[n, 1:2, :] = h
+        going = 1.0 - column(marks, n, 0)
+        for at in lane_groups(channels):
+            s = jax.nn.sigmoid(s_out[n, :, at] + coef[5:6, at])
+            q = jax.nn.sigmoid(q_out[n, :, at] + coef[6:7, at])
+            s_out[n, :, at] = s
+            q_out[n, :, at] = q
+            e, m = injection(s, coef[7:8, at])
+            inject = m * q * conv[n, :, at].astype(F32)
+            p_all, h_all, p, h = span_scan(e * going, inject, False)
+            prod[n, :, at] = p_all
+            part[n, :, at] = h_all
+            ends[n, 0:1, at] = p
+            ends[n, 1:2, at] = h
         return carry
 
     lax.fori_loop(0, count, scan, 0)
@@ -409,11 +424,13 @@
     join(ends, into, scalars, rows, into.shape[0] // rows, False)
 
     def finish(n, carry):
-        incoming = into[block_number(scalars, n, rows, step) * rows + n % rows]
-        h = part[n] + prod[n] * incoming
-        came[n] = incoming
-        state[n] = h
-        mixed[n] = (h * gelu_parts(branch[n])[0]).astype(BF16)
+        place = block_number(scalars, n, rows, step) * rows + n % rows
+        for at in lane_groups(prod.shape[2]):
+            incoming = into[place, :, at]
+            h = part[n, :, at] + prod[n, :, at] * incoming
+            came[n, :, at] = incoming
+            state[n, :, at] = h
+            mixed[n, :, at] = (h * gelu_parts(branch[n, :, at])[0]).astype(BF16)
         return carry
 
     lax.fori_loop(0, count, finish, 0)
@@ -426,16 +443,18 @@
     pad[span:, :] = jnp.ones((8, channels), F32)
 
     def scan(n, carry):
-        act, slope = gelu_parts(branch[n])
-        grad = grad_mixed[n]
-        grad_branch[n] = (grad * state[n] * slope).astype(BF16)
-        decay = jnp.exp(-coef[7:8, :] * s_in[n]) * (1.0 - marks[n][:, 0:1])
-        pad[:span, :] = decay
-        p_all, h_all, p, h = span_scan(pad[1 : span + 1, :], grad * act, True)
-        prod[n] = p_all
-        part[n] = h_all
-        ends[n, 0:1, :] = decay[0:1] * p
-        ends[n, 1:2, :] = decay[0:1] * h
+        going = 1.0 - column(marks, n, 0)
+        for at in lane_groups(channels):
+            act, slope = gelu_parts(branch[n, :, at])
+            grad = grad_mixed[n, :, at]
+            grad_branch[n, :, at] = (grad * state[n, :, at] * slope).astype(BF16)
+            decay = jnp.exp(-coef[7:8, at] * s_in[n, :, at]) * going
+            pad[:span, at] = decay
+            p_all, h_all, p, h = span_scan(pad[1 : span + 1, at], grad * act, True)
+            prod[n, :, at] = p_all
+            part[n, :, at] = h_all
+            ends[n, 0:1, at] = decay[0:1] * p
+            ends[n, 1:2, at] = decay[0:1] * h
         return carry
 
     lax.fori_loop(0, count, scan, 0)
@@ -451,23 +470,27 @@
     sums[...] = jnp.zeros((8, channels), F32)
 
     def terms(n, carry):
-        block = block_number(scalars, n, rows, step)
-        total = part[n] + prod[n] * into[block * rows + n % rows]
-        pad[7:8, :] = came[n]
-        pad[8:, :] = state[n]
-        s, q = s_in[n], q_in[n]
-        e, m = injection(s, coef[7:8, :])
-        c = conv[n].astype(F32)
-        first = marks[n][:, 0:1]
-        grad_log = total * (pad[7 : 7 + span, :] * e * (1.0 - first) - e * e * q * c / m)
-        rate = -coef[7:8, :] * s * (1.0 - s) * grad_log
-        gate = total * m * c * q * (1.0 - q)
-        grad_conv[n] = total * m * q
-        grad_rate[pl.ds(pl.multiple_of(n * span, span), span), :] = rate.astype(BF16)
-        grad_gate[pl.ds(pl.multiple_of(n * span, span), span), :] = gate.astype(BF16)
-        sums[5:6, :] += jnp.sum(rate, axis=0, keepdims=True)
-        sums[6:7, :] += jnp.sum(gate, axis=0, keepdims=True)
-        sums[7:8, :] += jnp.sum(coef[8:9, :] * s * grad_log, axis=0, keepdims=True)
+        place = block_number(scalars, n, rows, step) * rows + n % rows
+        going = 1.0 - column(marks, n, 0)
+        here = pl.ds(pl.multiple_of(n * span, span), span)
+        for at in lane_groups(channels):
+            total = part[n, :, at] + prod[n, :, at] * into[place, :, at]
+            pad[7:8, at] = came[n, :, at]
+            pad[8:, at] = state[n, :, at]
+            s, q = s_in[n, :, at], q_in[n, :, at]
+            speed = coef[7:8, at]
+            e, m = injection(s, speed)
+            c = conv[n, :, at].astype(F32)
+            qc = q * c
+            grad_log = total * e * (pad[7 : 7 + span, at] * going - e * qc / m)
+            rate = -speed * (s * (1.0 - s)) * grad_log
+            gate = total * m * qc * (1.0 - q)
+            grad_conv[n, :, at] = total * m * q
+            grad_rate[here, at] = rate.astype(BF16)
+            grad_gate[here, at] = gate.astype(BF16)
+            sums[5:6, at] += jnp.sum(rate, axis=0, keepdims=True)
+            sums[6:7, at] += jnp.sum(gate, axis=0, keepdims=True)
+            sums[7:8, at] += jnp.sum(coef[8:9, at] * s * grad_log, axis=0, keepdims=True)
         return carry
 
     lax.fori_loop(0, count, terms, 0)
@@ -478,15 +501,17 @@
     def kernel_terms(n, carry):
         block = block_number(scalars, n, rows, step)
         before = jnp.bitwise_xor(jnp.maximum(block - 1, 0), scalars[0])
-        pad_two[4:8, :] = halo[before * rows + n % rows]
-        pad_two[8:, :] = recur[n].astype(F32)
-        grad = grad_conv[n]
-        edges[n] = grad[:4].astype(BF16)
-        sums[4:5, :] += jnp.sum(grad, axis=0, keepdims=True)
-        sums[0:1, :] += jnp.sum(grad * pad_two[8:, :], axis=0, keepdims=True)
-        for k in range(1, TAPS):
-            term = grad * pad_two[8 - k : 8 - k + span, :] * marks[n][:, k : k + 1]
-            sums[k : k + 1, :] += jnp.sum(term, axis=0, keepdims=True)
+        same = [column(marks, n, k) for k in range(1, TAPS)]
+        for at in lane_groups(channels):
+            pad_two[4:8, at] = halo[before * rows + n % rows, :, at]
+            pad_two[8:, at] = recur[n, :, at].astype(F32)
+            grad = grad_conv[n, :, at]
+            edges[n, :, at] = grad[:4].astype(BF16)
+            sums[4:5, at] += jnp.sum(grad, axis=0, keepdims=True)
+            sums[0:1, at] += jnp.sum(grad * pad_two[8:, at], axis=0, keepdims=True)
+            for k in range(1, TAPS):
+                term = grad * pad_two[8 - k : 8 - k + span, at] * same[k - 1]
+                sums[k : k + 1, at] += jnp.sum(term, axis=0, keepdims=True)
         return carry
 
     lax.fori_loop(0, count, kernel_terms, 0)
@@ -505,13 +530,14 @@
     def body(n, carry):
         block = block_number(scalars, n, rows, step)
         behind = jnp.bitwise_xor(jnp.minimum(block + 1, blocks - 1), scalars[0])
-        pad[:span, :] = grad_conv[n]
-        pad[span : span + 4, :] = halo[behind * rows + n % rows]
-        total = coef[0:1, :] * pad[:span, :]
-        for k in range(1, TAPS):
-            seen = marks[n][:, 3 + k : 4 + k]
-            total = total + coef[k : k + 1, :] * pad[k : k + span, :] * seen
-        grad_recur[n] = total.astype(BF16)
+        seen = [column(marks, n, 3 + k) for k in range(1, TAPS)]
+        for at in lane_groups(channels):
+            pad[:span, at] = grad_conv[n, :, at]
+            pad[span : span + 4, at] = halo[behind * rows + n % rows, :, at]
+            total = coef[0:1, at] * pad[:span, at]
+            for k in range(1, TAPS):
+                total = total + coef[k : k + 1, at] * pad[k : k + span, at] * seen[k - 1]
+            grad_recur[n, :, at] = total.astype(BF16)
         return carry
 
     lax.fori_loop(0, count, body, 0)
@@ -652,8 +678,8 @@
         input_gate_weight,
     ).astype(BF16)
     small_shape = small.shape
-    one, two = (trade(fence(input_own, gains_got), mask) for mask in (low, 2 * low))
-    recur_pair = pair_up(recur_weight, above, me, small, one, two)
+    one, two = (trade(input_own, mask) for mask in (low, 2 * low))
+    recur_pair = pair_up(recur_weight, above, me, gains_got)
     recur_q = gather_along(recur_pair, below, 1).reshape(channels, width)
     small = fence(small, recur_pair)
     for i, b in enumerate(dp):
@@ -757,7 +783,7 @@
     unit_two = residual * scale_two
     normed_own = (unit_two * gain_two).astype(BF16)
     normed_far = trade(normed_own, wide)
-    near_list = share_direct(normed_own, low)
+    near_list = share_list(normed_own, low)
     far_list = share_direct(normed_far, low)
     near = place_tokens(near_list, low, me)
     cot_all = fence(cot_all, normed_own)
@@ -766,8 +792,7 @@
     ranks_shape = (4, tokens, width)
     far = place_tokens(fence_all(far_list, near_out[0]), low, me)
     far_out = feed_forward(far, cot_far, gate_q, up_q, down_q)
-    grad_two_near = sum_tokens(near_out[0].reshape(ranks_shape), step)
-    grad_far_parts = exchange(fence(far_out[0], grad_two_near).reshape(ranks_shape), step)
+    grad_far_parts = exchange(far_out[0].reshape(ranks_shape), step)
 
     def finish(partial, bits):
         partial = partial.reshape((2,) * len(bits) + partial.shape[1:])
@@ -784,6 +809,13 @@
     grad_far_parts = fence(grad_far_parts, down_grad)
     down_grad = finish(scatter_along(down_grad, below, 2), above_wide).reshape(8, out_rows, hidden)
     grad_two_far = jnp.sum(grad_far_parts.astype(F32), axis=0).astype(BF16)
+    grad_near_parts = exchange(fence(near_out[0], grad_two_far).reshape(ranks_shape), step)
+    gate_grad = both(near_out, far_out, 2).astype(BF16).reshape(high_wide, -1, width)
+    up_grad = both(near_out, far_out, 3).astype(BF16).reshape(high_wide, -1, width)
+    grad_near_parts = fence(grad_near_parts, gate_grad, up_grad)
+    gate_grad = finish(scatter_along(gate_grad, below, 1), above_wide)
+    up_grad = finish(scatter_along(up_grad, below, 1), above_wide)
+    grad_two_near = jnp.sum(grad_near_parts.astype(F32), axis=0)
     grad_two = grad_two_near + trade(grad_two_far, wide).astype(F32)
     scaled = grad_two * gain_two
     grad_residual = cot_own.astype(F32) + scale_two * (
@@ -794,16 +826,11 @@
     grad_mix_own = grad_residual.astype(BF16)
     grad_mix_list = share_list(grad_mix_own, low)
     down_far = project(fence(far_out[1], grad_mix_own), down_q).astype(BF16)
-    late = [fence_all(out[2:], grad_mix_own) for out in (near_out, far_out)]
-    gate_grad = both(*late, 0).astype(BF16).reshape(high_wide, -1, width)
-    up_grad = both(*late, 1).astype(BF16).reshape(high_wide, -1, width)
     down_far_parts = exchange(fence(down_far, *grad_mix_list[1:3]).reshape(ranks_shape), step)
     down_parts = fence(down_grad, grad_mix_own).reshape(2, 4, out_rows, hidden)
     down_sent, down_kept = halves(down_parts, 0, wide, me)
     down_got = trade(down_sent, wide)
-    grad_mix = place_tokens(fence_all(grad_mix_list, down_got, gate_grad, up_grad, down_far), low, me)
-    gate_grad = finish(scatter_along(gate_grad, below, 1), above_wide)
-    up_grad = finish(scatter_along(up_grad, below, 1), above_wide)
+    grad_mix = place_tokens(fence_all(grad_mix_list, down_got, down_far), low, me)
     grad_mixed = back_project(grad_mix, mixer_q).reshape(shape)
     grad_branch, prod_back, part_back, own_ends = call(
         adjoint_kernel,
@@ -883,9 +910,9 @@
         return Reduction(partial, range(len(above)), above, me)
 
     mixer_grad, branch_grad = halve(mixer_grad), halve(branch_grad)
-    mixer_sent = mixer_grad.send_to(0)
-    recur_sent = recur_grad.send_to(0, grad_normed, mixer_sent)
-    sent = branch_grad.send_to(0, recur_sent)
+    recur_sent = recur_grad.send_to(0, grad_normed)
+    mixer_sent = mixer_grad.send_to(0, recur_sent)
+    sent = branch_grad.send_to(0, mixer_sent)
     packed_sent = packed.send_to(0, sent)
     pair = jnp.stack([fence(part, packed_sent) for part in (down_kept, down_got)], axis=1)
     pair = exchange(pair, step)

time: 622 us -> 615 us (0.989)
  blocking collectives: 28.6 us -> 0 us
  waiting for transfers between devices: 197 us -> 210 us
  starting transfers between devices: 107 us -> 115 us
    all_to_all x8 -> x9, waiting for transfers between devices: 16.5 us -> 67.3 us  [exchange(): lax.all_to_all(parts, 'seq', 0, 0, axis_index_groups=groups, tiled=True)]
    all_to_all x1 -> x0, blocking collectives: 28.6 us -> none  [exchange(): lax.all_to_all(parts, 'seq', 0, 0, axis_index_groups=groups, tiled=True)]
    ppermute x47 -> x48, waiting for transfers between devices: 150 us -> 130 us  [trade(): return lax.ppermute(value, AXES, [(i, i ^ mask) for i in range(count)])]
    all_gather x5, waiting for transfers between devices: 19.4 us -> 3.19 us  [gather_along(): return lax.all_gather(own, axis=axis, tiled=True, **line_of(bits))]
    all_to_all x8 -> x9, starting transfers between devices: 43.6 us -> 50.1 us  [exchange(): lax.all_to_all(parts, 'seq', 0, 0, axis_index_groups=groups, tiled=True)]
    unnamed x155 -> x135, local copies, waits for them, and re-layouts: 14.9 us -> 12.8 us
    ppermute x47 -> x48, starting transfers between devices: 57.5 us -> 58.2 us  [trade(): return lax.ppermute(value, AXES, [(i, i ^ mask) for i in range(count)])]
  transfers between devices with their start and end apart: 66 -> 68, of which waited for: 24 -> 27; matrix products, arithmetic and copies ran while one was open for 29% -> 28% of each run, Pallas kernels for 11% -> 10%
where the time goes in v6:
time: 615 us; the launch traced here: 604 us
  waiting for transfers between devices  210 us (34%)
  starting transfers between devices  115 us (19%)
  matrix products  101 us (16%)
  Pallas kernels  66.4 us (11%)
  other arithmetic  49.1 us (8%)
  local copies, waits for them, and re-layouts  45.6 us (7%)
  between operations  15.8 us (3%)
    ppermute x48, waiting for transfers between devices, trade(): return lax.ppermute(value, AXES, [(i, i ^ mask) for i in range(count)])  130 us
    all_to_all x9, waiting for transfers between devices, exchange(): lax.all_to_all(parts, 'seq', 0, 0, axis_index_groups=groups, tiled=True)  67.3 us
    ppermute x48, starting transfers between devices, trade(): return lax.ppermute(value, AXES, [(i, i ^ mask) for i in range(count)])  58.2 us
    all_to_all x9, starting transfers between devices, exchange(): lax.all_to_all(parts, 'seq', 0, 0, axis_index_groups=groups, tiled=True)  50.1 us
    pallas_call x5, Pallas kernels, call(): pl.pallas_call(body, out_shape=[jax.ShapeDtypeStruct(shape, kind) for sha...  43.3 us
    dot_general x9, matrix products, project(): lax.dot_general(left, weight, (((1,), (1,)), ((), ())), preferred_element...  38.1 us
    dot_general x9, matrix products, back_project(): lax.dot_general(left, weight, (((1,), (0,)), ((), ())), preferred_element...  34.2 us
    dot_general x9, matrix products, outer(): lax.dot_general(grads, values, (((0,), (0,)), ((), ())), preferred_elemen...  28.8 us
  transfers between devices with their start and end apart: 68, of which 27 were waited for; matrix products, arithmetic and copies ran while one was open for 28% of the time, Pallas kernels for 10%

profile of v6, /device:TPU:20, one launch (start us, length us, event | category | flops | bytes accessed | tf_op | source)
XLA Modules:
  0.0 603.7 jit_solution(18340655349652402951)
XLA Ops:
  10.0 6.9 %collective-permute-done.4 = bf16[2,64]{1,0:T(2,128)(2,1)S(1)} collective-permute-done((bf16[2,64]{1,0:T(2,128)(2,1)S(1)}, bf16[2,64]{1,0:T(2,128)(2,1)S(1)}, u32[]{:S(2)}, u32[]{:S(2)}) %collective-permute-start.4) | collective-permute-done | bytes 288 | tf_op jit(solution)/shard_map/ppermute | solution.py:55
  18.2 3.1 collective-permute-done.5
  27.8 3.3 collective-permute-start.7
  31.2 3.3 collective-permute-done.7
  36.1 3.0 collective-permute-start.1
  41.4 4.9 all-to-all-start
  46.9 10.9 %collective-permute-done.1.refs_2_ = bf16[128,2048]{1,0:T(8,128)(2,1)S(1)} collective-permute-done((bf16[128,2048]{1,0:T(8,128)(2,1)S(1)}, bf16[128,2048]{1,0:T(8,128)(2,1)S(1)}, u32[]{:S(2)}, u32[]{:S(2)}) %collective-permute-start.1) | collective-permute-done | bytes 524320 | tf_op jit(solution)/shard_map/ppermute | solution.py:55
  69.0 10.5 %collective-permute-done.13 = bf16[4,64,640]{2,1,0:T(8,128)(2,1)S(1)} collective-permute-done((bf16[4,64,640]{2,1,0:T(8,128)(2,1)S(1)}, bf16[4,64,640]{2,1,0:T(8,128)(2,1)S(1)}, u32[]{:S(2)}, u32[]{:S(2)}) %collective-permute-start.13) | collective-permute-done | bytes 327712 | tf_op jit(solution)/shard_map/ppermute | solution.py:55
  90.1 3.6 convolution_convert_fusion.6
  94.6 3.4 collective-permute-start.10
  102.2 8.2 %all-to-all-start.1 = ((bf16[8,64,768]{2,1,0:T(8,128)(2,1)}), bf16[8,64,768]{2,1,0:T(8,128)(2,1)S(1)}, u32[]{:S(2)}, u32[]{:S(2)}) async-start(bf16[8,64,768]{2,1,0:T(8,128)(2,1)} %copy.117), calls=%async_computation.1 | async-start | bytes 1572864 | tf_op jit(solution)/shard_map/all_to_all | solution.py:235
  113.4 12.4 %shard_map.343 = (bf16[8,64,640]{2,1,0:T(8,128)(2,1)}, f32[8,64,640]{2,1,0:T(8,128)}, f32[8,64,640]{2,1,0:T(8,128)}, f32[8,64,640]{2,1,0:T(8,128)}, f32[8,64,640...) custom-call(s32[5]{0:T(128)} %pad_add_fusion.scalars, ...), custom_call_target="tpu_custom_call" | custom-call | bytes 39550976 | tf_op jit(solution)/shard_map/pallas_call | solution.py:269
  126.4 4.6 collective-permute-done.11
  132.5 4.6 fusion.58
  137.1 4.2 shard_map.344
  141.3 5.1 convolution_convert_fusion.5
  146.4 4.6 all-to-all-start.2
  154.6 18.8 %collective-permute-done.14.refs_1_ = bf16[192,2048]{1,0:T(8,128)(2,1)} collective-permute-done((bf16[192,2048]{1,0:T(8,128)(2,1)}, bf16[192,2048]{1,0:T(8,128)(2,1)}, u32[]{:S(2)}, u32[]{:S(2)}) %collective-permute-start.14) | collective-permute-done | bytes 786464 | tf_op jit(solution)/shard_map/ppermute | solution.py:55
  173.9 12.0 %collective-permute-done.17.refs_1_ = bf16[192,2048]{1,0:T(8,128)(2,1)S(1)} collective-permute-done((bf16[192,2048]{1,0:T(8,128)(2,1)}, bf16[192,2048]{1,0:T(8,128)(2,1)S(1)}, u32[]{:S(2)}, u32[]{:S(2)}) %collective-permute-start.17) | collective-permute-done | bytes 786464 | tf_op jit(solution)/shard_map/ppermute | solution.py:55
  185.9 3.8 shard_map.345
  189.7 3.6 shard_map.346
  201.0 27.6 %collective-permute-done.21.refs_2_ = bf16[128,2048]{1,0:T(8,128)(2,1)S(1)} collective-permute-done((bf16[128,2048]{1,0:T(8,128)(2,1)S(1)}, bf16[128,2048]{1,0:T(8,128)(2,1)S(1)}, u32[]{:S(2)}, u32[]{:S(2)}) %collective-permute-start.21) | collective-permute-done | bytes 524320 | tf_op jit(solution)/shard_map/ppermute | solution.py:55
  234.7 3.1 collective-permute-start.27
  238.8 3.1 collective-permute-done.23.refs_4_
  244.8 4.6 fusion.64
  249.4 3.2 all-gather.16.cloned.1.call-done
  264.3 3.3 add_convert_fusion.5
  267.5 3.1 fusion.9
  273.5 4.5 fusion.66
  280.1 4.0 fusion.32
  284.1 3.5 add_convert_fusion.2
  288.2 3.6 fusion.68
  291.8 3.5 fusion.5
  295.3 4.7 fusion.67
  300.0 3.1 add_convert_fusion.4
  303.1 5.0 all-to-all-start.3
  308.1 3.6 fusion.69
  311.7 3.5 fusion.6
  315.2 18.0 %all-to-all-done.3 = bf16[4,128,2048]{2,1,0:T(8,128)(2,1)} async-done(((bf16[4,128,2048]{2,1,0:T(8,128)(2,1)}), bf16[4,128,2048]{2,1,0:T(8,128)(2,1)}, u32[]{:S(2)}, u32[]{:S(2)}) %all-to-all-start.3) | async-done | bytes 2097184 | tf_op jit(solution)/shard_map/all_to_all | solution.py:235
  335.8 5.2 all-to-all-start.4
  341.3 32.7 %all-to-all-done.4 = bf16[4,128,2048]{2,1,0:T(8,128)(2,1)} async-done(((bf16[4,128,2048]{2,1,0:T(8,128)(2,1)}), bf16[4,128,2048]{2,1,0:T(8,128)(2,1)}, u32[]{:S(2)}, u32[]{:S(2)}) %all-to-all-start.4) | async-done | bytes 2097184 | tf_op jit(solution)/shard_map/all_to_all | solution.py:235
  384.9 12.6 %collective-permute-done.30.refs_2_ = bf16[128,2048]{1,0:T(8,128)(2,1)S(1)} collective-permute-done((bf16[128,2048]{1,0:T(8,128)(2,1)S(1)}, bf16[128,2048]{1,0:T(8,128)(2,1)S(1)}, u32[]{:S(2)}, u32[]{:S(2)}) %collective-permute-start.30) | collective-permute-done | bytes 524320 | tf_op jit(solution)/shard_map/ppermute | solution.py:55
  403.8 5.1 convolution_convert_fusion.4
  408.9 4.5 all-to-all-start.5
  413.5 3.0 shard_map.349
  416.6 4.5 fusion.70.grad_mixed
  421.1 8.9 %shard_map.350 = (bf16[8,64,640]{2,1,0:T(8,128)(2,1)}, f32[8,64,640]{2,1,0:T(8,128)}, f32[8,64,640]{2,1,0:T(8,128)}, f32[8,2,640]{2,1,0:T(2,128)}) custom-call(s32[5]{0:T(128)} %pad_add_fusion.scalars, f32[8,64,640]{2,1,0:T(8,128)} %fusion.70.grad_mixed, f32[8,64,640]{2,1,0:T(8,128)} %get-tuple-element.131.state, f32[8,64,640]{2,1,0:T(8,128)} %bitcast.287, ...), custom_call_target="tpu_custom_call" | custom-call | bytes 25853952 | tf_op jit(solution)/shard_map/pallas_call | solution.py:269
  430.0 3.3 convolution_convert_fusion.2
  434.4 5.6 fusion.71
  445.8 14.3 %shard_map.351 = (f32[8,64,640]{2,1,0:T(8,128)}, bf16[8,4,640]{2,1,0:T(4,128)(2,1)}, bf16[640,384]{1,0:T(8,128)(2,1)}) custom-call(s32[5]{0:T(128)} %pad_add_fusion.scalars, f32[8,64,640]{2,1,0:T(8,128)} %get-tuple-element.136.prod, f32[8,64,640]{2,1,0:T(8,128)} %get-tuple-element.137.part, f32[16,2,640]{2,1,0:T(2,128)} %bitcast.330, ...), custom_call_target="tpu_custom_call" | custom-call | bytes 59129856 | tf_op jit(solution)/shard_map/pallas_call | solution.py:269
  460.2 3.2 convolution_convert_fusion.1
  466.6 3.5 shard_map.352
  476.1 6.4 %add_convert_fusion.3 = bf16[512,2048]{1,0:T(8,128)(2,1)} fusion(f32[512,2048]{1,0:T(8,128)} %fusion.71, bf16[512,640]{1,0:T(8,128)(2,1)} %bitcast.325, bf16[640,2048]{1,0:T(8,128)(2,1)} %bitcast.361), kind=kOutput, calls=%fused_computation.12 | convolution fusion | flops 1344274432 | bytes 9568256 | tf_op jit(solution)/shard_map/dot_general | solution.py:247
  485.5 7.0 %all-to-all-start.6 = ((bf16[4,128,2048]{2,1,0:T(8,128)(2,1)}), bf16[4,128,2048]{2,1,0:T(8,128)(2,1)}, u32[]{:S(2)}, u32[]{:S(2)}) async-start(bf16[4,128,2048]{2,1,0:T(8,128)(2,1)} %bitcast.285), calls=%async_computation.8 | async-start | bytes 4194304 | tf_op jit(solution)/shard_map/all_to_all | solution.py:235
  498.2 3.8 convolution_convert_fusion.3
  508.7 9.8 %all-to-all-done.6 = bf16[4,128,2048]{2,1,0:T(8,128)(2,1)} async-done(((bf16[4,128,2048]{2,1,0:T(8,128)(2,1)}), bf16[4,128,2048]{2,1,0:T(8,128)(2,1)}, u32[]{:S(2)}, u32[]{:S(2)}) %all-to-all-start.6) | async-done | bytes 2097184 | tf_op jit(solution)/shard_map/all_to_all | solution.py:235
  530.9 5.9 all-to-all-start.7
  539.2 9.5 %all-to-all-done.7 = bf16[32,2,64]{2,1,0:T(2,128)(2,1)S(1)} async-done(((bf16[32,2,64]{2,1,0:T(2,128)(2,1)}), bf16[32,2,64]{2,1,0:T(2,128)(2,1)S(1)}, u32[]{:S(2)}, u32[]{:S(2)}) %all-to-all-start.7) | async-done | bytes 8224 | tf_op jit(solution)/shard_map/all_to_all | solution.py:938
  553.6 5.6 all-to-all-start.8
  560.1 4.0 fusion.38
  564.1 3.0 collective-permute-done.44
  567.2 3.5 collective-permute-start.47
  571.7 6.6 %all-to-all-done.8 = bf16[4,64,640]{2,1,0:T(8,128)(2,1)} async-done(((bf16[4,64,640]{2,1,0:T(8,128)(2,1)}), bf16[4,64,640]{2,1,0:T(8,128)(2,1)}, u32[]{:S(2)}, u32[]{:S(2)}) %all-to-all-start.8) | async-done | bytes 327712 | tf_op jit(solution)/shard_map/all_to_all | solution.py:235
  578.3 5.2 all-to-all-start.9
  (375 shorter events, 171.4 us)
Async XLA Ops:
  7.2 82.3 %all-gather.8.cloned.1.call-start = ((), (), s32[]{:S(2)}) async-start(), calls=%async_computation.15 | async-start | bytes 3276800 | tf_op jit(solution)/shard_map/all_gather | solution.py:215
  7.3 14.7 %collective-permute-start.6 = (bf16[80,2048]{1,0:T(8,128)(2,1)}, bf16[80,2048]{1,0:T(8,128)(2,1)S(1)}, u32[]{:S(2)}, u32[]{:S(2)}) collective-permute-start(bf16[80,2048]{1,0:T(8,128)(2,1)} %param.26), channel_id=1, source_target_pairs={{0,16},{1,17},{2,18},{3,19},{4,20},{5,21},{6,22},{7,23},{8,24},{9,... | collective-permute-start | bytes 983048 | tf_op jit(solution)/shard_map/ppermute | solution.py:55
  8.3 8.6 %collective-permute-start.4 = (bf16[2,64]{1,0:T(2,128)(2,1)S(1)}, bf16[2,64]{1,0:T(2,128)(2,1)S(1)}, u32[]{:S(2)}, u32[]{:S(2)}) collective-permute-start(bf16[2,64]{1,0:T(2,128)(2,1)S(1)} %pad_maximum_fusion.13), channel_id=1, source_target_pairs={{0,8},{1,9},{2,10},{3,11},{4,12},{5,13},{6,14},{7,15},{8,0},{9,1},... | collective-permute-start | bytes 776 | tf_op jit(solution)/shard_map/ppermute | solution.py:55
  27.8 6.7 %collective-permute-start.7 = (bf16[96,384]{1,0:T(8,128)(2,1)S(1)}, bf16[96,384]{1,0:T(8,128)(2,1)S(1)}, u32[]{:S(2)}, u32[]{:S(2)}) collective-permute-start(bf16[96,384]{1,0:T(8,128)(2,1)S(1)} %convert_element_type.280), channel_id=1, source_target_pairs={{0,16},{1,17},{2,18},{3,19},{4,20},{5,21},{6,22},{7,23},{8,24},{9,... | collective-permute-start | bytes 221192 | tf_op jit(solution)/shard_map/ppermute | solution.py:55
  34.6 12.1 %collective-permute-start.8 = (bf16[2,96,384]{2,1,0:T(8,128)(2,1)S(1)}, bf16[2,96,384]{2,1,0:T(8,128)(2,1)S(1)}, u32[]{:S(2)}, u32[]{:S(2)}) collective-permute-start(bf16[2,96,384]{2,1,0:T(8,128)(2,1)S(1)} %pad_maximum_fusion.6), channel_id=1, source_target_pairs={{0,2},{1,3},{2,0},{3,1},{4,6},{5,7},{6,4},{7,5},{8,10},{9,11},{10,... | collective-permute-start | bytes 442376 | tf_op jit(solution)/shard_map/ppermute | solution.py:55
  36.1 21.7 %collective-permute-start.1 = (bf16[128,2048]{1,0:T(8,128)(2,1)S(1)}, bf16[128,2048]{1,0:T(8,128)(2,1)S(1)}, u32[]{:S(2)}, u32[]{:S(2)}) collective-permute-start(bf16[128,2048]{1,0:T(8,128)(2,1)S(1)} %bitcast.282), channel_id=1, source_target_pairs={{0,8},{1,9},{2,10},{3,11},{4,12},{5,13},{6,14},{7,15},{8,0},{9,1},... | collective-permute-start | bytes 1572872 | tf_op jit(solution)/shard_map/ppermute | solution.py:55
  39.2 19.2 %collective-permute-start = (bf16[128,2048]{1,0:T(8,128)(2,1)S(1)}, bf16[128,2048]{1,0:T(8,128)(2,1)S(1)}, u32[]{:S(2)}, u32[]{:S(2)}) collective-permute-start(bf16[128,2048]{1,0:T(8,128)(2,1)S(1)} %bitcast.283), channel_id=1, source_target_pairs={{0,4},{1,5},{2,6},{3,7},{4,0},{5,1},{6,2},{7,3},{8,12},{9,13},{10,... | collective-permute-start | bytes 1572872 | tf_op jit(solution)/shard_map/ppermute | solution.py:55
  41.4 24.6 %all-to-all-start = ((bf16[4,64,640]{2,1,0:T(8,128)(2,1)}), bf16[4,64,640]{2,1,0:T(8,128)(2,1)S(1)}, u32[]{:S(2)}, u32[]{:S(2)}) async-start(bf16[4,64,640]{2,1,0:T(8,128)(2,1)} %reshape.336), calls=%async_computation | async-start | bytes 655360 | tf_op jit(solution)/shard_map/all_to_all | solution.py:235
  46.4 86.1 %all-gather.10.cloned.1.call-start = ((), (), s32[]{:S(2)}) async-start(), calls=%async_computation.16 | async-start | bytes 3276800 | tf_op jit(solution)/shard_map/all_gather | solution.py:215
  46.4 16.6 %collective-permute-start.12 = (bf16[80,2048]{1,0:T(8,128)(2,1)S(1)}, bf16[80,2048]{1,0:T(8,128)(2,1)S(1)}, u32[]{:S(2)}, u32[]{:S(2)}) collective-permute-start(bf16[80,2048]{1,0:T(8,128)(2,1)S(1)} %copy-done.41), channel_id=1, source_target_pairs={{0,16},{1,17},{2,18},{3,19},{4,20},{5,21},{6,22},{7,23},{8,24},{9,... | collective-permute-start | bytes 983048 | tf_op jit(solution)/shard_map/ppermute | solution.py:55
  46.8 14.1 %collective-permute-start.9 = (bf16[2,2,96,384]{3,2,0,1:T(8,128)(2,1)S(1)}, bf16[2,2,96,384]{3,2,0,1:T(8,128)(2,1)S(1)}, u32[]{:S(2)}, u32[]{:S(2)}) collective-permute-start(bf16[2,2,96,384]{3,2,0,1:T(8,128)(2,1)S(1)} %pad_maximum_fusion.5), channel_id=1, source_target_pairs={{0,1},{1,0},{2,3},{3,2},{4,5},{5,4},{6,7},{7,6},{8,9},{9,8},{10,11... | collective-permute-start | bytes 884744 | tf_op jit(solution)/shard_map/ppermute | solution.py:55
  57.8 6.4 %collective-permute-start.2 = (bf16[64,2048]{1,0:T(8,128)(2,1)S(1)}, bf16[64,2048]{1,0:T(8,128)(2,1)S(1)}, u32[]{:S(2)}, u32[]{:S(2)}) collective-permute-start(bf16[64,2048]{1,0:T(8,128)(2,1)S(1)} %slice.145), channel_id=1, source_target_pairs={{0,4},{1,5},{2,6},{3,7},{4,0},{5,1},{6,2},{7,3},{8,12},{9,13},{10,... | collective-permute-start | bytes 786440 | tf_op jit(solution)/shard_map/ppermute | solution.py:55
  58.4 7.6 %collective-permute-start.3 = (bf16[64,2048]{1,0:T(8,128)(2,1)S(1)}, bf16[64,2048]{1,0:T(8,128)(2,1)S(1)}, u32[]{:S(2)}, u32[]{:S(2)}) collective-permute-start(bf16[64,2048]{1,0:T(8,128)(2,1)S(1)} %slice.146), channel_id=1, source_target_pairs={{0,8},{1,9},{2,10},{3,11},{4,12},{5,13},{6,14},{7,15},{8,0},{9,1},... | collective-permute-start | bytes 786440 | tf_op jit(solution)/shard_map/ppermute | solution.py:55
  67.0 74.3 %all-gather.12.cloned.1.call-start = ((), (), s32[]{:S(2)}) async-start(), calls=%async_computation.17 | async-start | bytes 3276800 | tf_op jit(solution)/shard_map/all_gather | solution.py:215
  67.0 12.5 %collective-permute-start.13 = (bf16[4,64,640]{2,1,0:T(8,128)(2,1)S(1)}, bf16[4,64,640]{2,1,0:T(8,128)(2,1)S(1)}, u32[]{:S(2)}, u32[]{:S(2)}) collective-permute-start(bf16[4,64,640]{2,1,0:T(8,128)(2,1)S(1)} %all-to-all-done), channel_id=1, source_target_pairs={{0,16},{1,17},{2,18},{3,19},{4,20},{5,21},{6,22},{7,23},{8,24},{9,... | collective-permute-start | bytes 983048 | tf_op jit(solution)/shard_map/ppermute | solution.py:55
  80.5 153.9 %all-gather.14.cloned.1.call-start = ((), (), s32[]{:S(2)}) async-start(), calls=%async_computation.23 | async-start | bytes 4718592 | tf_op jit(solution)/shard_map/all_gather | solution.py:215
  94.6 5.8 collective-permute-start.10
  102.2 39.1 %all-to-all-start.1 = ((bf16[8,64,768]{2,1,0:T(8,128)(2,1)}), bf16[8,64,768]{2,1,0:T(8,128)(2,1)S(1)}, u32[]{:S(2)}, u32[]{:S(2)}) async-start(bf16[8,64,768]{2,1,0:T(8,128)(2,1)} %copy.117), calls=%async_computation.1 | async-start | bytes 1572864 | tf_op jit(solution)/shard_map/all_to_all | solution.py:235
  146.4 47.0 %all-to-all-start.2 = ((bf16[4,128,2048]{2,1,0:T(8,128)(2,1)}), bf16[4,128,2048]{2,1,0:T(8,128)(2,1)S(1)}, u32[]{:S(2)}, u32[]{:S(2)}) async-start(bf16[4,128,2048]{2,1,0:T(8,128)(2,1)} %bitcast.315), calls=%async_computation.2 | async-start | bytes 4194304 | tf_op jit(solution)/shard_map/all_to_all | solution.py:235
  151.0 101.6 %all-gather.16.cloned.1.call-start = ((), (), s32[]{:S(2)}) async-start(), calls=%async_computation.24 | async-start | bytes 3932160 | tf_op jit(solution)/shard_map/all_gather | solution.py:215
  152.3 229.4 %reduce-scatter.6.cloned.1.call-start = ((), (), s32[]{:S(2)}) async-start(), calls=%async_computation.18 | async-start | bytes 3932160 | tf_op jit(solution)/shard_map/reduce_scatter | solution.py:219
  152.5 20.9 %collective-permute-start.14 = (bf16[192,2048]{1,0:T(8,128)(2,1)}, bf16[192,2048]{1,0:T(8,128)(2,1)}, u32[]{:S(2)}, u32[]{:S(2)}) collective-permute-start(bf16[192,2048]{1,0:T(8,128)(2,1)} %refs_0_), channel_id=1, source_target_pairs={{0,2},{1,3},{2,0},{3,1},{4,6},{5,7},{6,4},{7,5},{8,10},{9,11},{10,... | collective-permute-start | bytes 2359304 | tf_op jit(solution)/shard_map/ppermute | solution.py:55
  153.2 32.7 %collective-permute-start.17 = (bf16[192,2048]{1,0:T(8,128)(2,1)}, bf16[192,2048]{1,0:T(8,128)(2,1)S(1)}, u32[]{:S(2)}, u32[]{:S(2)}) collective-permute-start(bf16[192,2048]{1,0:T(8,128)(2,1)} %refs_0_.1), channel_id=1, source_target_pairs={{0,2},{1,3},{2,0},{3,1},{4,6},{5,7},{6,4},{7,5},{8,10},{9,11},{10,... | collective-permute-start | bytes 2359304 | tf_op jit(solution)/shard_map/ppermute | solution.py:55
  154.6 31.3 %collective-permute-start.15 = (bf16[192,2048]{1,0:T(8,128)(2,1)}, bf16[192,2048]{1,0:T(8,128)(2,1)}, u32[]{:S(2)}, u32[]{:S(2)}) collective-permute-start(bf16[192,2048]{1,0:T(8,128)(2,1)} %refs_0_), channel_id=1, source_target_pairs={{0,1},{1,0},{2,3},{3,2},{4,5},{5,4},{6,7},{7,6},{8,9},{9,8},{10,11... | collective-permute-start | bytes 2359304 | tf_op jit(solution)/shard_map/ppermute | solution.py:55
  173.4 12.6 %collective-permute-start.16 = (bf16[192,2048]{1,0:T(8,128)(2,1)}, bf16[192,2048]{1,0:T(8,128)(2,1)}, u32[]{:S(2)}, u32[]{:S(2)}) collective-permute-start(bf16[192,2048]{1,0:T(8,128)(2,1)} %collective-permute-done.14.refs_1_), channel_id=1, source_target_pairs={{0,1},{1,0},{2,3},{3,2},{4,5},{5,4},{6,7},{7,6},{8,9},{9,8},{10,11... | collective-permute-start | bytes 2359304 | tf_op jit(solution)/shard_map/ppermute | solution.py:55
  173.4 16.3 %collective-permute-start.18 = (bf16[192,2048]{1,0:T(8,128)(2,1)}, bf16[192,2048]{1,0:T(8,128)(2,1)}, u32[]{:S(2)}, u32[]{:S(2)}) collective-permute-start(bf16[192,2048]{1,0:T(8,128)(2,1)} %refs_0_.1), channel_id=1, source_target_pairs={{0,1},{1,0},{2,3},{3,2},{4,5},{5,4},{6,7},{7,6},{8,9},{9,8},{10,11... | collective-permute-start | bytes 2359304 | tf_op jit(solution)/shard_map/ppermute | solution.py:55
  198.2 30.4 %collective-permute-start.21 = (bf16[128,2048]{1,0:T(8,128)(2,1)S(1)}, bf16[128,2048]{1,0:T(8,128)(2,1)S(1)}, u32[]{:S(2)}, u32[]{:S(2)}) collective-permute-start(bf16[128,2048]{1,0:T(8,128)(2,1)S(1)} %multiply_convert_fusion.4.refs_0_), channel_id=1, source_target_pairs={{0,8},{1,9},{2,10},{3,11},{4,12},{5,13},{6,14},{7,15},{8,0},{9,1},... | collective-permute-start | bytes 1572872 | tf_op jit(solution)/shard_map/ppermute | solution.py:55
  200.5 30.6 %collective-permute-start.20 = (bf16[128,2048]{1,0:T(8,128)(2,1)S(1)}, bf16[128,2048]{1,0:T(8,128)(2,1)S(1)}, u32[]{:S(2)}, u32[]{:S(2)}) collective-permute-start(bf16[128,2048]{1,0:T(8,128)(2,1)S(1)} %multiply_convert_fusion.4.refs_0_), channel_id=1, source_target_pairs={{0,4},{1,5},{2,6},{3,7},{4,0},{5,1},{6,2},{7,3},{8,12},{9,13},{10,... | collective-permute-start | bytes 1572872 | tf_op jit(solution)/shard_map/ppermute | solution.py:55
  200.5 33.9 %collective-permute-start.24 = (bf16[128,2048]{1,0:T(8,128)(2,1)S(1)}, bf16[128,2048]{1,0:T(8,128)(2,1)}, u32[]{:S(2)}, u32[]{:S(2)}) collective-permute-start(bf16[128,2048]{1,0:T(8,128)(2,1)S(1)} %multiply_convert_fusion.4.refs_0_), channel_id=1, source_target_pairs={{0,16},{1,17},{2,18},{3,19},{4,20},{5,21},{6,22},{7,23},{8,24},{9,... | collective-permute-start | bytes 1572872 | tf_op jit(solution)/shard_map/ppermute | solution.py:55
  229.4 9.4 %collective-permute-start.22 = (bf16[64,2048]{1,0:T(8,128)(2,1)}, bf16[64,2048]{1,0:T(8,128)(2,1)S(1)}, u32[]{:S(2)}, u32[]{:S(2)}) collective-permute-start(bf16[64,2048]{1,0:T(8,128)(2,1)} %slice.157), channel_id=1, source_target_pairs={{0,4},{1,5},{2,6},{3,7},{4,0},{5,1},{6,2},{7,3},{8,12},{9,13},{10,... | collective-permute-start | bytes 786440 | tf_op jit(solution)/shard_map/ppermute | solution.py:55
  231.9 10.0 %collective-permute-start.23 = (bf16[64,2048]{1,0:T(8,128)(2,1)}, bf16[64,2048]{1,0:T(8,128)(2,1)}, u32[]{:S(2)}, u32[]{:S(2)}) collective-permute-start(bf16[64,2048]{1,0:T(8,128)(2,1)} %slice.158), channel_id=1, source_target_pairs={{0,8},{1,9},{2,10},{3,11},{4,12},{5,13},{6,14},{7,15},{8,0},{9,1},... | collective-permute-start | bytes 786440 | tf_op jit(solution)/shard_map/ppermute | solution.py:55
  234.4 36.3 %collective-permute-start.25 = (bf16[128,2048]{1,0:T(8,128)(2,1)}, bf16[128,2048]{1,0:T(8,128)(2,1)}, u32[]{:S(2)}, u32[]{:S(2)}) collective-permute-start(bf16[128,2048]{1,0:T(8,128)(2,1)} %collective-permute-done.24.refs_0_), channel_id=1, source_target_pairs={{0,4},{1,5},{2,6},{3,7},{4,0},{5,1},{6,2},{7,3},{8,12},{9,13},{10,... | collective-permute-start | bytes 1572872 | tf_op jit(solution)/shard_map/ppermute | solution.py:55
  234.7 36.0 %collective-permute-start.26 = (bf16[128,2048]{1,0:T(8,128)(2,1)}, bf16[128,2048]{1,0:T(8,128)(2,1)}, u32[]{:S(2)}, u32[]{:S(2)}) collective-permute-start(bf16[128,2048]{1,0:T(8,128)(2,1)} %collective-permute-done.24.refs_0_), channel_id=1, source_target_pairs={{0,8},{1,9},{2,10},{3,11},{4,12},{5,13},{6,14},{7,15},{8,0},{9,1},... | collective-permute-start | bytes 1572872 | tf_op jit(solution)/shard_map/ppermute | solution.py:55
  234.7 35.9 %collective-permute-start.27 = (bf16[128,2048]{1,0:T(8,128)(2,1)}, bf16[128,2048]{1,0:T(8,128)(2,1)}, u32[]{:S(2)}, u32[]{:S(2)}) collective-permute-start(bf16[128,2048]{1,0:T(8,128)(2,1)} %collective-permute-done.24.refs_0_), channel_id=1, source_target_pairs={{0,12},{1,13},{2,14},{3,15},{4,8},{5,9},{6,10},{7,11},{8,4},{9,5},... | collective-permute-start | bytes 1572872 | tf_op jit(solution)/shard_map/ppermute | solution.py:55
  287.7 205.5 %reduce-scatter.12.cloned.1.call-start = ((), (), s32[]{:S(2)}) async-start(), calls=%async_computation.21 | async-start | bytes 3932160 | tf_op jit(solution)/shard_map/reduce_scatter | solution.py:219
  303.1 30.1 %all-to-all-start.3 = ((bf16[4,128,2048]{2,1,0:T(8,128)(2,1)}), bf16[4,128,2048]{2,1,0:T(8,128)(2,1)}, u32[]{:S(2)}, u32[]{:S(2)}) async-start(bf16[4,128,2048]{2,1,0:T(8,128)(2,1)} %bitcast.317), calls=%async_computation.3 | async-start | bytes 4194304 | tf_op jit(solution)/shard_map/all_to_all | solution.py:235
  308.1 187.7 %reduce-scatter.14.cloned.1.call-start = ((), (), s32[]{:S(2)}) async-start(), calls=%async_computation.22 | async-start | bytes 3932160 | tf_op jit(solution)/shard_map/reduce_scatter | solution.py:219
  335.8 38.3 %all-to-all-start.4 = ((bf16[4,128,2048]{2,1,0:T(8,128)(2,1)}), bf16[4,128,2048]{2,1,0:T(8,128)(2,1)}, u32[]{:S(2)}, u32[]{:S(2)}) async-start(bf16[4,128,2048]{2,1,0:T(8,128)(2,1)} %bitcast.314), calls=%async_computation.4 | async-start | bytes 4194304 | tf_op jit(solution)/shard_map/all_to_all | solution.py:235
  340.9 35.6 %collective-permute-start.28 = (bf16[128,2048]{1,0:T(8,128)(2,1)S(1)}, bf16[128,2048]{1,0:T(8,128)(2,1)S(1)}, u32[]{:S(2)}, u32[]{:S(2)}) collective-permute-start(bf16[128,2048]{1,0:T(8,128)(2,1)S(1)} %reduce_sum.131), channel_id=1, source_target_pairs={{0,16},{1,17},{2,18},{3,19},{4,20},{5,21},{6,22},{7,23},{8,24},{9,... | collective-permute-start | bytes 1572872 | tf_op jit(solution)/shard_map/ppermute | solution.py:55
  379.2 18.3 %collective-permute-start.30 = (bf16[128,2048]{1,0:T(8,128)(2,1)S(1)}, bf16[128,2048]{1,0:T(8,128)(2,1)S(1)}, u32[]{:S(2)}, u32[]{:S(2)}) collective-permute-start(bf16[128,2048]{1,0:T(8,128)(2,1)S(1)} %get-tuple-element.126.refs_0_), channel_id=1, source_target_pairs={{0,8},{1,9},{2,10},{3,11},{4,12},{5,13},{6,14},{7,15},{8,0},{9,1},... | collective-permute-start | bytes 1572872 | tf_op jit(solution)/shard_map/ppermute | solution.py:55
  381.5 19.1 %collective-permute-start.29 = (bf16[128,2048]{1,0:T(8,128)(2,1)S(1)}, bf16[128,2048]{1,0:T(8,128)(2,1)S(1)}, u32[]{:S(2)}, u32[]{:S(2)}) collective-permute-start(bf16[128,2048]{1,0:T(8,128)(2,1)S(1)} %get-tuple-element.126.refs_0_), channel_id=1, source_target_pairs={{0,4},{1,5},{2,6},{3,7},{4,0},{5,1},{6,2},{7,3},{8,12},{9,13},{10,... | collective-permute-start | bytes 1572872 | tf_op jit(solution)/shard_map/ppermute | solution.py:55
  383.9 29.6 %collective-permute-start.33 = (bf16[4,64,768]{2,1,0:T(8,128)(2,1)}, bf16[4,64,768]{2,1,0:T(8,128)(2,1)S(1)}, u32[]{:S(2)}, u32[]{:S(2)}) collective-permute-start(bf16[4,64,768]{2,1,0:T(8,128)(2,1)} %get-tuple-element.308), channel_id=1, source_target_pairs={{0,16},{1,17},{2,18},{3,19},{4,20},{5,21},{6,22},{7,23},{8,24},{9,... | collective-permute-start | bytes 1179656 | tf_op jit(solution)/shard_map/ppermute | solution.py:55
  398.3 15.2 %collective-permute-start.31 = (bf16[64,2048]{1,0:T(8,128)(2,1)}, bf16[64,2048]{1,0:T(8,128)(2,1)}, u32[]{:S(2)}, u32[]{:S(2)}) collective-permute-start(bf16[64,2048]{1,0:T(8,128)(2,1)} %slice.159), channel_id=1, source_target_pairs={{0,4},{1,5},{2,6},{3,7},{4,0},{5,1},{6,2},{7,3},{8,12},{9,13},{10,... | collective-permute-start | bytes 786440 | tf_op jit(solution)/shard_map/ppermute | solution.py:55
  401.3 12.2 %collective-permute-start.32 = (bf16[64,2048]{1,0:T(8,128)(2,1)}, bf16[64,2048]{1,0:T(8,128)(2,1)}, u32[]{:S(2)}, u32[]{:S(2)}) collective-permute-start(bf16[64,2048]{1,0:T(8,128)(2,1)} %slice.160), channel_id=1, source_target_pairs={{0,8},{1,9},{2,10},{3,11},{4,12},{5,13},{6,14},{7,15},{8,0},{9,1},... | collective-permute-start | bytes 786440 | tf_op jit(solution)/shard_map/ppermute | solution.py:55
  408.9 31.1 %all-to-all-start.5 = ((bf16[4,128,2048]{2,1,0:T(8,128)(2,1)}), bf16[4,128,2048]{2,1,0:T(8,128)(2,1)}, u32[]{:S(2)}, u32[]{:S(2)}) async-start(bf16[4,128,2048]{2,1,0:T(8,128)(2,1)} %bitcast.316), calls=%async_computation.6 | async-start | bytes 4194304 | tf_op jit(solution)/shard_map/all_to_all | solution.py:235
  413.4 107.2 %reduce-scatter.8.cloned.1.call-start = ((), (), s32[]{:S(2)}) async-start(), calls=%async_computation.19 | async-start | bytes 3276800 | tf_op jit(solution)/shard_map/reduce_scatter | solution.py:219
  433.3 95.3 %reduce-scatter.10.cloned.1.call-start = ((), (), s32[]{:S(2)}) async-start(), calls=%async_computation.20 | async-start | bytes 3276800 | tf_op jit(solution)/shard_map/reduce_scatter | solution.py:219
  434.1 11.0 %collective-permute-start.34 = (f32[4,2,2,640]{3,2,1,0:T(2,128)S(1)}, f32[4,2,2,640]{3,2,1,0:T(2,128)S(1)}, u32[]{:S(2)}, u32[]{:S(2)}) collective-permute-start(f32[4,2,2,640]{3,2,1,0:T(2,128)S(1)} %bitcast.337), channel_id=1, source_target_pairs={{0,16},{1,17},{2,18},{3,19},{4,20},{5,21},{6,22},{7,23},{8,24},{9,... | collective-permute-start | bytes 122888 | tf_op jit(solution)/shard_map/ppermute | solution.py:55
  442.2 23.7 %collective-permute-start.36 = (bf16[128,2048]{1,0:T(8,128)(2,1)S(1)}, bf16[128,2048]{1,0:T(8,128)(2,1)}, u32[]{:S(2)}, u32[]{:S(2)}) collective-permute-start(bf16[128,2048]{1,0:T(8,128)(2,1)S(1)} %reduce_sum.134), channel_id=1, source_target_pairs={{0,16},{1,17},{2,18},{3,19},{4,20},{5,21},{6,22},{7,23},{8,24},{9,... | collective-permute-start | bytes 1572872 | tf_op jit(solution)/shard_map/ppermute | solution.py:55
  474.2 8.3 %collective-permute-start.37 = (bf16[2,2,80,2048]{3,2,0,1:T(8,128)(2,1)}, bf16[2,2,80,2048]{3,2,0,1:T(8,128)(2,1)}, u32[]{:S(2)}, u32[]{:S(2)}) collective-permute-start(bf16[2,2,80,2048]{3,2,0,1:T(8,128)(2,1)} %bitcast.276), channel_id=1, source_target_pairs={{0,1},{1,0},{2,3},{3,2},{4,5},{5,4},{6,7},{7,6},{8,9},{9,8},{10,11... | collective-permute-start | bytes 3932168 | tf_op jit(solution)/shard_map/ppermute | solution.py:55
  485.5 33.0 %all-to-all-start.6 = ((bf16[4,128,2048]{2,1,0:T(8,128)(2,1)}), bf16[4,128,2048]{2,1,0:T(8,128)(2,1)}, u32[]{:S(2)}, u32[]{:S(2)}) async-start(bf16[4,128,2048]{2,1,0:T(8,128)(2,1)} %bitcast.285), calls=%async_computation.8 | async-start | bytes 4194304 | tf_op jit(solution)/shard_map/all_to_all | solution.py:235
  503.4 55.8 %collective-permute-start.41 = (bf16[128,2048]{1,0:T(8,128)(2,1)}, bf16[128,2048]{1,0:T(8,128)(2,1)}, u32[]{:S(2)}, u32[]{:S(2)}) collective-permute-start(bf16[128,2048]{1,0:T(8,128)(2,1)} %get-tuple-element.296), channel_id=1, source_target_pairs={{0,12},{1,13},{2,14},{3,15},{4,8},{5,9},{6,10},{7,11},{8,4},{9,5},... | collective-permute-start | bytes 1572872 | tf_op jit(solution)/shard_map/ppermute | solution.py:55
  504.9 55.2 %collective-permute-start.40 = (bf16[128,2048]{1,0:T(8,128)(2,1)}, bf16[128,2048]{1,0:T(8,128)(2,1)}, u32[]{:S(2)}, u32[]{:S(2)}) collective-permute-start(bf16[128,2048]{1,0:T(8,128)(2,1)} %get-tuple-element.297), channel_id=1, source_target_pairs={{0,8},{1,9},{2,10},{3,11},{4,12},{5,13},{6,14},{7,15},{8,0},{9,1},... | collective-permute-start | bytes 1572872 | tf_op jit(solution)/shard_map/ppermute | solution.py:55
  505.1 55.0 %collective-permute-start.39 = (bf16[128,2048]{1,0:T(8,128)(2,1)}, bf16[128,2048]{1,0:T(8,128)(2,1)}, u32[]{:S(2)}, u32[]{:S(2)}) collective-permute-start(bf16[128,2048]{1,0:T(8,128)(2,1)} %get-tuple-element.298), channel_id=1, source_target_pairs={{0,4},{1,5},{2,6},{3,7},{4,0},{5,1},{6,2},{7,3},{8,12},{9,13},{10,... | collective-permute-start | bytes 1572872 | tf_op jit(solution)/shard_map/ppermute | solution.py:55
  506.9 30.0 %collective-permute-start.45 = (bf16[2,2,80,384]{3,2,0,1:T(8,128)(2,1)}, bf16[2,2,80,384]{3,2,0,1:T(8,128)(2,1)}, u32[]{:S(2)}, u32[]{:S(2)}) collective-permute-start(bf16[2,2,80,384]{3,2,0,1:T(8,128)(2,1)} %bitcast.278), channel_id=1, source_target_pairs={{0,1},{1,0},{2,3},{3,2},{4,5},{5,4},{6,7},{7,6},{8,9},{9,8},{10,11... | collective-permute-start | bytes 737288 | tf_op jit(solution)/shard_map/ppermute | solution.py:55
  506.9 18.2 %collective-permute-start.43 = (bf16[2,80,2048]{2,1,0:T(8,128)(2,1)S(1)}, bf16[2,80,2048]{2,1,0:T(8,128)(2,1)}, u32[]{:S(2)}, u32[]{:S(2)}) collective-permute-start(bf16[2,80,2048]{2,1,0:T(8,128)(2,1)S(1)} %dynamic-slice_bitcast_fusion), channel_id=1, source_target_pairs={{0,2},{1,3},{2,0},{3,1},{4,6},{5,7},{6,4},{7,5},{8,10},{9,11},{10,... | collective-permute-start | bytes 1966088 | tf_op jit(solution)/shard_map/ppermute | solution.py:55
  525.0 24.2 %collective-permute-start.38 = (bf16[4,64,640]{2,1,0:T(8,128)(2,1)}, bf16[4,64,640]{2,1,0:T(8,128)(2,1)}, u32[]{:S(2)}, u32[]{:S(2)}) collective-permute-start(bf16[4,64,640]{2,1,0:T(8,128)(2,1)} %dynamic-slice_bitcast_fusion.9), channel_id=1, source_target_pairs={{0,16},{1,17},{2,18},{3,19},{4,20},{5,21},{6,22},{7,23},{8,24},{9,... | collective-permute-start | bytes 983048 | tf_op jit(solution)/shard_map/ppermute | solution.py:55
  530.9 17.7 %all-to-all-start.7 = ((bf16[32,2,64]{2,1,0:T(2,128)(2,1)}), bf16[32,2,64]{2,1,0:T(2,128)(2,1)S(1)}, u32[]{:S(2)}, u32[]{:S(2)}) async-start(bf16[32,2,64]{2,1,0:T(2,128)(2,1)} %copy.123), calls=%async_computation.10 | async-start | bytes 32768 | tf_op jit(solution)/shard_map/all_to_all | solution.py:938
  536.9 30.3 %collective-permute-start.44 = (bf16[80,2048]{1,0:T(8,128)(2,1)}, bf16[80,2048]{1,0:T(8,128)(2,1)}, u32[]{:S(2)}, u32[]{:S(2)}) collective-permute-start(bf16[80,2048]{1,0:T(8,128)(2,1)} %dynamic-slice_bitcast_fusion.7), channel_id=1, source_target_pairs={{0,16},{1,17},{2,18},{3,19},{4,20},{5,21},{6,22},{7,23},{8,24},{9,... | collective-permute-start | bytes 983048 | tf_op jit(solution)/shard_map/ppermute | solution.py:55
  549.2 38.5 %collective-permute-start.42 = (bf16[80,2048]{1,0:T(8,128)(2,1)}, bf16[80,2048]{1,0:T(8,128)(2,1)}, u32[]{:S(2)}, u32[]{:S(2)}) collective-permute-start(bf16[80,2048]{1,0:T(8,128)(2,1)} %dynamic-slice_bitcast_fusion.8), channel_id=1, source_target_pairs={{0,16},{1,17},{2,18},{3,19},{4,20},{5,21},{6,22},{7,23},{8,24},{9,... | collective-permute-start | bytes 983048 | tf_op jit(solution)/shard_map/ppermute | solution.py:55
  553.6 24.7 %all-to-all-start.8 = ((bf16[4,64,640]{2,1,0:T(8,128)(2,1)}), bf16[4,64,640]{2,1,0:T(8,128)(2,1)}, u32[]{:S(2)}, u32[]{:S(2)}) async-start(bf16[4,64,640]{2,1,0:T(8,128)(2,1)} %fusion.44), calls=%async_computation.11 | async-start | bytes 655360 | tf_op jit(solution)/shard_map/all_to_all | solution.py:235
  559.2 8.0 %collective-permute-start.46 = (bf16[2,80,384]{2,1,0:T(8,128)(2,1)S(1)}, bf16[2,80,384]{2,1,0:T(8,128)(2,1)S(1)}, u32[]{:S(2)}, u32[]{:S(2)}) collective-permute-start(bf16[2,80,384]{2,1,0:T(8,128)(2,1)S(1)} %dynamic-slice_bitcast_fusion.10), channel_id=1, source_target_pairs={{0,2},{1,3},{2,0},{3,1},{4,6},{5,7},{6,4},{7,5},{8,10},{9,11},{10,... | collective-permute-start | bytes 368648 | tf_op jit(solution)/shard_map/ppermute | solution.py:55
  567.2 18.2 %collective-permute-start.47 = (bf16[80,384]{1,0:T(8,128)(2,1)S(1)}, bf16[80,384]{1,0:T(8,128)(2,1)S(1)}, u32[]{:S(2)}, u32[]{:S(2)}) collective-permute-start(bf16[80,384]{1,0:T(8,128)(2,1)S(1)} %dynamic-slice_bitcast_fusion.11), channel_id=1, source_target_pairs={{0,16},{1,17},{2,18},{3,19},{4,20},{5,21},{6,22},{7,23},{8,24},{9,... | collective-permute-start | bytes 184328 | tf_op jit(solution)/shard_map/ppermute | solution.py:55
  578.3 14.7 %all-to-all-start.9 = ((bf16[4,2,64,768]{3,2,1,0:T(8,128)(2,1)}), bf16[4,2,64,768]{3,2,1,0:T(8,128)(2,1)S(1)}, u32[]{:S(2)}, u32[]{:S(2)}) async-start(bf16[4,2,64,768]{3,2,1,0:T(8,128)(2,1)} %pad_maximum_fusion), calls=%async_computation.14 | async-start | bytes 1572864 | tf_op jit(solution)/shard_map/all_to_all | solution.py:235
  (70 other events, 644.3 us)
Sparse Core Ops, SparseCore 0:
  24.0 30.9 all-gather.7
  67.1 25.8 all-gather.9
  94.5 25.5 all-gather.11
  122.1 98.0 all-gather.13
  221.6 30.8 all-gather.15
  287.8 37.9 reduce-scatter.5
  328.5 37.9 reduce-scatter.11
  369.1 37.9 reduce-scatter.13
  433.4 35.9 reduce-scatter.7
  474.4 38.6 reduce-scatter.9
